TPU v7x, 32 devices: a whole 2x2x4 slice. The times are simulated.
32 devices in a mesh: src: 4 (over y, core), tgt: 8 (over z, x).
Axes of the slice: x: 2, y: 2, z: 4, core: 2. Of those that a mesh axis runs over, the one named last changes fastest.
Arguments:
- source: bfloat16 [8192, 128], P('src'), may hold values from -6 to 6
- target: bfloat16 [8192, 128], P('tgt'), may hold values from -5 to 5
- start_map: float32 [128, 128], replicated, may hold values from -1 to 1
- warm_potential: float32 [8192], P('tgt'), may hold values from -60 to 24
Outputs:
- row_potential: float32 [8192], P('src')
- col_potential: float32 [8192], P('tgt')
- new_map: float32 [128, 128], replicated
All inputs are finite; a program needn't handle non-finite values.
Results may differ from a plain program's by a relative error of at most 0.0078.
Values sent between devices are 32-bit elements; how exact they have to be, the bound alone decides.
No kernel may reach another device: no remote copies, remote signals or barrier semaphores. Data moves between devices by JAX's collectives and lax.ppermute only.
A program may use at most 64 MiB of HBM per device.

v0:
```python
import functools
import math

import jax
import jax.numpy as jnp
from jax import lax
from jax.experimental import pallas as pl
from jax.experimental.pallas import tpu as pltpu
from jax.sharding import PartitionSpec as P

NEWTON = 10
EPS = 0.05
LANES = 128
CHUNK = 256
VMEM_LIMIT = 40 * 1024 * 1024

F32 = jnp.float32
BF16 = jnp.bfloat16


def call(body, name, out_shape, scratch=(), flops=0, space=pltpu.VMEM):
    return lambda *args: pl.pallas_call(
        body,
        name=name,
        out_shape=out_shape,
        in_specs=[pl.BlockSpec(memory_space=space)] * len(args),
        out_specs=jax.tree.map(lambda _: pl.BlockSpec(memory_space=pltpu.VMEM), out_shape),
        scratch_shapes=scratch,
        compiler_params=pltpu.CompilerParams(vmem_limit_bytes=VMEM_LIMIT),
        cost_estimate=pl.CostEstimate(flops=flops, bytes_accessed=8 << 20, transcendentals=0),
    )(*args)


def eye_mask(shift=0):
    shape = (LANES, LANES)
    row, lane = (lax.broadcasted_iota(jnp.int32, shape, k) for k in range(2))
    return (row + shift) % LANES == lane if shift else row == lane


def to_lanes(column, shift=0):
    wide = jnp.broadcast_to(column, (LANES, LANES))
    return jnp.sum(jnp.where(eye_mask(shift), wide, 0.0), axis=0, keepdims=True)


def to_column(row):
    wide = jnp.broadcast_to(row, (LANES, LANES))
    return jnp.broadcast_to(jnp.sum(jnp.where(eye_mask(), wide, 0.0), axis=1, keepdims=True), (LANES, LANES))


def split(x):
    high = x.astype(BF16)
    return high, (x - high.astype(F32)).astype(BF16)


def lane_parts(wide, first, fill):
    lane = lax.broadcasted_iota(jnp.int32, wide.shape, 1)
    out = jnp.where((lane >= fill) & (lane < fill + 3), 1.0, 0.0)
    rest = wide
    for k in range(3):
        part = rest.astype(BF16).astype(F32)
        out = jnp.where(lane == first + k, part, out)
        rest = rest - part
    return out.astype(BF16)


def tree(combine, values):
    values = list(values)
    while len(values) > 1:
        values = [combine(a, b) for a, b in zip(values[::2], values[1::2])]
    return values[0]


def tree_sum(parts):
    return tree(jnp.add, parts)


def tree_lse(unit, parts):
    peak = tree(jnp.maximum, parts)
    total = tree(jnp.add, [jnp.exp2(unit * (part - peak)) for part in parts])
    return peak + jnp.log(total) * (1.0 / (unit * math.log(2.0)))


def received(refs, group):
    if len(refs[0].shape) == 3:
        return [refs[0][k] for k in range(group)], refs[1:]
    return [ref[...] for ref in refs[:group]], refs[group:]


def dot_t(a, b):
    return lax.dot_general(a, b, (((1,), (1,)), ((), ())), preferred_element_type=F32)


def row_first(
    unit, scale, source_hbm, map_hbm, target_hbm, pot_hbm, left_out, right_out, lse_out, turned_out,
    source, start_map, target, pot, work, peaks, totals, sums, sems,
):
    copies = [
        pltpu.make_async_copy(src, dst, sems.at[k])
        for k, (src, dst) in enumerate(
            [(source_hbm, source), (map_hbm, start_map), (target_hbm, target), (pot_hbm, pot)]
        )
    ]
    for copy in copies:
        copy.start()
    for copy in copies:
        copy.wait()
    width = source.shape[1]
    rows = source.shape[0]
    for part in range(target.shape[0] // LANES):
        at = pl.ds(part * LANES, LANES)
        right_out[at, :width] = target[at, :]
        right_out[at, width:] = lane_parts(to_column(pot[:, at] * (1.0 / scale)), 0, 3)
    left_out[...] = jnp.dot(source[...], start_map[...].astype(BF16), preferred_element_type=F32).astype(BF16)
    for part in range(rows // LANES):
        here = slice(part * LANES, (part + 1) * LANES)
        turned_out[:, here] = source[here, :].T
    lane = lax.broadcasted_iota(jnp.int32, (CHUNK, LANES), 1)
    ones = jnp.where(lane < 3, 1.0, 0.0).astype(BF16)
    group = 16
    for start in range(0, rows, CHUNK):
        left = jnp.concatenate([left_out[start : start + CHUNK, :], ones], axis=1)
        work[start : start + CHUNK, :] = dot_t(left, right_out[...])
        for at in range(start, start + CHUNK, group):
            tiles = [work[at : at + group, k : k + LANES] for k in range(0, work.shape[1], LANES)]
            peak = functools.reduce(jnp.maximum, tiles)
            peaks[at : at + group, :] = peak
            totals[at : at + group, :] = functools.reduce(jnp.add, [jnp.exp2((tile - peak) * unit) for tile in tiles])
    for part in range(rows // LANES):
        here = slice(part * LANES, (part + 1) * LANES)
        lane_peak = peaks[here, :]
        peak = jnp.max(lane_peak, axis=1, keepdims=True)
        total = jnp.sum(totals[here, :] * jnp.exp2((lane_peak - peak) * unit), axis=1, keepdims=True)
        lse_out[part : part + 1, :] = to_lanes(peak)
        sums[part : part + 1, :] = to_lanes(total)
    lse_out[...] = lse_out[...] + jnp.log(sums[...]) * (1.0 / (unit * math.log(2.0)))


def col_first(group, unit, log_rows, left_in, right, *refs):
    parts, (block_out, pot_out, peak_out, lse_out, left, work) = received(refs, group)
    row_pot = -log_rows - tree_lse(unit, parts)
    pot_out[...] = row_pot
    rows, width = left_in.shape
    cols = right.shape[0]
    left[:, :width] = left_in[...]
    for part in range(rows // LANES):
        left[part * LANES : (part + 1) * LANES, width:] = lane_parts(to_column(row_pot[part : part + 1, :]), 3, 0)
    peak = None
    for start in range(0, rows, CHUNK):
        value = dot_t(left[start : start + CHUNK, :], right[...])
        work[start : start + CHUNK, :] = value
        top = jnp.max(value.reshape(CHUNK // 8, 8, cols), axis=0)
        peak = top if peak is None else jnp.maximum(peak, top)
    peak = jnp.max(peak, axis=0, keepdims=True)
    group_rows = 16

    def sums(step, total):
        for k in range(0, LANES, group_rows):
            at = pl.ds(pl.multiple_of(step * LANES + k, group_rows), group_rows)
            value = jnp.exp2((work[at, :] - peak) * unit)
            block_out[at, :] = value.astype(BF16)
            total = total + value[:8] + value[8:]
        return total

    total = lax.fori_loop(0, rows // LANES, sums, jnp.zeros((8, cols), F32))
    peak_out[...] = peak
    lse_out[...] = peak + jnp.log(jnp.sum(total, axis=0, keepdims=True)) * (1.0 / (unit * math.log(2.0)))


def column_factors(row):
    pieces = [to_column(row[:, at : at + LANES]) for at in range(0, row.shape[1], LANES)]
    return jnp.concatenate(pieces, axis=0)


def row_sums(block, row, sums_out):
    weights = jnp.concatenate(split(column_factors(row)), axis=1)
    for start in range(0, block.shape[0], CHUNK):
        wide = jnp.dot(block[start : start + CHUNK, :], weights, preferred_element_type=F32)
        sums = wide[:, :LANES] + wide[:, LANES:]
        for part in range(CHUNK // LANES):
            at = start // LANES + part
            sums_out[at : at + 1, :] = to_lanes(sums[part * LANES : (part + 1) * LANES])


def row_second(group, unit, log_cols, block, peak, pot, *refs):
    parts, (pot_out, scale_out, sums_out) = received(refs, group)
    lse = tree_lse(unit, parts)
    pot_out[...] = pot[...] - log_cols - lse
    scale = jnp.exp2(unit * (peak[...] - lse))
    scale_out[...] = scale
    row_sums(block, scale, sums_out)


def col_later(group, ratio, block, scale, *refs):
    parts, (sums_out, factor) = received(refs, group)
    factors = ratio / tree_sum(parts)
    rows, cols = block.shape
    for part in range(rows // LANES):
        factor[part * LANES : (part + 1) * LANES, :] = to_column(factors[part : part + 1, :])
    group_rows = 16

    def sums(step, total):
        for k in range(0, LANES, group_rows):
            at = pl.ds(pl.multiple_of(step * LANES + k, group_rows), group_rows)
            value = block[at, :].astype(F32) * jnp.concatenate([factor[at, :]] * (cols // LANES), axis=1)
            total = total + value[:8] + value[8:]
        return total

    total = lax.fori_loop(0, rows // LANES, sums, jnp.zeros((8, cols), F32))
    sums_out[...] = scale[...] * jnp.sum(total, axis=0, keepdims=True)


def row_later(group, block, scale, *refs):
    parts, (sums_out,) = received(refs, group)
    row_sums(block, scale[...] / tree_sum(parts), sums_out)


def row_last(group, unit, block, scale, pot, target, *refs):
    parts, (col_out, sums_out, bary_out, other) = received(refs, group)
    totals = tree_sum(parts)
    col_out[...] = (EPS * math.log(2.0)) * (unit * pot[...] - jnp.log(totals) * (1.0 / math.log(2.0)))
    factors = column_factors(scale[...] / totals)
    high, low = split(factors)
    lane = lax.broadcasted_iota(jnp.int32, factors.shape, 1)
    sides = jnp.where(lane < LANES // 2, high.astype(F32), low.astype(F32)).astype(BF16)
    scaled = (target[:, : factors.shape[1]].astype(F32) * factors).astype(BF16)
    weights = jnp.concatenate([scaled, sides], axis=1)
    for start in range(0, block.shape[0], CHUNK):
        wide = jnp.dot(block[start : start + CHUNK, :], weights, preferred_element_type=F32)
        bary_out[start : start + CHUNK, :] = wide[:, :LANES]
        for part in range(CHUNK // LANES):
            at = start // LANES + part
            sides = wide[part * LANES : (part + 1) * LANES, LANES:]
            sums_out[at : at + 1, :] = to_lanes(sides)
            other[at : at + 1, :] = to_lanes(sides, LANES // 2)
    sums_out[...] += pltpu.roll(other[...], LANES // 2, 1)


def cross_local(group, unit, ratio, turned, bary, pot, *refs):
    parts, (row_out, *share_outs, square) = received(refs, group)
    totals = tree_sum(parts)
    row_out[...] = (EPS * math.log(2.0)) * (unit * pot[...] + jnp.log(ratio / totals) * (1.0 / math.log(2.0)))
    inverse = 1.0 / totals
    pieces = []
    for part in range(totals.shape[0]):
        piece = bary[part * LANES : (part + 1) * LANES, :] * to_column(inverse[part : part + 1, :])
        pieces.append(jnp.concatenate(split(piece), axis=1))
    cross = jnp.dot(turned[...], jnp.concatenate(pieces, axis=0), preferred_element_type=F32)
    width = square.shape[0]
    square[...] = cross[:, :width] + cross[:, width:]
    index = lax.axis_index("src")
    count = len(share_outs)
    height = width // count
    for k, out in zip(range(count - 1, -1, -1), share_outs):
        out[...] = square[pl.ds(pl.multiple_of((index ^ k) * height, height), height), :]


def share_sum(*refs):
    total = tree_sum([ref[...] for ref in refs[:-1]])
    for k in range(refs[-1].shape[0]):
        refs[-1][k] = total


def precise(a, b, axis=1):
    ah, al = split(a)
    bh, bl = split(b)
    return lax.dot_general(
        jnp.concatenate([ah, ah, al], axis=axis),
        jnp.concatenate([bh, bl, bh], axis=0),
        (((axis,), (0,)), ((), ())),
        preferred_element_type=F32,
    )


def polar(*refs):
    shares, (out, square) = refs[:-2], refs[-2:]
    index = lax.axis_index("src")
    height = shares[0].shape[0]
    for k, share in enumerate(shares):
        square[pl.ds(pl.multiple_of((index ^ k) * height, height), height), :] = share[...]
    cross = square[...]
    iterate = cross / jnp.sqrt(jnp.sum(cross * cross) + 1e-06)
    gram = precise(iterate, iterate, 0)
    for step in range(NEWTON):
        factor = jnp.where(eye_mask(), 1.5, 0.0) - 0.5 * gram
        if step < NEWTON - 1:
            gram = precise(precise(factor, gram), factor)
        iterate = precise(iterate, factor)
    out[...] = iterate


def partners(values, axis, order):
    size = lax.axis_size(axis)
    return [lax.ppermute(values[k], axis, [(me, me ^ k) for me in range(size)]) if k else values[0] for k in order]


def exchange(x, axis):
    size = lax.axis_size(axis)
    if axis == "src":
        return partners([x] * size, axis, range(size))
    return [lax.all_to_all(jnp.broadcast_to(x, (size,) + x.shape), axis, 0, 0)]


def shards(source, target, start_map, warm_potential):
    rows, width = source.shape
    cols = target.shape[0]
    n_src, n_tgt = lax.axis_size("src"), lax.axis_size("tgt")
    ratio = (cols * n_tgt) / (rows * n_src)
    scale = 1.0 / (math.sqrt(width) * EPS)
    unit = scale / math.log(2.0)
    log_rows, log_cols = math.log(rows * n_src) / scale, math.log(cols * n_tgt) / scale
    row_vec = jax.ShapeDtypeStruct((rows // LANES, LANES), F32)
    col_vec = jax.ShapeDtypeStruct((1, cols), F32)
    pot = warm_potential.reshape(1, cols)
    mac = rows * cols * width

    left, right, lse, turned = call(
        functools.partial(row_first, unit, scale),
        "row_first",
        (
            jax.ShapeDtypeStruct((rows, width), BF16),
            jax.ShapeDtypeStruct((cols, width + LANES), BF16),
            row_vec,
            jax.ShapeDtypeStruct((width, rows), BF16),
        ),
        scratch=[
            pltpu.VMEM((rows, width), BF16),
            pltpu.VMEM((width, width), F32),
            pltpu.VMEM((cols, width), BF16),
            pltpu.VMEM((1, cols), F32),
            pltpu.VMEM((rows, cols), F32),
            pltpu.VMEM((rows, LANES), F32),
            pltpu.VMEM((rows, LANES), F32),
            pltpu.VMEM(row_vec.shape, F32),
            pltpu.SemaphoreType.DMA((4,)),
        ],
        flops=4 * mac,
        space=pltpu.HBM,
    )(*[pltpu.with_memory_space_constraint(x, pltpu.HBM) for x in (source, start_map, target, pot)])
    block, row_pot, peak, lse = call(
        functools.partial(col_first, n_tgt, unit, log_rows),
        "col_first",
        (jax.ShapeDtypeStruct((rows, cols), BF16), row_vec, col_vec, col_vec),
        scratch=[pltpu.VMEM((rows, width + LANES), BF16), pltpu.VMEM((rows, cols), F32)],
        flops=4 * mac,
    )(left, right, *exchange(lse, "tgt"))
    col_pot, col_scale, sums = call(
        functools.partial(row_second, n_src, unit, log_cols), "row_second", (col_vec, col_vec, row_vec), flops=2 * mac
    )(block, peak, pot * (1.0 / scale), *exchange(lse, "src"))
    col_later_call = call(
        functools.partial(col_later, n_tgt, ratio),
        "col_later",
        col_vec,
        scratch=[pltpu.VMEM((rows, LANES), F32)],
        flops=2 * mac,
    )
    sums = col_later_call(block, col_scale, *exchange(sums, "tgt"))
    sums = call(functools.partial(row_later, n_src), "row_later", row_vec, flops=2 * mac)(
        block, col_scale, *exchange(sums, "src")
    )
    sums = col_later_call(block, col_scale, *exchange(sums, "tgt"))
    col_out, sums, bary = call(
        functools.partial(row_last, n_src, unit),
        "row_last",
        (col_vec, row_vec, jax.ShapeDtypeStruct((rows, width), F32)),
        scratch=[pltpu.VMEM(row_vec.shape, F32)],
        flops=4 * mac,
    )(block, col_scale, col_pot, right, *exchange(sums, "src"))
    square = jax.ShapeDtypeStruct((width, width), F32)
    share_shape = (width // n_src, width)
    row_out, *shares = call(
        functools.partial(cross_local, n_tgt, unit, ratio),
        "cross_local",
        (row_vec,) + (jax.ShapeDtypeStruct(share_shape, F32),) * n_src,
        scratch=[pltpu.VMEM((width, width), F32)],
        flops=2 * rows * width * width,
    )(turned, bary, row_pot, *exchange(sums, "tgt"))
    share = call(share_sum, "share_sum", jax.ShapeDtypeStruct((n_tgt,) + share_shape, F32))(
        *partners(shares[::-1], "src", range(n_src - 1, -1, -1))
    )
    share = jnp.sum(lax.all_to_all(share, "tgt", 0, 0), axis=0)
    new_map = call(polar, "polar", square, scratch=[pltpu.VMEM((width, width), F32)], flops=1 << 27)(
        *exchange(share, "src")
    )
    return row_out.reshape(rows), col_out.reshape(cols), new_map


def solution(mesh):
    placed = (P("src", None), P("tgt", None), P(), P("tgt"))
    return jax.shard_map(
        shards, mesh=mesh, in_specs=placed, out_specs=(P("src"), P("tgt"), P()), check_vma=False
    )
```

profile of v0, /device:TPU:0, one launch (start us, length us, event | category | flops | bytes accessed | tf_op | source)
XLA Modules:
  0.0 90.5 jit_solution(10209280301189122741)
XLA Ops:
  0.6 3.8 %row_first.1 = (bf16[2048,128]{1,0:T(8,128)(2,1)S(1)}, bf16[1024,256]{1,0:T(8,128)(2,1)S(1)}, f32[16,128]{1,0:T(8,128)S(1)}, bf16[128,2048]{1,0:T(8,128)(2,1)S(1)}) custom-call(bf16[2048,128]{1,0:T(8,128)(2,1)} %source_hbm.1, f32[128,128]{1,0:T(8,128)} %map_hbm.1, bf16[1024,128]{1,0:T(8,128)(2,1)} %target_hbm.1, f32[1,1024]{1,0:T(1,128)} %bitcast.5), custom_call_target="tpu_custom_call" | custom-call | flops 1073741824 | bytes 8388608 | tf_op jit(solution)/shard_map/row_first/pallas_call | solution.py:22
  4.4 14.0 %all_to_all.25.refs_0_ = f32[8,16,128]{2,1,0:T(8,128)S(1)} all-to-all(f32[8,16,128]{2,1,0:T(8,128)S(1)} %broadcast_in_dim.12), channel_id=1, replica_groups=mesh['src'=4,'tgt'=8] {'tgt'}, dimensions={0} | all-to-all | bytes 131072 | tf_op jit(solution)/shard_map/all_to_all | solution.py:300
  18.4 2.8 %col_first.1 = (bf16[2048,1024]{1,0:T(8,128)(2,1)S(1)}, f32[16,128]{1,0:T(8,128)S(1)}, f32[1,1024]{1,0:T(1,128)S(1)}, f32[1,1024]{1,0:T(1,128)S(1)}) custom-call(bf16[2048,128]{1,0:T(8,128)(2,1)S(1)} %get-tuple-element.23.left_in, bf16[1024,256]{1,0:T(8,128)(2,1)S(1)} %get-tuple-element.24.right.target, f32[8,16,128]{2,1,0:T(8,128)S(1)} %all_to_all.25.refs_0_), custom_call_target="tpu_custom_call" | custom-call | flops 1073741824 | bytes 8388608 | tf_op jit(solution)/shard_map/col_first/pallas_call | solution.py:22
  21.3 1.6 %collective-permute-start.1 = (f32[1,1024]{1,0:T(1,128)S(1)}, f32[1,1024]{1,0:T(1,128)S(1)}, u32[]{:S(2)}, u32[]{:S(2)}) collective-permute-start(f32[1,1024]{1,0:T(1,128)S(1)} %get-tuple-element.28.refs_0_), channel_id=1, source_target_pairs={{0,16},{8,24},{16,0},{24,8},{1,17},{9,25},{17,1},{25,9},{2,18},{10... | collective-permute-start | bytes 12296 | tf_op jit(solution)/shard_map/ppermute | solution.py:293
  22.9 0.3 collective-permute-start
  23.1 1.2 %collective-permute-done.2.refs_3_ = f32[1,1024]{1,0:T(1,128)S(1)} collective-permute-done((f32[1,1024]{1,0:T(1,128)S(1)}, f32[1,1024]{1,0:T(1,128)S(1)}, u32[]{:S(2)}, u32[]{:S(2)}) %collective-permute-start.2) | collective-permute-done | bytes 4128 | tf_op jit(solution)/shard_map/ppermute | solution.py:293
  24.3 0.7 collective-permute-done.1.refs_2_
  25.0 1.4 %row_second.1 = (f32[1,1024]{1,0:T(1,128)S(1)}, f32[1,1024]{1,0:T(1,128)S(1)}, f32[16,128]{1,0:T(8,128)S(1)}) custom-call(bf16[2048,1024]{1,0:T(8,128)(2,1)S(1)} %get-tuple-element.26.block, f32[1,1024]{1,0:T(1,128)S(1)} %get-tuple-element.27.peak, f32[1,1024]{1,0:T(1,128)S(1)} %bitcast.4, f32[1,1024]{1,0:T(1,128)S(1)} %get-tuple-element.28.refs_0_, ...), custom_call_target="tpu_custom_call" | custom-call | flops 536870912 | bytes 8388608 | tf_op jit(solution)/shard_map/row_second/pallas_call | solution.py:22
  26.4 9.3 %all_to_all.26.refs_0_ = f32[8,16,128]{2,1,0:T(8,128)S(1)} all-to-all(f32[8,16,128]{2,1,0:T(8,128)S(1)} %broadcast_in_dim.13), channel_id=1, replica_groups=mesh['src'=4,'tgt'=8] {'tgt'}, dimensions={0} | all-to-all | bytes 131072 | tf_op jit(solution)/shard_map/all_to_all | solution.py:300
  35.7 1.2 %col_later.2.refs_0_ = f32[1,1024]{1,0:T(1,128)S(1)} custom-call(bf16[2048,1024]{1,0:T(8,128)(2,1)S(1)} %get-tuple-element.26.block, f32[1,1024]{1,0:T(1,128)S(1)} %get-tuple-element.29.scale, f32[8,16,128]{2,1,0:T(8,128)S(1)} %all_to_all.26.refs_0_), custom_call_target="tpu_custom_call" | custom-call | flops 536870912 | bytes 8388608 | tf_op jit(solution)/shard_map/col_later/pallas_call | solution.py:22
  37.0 1.6 %collective-permute-start.4 = (f32[1,1024]{1,0:T(1,128)S(1)}, f32[1,1024]{1,0:T(1,128)S(1)}, u32[]{:S(2)}, u32[]{:S(2)}) collective-permute-start(f32[1,1024]{1,0:T(1,128)S(1)} %col_later.2.refs_0_), channel_id=1, source_target_pairs={{0,16},{8,24},{16,0},{24,8},{1,17},{9,25},{17,1},{25,9},{2,18},{10... | collective-permute-start | bytes 12296 | tf_op jit(solution)/shard_map/ppermute | solution.py:293
  38.8 1.2 %collective-permute-done.5.refs_3_ = f32[1,1024]{1,0:T(1,128)S(1)} collective-permute-done((f32[1,1024]{1,0:T(1,128)S(1)}, f32[1,1024]{1,0:T(1,128)S(1)}, u32[]{:S(2)}, u32[]{:S(2)}) %collective-permute-start.5) | collective-permute-done | bytes 4128 | tf_op jit(solution)/shard_map/ppermute | solution.py:293
  40.0 0.7 collective-permute-done.4.refs_2_
  40.6 1.4 %row_later.1 = f32[16,128]{1,0:T(8,128)S(1)} custom-call(bf16[2048,1024]{1,0:T(8,128)(2,1)S(1)} %get-tuple-element.26.block, f32[1,1024]{1,0:T(1,128)S(1)} %get-tuple-element.29.scale, f32[1,1024]{1,0:T(1,128)S(1)} %col_later.2.refs_0_, f32[1,1024]{1,0:T(1,128)S(1)} %collective-permute-done.3.refs_1_, f32[1,1024]{1,0:T(1,128)S(1)} %collective-permute-done.4.refs_2_, ...), custom_call_target="tpu_custom_call" | custom-call | flops 536870912 | bytes 8388608 | tf_op jit(solution)/shard_map/row_later/pallas_call | solution.py:22
  42.0 9.3 %all_to_all.27.refs_0_ = f32[8,16,128]{2,1,0:T(8,128)S(1)} all-to-all(f32[8,16,128]{2,1,0:T(8,128)S(1)} %broadcast_in_dim.14), channel_id=1, replica_groups=mesh['src'=4,'tgt'=8] {'tgt'}, dimensions={0} | all-to-all | bytes 131072 | tf_op jit(solution)/shard_map/all_to_all | solution.py:300
  51.3 1.2 %col_later.3.refs_0_ = f32[1,1024]{1,0:T(1,128)S(1)} custom-call(bf16[2048,1024]{1,0:T(8,128)(2,1)S(1)} %get-tuple-element.26.block, f32[1,1024]{1,0:T(1,128)S(1)} %get-tuple-element.29.scale, f32[8,16,128]{2,1,0:T(8,128)S(1)} %all_to_all.27.refs_0_), custom_call_target="tpu_custom_call" | custom-call | flops 536870912 | bytes 8388608 | tf_op jit(solution)/shard_map/col_later/pallas_call | solution.py:22
  52.6 1.6 %collective-permute-start.7 = (f32[1,1024]{1,0:T(1,128)S(1)}, f32[1,1024]{1,0:T(1,128)S(1)}, u32[]{:S(2)}, u32[]{:S(2)}) collective-permute-start(f32[1,1024]{1,0:T(1,128)S(1)} %col_later.3.refs_0_), channel_id=1, source_target_pairs={{0,16},{8,24},{16,0},{24,8},{1,17},{9,25},{17,1},{25,9},{2,18},{10... | collective-permute-start | bytes 12296 | tf_op jit(solution)/shard_map/ppermute | solution.py:293
  54.5 1.2 %collective-permute-done.8.refs_3_ = f32[1,1024]{1,0:T(1,128)S(1)} collective-permute-done((f32[1,1024]{1,0:T(1,128)S(1)}, f32[1,1024]{1,0:T(1,128)S(1)}, u32[]{:S(2)}, u32[]{:S(2)}) %collective-permute-start.8) | collective-permute-done | bytes 4128 | tf_op jit(solution)/shard_map/ppermute | solution.py:293
  55.6 0.7 collective-permute-done.7.refs_2_
  56.3 2.0 %row_last.1 = (f32[1,1024]{1,0:T(1,128)}, f32[16,128]{1,0:T(8,128)S(1)}, f32[2048,128]{1,0:T(8,128)S(1)}) custom-call(bf16[2048,1024]{1,0:T(8,128)(2,1)S(1)} %get-tuple-element.26.block, f32[1,1024]{1,0:T(1,128)S(1)} %get-tuple-element.29.scale, f32[1,1024]{1,0:T(1,128)S(1)} %get-tuple-element.30.pot, bf16[1024,256]{1,0:T(8,128)(2,1)S(1)} %get-tuple-element.24.right.target, ...), custom_call_target="tpu_custom_call" | custom-call | flops 1073741824 | bytes 8388608 | tf_op jit(solution)/shard_map/row_last/pallas_call | solution.py:22
  58.3 9.3 %all_to_all.28.refs_0_ = f32[8,16,128]{2,1,0:T(8,128)S(1)} all-to-all(f32[8,16,128]{2,1,0:T(8,128)S(1)} %broadcast_in_dim.15), channel_id=1, replica_groups=mesh['src'=4,'tgt'=8] {'tgt'}, dimensions={0} | all-to-all | bytes 131072 | tf_op jit(solution)/shard_map/all_to_all | solution.py:300
  67.5 1.0 %cross_local.1 = (f32[16,128]{1,0:T(8,128)}, f32[32,128]{1,0:T(8,128)S(1)}, f32[32,128]{1,0:T(8,128)S(1)}, f32[32,128]{1,0:T(8,128)S(1)}, f32[32,128]{1,0:T(8,128)S(1)}) custom-call(bf16[128,2048]{1,0:T(8,128)(2,1)S(1)} %get-tuple-element.22.turned, f32[2048,128]{1,0:T(8,128)S(1)} %get-tuple-element.32.bary, f32[16,128]{1,0:T(8,128)S(1)} %get-tuple-element.33.pot, ...), custom_call_target="tpu_custom_call" | custom-call | flops 67108864 | bytes 8388608 | tf_op jit(solution)/shard_map/cross_local/pallas_call | solution.py:22
  68.6 1.6 %collective-permute-start.10 = (f32[32,128]{1,0:T(8,128)S(1)}, f32[32,128]{1,0:T(8,128)S(1)}, u32[]{:S(2)}, u32[]{:S(2)}) collective-permute-start(f32[32,128]{1,0:T(8,128)S(1)} %get-tuple-element.38), channel_id=1, source_target_pairs={{0,16},{8,24},{16,0},{24,8},{1,17},{9,25},{17,1},{25,9},{2,18},{10... | collective-permute-start | bytes 49160 | tf_op jit(solution)/shard_map/ppermute | solution.py:293
  70.1 0.3 collective-permute-start.11
  70.4 1.4 %collective-permute-done.9.refs_0_ = f32[32,128]{1,0:T(8,128)S(1)} collective-permute-done((f32[32,128]{1,0:T(8,128)S(1)}, f32[32,128]{1,0:T(8,128)S(1)}, u32[]{:S(2)}, u32[]{:S(2)}) %collective-permute-start.9) | collective-permute-done | bytes 16416 | tf_op jit(solution)/shard_map/ppermute | solution.py:293
  71.8 0.5 collective-permute-done.10.refs_1_
  72.4 10.3 %all_to_all.29 = f32[8,32,128]{2,1,0:T(8,128)S(1)} all-to-all(f32[8,32,128]{2,1,0:T(8,128)S(1)} %share_sum.1), channel_id=1, replica_groups=mesh['src'=4,'tgt'=8] {'tgt'}, dimensions={0} | all-to-all | bytes 262144 | tf_op jit(solution)/shard_map/all_to_all | solution.py:380
  82.7 1.0 %collective-permute-start.13 = (f32[32,128]{1,0:T(8,128)S(1)}, f32[32,128]{1,0:T(8,128)S(1)}, u32[]{:S(2)}, u32[]{:S(2)}) collective-permute-start(f32[32,128]{1,0:T(8,128)S(1)} %reduce_sum.9.refs_0_), channel_id=1, source_target_pairs={{0,16},{8,24},{16,0},{24,8},{1,17},{9,25},{17,1},{25,9},{2,18},{10... | collective-permute-start | bytes 49160 | tf_op jit(solution)/shard_map/ppermute | solution.py:293
  83.8 0.8 collective-permute-start.12
  84.6 1.3 %collective-permute-done.14.refs_3_ = f32[32,128]{1,0:T(8,128)S(1)} collective-permute-done((f32[32,128]{1,0:T(8,128)S(1)}, f32[32,128]{1,0:T(8,128)S(1)}, u32[]{:S(2)}, u32[]{:S(2)}) %collective-permute-start.14) | collective-permute-done | bytes 16416 | tf_op jit(solution)/shard_map/ppermute | solution.py:293
  85.9 0.8 collective-permute-done.13.refs_2_
  86.7 3.8 %polar.1 = f32[128,128]{1,0:T(8,128)} custom-call(f32[32,128]{1,0:T(8,128)S(1)} %reduce_sum.9.refs_0_, f32[32,128]{1,0:T(8,128)S(1)} %collective-permute-done.12.refs_1_, f32[32,128]{1,0:T(8,128)S(1)} %collective-permute-done.13.refs_2_, f32[32,128]{1,0:T(8,128)S(1)} %collective-permute-done.14.refs_3_), custom_call_target="tpu_custom_call" | custom-call | flops 134217728 | bytes 8388608 | tf_op jit(solution)/shard_map/polar/pallas_call | solution.py:22
  (21 shorter events, 0.9 us)
Async XLA Ops:
  0.6 22.5 %copy-start = (f32[1024]{0:T(1024)S(1)}, f32[1024]{0:T(1024)}, u32[]{:S(2)}) copy-start(f32[1024]{0:T(1024)} %param.7) | copy-start | bytes 12292
  21.2 3.1 %collective-permute-start.2 = (f32[1,1024]{1,0:T(1,128)S(1)}, f32[1,1024]{1,0:T(1,128)S(1)}, u32[]{:S(2)}, u32[]{:S(2)}) collective-permute-start(f32[1,1024]{1,0:T(1,128)S(1)} %get-tuple-element.28.refs_0_), channel_id=1, source_target_pairs={{0,24},{8,16},{16,8},{24,0},{1,25},{9,17},{17,9},{25,1},{2,26},{10... | collective-permute-start | bytes 12296 | tf_op jit(solution)/shard_map/ppermute | solution.py:293
  21.3 3.7 %collective-permute-start.1 = (f32[1,1024]{1,0:T(1,128)S(1)}, f32[1,1024]{1,0:T(1,128)S(1)}, u32[]{:S(2)}, u32[]{:S(2)}) collective-permute-start(f32[1,1024]{1,0:T(1,128)S(1)} %get-tuple-element.28.refs_0_), channel_id=1, source_target_pairs={{0,16},{8,24},{16,0},{24,8},{1,17},{9,25},{17,1},{25,9},{2,18},{10... | collective-permute-start | bytes 12296 | tf_op jit(solution)/shard_map/ppermute | solution.py:293
  22.9 2.1 %collective-permute-start = (f32[1,1024]{1,0:T(1,128)S(1)}, f32[1,1024]{1,0:T(1,128)S(1)}, u32[]{:S(2)}, u32[]{:S(2)}) collective-permute-start(f32[1,1024]{1,0:T(1,128)S(1)} %get-tuple-element.28.refs_0_), channel_id=1, source_target_pairs={{0,8},{8,0},{16,24},{24,16},{1,9},{9,1},{17,25},{25,17},{2,10},{10... | collective-permute-start | bytes 12296 | tf_op jit(solution)/shard_map/ppermute | solution.py:293
  36.9 3.1 %collective-permute-start.5 = (f32[1,1024]{1,0:T(1,128)S(1)}, f32[1,1024]{1,0:T(1,128)S(1)}, u32[]{:S(2)}, u32[]{:S(2)}) collective-permute-start(f32[1,1024]{1,0:T(1,128)S(1)} %col_later.2.refs_0_), channel_id=1, source_target_pairs={{0,24},{8,16},{16,8},{24,0},{1,25},{9,17},{17,9},{25,1},{2,26},{10... | collective-permute-start | bytes 12296 | tf_op jit(solution)/shard_map/ppermute | solution.py:293
  37.0 3.7 %collective-permute-start.4 = (f32[1,1024]{1,0:T(1,128)S(1)}, f32[1,1024]{1,0:T(1,128)S(1)}, u32[]{:S(2)}, u32[]{:S(2)}) collective-permute-start(f32[1,1024]{1,0:T(1,128)S(1)} %col_later.2.refs_0_), channel_id=1, source_target_pairs={{0,16},{8,24},{16,0},{24,8},{1,17},{9,25},{17,1},{25,9},{2,18},{10... | collective-permute-start | bytes 12296 | tf_op jit(solution)/shard_map/ppermute | solution.py:293
  38.6 2.1 %collective-permute-start.3 = (f32[1,1024]{1,0:T(1,128)S(1)}, f32[1,1024]{1,0:T(1,128)S(1)}, u32[]{:S(2)}, u32[]{:S(2)}) collective-permute-start(f32[1,1024]{1,0:T(1,128)S(1)} %col_later.2.refs_0_), channel_id=1, source_target_pairs={{0,8},{8,0},{16,24},{24,16},{1,9},{9,1},{17,25},{25,17},{2,10},{10... | collective-permute-start | bytes 12296 | tf_op jit(solution)/shard_map/ppermute | solution.py:293
  52.5 3.1 %collective-permute-start.8 = (f32[1,1024]{1,0:T(1,128)S(1)}, f32[1,1024]{1,0:T(1,128)S(1)}, u32[]{:S(2)}, u32[]{:S(2)}) collective-permute-start(f32[1,1024]{1,0:T(1,128)S(1)} %col_later.3.refs_0_), channel_id=1, source_target_pairs={{0,24},{8,16},{16,8},{24,0},{1,25},{9,17},{17,9},{25,1},{2,26},{10... | collective-permute-start | bytes 12296 | tf_op jit(solution)/shard_map/ppermute | solution.py:293
  52.6 3.7 %collective-permute-start.7 = (f32[1,1024]{1,0:T(1,128)S(1)}, f32[1,1024]{1,0:T(1,128)S(1)}, u32[]{:S(2)}, u32[]{:S(2)}) collective-permute-start(f32[1,1024]{1,0:T(1,128)S(1)} %col_later.3.refs_0_), channel_id=1, source_target_pairs={{0,16},{8,24},{16,0},{24,8},{1,17},{9,25},{17,1},{25,9},{2,18},{10... | collective-permute-start | bytes 12296 | tf_op jit(solution)/shard_map/ppermute | solution.py:293
  54.2 2.1 %collective-permute-start.6 = (f32[1,1024]{1,0:T(1,128)S(1)}, f32[1,1024]{1,0:T(1,128)S(1)}, u32[]{:S(2)}, u32[]{:S(2)}) collective-permute-start(f32[1,1024]{1,0:T(1,128)S(1)} %col_later.3.refs_0_), channel_id=1, source_target_pairs={{0,8},{8,0},{16,24},{24,16},{1,9},{9,1},{17,25},{25,17},{2,10},{10... | collective-permute-start | bytes 12296 | tf_op jit(solution)/shard_map/ppermute | solution.py:293
  68.6 3.3 %collective-permute-start.9 = (f32[32,128]{1,0:T(8,128)S(1)}, f32[32,128]{1,0:T(8,128)S(1)}, u32[]{:S(2)}, u32[]{:S(2)}) collective-permute-start(f32[32,128]{1,0:T(8,128)S(1)} %get-tuple-element.37), channel_id=1, source_target_pairs={{0,24},{8,16},{16,8},{24,0},{1,25},{9,17},{17,9},{25,1},{2,26},{10... | collective-permute-start | bytes 49160 | tf_op jit(solution)/shard_map/ppermute | solution.py:293
  68.6 3.8 %collective-permute-start.10 = (f32[32,128]{1,0:T(8,128)S(1)}, f32[32,128]{1,0:T(8,128)S(1)}, u32[]{:S(2)}, u32[]{:S(2)}) collective-permute-start(f32[32,128]{1,0:T(8,128)S(1)} %get-tuple-element.38), channel_id=1, source_target_pairs={{0,16},{8,24},{16,0},{24,8},{1,17},{9,25},{17,1},{25,9},{2,18},{10... | collective-permute-start | bytes 49160 | tf_op jit(solution)/shard_map/ppermute | solution.py:293
  70.1 2.2 %collective-permute-start.11 = (f32[32,128]{1,0:T(8,128)S(1)}, f32[32,128]{1,0:T(8,128)S(1)}, u32[]{:S(2)}, u32[]{:S(2)}) collective-permute-start(f32[32,128]{1,0:T(8,128)S(1)} %get-tuple-element.39), channel_id=1, source_target_pairs={{0,8},{8,0},{16,24},{24,16},{1,9},{9,1},{17,25},{25,17},{2,10},{10... | collective-permute-start | bytes 49160 | tf_op jit(solution)/shard_map/ppermute | solution.py:293
  82.6 3.2 %collective-permute-start.14 = (f32[32,128]{1,0:T(8,128)S(1)}, f32[32,128]{1,0:T(8,128)S(1)}, u32[]{:S(2)}, u32[]{:S(2)}) collective-permute-start(f32[32,128]{1,0:T(8,128)S(1)} %reduce_sum.9.refs_0_), channel_id=1, source_target_pairs={{0,24},{8,16},{16,8},{24,0},{1,25},{9,17},{17,9},{25,1},{2,26},{10... | collective-permute-start | bytes 49160 | tf_op jit(solution)/shard_map/ppermute | solution.py:293
  82.7 3.9 %collective-permute-start.13 = (f32[32,128]{1,0:T(8,128)S(1)}, f32[32,128]{1,0:T(8,128)S(1)}, u32[]{:S(2)}, u32[]{:S(2)}) collective-permute-start(f32[32,128]{1,0:T(8,128)S(1)} %reduce_sum.9.refs_0_), channel_id=1, source_target_pairs={{0,16},{8,24},{16,0},{24,8},{1,17},{9,25},{17,1},{25,9},{2,18},{10... | collective-permute-start | bytes 49160 | tf_op jit(solution)/shard_map/ppermute | solution.py:293
  83.8 2.9 %collective-permute-start.12 = (f32[32,128]{1,0:T(8,128)S(1)}, f32[32,128]{1,0:T(8,128)S(1)}, u32[]{:S(2)}, u32[]{:S(2)}) collective-permute-start(f32[32,128]{1,0:T(8,128)S(1)} %reduce_sum.9.refs_0_), channel_id=1, source_target_pairs={{0,8},{8,0},{16,24},{24,16},{1,9},{9,1},{17,25},{25,17},{2,10},{10... | collective-permute-start | bytes 49160 | tf_op jit(solution)/shard_map/ppermute | solution.py:293
where the time goes:
time: 90.8 us; the launch traced here: 90.5 us
  blocking collectives  52.1 us (57%)
  Pallas kernels  18.6 us (20%)
  starting transfers between devices  9.54 us (11%)
  waiting for transfers between devices  9.46 us (10%)
    all_to_all x4, blocking collectives, exchange(): return [lax.all_to_all(jnp.broadcast_to(x, (size,) + x.shape), axis, 0, 0)]  41.8 us
    pallas_call x10, Pallas kernels, call(): pl.pallas_call(body, name=name, out_shape=out_shape, in_specs=[pl.BlockSp...  18.6 us
    all_to_all x1, blocking collectives, shards(): share = jnp.sum(lax.all_to_all(share, 'tgt', 0, 0), axis=0)  10.3 us
    ppermute x15, starting transfers between devices, partners(): lax.ppermute(values[k], axis, [(me, me ^ k) for me in range(size)])  9.54 us
    ppermute x15, waiting for transfers between devices, partners(): lax.ppermute(values[k], axis, [(me, me ^ k) for me in range(size)])  9.46 us
  transfers between devices with their start and end apart: 15, of which 10 were waited for; matrix products, arithmetic and copies ran while one was open for 0% of the time, Pallas kernels for 0%

commit v1 on v0

--- a/solution.py
+++ b/solution.py
@@ -52,13 +52,13 @@
     return high, (x - high.astype(F32)).astype(BF16)
 
 
-def lane_parts(wide, first, fill):
+def lane_parts(wide):
     lane = lax.broadcasted_iota(jnp.int32, wide.shape, 1)
-    out = jnp.where((lane >= fill) & (lane < fill + 3), 1.0, 0.0)
     rest = wide
+    out = jnp.zeros_like(wide)
     for k in range(3):
         part = rest.astype(BF16).astype(F32)
-        out = jnp.where(lane == first + k, part, out)
+        out = jnp.where(lane == k, part, out)
         rest = rest - part
     return out.astype(BF16)
 
@@ -109,7 +109,7 @@
     for part in range(target.shape[0] // LANES):
         at = pl.ds(part * LANES, LANES)
         right_out[at, :width] = target[at, :]
-        right_out[at, width:] = lane_parts(to_column(pot[:, at] * (1.0 / scale)), 0, 3)
+        right_out[at, width:] = lane_parts(to_column(pot[:, at] * (1.0 / scale)))
     left_out[...] = jnp.dot(source[...], start_map[...].astype(BF16), preferred_element_type=F32).astype(BF16)
     for part in range(rows // LANES):
         here = slice(part * LANES, (part + 1) * LANES)
@@ -135,15 +135,22 @@
     lse_out[...] = lse_out[...] + jnp.log(sums[...]) * (1.0 / (unit * math.log(2.0)))
 
 
-def col_first(group, unit, log_rows, left_in, right, *refs):
-    parts, (block_out, pot_out, peak_out, lse_out, left, work) = received(refs, group)
+def col_first(group, unit, log_rows, left_in, own, other, *refs):
+    parts, (block_out, target_out, pot_out, peak_out, lse_out, left, right, work) = received(refs, group)
     row_pot = -log_rows - tree_lse(unit, parts)
     pot_out[...] = row_pot
     rows, width = left_in.shape
-    cols = right.shape[0]
+    half = own.shape[0]
+    cols = 2 * half
+    odd = lax.axis_index("tgt") & 1
+    target_out[pl.ds(pl.multiple_of(odd * half, half), half), :] = own[:, :width]
+    target_out[pl.ds(pl.multiple_of((1 - odd) * half, half), half), :] = other[...].astype(BF16)
+    right[:, :width] = target_out[...]
+    lane = lax.broadcasted_iota(jnp.int32, (cols, LANES), 1)
+    right[:, width:] = jnp.where(lane < 3, 1.0, 0.0).astype(BF16)
     left[:, :width] = left_in[...]
     for part in range(rows // LANES):
-        left[part * LANES : (part + 1) * LANES, width:] = lane_parts(to_column(row_pot[part : part + 1, :]), 3, 0)
+        left[part * LANES : (part + 1) * LANES, width:] = lane_parts(to_column(row_pot[part : part + 1, :]))
     peak = None
     for start in range(0, rows, CHUNK):
         value = dot_t(left[start : start + CHUNK, :], right[...])
@@ -181,10 +188,10 @@
             sums_out[at : at + 1, :] = to_lanes(sums[part * LANES : (part + 1) * LANES])
 
 
-def row_second(group, unit, log_cols, block, peak, pot, *refs):
+def row_second(group, unit, log_cols, block, peak, *refs):
     parts, (pot_out, scale_out, sums_out) = received(refs, group)
     lse = tree_lse(unit, parts)
-    pot_out[...] = pot[...] - log_cols - lse
+    pot_out[...] = -log_cols - lse
     scale = jnp.exp2(unit * (peak[...] - lse))
     scale_out[...] = scale
     row_sums(block, scale, sums_out)
@@ -217,12 +224,14 @@
 def row_last(group, unit, block, scale, pot, target, *refs):
     parts, (col_out, sums_out, bary_out, other) = received(refs, group)
     totals = tree_sum(parts)
-    col_out[...] = (EPS * math.log(2.0)) * (unit * pot[...] - jnp.log(totals) * (1.0 / math.log(2.0)))
+    pots = (EPS * math.log(2.0)) * (unit * pot[...] - jnp.log(totals) * (1.0 / math.log(2.0)))
+    half = col_out.shape[1]
+    col_out[...] = jnp.where((lax.axis_index("tgt") & 1) == 0, pots[:, :half], pots[:, half:])
     factors = column_factors(scale[...] / totals)
     high, low = split(factors)
     lane = lax.broadcasted_iota(jnp.int32, factors.shape, 1)
     sides = jnp.where(lane < LANES // 2, high.astype(F32), low.astype(F32)).astype(BF16)
-    scaled = (target[:, : factors.shape[1]].astype(F32) * factors).astype(BF16)
+    scaled = (target[...].astype(F32) * factors).astype(BF16)
     weights = jnp.concatenate([scaled, sides], axis=1)
     for start in range(0, block.shape[0], CHUNK):
         wide = jnp.dot(block[start : start + CHUNK, :], weights, preferred_element_type=F32)
@@ -255,9 +264,7 @@
 
 
 def share_sum(*refs):
-    total = tree_sum([ref[...] for ref in refs[:-1]])
-    for k in range(refs[-1].shape[0]):
-        refs[-1][k] = total
+    refs[-1][...] = tree_sum([ref[...] for ref in refs[:-1]])
 
 
 def precise(a, b, axis=1):
@@ -293,11 +300,18 @@
     return [lax.ppermute(values[k], axis, [(me, me ^ k) for me in range(size)]) if k else values[0] for k in order]
 
 
-def exchange(x, axis):
-    size = lax.axis_size(axis)
-    if axis == "src":
-        return partners([x] * size, axis, range(size))
-    return [lax.all_to_all(jnp.broadcast_to(x, (size,) + x.shape), axis, 0, 0)]
+def over_src(x):
+    size = lax.axis_size("src")
+    return partners([x] * size, "src", range(size))
+
+
+def over_pairs(x):
+    size = lax.axis_size("tgt")
+    return partners([x] * size, "tgt", range(0, size, 2))
+
+
+def over_tgt(x):
+    return lax.all_to_all(jnp.broadcast_to(x, (lax.axis_size("tgt"),) + x.shape), "tgt", 0, 0)
 
 
 def shards(source, target, start_map, warm_potential):
@@ -308,11 +322,12 @@
     scale = 1.0 / (math.sqrt(width) * EPS)
     unit = scale / math.log(2.0)
     log_rows, log_cols = math.log(rows * n_src) / scale, math.log(cols * n_tgt) / scale
+    n_pairs = n_tgt // 2
     row_vec = jax.ShapeDtypeStruct((rows // LANES, LANES), F32)
-    col_vec = jax.ShapeDtypeStruct((1, cols), F32)
-    pot = warm_potential.reshape(1, cols)
+    pair_vec = jax.ShapeDtypeStruct((1, 2 * cols), F32)
     mac = rows * cols * width
 
+    other = lax.ppermute(target.astype(F32), "tgt", [(me, me ^ 1) for me in range(n_tgt)])
     left, right, lse, turned = call(
         functools.partial(row_first, unit, scale),
         "row_first",
@@ -335,52 +350,58 @@
         ],
         flops=4 * mac,
         space=pltpu.HBM,
-    )(*[pltpu.with_memory_space_constraint(x, pltpu.HBM) for x in (source, start_map, target, pot)])
-    block, row_pot, peak, lse = call(
+    )(*[pltpu.with_memory_space_constraint(x, pltpu.HBM) for x in (source, start_map, target, warm_potential.reshape(1, cols))])
+    block, targets, row_pot, peak, lse = call(
         functools.partial(col_first, n_tgt, unit, log_rows),
         "col_first",
-        (jax.ShapeDtypeStruct((rows, cols), BF16), row_vec, col_vec, col_vec),
-        scratch=[pltpu.VMEM((rows, width + LANES), BF16), pltpu.VMEM((rows, cols), F32)],
+        (
+            jax.ShapeDtypeStruct((rows, 2 * cols), BF16),
+            jax.ShapeDtypeStruct((2 * cols, width), BF16),
+            row_vec,
+            pair_vec,
+            pair_vec,
+        ),
+        scratch=[
+            pltpu.VMEM((rows, width + LANES), BF16),
+            pltpu.VMEM((2 * cols, width + LANES), BF16),
+            pltpu.VMEM((rows, 2 * cols), F32),
+        ],
+        flops=8 * mac,
+    )(left, right, other, over_tgt(lse))
+    col_pot, col_scale, sums = call(
+        functools.partial(row_second, n_src, unit, log_cols), "row_second", (pair_vec, pair_vec, row_vec), flops=4 * mac
+    )(block, peak, *over_src(lse))
+    col_later_call = call(
+        functools.partial(col_later, n_pairs, ratio),
+        "col_later",
+        pair_vec,
+        scratch=[pltpu.VMEM((rows, LANES), F32)],
         flops=4 * mac,
-    )(left, right, *exchange(lse, "tgt"))
-    col_pot, col_scale, sums = call(
-        functools.partial(row_second, n_src, unit, log_cols), "row_second", (col_vec, col_vec, row_vec), flops=2 * mac
-    )(block, peak, pot * (1.0 / scale), *exchange(lse, "src"))
-    col_later_call = call(
-        functools.partial(col_later, n_tgt, ratio),
-        "col_later",
-        col_vec,
-        scratch=[pltpu.VMEM((rows, LANES), F32)],
-        flops=2 * mac,
     )
-    sums = col_later_call(block, col_scale, *exchange(sums, "tgt"))
-    sums = call(functools.partial(row_later, n_src), "row_later", row_vec, flops=2 * mac)(
-        block, col_scale, *exchange(sums, "src")
+    sums = col_later_call(block, col_scale, *over_pairs(sums))
+    sums = call(functools.partial(row_later, n_src), "row_later", row_vec, flops=4 * mac)(
+        block, col_scale, *over_src(sums)
     )
-    sums = col_later_call(block, col_scale, *exchange(sums, "tgt"))
+    sums = col_later_call(block, col_scale, *over_pairs(sums))
     col_out, sums, bary = call(
         functools.partial(row_last, n_src, unit),
         "row_last",
-        (col_vec, row_vec, jax.ShapeDtypeStruct((rows, width), F32)),
+        (jax.ShapeDtypeStruct((1, cols), F32), row_vec, jax.ShapeDtypeStruct((rows, width), F32)),
         scratch=[pltpu.VMEM(row_vec.shape, F32)],
         flops=4 * mac,
-    )(block, col_scale, col_pot, right, *exchange(sums, "src"))
+    )(block, col_scale, col_pot, targets, *over_src(sums))
     square = jax.ShapeDtypeStruct((width, width), F32)
-    share_shape = (width // n_src, width)
+    share_shape = jax.ShapeDtypeStruct((width // n_src, width), F32)
     row_out, *shares = call(
-        functools.partial(cross_local, n_tgt, unit, ratio),
+        functools.partial(cross_local, n_pairs, unit, ratio),
         "cross_local",
-        (row_vec,) + (jax.ShapeDtypeStruct(share_shape, F32),) * n_src,
+        (row_vec,) + (share_shape,) * n_src,
         scratch=[pltpu.VMEM((width, width), F32)],
         flops=2 * rows * width * width,
-    )(turned, bary, row_pot, *exchange(sums, "tgt"))
-    share = call(share_sum, "share_sum", jax.ShapeDtypeStruct((n_tgt,) + share_shape, F32))(
-        *partners(shares[::-1], "src", range(n_src - 1, -1, -1))
-    )
-    share = jnp.sum(lax.all_to_all(share, "tgt", 0, 0), axis=0)
-    new_map = call(polar, "polar", square, scratch=[pltpu.VMEM((width, width), F32)], flops=1 << 27)(
-        *exchange(share, "src")
-    )
+    )(turned, bary, row_pot, *over_pairs(sums))
+    share = call(share_sum, "share_sum", share_shape)(*partners(shares[::-1], "src", range(n_src - 1, -1, -1)))
+    share = call(share_sum, "share_sum", share_shape)(*over_pairs(share))
+    new_map = call(polar, "polar", square, scratch=[pltpu.VMEM((width, width), F32)], flops=1 << 27)(*over_src(share))
     return row_out.reshape(rows), col_out.reshape(cols), new_map
 
 

time: 90.8 us -> 88.8 us (0.978)
  blocking collectives: 52.1 us -> 11.6 us
  starting transfers between devices: 9.54 us -> 30.3 us
  waiting for transfers between devices: 9.46 us -> 18.4 us
  Pallas kernels: 18.6 us -> 26.7 us
  other arithmetic: 0.02 us -> 0.99 us
    all_to_all x5 -> x1, blocking collectives: 52.1 us -> 11.6 us  [over_tgt(): lax.all_to_all(jnp.broadcast_to(x, (lax.axis_size('tgt'),) + x.shape), 't...]
    ppermute x15 -> x27, starting transfers between devices: 9.54 us -> 27.3 us  [partners(): lax.ppermute(values[k], axis, [(me, me ^ k) for me in range(size)])]
    ppermute x15 -> x27, waiting for transfers between devices: 9.46 us -> 18.4 us  [partners(): lax.ppermute(values[k], axis, [(me, me ^ k) for me in range(size)])]
    pallas_call x10 -> x11, Pallas kernels: 18.6 us -> 26.7 us  [call(): pl.pallas_call(body, name=name, out_shape=out_shape, in_specs=[pl.BlockSp...]
    ppermute x0 -> x1, starting transfers between devices: none -> 3 us  [shards(): lax.ppermute(target.astype(F32), 'tgt', [(me, me ^ 1) for me in range(n_t...]
    convert_element_type x0 -> x1, other arithmetic: none -> 0.99 us  [shards(): target.astype(F32)]
  transfers between devices with their start and end apart: 15 -> 28, of which waited for: 10 -> 22; matrix products, arithmetic and copies ran while one was open for 0% -> 0% of each run, Pallas kernels for 0% -> 4%
where the time goes in v1:
time: 88.8 us; the launch traced here: 88.6 us
  starting transfers between devices  30.3 us (34%)
  Pallas kernels  26.7 us (30%)
  waiting for transfers between devices  18.4 us (21%)
  blocking collectives  11.6 us (13%)
  other arithmetic  0.99 us (1%)
    ppermute x27, starting transfers between devices, partners(): lax.ppermute(values[k], axis, [(me, me ^ k) for me in range(size)])  27.3 us
    pallas_call x11, Pallas kernels, call(): pl.pallas_call(body, name=name, out_shape=out_shape, in_specs=[pl.BlockSp...  26.7 us
    ppermute x27, waiting for transfers between devices, partners(): lax.ppermute(values[k], axis, [(me, me ^ k) for me in range(size)])  18.4 us
    all_to_all x1, blocking collectives, over_tgt(): lax.all_to_all(jnp.broadcast_to(x, (lax.axis_size('tgt'),) + x.shape), 't...  11.6 us
    ppermute x1, starting transfers between devices, shards(): lax.ppermute(target.astype(F32), 'tgt', [(me, me ^ 1) for me in range(n_t...  3 us
  transfers between devices with their start and end apart: 28, of which 22 were waited for; matrix products, arithmetic and copies ran while one was open for 0% of the time, Pallas kernels for 4%

profile of v1, /device:TPU:0, one launch (start us, length us, event | category | flops | bytes accessed | tf_op | source)
XLA Modules:
  0.0 88.6 jit_solution(17761875472644752218)
XLA Ops:
  1.6 3.0 %collective-permute-start = (f32[1024,128]{1,0:T(8,128)S(1)}, f32[1024,128]{1,0:T(8,128)S(1)}, u32[]{:S(2)}, u32[]{:S(2)}) collective-permute-start(f32[1024,128]{1,0:T(8,128)S(1)} %convert_element_type.3), channel_id=1, source_target_pairs={{0,1},{1,0},{2,3},{3,2},{4,5},{5,4},{6,7},{7,6},{8,9},{9,8},{10,11... | collective-permute-start | bytes 1572872 | tf_op jit(solution)/shard_map/ppermute | solution.py:330
  4.6 3.5 %row_first.1 = (bf16[2048,128]{1,0:T(8,128)(2,1)S(1)}, bf16[1024,256]{1,0:T(8,128)(2,1)S(1)}, f32[16,128]{1,0:T(8,128)S(1)}, bf16[128,2048]{1,0:T(8,128)(2,1)S(1)}) custom-call(bf16[2048,128]{1,0:T(8,128)(2,1)} %source_hbm.1, f32[128,128]{1,0:T(8,128)} %map_hbm.1, bf16[1024,128]{1,0:T(8,128)(2,1)} %target_hbm.1, f32[1,1024]{1,0:T(1,128)} %bitcast.4), custom_call_target="tpu_custom_call" | custom-call | flops 1073741824 | bytes 8388608 | tf_op jit(solution)/shard_map/row_first/pallas_call | solution.py:22
  8.2 11.6 %all_to_all.5.refs_0_ = f32[8,16,128]{2,1,0:T(8,128)S(1)} all-to-all(f32[8,16,128]{2,1,0:T(8,128)S(1)} %broadcast_in_dim.3), channel_id=1, replica_groups=mesh['src'=4,'tgt'=8] {'tgt'}, dimensions={0} | all-to-all | bytes 131072 | tf_op jit(solution)/shard_map/all_to_all | solution.py:314
  19.7 5.5 %col_first.1 = (bf16[2048,2048]{1,0:T(8,128)(2,1)S(1)}, bf16[2048,128]{1,0:T(8,128)(2,1)S(1)}, f32[16,128]{1,0:T(8,128)S(1)}, f32[1,2048]{1,0:T(1,128)S(1)}, f32[1,2048]{1,0:T(1,128)S(1)}) custom-call(bf16[2048,128]{1,0:T(8,128)(2,1)S(1)} %get-tuple-element.24.left_in, bf16[1024,256]{1,0:T(8,128)(2,1)S(1)} %get-tuple-element.25.own, ...), custom_call_target="tpu_custom_call" | custom-call | flops 2147483648 | bytes 8388608 | tf_op jit(solution)/shard_map/col_first/pallas_call | solution.py:22
  25.3 1.6 %collective-permute-start.2 = (f32[1,2048]{1,0:T(1,128)S(1)}, f32[1,2048]{1,0:T(1,128)S(1)}, u32[]{:S(2)}, u32[]{:S(2)}) collective-permute-start(f32[1,2048]{1,0:T(1,128)S(1)} %get-tuple-element.29.refs_0_), channel_id=1, source_target_pairs={{0,16},{8,24},{16,0},{24,8},{1,17},{9,25},{17,1},{25,9},{2,18},{10... | collective-permute-start | bytes 24584 | tf_op jit(solution)/shard_map/ppermute | solution.py:300
  27.2 1.2 %collective-permute-done.3.refs_3_ = f32[1,2048]{1,0:T(1,128)S(1)} collective-permute-done((f32[1,2048]{1,0:T(1,128)S(1)}, f32[1,2048]{1,0:T(1,128)S(1)}, u32[]{:S(2)}, u32[]{:S(2)}) %collective-permute-start.3) | collective-permute-done | bytes 8224 | tf_op jit(solution)/shard_map/ppermute | solution.py:300
  29.0 2.5 %row_second.1 = (f32[1,2048]{1,0:T(1,128)S(1)}, f32[1,2048]{1,0:T(1,128)S(1)}, f32[16,128]{1,0:T(8,128)S(1)}) custom-call(bf16[2048,2048]{1,0:T(8,128)(2,1)S(1)} %get-tuple-element.27.block, f32[1,2048]{1,0:T(1,128)S(1)} %get-tuple-element.28.peak, f32[1,2048]{1,0:T(1,128)S(1)} %get-tuple-element.29.refs_0_, f32[1,2048]{1,0:T(1,128)S(1)} %collective-permute-done.1.refs_1_, ...), custom_call_target="tpu_custom_call" | custom-call | flops 1073741824 | bytes 8388608 | tf_op jit(solution)/shard_map/row_second/pallas_call | solution.py:22
  31.5 1.4 %collective-permute-start.6 = (f32[16,128]{1,0:T(8,128)S(1)}, f32[16,128]{1,0:T(8,128)S(1)}, u32[]{:S(2)}, u32[]{:S(2)}) collective-permute-start(f32[16,128]{1,0:T(8,128)S(1)} %get-tuple-element.33.refs_0_), channel_id=1, source_target_pairs={{0,6},{1,7},{2,4},{3,5},{4,2},{5,3},{6,0},{7,1},{8,14},{9,15},{10,... | collective-permute-start | bytes 24584 | tf_op jit(solution)/shard_map/ppermute | solution.py:300
  33.3 2.7 %collective-permute-start.4 = (f32[16,128]{1,0:T(8,128)S(1)}, f32[16,128]{1,0:T(8,128)S(1)}, u32[]{:S(2)}, u32[]{:S(2)}) collective-permute-start(f32[16,128]{1,0:T(8,128)S(1)} %get-tuple-element.33.refs_0_), channel_id=1, source_target_pairs={{0,2},{1,3},{2,0},{3,1},{4,6},{5,7},{6,4},{7,5},{8,10},{9,11},{10,... | collective-permute-start | bytes 24584 | tf_op jit(solution)/shard_map/ppermute | solution.py:300
  36.0 1.1 %collective-permute-done.6.refs_3_ = f32[16,128]{1,0:T(8,128)S(1)} collective-permute-done((f32[16,128]{1,0:T(8,128)S(1)}, f32[16,128]{1,0:T(8,128)S(1)}, u32[]{:S(2)}, u32[]{:S(2)}) %collective-permute-start.6) | collective-permute-done | bytes 8224 | tf_op jit(solution)/shard_map/ppermute | solution.py:300
  37.6 2.3 %col_later.2.refs_0_ = f32[1,2048]{1,0:T(1,128)S(1)} custom-call(bf16[2048,2048]{1,0:T(8,128)(2,1)S(1)} %get-tuple-element.27.block, f32[1,2048]{1,0:T(1,128)S(1)} %get-tuple-element.30.scale, f32[16,128]{1,0:T(8,128)S(1)} %get-tuple-element.33.refs_0_, f32[16,128]{1,0:T(8,128)S(1)} %collective-permute-done.4.refs_1_, ...), custom_call_target="tpu_custom_call" | custom-call | flops 1073741824 | bytes 8388608 | tf_op jit(solution)/shard_map/col_later/pallas_call | solution.py:22
  40.0 1.6 %collective-permute-start.8 = (f32[1,2048]{1,0:T(1,128)S(1)}, f32[1,2048]{1,0:T(1,128)S(1)}, u32[]{:S(2)}, u32[]{:S(2)}) collective-permute-start(f32[1,2048]{1,0:T(1,128)S(1)} %col_later.2.refs_0_), channel_id=1, source_target_pairs={{0,16},{8,24},{16,0},{24,8},{1,17},{9,25},{17,1},{25,9},{2,18},{10... | collective-permute-start | bytes 24584 | tf_op jit(solution)/shard_map/ppermute | solution.py:300
  41.8 1.2 %collective-permute-done.9.refs_3_ = f32[1,2048]{1,0:T(1,128)S(1)} collective-permute-done((f32[1,2048]{1,0:T(1,128)S(1)}, f32[1,2048]{1,0:T(1,128)S(1)}, u32[]{:S(2)}, u32[]{:S(2)}) %collective-permute-start.9) | collective-permute-done | bytes 8224 | tf_op jit(solution)/shard_map/ppermute | solution.py:300
  43.7 2.4 %row_later.1.refs_0_ = f32[16,128]{1,0:T(8,128)S(1)} custom-call(bf16[2048,2048]{1,0:T(8,128)(2,1)S(1)} %get-tuple-element.27.block, f32[1,2048]{1,0:T(1,128)S(1)} %get-tuple-element.30.scale, f32[1,2048]{1,0:T(1,128)S(1)} %col_later.2.refs_0_, f32[1,2048]{1,0:T(1,128)S(1)} %collective-permute-done.7.refs_1_, f32[1,2048]{1,0:T(1,128)S(1)} %collective-permute-done.8.refs_2_, ...), custom_call_target="tpu_custom_call" | custom-call | flops 1073741824 | bytes 8388608 | tf_op jit(solution)/shard_map/row_later/pallas_call | solution.py:22
  46.2 2.4 %collective-permute-start.12 = (f32[16,128]{1,0:T(8,128)S(1)}, f32[16,128]{1,0:T(8,128)S(1)}, u32[]{:S(2)}, u32[]{:S(2)}) collective-permute-start(f32[16,128]{1,0:T(8,128)S(1)} %row_later.1.refs_0_), channel_id=1, source_target_pairs={{0,6},{1,7},{2,4},{3,5},{4,2},{5,3},{6,0},{7,1},{8,14},{9,15},{10,... | collective-permute-start | bytes 24584 | tf_op jit(solution)/shard_map/ppermute | solution.py:300
  48.6 1.1 %collective-permute-start.11 = (f32[16,128]{1,0:T(8,128)S(1)}, f32[16,128]{1,0:T(8,128)S(1)}, u32[]{:S(2)}, u32[]{:S(2)}) collective-permute-start(f32[16,128]{1,0:T(8,128)S(1)} %row_later.1.refs_0_), channel_id=1, source_target_pairs={{0,4},{1,5},{2,6},{3,7},{4,0},{5,1},{6,2},{7,3},{8,12},{9,13},{10,... | collective-permute-start | bytes 24584 | tf_op jit(solution)/shard_map/ppermute | solution.py:300
  51.7 1.5 %collective-permute-done.11.refs_2_ = f32[16,128]{1,0:T(8,128)S(1)} collective-permute-done((f32[16,128]{1,0:T(8,128)S(1)}, f32[16,128]{1,0:T(8,128)S(1)}, u32[]{:S(2)}, u32[]{:S(2)}) %collective-permute-start.11) | collective-permute-done | bytes 8224 | tf_op jit(solution)/shard_map/ppermute | solution.py:300
  53.4 2.5 %col_later.3.refs_0_ = f32[1,2048]{1,0:T(1,128)S(1)} custom-call(bf16[2048,2048]{1,0:T(8,128)(2,1)S(1)} %get-tuple-element.27.block, f32[1,2048]{1,0:T(1,128)S(1)} %get-tuple-element.30.scale, f32[16,128]{1,0:T(8,128)S(1)} %row_later.1.refs_0_, f32[16,128]{1,0:T(8,128)S(1)} %collective-permute-done.10.refs_1_, ...), custom_call_target="tpu_custom_call" | custom-call | flops 1073741824 | bytes 8388608 | tf_op jit(solution)/shard_map/col_later/pallas_call | solution.py:22
  55.9 1.6 %collective-permute-start.14 = (f32[1,2048]{1,0:T(1,128)S(1)}, f32[1,2048]{1,0:T(1,128)S(1)}, u32[]{:S(2)}, u32[]{:S(2)}) collective-permute-start(f32[1,2048]{1,0:T(1,128)S(1)} %col_later.3.refs_0_), channel_id=1, source_target_pairs={{0,16},{8,24},{16,0},{24,8},{1,17},{9,25},{17,1},{25,9},{2,18},{10... | collective-permute-start | bytes 24584 | tf_op jit(solution)/shard_map/ppermute | solution.py:300
  57.8 1.2 %collective-permute-done.15.refs_3_ = f32[1,2048]{1,0:T(1,128)S(1)} collective-permute-done((f32[1,2048]{1,0:T(1,128)S(1)}, f32[1,2048]{1,0:T(1,128)S(1)}, u32[]{:S(2)}, u32[]{:S(2)}) %collective-permute-start.15) | collective-permute-done | bytes 8224 | tf_op jit(solution)/shard_map/ppermute | solution.py:300
  59.6 3.1 %row_last.1 = (f32[1,1024]{1,0:T(1,128)}, f32[16,128]{1,0:T(8,128)S(1)}, f32[2048,128]{1,0:T(8,128)S(1)}) custom-call(bf16[2048,2048]{1,0:T(8,128)(2,1)S(1)} %get-tuple-element.27.block, f32[1,2048]{1,0:T(1,128)S(1)} %get-tuple-element.30.scale, f32[1,2048]{1,0:T(1,128)S(1)} %get-tuple-element.31.pot, bf16[2048,128]{1,0:T(8,128)(2,1)S(1)} %get-tuple-element.32.target, ...), custom_call_target="tpu_custom_call" | custom-call | flops 1073741824 | bytes 8388608 | tf_op jit(solution)/shard_map/row_last/pallas_call | solution.py:22
  62.7 1.4 %collective-permute-start.18 = (f32[16,128]{1,0:T(8,128)S(1)}, f32[16,128]{1,0:T(8,128)S(1)}, u32[]{:S(2)}, u32[]{:S(2)}) collective-permute-start(f32[16,128]{1,0:T(8,128)S(1)} %get-tuple-element.36.refs_0_), channel_id=1, source_target_pairs={{0,6},{1,7},{2,4},{3,5},{4,2},{5,3},{6,0},{7,1},{8,14},{9,15},{10,... | collective-permute-start | bytes 24584 | tf_op jit(solution)/shard_map/ppermute | solution.py:300
  65.1 2.0 %collective-permute-start.16 = (f32[16,128]{1,0:T(8,128)S(1)}, f32[16,128]{1,0:T(8,128)S(1)}, u32[]{:S(2)}, u32[]{:S(2)}) collective-permute-start(f32[16,128]{1,0:T(8,128)S(1)} %get-tuple-element.36.refs_0_), channel_id=1, source_target_pairs={{0,2},{1,3},{2,0},{3,1},{4,6},{5,7},{6,4},{7,5},{8,10},{9,11},{10,... | collective-permute-start | bytes 24584 | tf_op jit(solution)/shard_map/ppermute | solution.py:300
  67.1 1.1 %collective-permute-done.18.refs_3_ = f32[16,128]{1,0:T(8,128)S(1)} collective-permute-done((f32[16,128]{1,0:T(8,128)S(1)}, f32[16,128]{1,0:T(8,128)S(1)}, u32[]{:S(2)}, u32[]{:S(2)}) %collective-permute-start.18) | collective-permute-done | bytes 8224 | tf_op jit(solution)/shard_map/ppermute | solution.py:300
  69.8 1.6 %collective-permute-start.20 = (f32[32,128]{1,0:T(8,128)S(1)}, f32[32,128]{1,0:T(8,128)S(1)}, u32[]{:S(2)}, u32[]{:S(2)}) collective-permute-start(f32[32,128]{1,0:T(8,128)S(1)} %get-tuple-element.40), channel_id=1, source_target_pairs={{0,16},{8,24},{16,0},{24,8},{1,17},{9,25},{17,1},{25,9},{2,18},{10... | collective-permute-start | bytes 49160 | tf_op jit(solution)/shard_map/ppermute | solution.py:300
  71.6 1.4 %collective-permute-done.19.refs_0_ = f32[32,128]{1,0:T(8,128)S(1)} collective-permute-done((f32[32,128]{1,0:T(8,128)S(1)}, f32[32,128]{1,0:T(8,128)S(1)}, u32[]{:S(2)}, u32[]{:S(2)}) %collective-permute-start.19) | collective-permute-done | bytes 16416 | tf_op jit(solution)/shard_map/ppermute | solution.py:300
  73.5 2.5 %collective-permute-start.24 = (f32[32,128]{1,0:T(8,128)S(1)}, f32[32,128]{1,0:T(8,128)S(1)}, u32[]{:S(2)}, u32[]{:S(2)}) collective-permute-start(f32[32,128]{1,0:T(8,128)S(1)} %share_sum.2.refs_0_), channel_id=1, source_target_pairs={{0,6},{1,7},{2,4},{3,5},{4,2},{5,3},{6,0},{7,1},{8,14},{9,15},{10,... | collective-permute-start | bytes 49160 | tf_op jit(solution)/shard_map/ppermute | solution.py:300
  78.0 1.1 %collective-permute-done.24.refs_3_ = f32[32,128]{1,0:T(8,128)S(1)} collective-permute-done((f32[32,128]{1,0:T(8,128)S(1)}, f32[32,128]{1,0:T(8,128)S(1)}, u32[]{:S(2)}, u32[]{:S(2)}) %collective-permute-start.24) | collective-permute-done | bytes 16416 | tf_op jit(solution)/shard_map/ppermute | solution.py:300
  79.1 1.5 %collective-permute-done.23.refs_2_ = f32[32,128]{1,0:T(8,128)S(1)} collective-permute-done((f32[32,128]{1,0:T(8,128)S(1)}, f32[32,128]{1,0:T(8,128)S(1)}, u32[]{:S(2)}, u32[]{:S(2)}) %collective-permute-start.23) | collective-permute-done | bytes 16416 | tf_op jit(solution)/shard_map/ppermute | solution.py:300
  80.9 1.6 %collective-permute-start.26 = (f32[32,128]{1,0:T(8,128)S(1)}, f32[32,128]{1,0:T(8,128)S(1)}, u32[]{:S(2)}, u32[]{:S(2)}) collective-permute-start(f32[32,128]{1,0:T(8,128)S(1)} %share_sum.3.refs_0_), channel_id=1, source_target_pairs={{0,16},{8,24},{16,0},{24,8},{1,17},{9,25},{17,1},{25,9},{2,18},{10... | collective-permute-start | bytes 49160 | tf_op jit(solution)/shard_map/ppermute | solution.py:300
  82.8 1.4 %collective-permute-done.27.refs_3_ = f32[32,128]{1,0:T(8,128)S(1)} collective-permute-done((f32[32,128]{1,0:T(8,128)S(1)}, f32[32,128]{1,0:T(8,128)S(1)}, u32[]{:S(2)}, u32[]{:S(2)}) %collective-permute-start.27) | collective-permute-done | bytes 16416 | tf_op jit(solution)/shard_map/ppermute | solution.py:300
  84.7 3.8 %polar.1 = f32[128,128]{1,0:T(8,128)} custom-call(f32[32,128]{1,0:T(8,128)S(1)} %share_sum.3.refs_0_, f32[32,128]{1,0:T(8,128)S(1)} %collective-permute-done.25.refs_1_, f32[32,128]{1,0:T(8,128)S(1)} %collective-permute-done.26.refs_2_, f32[32,128]{1,0:T(8,128)S(1)} %collective-permute-done.27.refs_3_), custom_call_target="tpu_custom_call" | custom-call | flops 134217728 | bytes 8388608 | tf_op jit(solution)/shard_map/polar/pallas_call | solution.py:22
  (38 shorter events, 13.5 us)
Async XLA Ops:
  1.6 18.1 %collective-permute-start = (f32[1024,128]{1,0:T(8,128)S(1)}, f32[1024,128]{1,0:T(8,128)S(1)}, u32[]{:S(2)}, u32[]{:S(2)}) collective-permute-start(f32[1024,128]{1,0:T(8,128)S(1)} %convert_element_type.3), channel_id=1, source_target_pairs={{0,1},{1,0},{2,3},{3,2},{4,5},{5,4},{6,7},{7,6},{8,9},{9,8},{10,11... | collective-permute-start | bytes 1572872 | tf_op jit(solution)/shard_map/ppermute | solution.py:330
  25.2 3.1 %collective-permute-start.3 = (f32[1,2048]{1,0:T(1,128)S(1)}, f32[1,2048]{1,0:T(1,128)S(1)}, u32[]{:S(2)}, u32[]{:S(2)}) collective-permute-start(f32[1,2048]{1,0:T(1,128)S(1)} %get-tuple-element.29.refs_0_), channel_id=1, source_target_pairs={{0,24},{8,16},{16,8},{24,0},{1,25},{9,17},{17,9},{25,1},{2,26},{10... | collective-permute-start | bytes 24584 | tf_op jit(solution)/shard_map/ppermute | solution.py:300
  25.3 3.7 %collective-permute-start.2 = (f32[1,2048]{1,0:T(1,128)S(1)}, f32[1,2048]{1,0:T(1,128)S(1)}, u32[]{:S(2)}, u32[]{:S(2)}) collective-permute-start(f32[1,2048]{1,0:T(1,128)S(1)} %get-tuple-element.29.refs_0_), channel_id=1, source_target_pairs={{0,16},{8,24},{16,0},{24,8},{1,17},{9,25},{17,1},{25,9},{2,18},{10... | collective-permute-start | bytes 24584 | tf_op jit(solution)/shard_map/ppermute | solution.py:300
  26.9 2.1 %collective-permute-start.1 = (f32[1,2048]{1,0:T(1,128)S(1)}, f32[1,2048]{1,0:T(1,128)S(1)}, u32[]{:S(2)}, u32[]{:S(2)}) collective-permute-start(f32[1,2048]{1,0:T(1,128)S(1)} %get-tuple-element.29.refs_0_), channel_id=1, source_target_pairs={{0,8},{8,0},{16,24},{24,16},{1,9},{9,1},{17,25},{25,17},{2,10},{10... | collective-permute-start | bytes 24584 | tf_op jit(solution)/shard_map/ppermute | solution.py:300
  31.5 5.5 %collective-permute-start.6 = (f32[16,128]{1,0:T(8,128)S(1)}, f32[16,128]{1,0:T(8,128)S(1)}, u32[]{:S(2)}, u32[]{:S(2)}) collective-permute-start(f32[16,128]{1,0:T(8,128)S(1)} %get-tuple-element.33.refs_0_), channel_id=1, source_target_pairs={{0,6},{1,7},{2,4},{3,5},{4,2},{5,3},{6,0},{7,1},{8,14},{9,15},{10,... | collective-permute-start | bytes 24584 | tf_op jit(solution)/shard_map/ppermute | solution.py:300
  32.9 4.5 %collective-permute-start.5 = (f32[16,128]{1,0:T(8,128)S(1)}, f32[16,128]{1,0:T(8,128)S(1)}, u32[]{:S(2)}, u32[]{:S(2)}) collective-permute-start(f32[16,128]{1,0:T(8,128)S(1)} %get-tuple-element.33.refs_0_), channel_id=1, source_target_pairs={{0,4},{1,5},{2,6},{3,7},{4,0},{5,1},{6,2},{7,3},{8,12},{9,13},{10,... | collective-permute-start | bytes 24584 | tf_op jit(solution)/shard_map/ppermute | solution.py:300
  33.3 4.3 %collective-permute-start.4 = (f32[16,128]{1,0:T(8,128)S(1)}, f32[16,128]{1,0:T(8,128)S(1)}, u32[]{:S(2)}, u32[]{:S(2)}) collective-permute-start(f32[16,128]{1,0:T(8,128)S(1)} %get-tuple-element.33.refs_0_), channel_id=1, source_target_pairs={{0,2},{1,3},{2,0},{3,1},{4,6},{5,7},{6,4},{7,5},{8,10},{9,11},{10,... | collective-permute-start | bytes 24584 | tf_op jit(solution)/shard_map/ppermute | solution.py:300
  39.9 3.1 %collective-permute-start.9 = (f32[1,2048]{1,0:T(1,128)S(1)}, f32[1,2048]{1,0:T(1,128)S(1)}, u32[]{:S(2)}, u32[]{:S(2)}) collective-permute-start(f32[1,2048]{1,0:T(1,128)S(1)} %col_later.2.refs_0_), channel_id=1, source_target_pairs={{0,24},{8,16},{16,8},{24,0},{1,25},{9,17},{17,9},{25,1},{2,26},{10... | collective-permute-start | bytes 24584 | tf_op jit(solution)/shard_map/ppermute | solution.py:300
  40.0 3.7 %collective-permute-start.8 = (f32[1,2048]{1,0:T(1,128)S(1)}, f32[1,2048]{1,0:T(1,128)S(1)}, u32[]{:S(2)}, u32[]{:S(2)}) collective-permute-start(f32[1,2048]{1,0:T(1,128)S(1)} %col_later.2.refs_0_), channel_id=1, source_target_pairs={{0,16},{8,24},{16,0},{24,8},{1,17},{9,25},{17,1},{25,9},{2,18},{10... | collective-permute-start | bytes 24584 | tf_op jit(solution)/shard_map/ppermute | solution.py:300
  41.6 2.1 %collective-permute-start.7 = (f32[1,2048]{1,0:T(1,128)S(1)}, f32[1,2048]{1,0:T(1,128)S(1)}, u32[]{:S(2)}, u32[]{:S(2)}) collective-permute-start(f32[1,2048]{1,0:T(1,128)S(1)} %col_later.2.refs_0_), channel_id=1, source_target_pairs={{0,8},{8,0},{16,24},{24,16},{1,9},{9,1},{17,25},{25,17},{2,10},{10... | collective-permute-start | bytes 24584 | tf_op jit(solution)/shard_map/ppermute | solution.py:300
  46.2 5.5 %collective-permute-start.12 = (f32[16,128]{1,0:T(8,128)S(1)}, f32[16,128]{1,0:T(8,128)S(1)}, u32[]{:S(2)}, u32[]{:S(2)}) collective-permute-start(f32[16,128]{1,0:T(8,128)S(1)} %row_later.1.refs_0_), channel_id=1, source_target_pairs={{0,6},{1,7},{2,4},{3,5},{4,2},{5,3},{6,0},{7,1},{8,14},{9,15},{10,... | collective-permute-start | bytes 24584 | tf_op jit(solution)/shard_map/ppermute | solution.py:300
  48.6 4.5 %collective-permute-start.11 = (f32[16,128]{1,0:T(8,128)S(1)}, f32[16,128]{1,0:T(8,128)S(1)}, u32[]{:S(2)}, u32[]{:S(2)}) collective-permute-start(f32[16,128]{1,0:T(8,128)S(1)} %row_later.1.refs_0_), channel_id=1, source_target_pairs={{0,4},{1,5},{2,6},{3,7},{4,0},{5,1},{6,2},{7,3},{8,12},{9,13},{10,... | collective-permute-start | bytes 24584 | tf_op jit(solution)/shard_map/ppermute | solution.py:300
  49.7 3.7 %collective-permute-start.10 = (f32[16,128]{1,0:T(8,128)S(1)}, f32[16,128]{1,0:T(8,128)S(1)}, u32[]{:S(2)}, u32[]{:S(2)}) collective-permute-start(f32[16,128]{1,0:T(8,128)S(1)} %row_later.1.refs_0_), channel_id=1, source_target_pairs={{0,2},{1,3},{2,0},{3,1},{4,6},{5,7},{6,4},{7,5},{8,10},{9,11},{10,... | collective-permute-start | bytes 24584 | tf_op jit(solution)/shard_map/ppermute | solution.py:300
  55.8 3.1 %collective-permute-start.15 = (f32[1,2048]{1,0:T(1,128)S(1)}, f32[1,2048]{1,0:T(1,128)S(1)}, u32[]{:S(2)}, u32[]{:S(2)}) collective-permute-start(f32[1,2048]{1,0:T(1,128)S(1)} %col_later.3.refs_0_), channel_id=1, source_target_pairs={{0,24},{8,16},{16,8},{24,0},{1,25},{9,17},{17,9},{25,1},{2,26},{10... | collective-permute-start | bytes 24584 | tf_op jit(solution)/shard_map/ppermute | solution.py:300
  55.9 3.7 %collective-permute-start.14 = (f32[1,2048]{1,0:T(1,128)S(1)}, f32[1,2048]{1,0:T(1,128)S(1)}, u32[]{:S(2)}, u32[]{:S(2)}) collective-permute-start(f32[1,2048]{1,0:T(1,128)S(1)} %col_later.3.refs_0_), channel_id=1, source_target_pairs={{0,16},{8,24},{16,0},{24,8},{1,17},{9,25},{17,1},{25,9},{2,18},{10... | collective-permute-start | bytes 24584 | tf_op jit(solution)/shard_map/ppermute | solution.py:300
  57.5 2.1 %collective-permute-start.13 = (f32[1,2048]{1,0:T(1,128)S(1)}, f32[1,2048]{1,0:T(1,128)S(1)}, u32[]{:S(2)}, u32[]{:S(2)}) collective-permute-start(f32[1,2048]{1,0:T(1,128)S(1)} %col_later.3.refs_0_), channel_id=1, source_target_pairs={{0,8},{8,0},{16,24},{24,16},{1,9},{9,1},{17,25},{25,17},{2,10},{10... | collective-permute-start | bytes 24584 | tf_op jit(solution)/shard_map/ppermute | solution.py:300
  62.7 5.5 %collective-permute-start.18 = (f32[16,128]{1,0:T(8,128)S(1)}, f32[16,128]{1,0:T(8,128)S(1)}, u32[]{:S(2)}, u32[]{:S(2)}) collective-permute-start(f32[16,128]{1,0:T(8,128)S(1)} %get-tuple-element.36.refs_0_), channel_id=1, source_target_pairs={{0,6},{1,7},{2,4},{3,5},{4,2},{5,3},{6,0},{7,1},{8,14},{9,15},{10,... | collective-permute-start | bytes 24584 | tf_op jit(solution)/shard_map/ppermute | solution.py:300
  64.1 4.5 %collective-permute-start.17 = (f32[16,128]{1,0:T(8,128)S(1)}, f32[16,128]{1,0:T(8,128)S(1)}, u32[]{:S(2)}, u32[]{:S(2)}) collective-permute-start(f32[16,128]{1,0:T(8,128)S(1)} %get-tuple-element.36.refs_0_), channel_id=1, source_target_pairs={{0,4},{1,5},{2,6},{3,7},{4,0},{5,1},{6,2},{7,3},{8,12},{9,13},{10,... | collective-permute-start | bytes 24584 | tf_op jit(solution)/shard_map/ppermute | solution.py:300
  65.1 3.7 %collective-permute-start.16 = (f32[16,128]{1,0:T(8,128)S(1)}, f32[16,128]{1,0:T(8,128)S(1)}, u32[]{:S(2)}, u32[]{:S(2)}) collective-permute-start(f32[16,128]{1,0:T(8,128)S(1)} %get-tuple-element.36.refs_0_), channel_id=1, source_target_pairs={{0,2},{1,3},{2,0},{3,1},{4,6},{5,7},{6,4},{7,5},{8,10},{9,11},{10,... | collective-permute-start | bytes 24584 | tf_op jit(solution)/shard_map/ppermute | solution.py:300
  69.8 3.3 %collective-permute-start.19 = (f32[32,128]{1,0:T(8,128)S(1)}, f32[32,128]{1,0:T(8,128)S(1)}, u32[]{:S(2)}, u32[]{:S(2)}) collective-permute-start(f32[32,128]{1,0:T(8,128)S(1)} %get-tuple-element.39), channel_id=1, source_target_pairs={{0,24},{8,16},{16,8},{24,0},{1,25},{9,17},{17,9},{25,1},{2,26},{10... | collective-permute-start | bytes 49160 | tf_op jit(solution)/shard_map/ppermute | solution.py:300
  69.8 3.8 %collective-permute-start.20 = (f32[32,128]{1,0:T(8,128)S(1)}, f32[32,128]{1,0:T(8,128)S(1)}, u32[]{:S(2)}, u32[]{:S(2)}) collective-permute-start(f32[32,128]{1,0:T(8,128)S(1)} %get-tuple-element.40), channel_id=1, source_target_pairs={{0,16},{8,24},{16,0},{24,8},{1,17},{9,25},{17,1},{25,9},{2,18},{10... | collective-permute-start | bytes 49160 | tf_op jit(solution)/shard_map/ppermute | solution.py:300
  71.3 2.2 %collective-permute-start.21 = (f32[32,128]{1,0:T(8,128)S(1)}, f32[32,128]{1,0:T(8,128)S(1)}, u32[]{:S(2)}, u32[]{:S(2)}) collective-permute-start(f32[32,128]{1,0:T(8,128)S(1)} %get-tuple-element.41), channel_id=1, source_target_pairs={{0,8},{8,0},{16,24},{24,16},{1,9},{9,1},{17,25},{25,17},{2,10},{10... | collective-permute-start | bytes 49160 | tf_op jit(solution)/shard_map/ppermute | solution.py:300
  73.5 5.6 %collective-permute-start.24 = (f32[32,128]{1,0:T(8,128)S(1)}, f32[32,128]{1,0:T(8,128)S(1)}, u32[]{:S(2)}, u32[]{:S(2)}) collective-permute-start(f32[32,128]{1,0:T(8,128)S(1)} %share_sum.2.refs_0_), channel_id=1, source_target_pairs={{0,6},{1,7},{2,4},{3,5},{4,2},{5,3},{6,0},{7,1},{8,14},{9,15},{10,... | collective-permute-start | bytes 49160 | tf_op jit(solution)/shard_map/ppermute | solution.py:300
  76.0 4.6 %collective-permute-start.23 = (f32[32,128]{1,0:T(8,128)S(1)}, f32[32,128]{1,0:T(8,128)S(1)}, u32[]{:S(2)}, u32[]{:S(2)}) collective-permute-start(f32[32,128]{1,0:T(8,128)S(1)} %share_sum.2.refs_0_), channel_id=1, source_target_pairs={{0,4},{1,5},{2,6},{3,7},{4,0},{5,1},{6,2},{7,3},{8,12},{9,13},{10,... | collective-permute-start | bytes 49160 | tf_op jit(solution)/shard_map/ppermute | solution.py:300
  77.1 3.8 %collective-permute-start.22 = (f32[32,128]{1,0:T(8,128)S(1)}, f32[32,128]{1,0:T(8,128)S(1)}, u32[]{:S(2)}, u32[]{:S(2)}) collective-permute-start(f32[32,128]{1,0:T(8,128)S(1)} %share_sum.2.refs_0_), channel_id=1, source_target_pairs={{0,2},{1,3},{2,0},{3,1},{4,6},{5,7},{6,4},{7,5},{8,10},{9,11},{10,... | collective-permute-start | bytes 49160 | tf_op jit(solution)/shard_map/ppermute | solution.py:300
  80.9 3.3 %collective-permute-start.27 = (f32[32,128]{1,0:T(8,128)S(1)}, f32[32,128]{1,0:T(8,128)S(1)}, u32[]{:S(2)}, u32[]{:S(2)}) collective-permute-start(f32[32,128]{1,0:T(8,128)S(1)} %share_sum.3.refs_0_), channel_id=1, source_target_pairs={{0,24},{8,16},{16,8},{24,0},{1,25},{9,17},{17,9},{25,1},{2,26},{10... | collective-permute-start | bytes 49160 | tf_op jit(solution)/shard_map/ppermute | solution.py:300
  80.9 3.8 %collective-permute-start.26 = (f32[32,128]{1,0:T(8,128)S(1)}, f32[32,128]{1,0:T(8,128)S(1)}, u32[]{:S(2)}, u32[]{:S(2)}) collective-permute-start(f32[32,128]{1,0:T(8,128)S(1)} %share_sum.3.refs_0_), channel_id=1, source_target_pairs={{0,16},{8,24},{16,0},{24,8},{1,17},{9,25},{17,1},{25,9},{2,18},{10... | collective-permute-start | bytes 49160 | tf_op jit(solution)/shard_map/ppermute | solution.py:300
  82.5 2.2 %collective-permute-start.25 = (f32[32,128]{1,0:T(8,128)S(1)}, f32[32,128]{1,0:T(8,128)S(1)}, u32[]{:S(2)}, u32[]{:S(2)}) collective-permute-start(f32[32,128]{1,0:T(8,128)S(1)} %share_sum.3.refs_0_), channel_id=1, source_target_pairs={{0,8},{8,0},{16,24},{24,16},{1,9},{9,1},{17,25},{25,17},{2,10},{10... | collective-permute-start | bytes 49160 | tf_op jit(solution)/shard_map/ppermute | solution.py:300

commit v2 on v1

--- a/solution.py
+++ b/solution.py
@@ -91,7 +91,7 @@
 
 
 def row_first(
-    unit, scale, source_hbm, map_hbm, target_hbm, pot_hbm, left_out, right_out, lse_out, turned_out,
+    unit, scale, source_hbm, map_hbm, target_hbm, pot_hbm, left_out, right_out, lse_out, turned_out, plain_out,
     source, start_map, target, pot, work, peaks, totals, sums, sems,
 ):
     copies = [
@@ -111,6 +111,7 @@
         right_out[at, :width] = target[at, :]
         right_out[at, width:] = lane_parts(to_column(pot[:, at] * (1.0 / scale)))
     left_out[...] = jnp.dot(source[...], start_map[...].astype(BF16), preferred_element_type=F32).astype(BF16)
+    plain_out[...] = target[...].astype(F32)
     for part in range(rows // LANES):
         here = slice(part * LANES, (part + 1) * LANES)
         turned_out[:, here] = source[here, :].T
@@ -136,7 +137,7 @@
 
 
 def col_first(group, unit, log_rows, left_in, own, other, *refs):
-    parts, (block_out, target_out, pot_out, peak_out, lse_out, left, right, work) = received(refs, group)
+    parts, (block_out, target_out, pot_out, peak_out, lse_out, left, right, *work) = received(refs, group)
     row_pot = -log_rows - tree_lse(unit, parts)
     pot_out[...] = row_pot
     rows, width = left_in.shape
@@ -151,26 +152,39 @@
     left[:, :width] = left_in[...]
     for part in range(rows // LANES):
         left[part * LANES : (part + 1) * LANES, width:] = lane_parts(to_column(row_pot[part : part + 1, :]))
-    peak = None
-    for start in range(0, rows, CHUNK):
-        value = dot_t(left[start : start + CHUNK, :], right[...])
-        work[start : start + CHUNK, :] = value
-        top = jnp.max(value.reshape(CHUNK // 8, 8, cols), axis=0)
-        peak = top if peak is None else jnp.maximum(peak, top)
-    peak = jnp.max(peak, axis=0, keepdims=True)
-    group_rows = 16
-
-    def sums(step, total):
-        for k in range(0, LANES, group_rows):
-            at = pl.ds(pl.multiple_of(step * LANES + k, group_rows), group_rows)
-            value = jnp.exp2((work[at, :] - peak) * unit)
-            block_out[at, :] = value.astype(BF16)
+    span = work[0].shape[1]
+    spans = [slice(at, at + span) for at in range(0, cols, span)]
+    low = jnp.full((8, span), -jnp.inf, F32)
+
+    def chunk_of(step):
+        return pl.ds(pl.multiple_of(step * CHUNK, CHUNK), CHUNK)
+
+    def product(step, top, k):
+        value = dot_t(left[chunk_of(step), :], right[spans[k], :])
+        work[k % 2][chunk_of(step), :] = value
+        return jnp.maximum(top, jnp.max(value.reshape(CHUNK // 8, 8, span), axis=0))
+
+    def weigh(step, total, k, peak):
+        for at in range(0, CHUNK, 16):
+            here = pl.ds(pl.multiple_of(step * CHUNK + at, 16), 16)
+            value = jnp.exp2((work[k % 2][here, :] - peak) * unit)
+            block_out[here, spans[k]] = value.astype(BF16)
             total = total + value[:8] + value[8:]
         return total
 
-    total = lax.fori_loop(0, rows // LANES, sums, jnp.zeros((8, cols), F32))
-    peak_out[...] = peak
-    lse_out[...] = peak + jnp.log(jnp.sum(total, axis=0, keepdims=True)) * (1.0 / (unit * math.log(2.0)))
+    top = lax.fori_loop(0, rows // CHUNK, functools.partial(product, k=0), low)
+    for k in range(len(spans)):
+        peak = jnp.max(top, axis=0, keepdims=True)
+
+        def both(step, carry):
+            total, top = carry
+            if k + 1 < len(spans):
+                top = product(step, top, k + 1)
+            return weigh(step, total, k, peak), top
+
+        total, top = lax.fori_loop(0, rows // CHUNK, both, (jnp.zeros((8, span), F32), low))
+        peak_out[:, spans[k]] = peak
+        lse_out[:, spans[k]] = peak + jnp.log(jnp.sum(total, axis=0, keepdims=True)) * (1.0 / (unit * math.log(2.0)))
 
 
 def column_factors(row):
@@ -179,10 +193,17 @@
 
 
 def row_sums(block, row, sums_out):
-    weights = jnp.concatenate(split(column_factors(row)), axis=1)
-    for start in range(0, block.shape[0], CHUNK):
-        wide = jnp.dot(block[start : start + CHUNK, :], weights, preferred_element_type=F32)
-        sums = wide[:, :LANES] + wide[:, LANES:]
+    rows, cols = block.shape
+    cut = cols * 5 // 8 // 256 * 256
+    weights = jnp.concatenate(split(column_factors(row[:, :cut])), axis=1)
+    tiles = [(at, jnp.broadcast_to(row[:, at : at + LANES], (16, LANES))) for at in range(cut, cols, LANES)]
+    for start in range(0, rows, CHUNK):
+        wide = jnp.dot(block[start : start + CHUNK, :cut], weights, preferred_element_type=F32)
+        rest = []
+        for here in range(start, start + CHUNK, 16):
+            terms = [block[here : here + 16, at : at + LANES].astype(F32) * factor for at, factor in tiles]
+            rest.append(jnp.sum(functools.reduce(jnp.add, terms), axis=1, keepdims=True))
+        sums = wide[:, :LANES] + wide[:, LANES:] + jnp.concatenate(rest, axis=0)
         for part in range(CHUNK // LANES):
             at = start // LANES + part
             sums_out[at : at + 1, :] = to_lanes(sums[part * LANES : (part + 1) * LANES])
@@ -198,22 +219,26 @@
 
 
 def col_later(group, ratio, block, scale, *refs):
-    parts, (sums_out, factor) = received(refs, group)
+    parts, (sums_out,) = received(refs, group)
     factors = ratio / tree_sum(parts)
     rows, cols = block.shape
-    for part in range(rows // LANES):
-        factor[part * LANES : (part + 1) * LANES, :] = to_column(factors[part : part + 1, :])
-    group_rows = 16
-
-    def sums(step, total):
-        for k in range(0, LANES, group_rows):
-            at = pl.ds(pl.multiple_of(step * LANES + k, group_rows), group_rows)
-            value = block[at, :].astype(F32) * jnp.concatenate([factor[at, :]] * (cols // LANES), axis=1)
-            total = total + value[:8] + value[8:]
-        return total
-
-    total = lax.fori_loop(0, rows // LANES, sums, jnp.zeros((8, cols), F32))
-    sums_out[...] = scale[...] * jnp.sum(total, axis=0, keepdims=True)
+    cut = cols // 2
+    row = jnp.concatenate([factors[k : k + 1, :] for k in range(rows // LANES)], axis=1)
+    high, low = split(row)
+    pair = jnp.concatenate([high.astype(F32), low.astype(F32), jnp.zeros((14, rows), F32)], axis=0).astype(BF16)
+    product = jnp.zeros((16, cut), F32)
+    total = jnp.zeros((8, cols - cut), F32)
+    for start in range(0, rows, CHUNK):
+        product += jnp.dot(pair[:, start : start + CHUNK], block[start : start + CHUNK, :cut], preferred_element_type=F32)
+        for part in range(start // LANES, (start + CHUNK) // LANES):
+            column = to_column(factors[part : part + 1, :])
+            for at in range(0, LANES, 16):
+                here = slice(part * LANES + at, part * LANES + at + 16)
+                factor = jnp.concatenate([column[at : at + 16]] * ((cols - cut) // LANES), axis=1)
+                value = block[here, cut:].astype(F32) * factor
+                total = total + value[:8] + value[8:]
+    sums_out[:, :cut] = scale[:, :cut] * (product[0:1] + product[1:2])
+    sums_out[:, cut:] = scale[:, cut:] * jnp.sum(total, axis=0, keepdims=True)
 
 
 def row_later(group, block, scale, *refs):
@@ -327,8 +352,7 @@
     pair_vec = jax.ShapeDtypeStruct((1, 2 * cols), F32)
     mac = rows * cols * width
 
-    other = lax.ppermute(target.astype(F32), "tgt", [(me, me ^ 1) for me in range(n_tgt)])
-    left, right, lse, turned = call(
+    left, right, lse, turned, plain = call(
         functools.partial(row_first, unit, scale),
         "row_first",
         (
@@ -336,6 +360,7 @@
             jax.ShapeDtypeStruct((cols, width + LANES), BF16),
             row_vec,
             jax.ShapeDtypeStruct((width, rows), BF16),
+            jax.ShapeDtypeStruct((cols, width), F32),
         ),
         scratch=[
             pltpu.VMEM((rows, width), BF16),
@@ -351,6 +376,7 @@
         flops=4 * mac,
         space=pltpu.HBM,
     )(*[pltpu.with_memory_space_constraint(x, pltpu.HBM) for x in (source, start_map, target, warm_potential.reshape(1, cols))])
+    other = lax.ppermute(plain, "tgt", [(me, me ^ 1) for me in range(n_tgt)])
     block, targets, row_pot, peak, lse = call(
         functools.partial(col_first, n_tgt, unit, log_rows),
         "col_first",
@@ -364,7 +390,8 @@
         scratch=[
             pltpu.VMEM((rows, width + LANES), BF16),
             pltpu.VMEM((2 * cols, width + LANES), BF16),
-            pltpu.VMEM((rows, 2 * cols), F32),
+            pltpu.VMEM((rows, math.gcd(2 * cols, 512)), F32),
+            pltpu.VMEM((rows, math.gcd(2 * cols, 512)), F32),
         ],
         flops=8 * mac,
     )(left, right, other, over_tgt(lse))
@@ -375,7 +402,6 @@
         functools.partial(col_later, n_pairs, ratio),
         "col_later",
         pair_vec,
-        scratch=[pltpu.VMEM((rows, LANES), F32)],
         flops=4 * mac,
     )
     sums = col_later_call(block, col_scale, *over_pairs(sums))

time: 88.8 us -> 92.1 us (1.037)
  Pallas kernels: 26.7 us -> 28.5 us
  waiting for transfers between devices: 18.4 us -> 19.7 us
  blocking collectives: 11.6 us -> 12.6 us
  other arithmetic: 0.99 us -> 0 us
    pallas_call x11, Pallas kernels: 26.7 us -> 28.5 us  [call(): pl.pallas_call(body, name=name, out_shape=out_shape, in_specs=[pl.BlockSp...]
    ppermute x27, waiting for transfers between devices: 18.4 us -> 19.7 us  [partners(): lax.ppermute(values[k], axis, [(me, me ^ k) for me in range(size)])]
    all_to_all x1, blocking collectives: 11.6 us -> 12.6 us  [over_tgt(): lax.all_to_all(jnp.broadcast_to(x, (lax.axis_size('tgt'),) + x.shape), 't...]
    convert_element_type x1 -> x0, other arithmetic: 0.99 us -> none  [shards(): target.astype(F32)]
  transfers between devices with their start and end apart: 28 -> 28, of which waited for: 22 -> 21; matrix products, arithmetic and copies ran while one was open for 0% -> 0% of each run, Pallas kernels for 4% -> 0%
where the time goes in v2:
time: 92.1 us; the launch traced here: 91.9 us
  starting transfers between devices  30.4 us (33%)
  Pallas kernels  28.5 us (31%)
  waiting for transfers between devices  19.7 us (21%)
  blocking collectives  12.6 us (14%)
    pallas_call x11, Pallas kernels, call(): pl.pallas_call(body, name=name, out_shape=out_shape, in_specs=[pl.BlockSp...  28.5 us
    ppermute x27, starting transfers between devices, partners(): lax.ppermute(values[k], axis, [(me, me ^ k) for me in range(size)])  27.4 us
    ppermute x27, waiting for transfers between devices, partners(): lax.ppermute(values[k], axis, [(me, me ^ k) for me in range(size)])  19.7 us
    all_to_all x1, blocking collectives, over_tgt(): lax.all_to_all(jnp.broadcast_to(x, (lax.axis_size('tgt'),) + x.shape), 't...  12.6 us
    ppermute x1, starting transfers between devices, shards(): other = lax.ppermute(plain, 'tgt', [(me, me ^ 1) for me in range(n_tgt)])  3 us
  transfers between devices with their start and end apart: 28, of which 21 were waited for; matrix products, arithmetic and copies ran while one was open for 0% of the time, Pallas kernels for 0%

profile of v2, /device:TPU:0, one launch (start us, length us, event | category | flops | bytes accessed | tf_op | source)
XLA Modules:
  0.0 91.9 jit_solution(13336831262122115398)
XLA Ops:
  0.6 3.5 %row_first.1 = (bf16[2048,128]{1,0:T(8,128)(2,1)S(1)}, bf16[1024,256]{1,0:T(8,128)(2,1)S(1)}, f32[16,128]{1,0:T(8,128)S(1)}, bf16[128,2048]{1,0:T(8,128)(2,1)S(1)}, f32[1024,128]{1,0:T(8,128)S(1)}) custom-call(bf16[2048,128]{1,0:T(8,128)(2,1)} %source_hbm.1, f32[128,128]{1,0:T(8,128)} %map_hbm.1, bf16[1024,128]{1,0:T(8,128)(2,1)} %target_hbm.1, ...), custom_call_target="tpu_custom_call" | custom-call | flops 1073741824 | bytes 8388608 | tf_op jit(solution)/shard_map/row_first/pallas_call | solution.py:22
  4.2 3.0 %collective-permute-start = (f32[1024,128]{1,0:T(8,128)S(1)}, f32[1024,128]{1,0:T(8,128)S(1)}, u32[]{:S(2)}, u32[]{:S(2)}) collective-permute-start(f32[1024,128]{1,0:T(8,128)S(1)} %get-tuple-element.27), channel_id=1, source_target_pairs={{0,1},{1,0},{2,3},{3,2},{4,5},{5,4},{6,7},{7,6},{8,9},{9,8},{10,11... | collective-permute-start | bytes 1572872 | tf_op jit(solution)/shard_map/ppermute | solution.py:379
  7.2 12.6 %all_to_all.5.refs_0_ = f32[8,16,128]{2,1,0:T(8,128)S(1)} all-to-all(f32[8,16,128]{2,1,0:T(8,128)S(1)} %broadcast_in_dim.3), channel_id=1, replica_groups=mesh['src'=4,'tgt'=8] {'tgt'}, dimensions={0} | all-to-all | bytes 131072 | tf_op jit(solution)/shard_map/all_to_all | solution.py:339
  19.8 10.4 %col_first.1 = (bf16[2048,2048]{1,0:T(8,128)(2,1)S(1)}, bf16[2048,128]{1,0:T(8,128)(2,1)S(1)}, f32[16,128]{1,0:T(8,128)S(1)}, f32[1,2048]{1,0:T(1,128)S(1)}, f32[1,2048]{1,0:T(1,128)S(1)}) custom-call(bf16[2048,128]{1,0:T(8,128)(2,1)S(1)} %get-tuple-element.25.left_in, bf16[1024,256]{1,0:T(8,128)(2,1)S(1)} %get-tuple-element.26.own, ...), custom_call_target="tpu_custom_call" | custom-call | flops 2147483648 | bytes 8388608 | tf_op jit(solution)/shard_map/col_first/pallas_call | solution.py:22
  30.6 1.5 %collective-permute-start.2 = (f32[1,2048]{1,0:T(1,128)S(1)}, f32[1,2048]{1,0:T(1,128)S(1)}, u32[]{:S(2)}, u32[]{:S(2)}) collective-permute-start(f32[1,2048]{1,0:T(1,128)S(1)} %get-tuple-element.31.refs_0_), channel_id=1, source_target_pairs={{0,16},{8,24},{16,0},{24,8},{1,17},{9,25},{17,1},{25,9},{2,18},{10... | collective-permute-start | bytes 24584 | tf_op jit(solution)/shard_map/ppermute | solution.py:325
  32.2 1.2 %collective-permute-done.3.refs_3_ = f32[1,2048]{1,0:T(1,128)S(1)} collective-permute-done((f32[1,2048]{1,0:T(1,128)S(1)}, f32[1,2048]{1,0:T(1,128)S(1)}, u32[]{:S(2)}, u32[]{:S(2)}) %collective-permute-start.3) | collective-permute-done | bytes 8224 | tf_op jit(solution)/shard_map/ppermute | solution.py:325
  34.3 2.1 %row_second.1 = (f32[1,2048]{1,0:T(1,128)S(1)}, f32[1,2048]{1,0:T(1,128)S(1)}, f32[16,128]{1,0:T(8,128)S(1)}) custom-call(bf16[2048,2048]{1,0:T(8,128)(2,1)S(1)} %get-tuple-element.29.block, f32[1,2048]{1,0:T(1,128)S(1)} %get-tuple-element.30.peak, f32[1,2048]{1,0:T(1,128)S(1)} %get-tuple-element.31.refs_0_, f32[1,2048]{1,0:T(1,128)S(1)} %collective-permute-done.1.refs_1_, ...), custom_call_target="tpu_custom_call" | custom-call | flops 1073741824 | bytes 8388608 | tf_op jit(solution)/shard_map/row_second/pallas_call | solution.py:22
  36.4 3.7 %collective-permute-start.6 = (f32[16,128]{1,0:T(8,128)S(1)}, f32[16,128]{1,0:T(8,128)S(1)}, u32[]{:S(2)}, u32[]{:S(2)}) collective-permute-start(f32[16,128]{1,0:T(8,128)S(1)} %get-tuple-element.35.refs_0_), channel_id=1, source_target_pairs={{0,6},{1,7},{2,4},{3,5},{4,2},{5,3},{6,0},{7,1},{8,14},{9,15},{10,... | collective-permute-start | bytes 24584 | tf_op jit(solution)/shard_map/ppermute | solution.py:325
  40.8 1.1 %collective-permute-done.6.refs_3_ = f32[16,128]{1,0:T(8,128)S(1)} collective-permute-done((f32[16,128]{1,0:T(8,128)S(1)}, f32[16,128]{1,0:T(8,128)S(1)}, u32[]{:S(2)}, u32[]{:S(2)}) %collective-permute-start.6) | collective-permute-done | bytes 8224 | tf_op jit(solution)/shard_map/ppermute | solution.py:325
  41.9 2.7 %collective-permute-done.5.refs_2_ = f32[16,128]{1,0:T(8,128)S(1)} collective-permute-done((f32[16,128]{1,0:T(8,128)S(1)}, f32[16,128]{1,0:T(8,128)S(1)}, u32[]{:S(2)}, u32[]{:S(2)}) %collective-permute-start.5) | collective-permute-done | bytes 8224 | tf_op jit(solution)/shard_map/ppermute | solution.py:325
  44.6 1.2 %col_later.2.refs_0_ = f32[1,2048]{1,0:T(1,128)S(1)} custom-call(bf16[2048,2048]{1,0:T(8,128)(2,1)S(1)} %get-tuple-element.29.block, f32[1,2048]{1,0:T(1,128)S(1)} %get-tuple-element.32.scale, f32[16,128]{1,0:T(8,128)S(1)} %get-tuple-element.35.refs_0_, f32[16,128]{1,0:T(8,128)S(1)} %collective-permute-done.4.refs_1_, ...), custom_call_target="tpu_custom_call" | custom-call | flops 1073741824 | bytes 8388608 | tf_op jit(solution)/shard_map/col_later/pallas_call | solution.py:22
  45.9 1.6 %collective-permute-start.8 = (f32[1,2048]{1,0:T(1,128)S(1)}, f32[1,2048]{1,0:T(1,128)S(1)}, u32[]{:S(2)}, u32[]{:S(2)}) collective-permute-start(f32[1,2048]{1,0:T(1,128)S(1)} %col_later.2.refs_0_), channel_id=1, source_target_pairs={{0,16},{8,24},{16,0},{24,8},{1,17},{9,25},{17,1},{25,9},{2,18},{10... | collective-permute-start | bytes 24584 | tf_op jit(solution)/shard_map/ppermute | solution.py:325
  47.8 1.2 %collective-permute-done.9.refs_3_ = f32[1,2048]{1,0:T(1,128)S(1)} collective-permute-done((f32[1,2048]{1,0:T(1,128)S(1)}, f32[1,2048]{1,0:T(1,128)S(1)}, u32[]{:S(2)}, u32[]{:S(2)}) %collective-permute-start.9) | collective-permute-done | bytes 8224 | tf_op jit(solution)/shard_map/ppermute | solution.py:325
  49.7 2.1 %row_later.1.refs_0_ = f32[16,128]{1,0:T(8,128)S(1)} custom-call(bf16[2048,2048]{1,0:T(8,128)(2,1)S(1)} %get-tuple-element.29.block, f32[1,2048]{1,0:T(1,128)S(1)} %get-tuple-element.32.scale, f32[1,2048]{1,0:T(1,128)S(1)} %col_later.2.refs_0_, f32[1,2048]{1,0:T(1,128)S(1)} %collective-permute-done.7.refs_1_, f32[1,2048]{1,0:T(1,128)S(1)} %collective-permute-done.8.refs_2_, ...), custom_call_target="tpu_custom_call" | custom-call | flops 1073741824 | bytes 8388608 | tf_op jit(solution)/shard_map/row_later/pallas_call | solution.py:22
  51.7 1.5 %collective-permute-start.12 = (f32[16,128]{1,0:T(8,128)S(1)}, f32[16,128]{1,0:T(8,128)S(1)}, u32[]{:S(2)}, u32[]{:S(2)}) collective-permute-start(f32[16,128]{1,0:T(8,128)S(1)} %row_later.1.refs_0_), channel_id=1, source_target_pairs={{0,6},{1,7},{2,4},{3,5},{4,2},{5,3},{6,0},{7,1},{8,14},{9,15},{10,... | collective-permute-start | bytes 24584 | tf_op jit(solution)/shard_map/ppermute | solution.py:325
  53.9 2.3 %collective-permute-start.10 = (f32[16,128]{1,0:T(8,128)S(1)}, f32[16,128]{1,0:T(8,128)S(1)}, u32[]{:S(2)}, u32[]{:S(2)}) collective-permute-start(f32[16,128]{1,0:T(8,128)S(1)} %row_later.1.refs_0_), channel_id=1, source_target_pairs={{0,2},{1,3},{2,0},{3,1},{4,6},{5,7},{6,4},{7,5},{8,10},{9,11},{10,... | collective-permute-start | bytes 24584 | tf_op jit(solution)/shard_map/ppermute | solution.py:325
  56.2 1.1 %collective-permute-done.12.refs_3_ = f32[16,128]{1,0:T(8,128)S(1)} collective-permute-done((f32[16,128]{1,0:T(8,128)S(1)}, f32[16,128]{1,0:T(8,128)S(1)}, u32[]{:S(2)}, u32[]{:S(2)}) %collective-permute-start.12) | collective-permute-done | bytes 8224 | tf_op jit(solution)/shard_map/ppermute | solution.py:325
  57.9 1.2 %col_later.3.refs_0_ = f32[1,2048]{1,0:T(1,128)S(1)} custom-call(bf16[2048,2048]{1,0:T(8,128)(2,1)S(1)} %get-tuple-element.29.block, f32[1,2048]{1,0:T(1,128)S(1)} %get-tuple-element.32.scale, f32[16,128]{1,0:T(8,128)S(1)} %row_later.1.refs_0_, f32[16,128]{1,0:T(8,128)S(1)} %collective-permute-done.10.refs_1_, ...), custom_call_target="tpu_custom_call" | custom-call | flops 1073741824 | bytes 8388608 | tf_op jit(solution)/shard_map/col_later/pallas_call | solution.py:22
  59.2 1.6 %collective-permute-start.14 = (f32[1,2048]{1,0:T(1,128)S(1)}, f32[1,2048]{1,0:T(1,128)S(1)}, u32[]{:S(2)}, u32[]{:S(2)}) collective-permute-start(f32[1,2048]{1,0:T(1,128)S(1)} %col_later.3.refs_0_), channel_id=1, source_target_pairs={{0,16},{8,24},{16,0},{24,8},{1,17},{9,25},{17,1},{25,9},{2,18},{10... | collective-permute-start | bytes 24584 | tf_op jit(solution)/shard_map/ppermute | solution.py:325
  61.1 1.2 %collective-permute-done.15.refs_3_ = f32[1,2048]{1,0:T(1,128)S(1)} collective-permute-done((f32[1,2048]{1,0:T(1,128)S(1)}, f32[1,2048]{1,0:T(1,128)S(1)}, u32[]{:S(2)}, u32[]{:S(2)}) %collective-permute-start.15) | collective-permute-done | bytes 8224 | tf_op jit(solution)/shard_map/ppermute | solution.py:325
  63.0 3.1 %row_last.1 = (f32[1,1024]{1,0:T(1,128)}, f32[16,128]{1,0:T(8,128)S(1)}, f32[2048,128]{1,0:T(8,128)S(1)}) custom-call(bf16[2048,2048]{1,0:T(8,128)(2,1)S(1)} %get-tuple-element.29.block, f32[1,2048]{1,0:T(1,128)S(1)} %get-tuple-element.32.scale, f32[1,2048]{1,0:T(1,128)S(1)} %get-tuple-element.33.pot, bf16[2048,128]{1,0:T(8,128)(2,1)S(1)} %get-tuple-element.34.target, ...), custom_call_target="tpu_custom_call" | custom-call | flops 1073741824 | bytes 8388608 | tf_op jit(solution)/shard_map/row_last/pallas_call | solution.py:22
  66.0 2.5 %collective-permute-start.18 = (f32[16,128]{1,0:T(8,128)S(1)}, f32[16,128]{1,0:T(8,128)S(1)}, u32[]{:S(2)}, u32[]{:S(2)}) collective-permute-start(f32[16,128]{1,0:T(8,128)S(1)} %get-tuple-element.38.refs_0_), channel_id=1, source_target_pairs={{0,6},{1,7},{2,4},{3,5},{4,2},{5,3},{6,0},{7,1},{8,14},{9,15},{10,... | collective-permute-start | bytes 24584 | tf_op jit(solution)/shard_map/ppermute | solution.py:325
  70.4 1.1 %collective-permute-done.18.refs_3_ = f32[16,128]{1,0:T(8,128)S(1)} collective-permute-done((f32[16,128]{1,0:T(8,128)S(1)}, f32[16,128]{1,0:T(8,128)S(1)}, u32[]{:S(2)}, u32[]{:S(2)}) %collective-permute-start.18) | collective-permute-done | bytes 8224 | tf_op jit(solution)/shard_map/ppermute | solution.py:325
  71.5 1.6 %collective-permute-done.17.refs_2_ = f32[16,128]{1,0:T(8,128)S(1)} collective-permute-done((f32[16,128]{1,0:T(8,128)S(1)}, f32[16,128]{1,0:T(8,128)S(1)}, u32[]{:S(2)}, u32[]{:S(2)}) %collective-permute-start.17) | collective-permute-done | bytes 8224 | tf_op jit(solution)/shard_map/ppermute | solution.py:325
  74.2 1.5 %collective-permute-start.20 = (f32[32,128]{1,0:T(8,128)S(1)}, f32[32,128]{1,0:T(8,128)S(1)}, u32[]{:S(2)}, u32[]{:S(2)}) collective-permute-start(f32[32,128]{1,0:T(8,128)S(1)} %get-tuple-element.42), channel_id=1, source_target_pairs={{0,16},{8,24},{16,0},{24,8},{1,17},{9,25},{17,1},{25,9},{2,18},{10... | collective-permute-start | bytes 49160 | tf_op jit(solution)/shard_map/ppermute | solution.py:325
  76.0 1.4 %collective-permute-done.19.refs_0_ = f32[32,128]{1,0:T(8,128)S(1)} collective-permute-done((f32[32,128]{1,0:T(8,128)S(1)}, f32[32,128]{1,0:T(8,128)S(1)}, u32[]{:S(2)}, u32[]{:S(2)}) %collective-permute-start.19) | collective-permute-done | bytes 16416 | tf_op jit(solution)/shard_map/ppermute | solution.py:325
  78.0 1.4 %collective-permute-start.24 = (f32[32,128]{1,0:T(8,128)S(1)}, f32[32,128]{1,0:T(8,128)S(1)}, u32[]{:S(2)}, u32[]{:S(2)}) collective-permute-start(f32[32,128]{1,0:T(8,128)S(1)} %share_sum.2.refs_0_), channel_id=1, source_target_pairs={{0,6},{1,7},{2,4},{3,5},{4,2},{5,3},{6,0},{7,1},{8,14},{9,15},{10,... | collective-permute-start | bytes 49160 | tf_op jit(solution)/shard_map/ppermute | solution.py:325
  80.4 2.0 %collective-permute-start.22 = (f32[32,128]{1,0:T(8,128)S(1)}, f32[32,128]{1,0:T(8,128)S(1)}, u32[]{:S(2)}, u32[]{:S(2)}) collective-permute-start(f32[32,128]{1,0:T(8,128)S(1)} %share_sum.2.refs_0_), channel_id=1, source_target_pairs={{0,2},{1,3},{2,0},{3,1},{4,6},{5,7},{6,4},{7,5},{8,10},{9,11},{10,... | collective-permute-start | bytes 49160 | tf_op jit(solution)/shard_map/ppermute | solution.py:325
  82.4 1.2 %collective-permute-done.24.refs_3_ = f32[32,128]{1,0:T(8,128)S(1)} collective-permute-done((f32[32,128]{1,0:T(8,128)S(1)}, f32[32,128]{1,0:T(8,128)S(1)}, u32[]{:S(2)}, u32[]{:S(2)}) %collective-permute-start.24) | collective-permute-done | bytes 16416 | tf_op jit(solution)/shard_map/ppermute | solution.py:325
  84.3 1.6 %collective-permute-start.26 = (f32[32,128]{1,0:T(8,128)S(1)}, f32[32,128]{1,0:T(8,128)S(1)}, u32[]{:S(2)}, u32[]{:S(2)}) collective-permute-start(f32[32,128]{1,0:T(8,128)S(1)} %share_sum.3.refs_0_), channel_id=1, source_target_pairs={{0,16},{8,24},{16,0},{24,8},{1,17},{9,25},{17,1},{25,9},{2,18},{10... | collective-permute-start | bytes 49160 | tf_op jit(solution)/shard_map/ppermute | solution.py:325
  86.2 1.4 %collective-permute-done.27.refs_3_ = f32[32,128]{1,0:T(8,128)S(1)} collective-permute-done((f32[32,128]{1,0:T(8,128)S(1)}, f32[32,128]{1,0:T(8,128)S(1)}, u32[]{:S(2)}, u32[]{:S(2)}) %collective-permute-start.27) | collective-permute-done | bytes 16416 | tf_op jit(solution)/shard_map/ppermute | solution.py:325
  88.1 3.8 %polar.1 = f32[128,128]{1,0:T(8,128)} custom-call(f32[32,128]{1,0:T(8,128)S(1)} %share_sum.3.refs_0_, f32[32,128]{1,0:T(8,128)S(1)} %collective-permute-done.25.refs_1_, f32[32,128]{1,0:T(8,128)S(1)} %collective-permute-done.26.refs_2_, f32[32,128]{1,0:T(8,128)S(1)} %collective-permute-done.27.refs_3_), custom_call_target="tpu_custom_call" | custom-call | flops 134217728 | bytes 8388608 | tf_op jit(solution)/shard_map/polar/pallas_call | solution.py:22
  (37 shorter events, 11.8 us)
Async XLA Ops:
  4.2 15.6 %collective-permute-start = (f32[1024,128]{1,0:T(8,128)S(1)}, f32[1024,128]{1,0:T(8,128)S(1)}, u32[]{:S(2)}, u32[]{:S(2)}) collective-permute-start(f32[1024,128]{1,0:T(8,128)S(1)} %get-tuple-element.27), channel_id=1, source_target_pairs={{0,1},{1,0},{2,3},{3,2},{4,5},{5,4},{6,7},{7,6},{8,9},{9,8},{10,11... | collective-permute-start | bytes 1572872 | tf_op jit(solution)/shard_map/ppermute | solution.py:379
  30.2 3.1 %collective-permute-start.3 = (f32[1,2048]{1,0:T(1,128)S(1)}, f32[1,2048]{1,0:T(1,128)S(1)}, u32[]{:S(2)}, u32[]{:S(2)}) collective-permute-start(f32[1,2048]{1,0:T(1,128)S(1)} %get-tuple-element.31.refs_0_), channel_id=1, source_target_pairs={{0,24},{8,16},{16,8},{24,0},{1,25},{9,17},{17,9},{25,1},{2,26},{10... | collective-permute-start | bytes 24584 | tf_op jit(solution)/shard_map/ppermute | solution.py:325
  30.6 3.7 %collective-permute-start.2 = (f32[1,2048]{1,0:T(1,128)S(1)}, f32[1,2048]{1,0:T(1,128)S(1)}, u32[]{:S(2)}, u32[]{:S(2)}) collective-permute-start(f32[1,2048]{1,0:T(1,128)S(1)} %get-tuple-element.31.refs_0_), channel_id=1, source_target_pairs={{0,16},{8,24},{16,0},{24,8},{1,17},{9,25},{17,1},{25,9},{2,18},{10... | collective-permute-start | bytes 24584 | tf_op jit(solution)/shard_map/ppermute | solution.py:325
  32.1 2.1 %collective-permute-start.1 = (f32[1,2048]{1,0:T(1,128)S(1)}, f32[1,2048]{1,0:T(1,128)S(1)}, u32[]{:S(2)}, u32[]{:S(2)}) collective-permute-start(f32[1,2048]{1,0:T(1,128)S(1)} %get-tuple-element.31.refs_0_), channel_id=1, source_target_pairs={{0,8},{8,0},{16,24},{24,16},{1,9},{9,1},{17,25},{25,17},{2,10},{10... | collective-permute-start | bytes 24584 | tf_op jit(solution)/shard_map/ppermute | solution.py:325
  36.4 5.5 %collective-permute-start.6 = (f32[16,128]{1,0:T(8,128)S(1)}, f32[16,128]{1,0:T(8,128)S(1)}, u32[]{:S(2)}, u32[]{:S(2)}) collective-permute-start(f32[16,128]{1,0:T(8,128)S(1)} %get-tuple-element.35.refs_0_), channel_id=1, source_target_pairs={{0,6},{1,7},{2,4},{3,5},{4,2},{5,3},{6,0},{7,1},{8,14},{9,15},{10,... | collective-permute-start | bytes 24584 | tf_op jit(solution)/shard_map/ppermute | solution.py:325
  40.1 4.5 %collective-permute-start.5 = (f32[16,128]{1,0:T(8,128)S(1)}, f32[16,128]{1,0:T(8,128)S(1)}, u32[]{:S(2)}, u32[]{:S(2)}) collective-permute-start(f32[16,128]{1,0:T(8,128)S(1)} %get-tuple-element.35.refs_0_), channel_id=1, source_target_pairs={{0,4},{1,5},{2,6},{3,7},{4,0},{5,1},{6,2},{7,3},{8,12},{9,13},{10,... | collective-permute-start | bytes 24584 | tf_op jit(solution)/shard_map/ppermute | solution.py:325
  40.1 4.5 %collective-permute-start.4 = (f32[16,128]{1,0:T(8,128)S(1)}, f32[16,128]{1,0:T(8,128)S(1)}, u32[]{:S(2)}, u32[]{:S(2)}) collective-permute-start(f32[16,128]{1,0:T(8,128)S(1)} %get-tuple-element.35.refs_0_), channel_id=1, source_target_pairs={{0,2},{1,3},{2,0},{3,1},{4,6},{5,7},{6,4},{7,5},{8,10},{9,11},{10,... | collective-permute-start | bytes 24584 | tf_op jit(solution)/shard_map/ppermute | solution.py:325
  45.9 3.2 %collective-permute-start.9 = (f32[1,2048]{1,0:T(1,128)S(1)}, f32[1,2048]{1,0:T(1,128)S(1)}, u32[]{:S(2)}, u32[]{:S(2)}) collective-permute-start(f32[1,2048]{1,0:T(1,128)S(1)} %col_later.2.refs_0_), channel_id=1, source_target_pairs={{0,24},{8,16},{16,8},{24,0},{1,25},{9,17},{17,9},{25,1},{2,26},{10... | collective-permute-start | bytes 24584 | tf_op jit(solution)/shard_map/ppermute | solution.py:325
  45.9 3.7 %collective-permute-start.8 = (f32[1,2048]{1,0:T(1,128)S(1)}, f32[1,2048]{1,0:T(1,128)S(1)}, u32[]{:S(2)}, u32[]{:S(2)}) collective-permute-start(f32[1,2048]{1,0:T(1,128)S(1)} %col_later.2.refs_0_), channel_id=1, source_target_pairs={{0,16},{8,24},{16,0},{24,8},{1,17},{9,25},{17,1},{25,9},{2,18},{10... | collective-permute-start | bytes 24584 | tf_op jit(solution)/shard_map/ppermute | solution.py:325
  47.5 2.1 %collective-permute-start.7 = (f32[1,2048]{1,0:T(1,128)S(1)}, f32[1,2048]{1,0:T(1,128)S(1)}, u32[]{:S(2)}, u32[]{:S(2)}) collective-permute-start(f32[1,2048]{1,0:T(1,128)S(1)} %col_later.2.refs_0_), channel_id=1, source_target_pairs={{0,8},{8,0},{16,24},{24,16},{1,9},{9,1},{17,25},{25,17},{2,10},{10... | collective-permute-start | bytes 24584 | tf_op jit(solution)/shard_map/ppermute | solution.py:325
  51.7 5.5 %collective-permute-start.12 = (f32[16,128]{1,0:T(8,128)S(1)}, f32[16,128]{1,0:T(8,128)S(1)}, u32[]{:S(2)}, u32[]{:S(2)}) collective-permute-start(f32[16,128]{1,0:T(8,128)S(1)} %row_later.1.refs_0_), channel_id=1, source_target_pairs={{0,6},{1,7},{2,4},{3,5},{4,2},{5,3},{6,0},{7,1},{8,14},{9,15},{10,... | collective-permute-start | bytes 24584 | tf_op jit(solution)/shard_map/ppermute | solution.py:325
  53.3 4.5 %collective-permute-start.11 = (f32[16,128]{1,0:T(8,128)S(1)}, f32[16,128]{1,0:T(8,128)S(1)}, u32[]{:S(2)}, u32[]{:S(2)}) collective-permute-start(f32[16,128]{1,0:T(8,128)S(1)} %row_later.1.refs_0_), channel_id=1, source_target_pairs={{0,4},{1,5},{2,6},{3,7},{4,0},{5,1},{6,2},{7,3},{8,12},{9,13},{10,... | collective-permute-start | bytes 24584 | tf_op jit(solution)/shard_map/ppermute | solution.py:325
  53.9 4.0 %collective-permute-start.10 = (f32[16,128]{1,0:T(8,128)S(1)}, f32[16,128]{1,0:T(8,128)S(1)}, u32[]{:S(2)}, u32[]{:S(2)}) collective-permute-start(f32[16,128]{1,0:T(8,128)S(1)} %row_later.1.refs_0_), channel_id=1, source_target_pairs={{0,2},{1,3},{2,0},{3,1},{4,6},{5,7},{6,4},{7,5},{8,10},{9,11},{10,... | collective-permute-start | bytes 24584 | tf_op jit(solution)/shard_map/ppermute | solution.py:325
  59.2 3.2 %collective-permute-start.15 = (f32[1,2048]{1,0:T(1,128)S(1)}, f32[1,2048]{1,0:T(1,128)S(1)}, u32[]{:S(2)}, u32[]{:S(2)}) collective-permute-start(f32[1,2048]{1,0:T(1,128)S(1)} %col_later.3.refs_0_), channel_id=1, source_target_pairs={{0,24},{8,16},{16,8},{24,0},{1,25},{9,17},{17,9},{25,1},{2,26},{10... | collective-permute-start | bytes 24584 | tf_op jit(solution)/shard_map/ppermute | solution.py:325
  59.2 3.7 %collective-permute-start.14 = (f32[1,2048]{1,0:T(1,128)S(1)}, f32[1,2048]{1,0:T(1,128)S(1)}, u32[]{:S(2)}, u32[]{:S(2)}) collective-permute-start(f32[1,2048]{1,0:T(1,128)S(1)} %col_later.3.refs_0_), channel_id=1, source_target_pairs={{0,16},{8,24},{16,0},{24,8},{1,17},{9,25},{17,1},{25,9},{2,18},{10... | collective-permute-start | bytes 24584 | tf_op jit(solution)/shard_map/ppermute | solution.py:325
  60.8 2.1 %collective-permute-start.13 = (f32[1,2048]{1,0:T(1,128)S(1)}, f32[1,2048]{1,0:T(1,128)S(1)}, u32[]{:S(2)}, u32[]{:S(2)}) collective-permute-start(f32[1,2048]{1,0:T(1,128)S(1)} %col_later.3.refs_0_), channel_id=1, source_target_pairs={{0,8},{8,0},{16,24},{24,16},{1,9},{9,1},{17,25},{25,17},{2,10},{10... | collective-permute-start | bytes 24584 | tf_op jit(solution)/shard_map/ppermute | solution.py:325
  66.0 5.5 %collective-permute-start.18 = (f32[16,128]{1,0:T(8,128)S(1)}, f32[16,128]{1,0:T(8,128)S(1)}, u32[]{:S(2)}, u32[]{:S(2)}) collective-permute-start(f32[16,128]{1,0:T(8,128)S(1)} %get-tuple-element.38.refs_0_), channel_id=1, source_target_pairs={{0,6},{1,7},{2,4},{3,5},{4,2},{5,3},{6,0},{7,1},{8,14},{9,15},{10,... | collective-permute-start | bytes 24584 | tf_op jit(solution)/shard_map/ppermute | solution.py:325
  68.5 4.5 %collective-permute-start.17 = (f32[16,128]{1,0:T(8,128)S(1)}, f32[16,128]{1,0:T(8,128)S(1)}, u32[]{:S(2)}, u32[]{:S(2)}) collective-permute-start(f32[16,128]{1,0:T(8,128)S(1)} %get-tuple-element.38.refs_0_), channel_id=1, source_target_pairs={{0,4},{1,5},{2,6},{3,7},{4,0},{5,1},{6,2},{7,3},{8,12},{9,13},{10,... | collective-permute-start | bytes 24584 | tf_op jit(solution)/shard_map/ppermute | solution.py:325
  69.5 3.7 %collective-permute-start.16 = (f32[16,128]{1,0:T(8,128)S(1)}, f32[16,128]{1,0:T(8,128)S(1)}, u32[]{:S(2)}, u32[]{:S(2)}) collective-permute-start(f32[16,128]{1,0:T(8,128)S(1)} %get-tuple-element.38.refs_0_), channel_id=1, source_target_pairs={{0,2},{1,3},{2,0},{3,1},{4,6},{5,7},{6,4},{7,5},{8,10},{9,11},{10,... | collective-permute-start | bytes 24584 | tf_op jit(solution)/shard_map/ppermute | solution.py:325
  74.2 3.3 %collective-permute-start.19 = (f32[32,128]{1,0:T(8,128)S(1)}, f32[32,128]{1,0:T(8,128)S(1)}, u32[]{:S(2)}, u32[]{:S(2)}) collective-permute-start(f32[32,128]{1,0:T(8,128)S(1)} %get-tuple-element.41), channel_id=1, source_target_pairs={{0,24},{8,16},{16,8},{24,0},{1,25},{9,17},{17,9},{25,1},{2,26},{10... | collective-permute-start | bytes 49160 | tf_op jit(solution)/shard_map/ppermute | solution.py:325
  74.2 3.8 %collective-permute-start.20 = (f32[32,128]{1,0:T(8,128)S(1)}, f32[32,128]{1,0:T(8,128)S(1)}, u32[]{:S(2)}, u32[]{:S(2)}) collective-permute-start(f32[32,128]{1,0:T(8,128)S(1)} %get-tuple-element.42), channel_id=1, source_target_pairs={{0,16},{8,24},{16,0},{24,8},{1,17},{9,25},{17,1},{25,9},{2,18},{10... | collective-permute-start | bytes 49160 | tf_op jit(solution)/shard_map/ppermute | solution.py:325
  75.7 2.2 %collective-permute-start.21 = (f32[32,128]{1,0:T(8,128)S(1)}, f32[32,128]{1,0:T(8,128)S(1)}, u32[]{:S(2)}, u32[]{:S(2)}) collective-permute-start(f32[32,128]{1,0:T(8,128)S(1)} %get-tuple-element.43), channel_id=1, source_target_pairs={{0,8},{8,0},{16,24},{24,16},{1,9},{9,1},{17,25},{25,17},{2,10},{10... | collective-permute-start | bytes 49160 | tf_op jit(solution)/shard_map/ppermute | solution.py:325
  78.0 5.6 %collective-permute-start.24 = (f32[32,128]{1,0:T(8,128)S(1)}, f32[32,128]{1,0:T(8,128)S(1)}, u32[]{:S(2)}, u32[]{:S(2)}) collective-permute-start(f32[32,128]{1,0:T(8,128)S(1)} %share_sum.2.refs_0_), channel_id=1, source_target_pairs={{0,6},{1,7},{2,4},{3,5},{4,2},{5,3},{6,0},{7,1},{8,14},{9,15},{10,... | collective-permute-start | bytes 49160 | tf_op jit(solution)/shard_map/ppermute | solution.py:325
  79.4 4.6 %collective-permute-start.23 = (f32[32,128]{1,0:T(8,128)S(1)}, f32[32,128]{1,0:T(8,128)S(1)}, u32[]{:S(2)}, u32[]{:S(2)}) collective-permute-start(f32[32,128]{1,0:T(8,128)S(1)} %share_sum.2.refs_0_), channel_id=1, source_target_pairs={{0,4},{1,5},{2,6},{3,7},{4,0},{5,1},{6,2},{7,3},{8,12},{9,13},{10,... | collective-permute-start | bytes 49160 | tf_op jit(solution)/shard_map/ppermute | solution.py:325
  80.4 3.8 %collective-permute-start.22 = (f32[32,128]{1,0:T(8,128)S(1)}, f32[32,128]{1,0:T(8,128)S(1)}, u32[]{:S(2)}, u32[]{:S(2)}) collective-permute-start(f32[32,128]{1,0:T(8,128)S(1)} %share_sum.2.refs_0_), channel_id=1, source_target_pairs={{0,2},{1,3},{2,0},{3,1},{4,6},{5,7},{6,4},{7,5},{8,10},{9,11},{10,... | collective-permute-start | bytes 49160 | tf_op jit(solution)/shard_map/ppermute | solution.py:325
  84.2 3.3 %collective-permute-start.27 = (f32[32,128]{1,0:T(8,128)S(1)}, f32[32,128]{1,0:T(8,128)S(1)}, u32[]{:S(2)}, u32[]{:S(2)}) collective-permute-start(f32[32,128]{1,0:T(8,128)S(1)} %share_sum.3.refs_0_), channel_id=1, source_target_pairs={{0,24},{8,16},{16,8},{24,0},{1,25},{9,17},{17,9},{25,1},{2,26},{10... | collective-permute-start | bytes 49160 | tf_op jit(solution)/shard_map/ppermute | solution.py:325
  84.3 3.8 %collective-permute-start.26 = (f32[32,128]{1,0:T(8,128)S(1)}, f32[32,128]{1,0:T(8,128)S(1)}, u32[]{:S(2)}, u32[]{:S(2)}) collective-permute-start(f32[32,128]{1,0:T(8,128)S(1)} %share_sum.3.refs_0_), channel_id=1, source_target_pairs={{0,16},{8,24},{16,0},{24,8},{1,17},{9,25},{17,1},{25,9},{2,18},{10... | collective-permute-start | bytes 49160 | tf_op jit(solution)/shard_map/ppermute | solution.py:325
  85.9 2.2 %collective-permute-start.25 = (f32[32,128]{1,0:T(8,128)S(1)}, f32[32,128]{1,0:T(8,128)S(1)}, u32[]{:S(2)}, u32[]{:S(2)}) collective-permute-start(f32[32,128]{1,0:T(8,128)S(1)} %share_sum.3.refs_0_), channel_id=1, source_target_pairs={{0,8},{8,0},{16,24},{24,16},{1,9},{9,1},{17,25},{25,17},{2,10},{10... | collective-permute-start | bytes 49160 | tf_op jit(solution)/shard_map/ppermute | solution.py:325

commit v3 on v2

--- a/solution.py
+++ b/solution.py
@@ -90,9 +90,9 @@
     return lax.dot_general(a, b, (((1,), (1,)), ((), ())), preferred_element_type=F32)
 
 
-def row_first(
-    unit, scale, source_hbm, map_hbm, target_hbm, pot_hbm, left_out, right_out, lse_out, turned_out, plain_out,
-    source, start_map, target, pot, work, peaks, totals, sums, sems,
+def prepare(
+    scale, source_hbm, map_hbm, target_hbm, pot_hbm, left_out, right_out, turned_out, plain_out,
+    source, start_map, target, pot, sems,
 ):
     copies = [
         pltpu.make_async_copy(src, dst, sems.at[k])
@@ -105,22 +105,25 @@
     for copy in copies:
         copy.wait()
     width = source.shape[1]
-    rows = source.shape[0]
+    plain_out[...] = target[...].astype(F32)
     for part in range(target.shape[0] // LANES):
         at = pl.ds(part * LANES, LANES)
         right_out[at, :width] = target[at, :]
         right_out[at, width:] = lane_parts(to_column(pot[:, at] * (1.0 / scale)))
     left_out[...] = jnp.dot(source[...], start_map[...].astype(BF16), preferred_element_type=F32).astype(BF16)
-    plain_out[...] = target[...].astype(F32)
-    for part in range(rows // LANES):
+    for part in range(source.shape[0] // LANES):
         here = slice(part * LANES, (part + 1) * LANES)
         turned_out[:, here] = source[here, :].T
+
+
+def row_first(unit, left_in, right, lse_out, work, peaks, totals, sums):
+    rows = left_in.shape[0]
     lane = lax.broadcasted_iota(jnp.int32, (CHUNK, LANES), 1)
     ones = jnp.where(lane < 3, 1.0, 0.0).astype(BF16)
     group = 16
     for start in range(0, rows, CHUNK):
-        left = jnp.concatenate([left_out[start : start + CHUNK, :], ones], axis=1)
-        work[start : start + CHUNK, :] = dot_t(left, right_out[...])
+        left = jnp.concatenate([left_in[start : start + CHUNK, :], ones], axis=1)
+        work[start : start + CHUNK, :] = dot_t(left, right[...])
         for at in range(start, start + CHUNK, group):
             tiles = [work[at : at + group, k : k + LANES] for k in range(0, work.shape[1], LANES)]
             peak = functools.reduce(jnp.maximum, tiles)
@@ -156,33 +159,25 @@
     spans = [slice(at, at + span) for at in range(0, cols, span)]
     low = jnp.full((8, span), -jnp.inf, F32)
 
-    def chunk_of(step):
-        return pl.ds(pl.multiple_of(step * CHUNK, CHUNK), CHUNK)
-
-    def product(step, top, k):
-        value = dot_t(left[chunk_of(step), :], right[spans[k], :])
-        work[k % 2][chunk_of(step), :] = value
+    def product(start, top, k):
+        value = dot_t(left[start : start + CHUNK, :], right[spans[k], :])
+        work[k % 2][start : start + CHUNK, :] = value
         return jnp.maximum(top, jnp.max(value.reshape(CHUNK // 8, 8, span), axis=0))
 
-    def weigh(step, total, k, peak):
-        for at in range(0, CHUNK, 16):
-            here = pl.ds(pl.multiple_of(step * CHUNK + at, 16), 16)
-            value = jnp.exp2((work[k % 2][here, :] - peak) * unit)
-            block_out[here, spans[k]] = value.astype(BF16)
-            total = total + value[:8] + value[8:]
-        return total
-
-    top = lax.fori_loop(0, rows // CHUNK, functools.partial(product, k=0), low)
+    top = low
+    for start in range(0, rows, CHUNK):
+        top = product(start, top, 0)
     for k in range(len(spans)):
         peak = jnp.max(top, axis=0, keepdims=True)
-
-        def both(step, carry):
-            total, top = carry
+        total = jnp.zeros((8, span), F32)
+        top = low
+        for start in range(0, rows, CHUNK):
             if k + 1 < len(spans):
-                top = product(step, top, k + 1)
-            return weigh(step, total, k, peak), top
-
-        total, top = lax.fori_loop(0, rows // CHUNK, both, (jnp.zeros((8, span), F32), low))
+                top = product(start, top, k + 1)
+            for at in range(start, start + CHUNK, 16):
+                value = jnp.exp2((work[k % 2][at : at + 16, :] - peak) * unit)
+                block_out[at : at + 16, spans[k]] = value.astype(BF16)
+                total = total + value[:8] + value[8:]
         peak_out[:, spans[k]] = peak
         lse_out[:, spans[k]] = peak + jnp.log(jnp.sum(total, axis=0, keepdims=True)) * (1.0 / (unit * math.log(2.0)))
 
@@ -192,21 +187,20 @@
     return jnp.concatenate(pieces, axis=0)
 
 
+def two_rows(row):
+    high, low = split(row)
+    zeros = jnp.zeros((14, row.shape[1]), F32)
+    return jnp.concatenate([high.astype(F32), low.astype(F32), zeros], axis=0).astype(BF16)
+
+
 def row_sums(block, row, sums_out):
-    rows, cols = block.shape
-    cut = cols * 5 // 8 // 256 * 256
-    weights = jnp.concatenate(split(column_factors(row[:, :cut])), axis=1)
-    tiles = [(at, jnp.broadcast_to(row[:, at : at + LANES], (16, LANES))) for at in range(cut, cols, LANES)]
-    for start in range(0, rows, CHUNK):
-        wide = jnp.dot(block[start : start + CHUNK, :cut], weights, preferred_element_type=F32)
-        rest = []
-        for here in range(start, start + CHUNK, 16):
-            terms = [block[here : here + 16, at : at + LANES].astype(F32) * factor for at, factor in tiles]
-            rest.append(jnp.sum(functools.reduce(jnp.add, terms), axis=1, keepdims=True))
-        sums = wide[:, :LANES] + wide[:, LANES:] + jnp.concatenate(rest, axis=0)
+    pair = two_rows(row)
+    for start in range(0, block.shape[0], CHUNK):
+        both = dot_t(pair, block[start : start + CHUNK, :])
+        sums = both[0:1] + both[1:2]
         for part in range(CHUNK // LANES):
             at = start // LANES + part
-            sums_out[at : at + 1, :] = to_lanes(sums[part * LANES : (part + 1) * LANES])
+            sums_out[at : at + 1, :] = sums[:, part * LANES : (part + 1) * LANES]
 
 
 def row_second(group, unit, log_cols, block, peak, *refs):
@@ -222,10 +216,8 @@
     parts, (sums_out,) = received(refs, group)
     factors = ratio / tree_sum(parts)
     rows, cols = block.shape
-    cut = cols // 2
-    row = jnp.concatenate([factors[k : k + 1, :] for k in range(rows // LANES)], axis=1)
-    high, low = split(row)
-    pair = jnp.concatenate([high.astype(F32), low.astype(F32), jnp.zeros((14, rows), F32)], axis=0).astype(BF16)
+    cut = cols * 3 // 4 // LANES * LANES
+    pair = two_rows(jnp.concatenate([factors[k : k + 1, :] for k in range(rows // LANES)], axis=1))
     product = jnp.zeros((16, cut), F32)
     total = jnp.zeros((8, cols - cut), F32)
     for start in range(0, rows, CHUNK):
@@ -352,13 +344,12 @@
     pair_vec = jax.ShapeDtypeStruct((1, 2 * cols), F32)
     mac = rows * cols * width
 
-    left, right, lse, turned, plain = call(
-        functools.partial(row_first, unit, scale),
-        "row_first",
+    left, right, turned, plain = call(
+        functools.partial(prepare, scale),
+        "prepare",
         (
             jax.ShapeDtypeStruct((rows, width), BF16),
             jax.ShapeDtypeStruct((cols, width + LANES), BF16),
-            row_vec,
             jax.ShapeDtypeStruct((width, rows), BF16),
             jax.ShapeDtypeStruct((cols, width), F32),
         ),
@@ -367,16 +358,24 @@
             pltpu.VMEM((width, width), F32),
             pltpu.VMEM((cols, width), BF16),
             pltpu.VMEM((1, cols), F32),
+            pltpu.SemaphoreType.DMA((4,)),
+        ],
+        flops=2 * rows * width * width,
+        space=pltpu.HBM,
+    )(*[pltpu.with_memory_space_constraint(x, pltpu.HBM) for x in (source, start_map, target, warm_potential.reshape(1, cols))])
+    other = lax.ppermute(plain, "tgt", [(me, me ^ 1) for me in range(n_tgt)])
+    lse = call(
+        functools.partial(row_first, unit),
+        "row_first",
+        row_vec,
+        scratch=[
             pltpu.VMEM((rows, cols), F32),
             pltpu.VMEM((rows, LANES), F32),
             pltpu.VMEM((rows, LANES), F32),
             pltpu.VMEM(row_vec.shape, F32),
-            pltpu.SemaphoreType.DMA((4,)),
         ],
         flops=4 * mac,
-        space=pltpu.HBM,
-    )(*[pltpu.with_memory_space_constraint(x, pltpu.HBM) for x in (source, start_map, target, warm_potential.reshape(1, cols))])
-    other = lax.ppermute(plain, "tgt", [(me, me ^ 1) for me in range(n_tgt)])
+    )(left, right)
     block, targets, row_pot, peak, lse = call(
         functools.partial(col_first, n_tgt, unit, log_rows),
         "col_first",

time: 92.1 us -> 85.7 us (0.931)
  Pallas kernels: 28.5 us -> 24.3 us
  blocking collectives: 12.6 us -> 11.6 us
  waiting for transfers between devices: 19.7 us -> 18.7 us
    pallas_call x11 -> x12, Pallas kernels: 28.5 us -> 24.3 us  [call(): pl.pallas_call(body, name=name, out_shape=out_shape, in_specs=[pl.BlockSp...]
    all_to_all x1, blocking collectives: 12.6 us -> 11.6 us  [over_tgt(): lax.all_to_all(jnp.broadcast_to(x, (lax.axis_size('tgt'),) + x.shape), 't...]
    ppermute x27, waiting for transfers between devices: 19.7 us -> 18.7 us  [partners(): lax.ppermute(values[k], axis, [(me, me ^ k) for me in range(size)])]
  transfers between devices with their start and end apart: 28 -> 28, of which waited for: 21 -> 20; matrix products, arithmetic and copies ran while one was open for 0% -> 0% of each run, Pallas kernels for 0% -> 3%
where the time goes in v3:
time: 85.7 us; the launch traced here: 85.5 us
  starting transfers between devices  30.2 us (35%)
  Pallas kernels  24.3 us (28%)
  waiting for transfers between devices  18.7 us (22%)
  blocking collectives  11.6 us (14%)
    ppermute x27, starting transfers between devices, partners(): lax.ppermute(values[k], axis, [(me, me ^ k) for me in range(size)])  27.2 us
    pallas_call x12, Pallas kernels, call(): pl.pallas_call(body, name=name, out_shape=out_shape, in_specs=[pl.BlockSp...  24.3 us
    ppermute x27, waiting for transfers between devices, partners(): lax.ppermute(values[k], axis, [(me, me ^ k) for me in range(size)])  18.7 us
    all_to_all x1, blocking collectives, over_tgt(): lax.all_to_all(jnp.broadcast_to(x, (lax.axis_size('tgt'),) + x.shape), 't...  11.6 us
    ppermute x1, starting transfers between devices, shards(): other = lax.ppermute(plain, 'tgt', [(me, me ^ 1) for me in range(n_tgt)])  3 us
  transfers between devices with their start and end apart: 28, of which 20 were waited for; matrix products, arithmetic and copies ran while one was open for 0% of the time, Pallas kernels for 3%

profile of v3, /device:TPU:0, one launch (start us, length us, event | category | flops | bytes accessed | tf_op | source)
XLA Modules:
  0.0 85.5 jit_solution(11850648787895232092)
XLA Ops:
  0.6 1.7 %prepare.1 = (bf16[2048,128]{1,0:T(8,128)(2,1)S(1)}, bf16[1024,256]{1,0:T(8,128)(2,1)S(1)}, bf16[128,2048]{1,0:T(8,128)(2,1)S(1)}, f32[1024,128]{1,0:T(8,128)S(1)}) custom-call(bf16[2048,128]{1,0:T(8,128)(2,1)} %source_hbm.1, f32[128,128]{1,0:T(8,128)} %map_hbm.1, bf16[1024,128]{1,0:T(8,128)(2,1)} %target_hbm.1, f32[1,1024]{1,0:T(1,128)} %bitcast.3), custom_call_target="tpu_custom_call" | custom-call | flops 67108864 | bytes 8388608 | tf_op jit(solution)/shard_map/prepare/pallas_call | solution.py:22
  2.3 3.0 %collective-permute-start = (f32[1024,128]{1,0:T(8,128)S(1)}, f32[1024,128]{1,0:T(8,128)S(1)}, u32[]{:S(2)}, u32[]{:S(2)}) collective-permute-start(f32[1024,128]{1,0:T(8,128)S(1)} %get-tuple-element.26), channel_id=1, source_target_pairs={{0,1},{1,0},{2,3},{3,2},{4,5},{5,4},{6,7},{7,6},{8,9},{9,8},{10,11... | collective-permute-start | bytes 1572872 | tf_op jit(solution)/shard_map/ppermute | solution.py:366
  5.3 2.2 %row_first.1 = f32[16,128]{1,0:T(8,128)S(1)} custom-call(bf16[2048,128]{1,0:T(8,128)(2,1)S(1)} %get-tuple-element.24.left_in, bf16[1024,256]{1,0:T(8,128)(2,1)S(1)} %get-tuple-element.25.right.own), custom_call_target="tpu_custom_call" | custom-call | flops 1073741824 | bytes 8388608 | tf_op jit(solution)/shard_map/row_first/pallas_call | solution.py:22
  7.5 11.6 %all_to_all.5.refs_0_ = f32[8,16,128]{2,1,0:T(8,128)S(1)} all-to-all(f32[8,16,128]{2,1,0:T(8,128)S(1)} %broadcast_in_dim.3), channel_id=1, replica_groups=mesh['src'=4,'tgt'=8] {'tgt'}, dimensions={0} | all-to-all | bytes 131072 | tf_op jit(solution)/shard_map/all_to_all | solution.py:331
  19.1 5.6 %col_first.1 = (bf16[2048,2048]{1,0:T(8,128)(2,1)S(1)}, bf16[2048,128]{1,0:T(8,128)(2,1)S(1)}, f32[16,128]{1,0:T(8,128)S(1)}, f32[1,2048]{1,0:T(1,128)S(1)}, f32[1,2048]{1,0:T(1,128)S(1)}) custom-call(bf16[2048,128]{1,0:T(8,128)(2,1)S(1)} %get-tuple-element.24.left_in, bf16[1024,256]{1,0:T(8,128)(2,1)S(1)} %get-tuple-element.25.right.own, ...), custom_call_target="tpu_custom_call" | custom-call | flops 2147483648 | bytes 8388608 | tf_op jit(solution)/shard_map/col_first/pallas_call | solution.py:22
  24.7 1.6 %collective-permute-start.2 = (f32[1,2048]{1,0:T(1,128)S(1)}, f32[1,2048]{1,0:T(1,128)S(1)}, u32[]{:S(2)}, u32[]{:S(2)}) collective-permute-start(f32[1,2048]{1,0:T(1,128)S(1)} %get-tuple-element.29.refs_0_), channel_id=1, source_target_pairs={{0,16},{8,24},{16,0},{24,8},{1,17},{9,25},{17,1},{25,9},{2,18},{10... | collective-permute-start | bytes 24584 | tf_op jit(solution)/shard_map/ppermute | solution.py:317
  26.6 1.2 %collective-permute-done.3.refs_3_ = f32[1,2048]{1,0:T(1,128)S(1)} collective-permute-done((f32[1,2048]{1,0:T(1,128)S(1)}, f32[1,2048]{1,0:T(1,128)S(1)}, u32[]{:S(2)}, u32[]{:S(2)}) %collective-permute-start.3) | collective-permute-done | bytes 8224 | tf_op jit(solution)/shard_map/ppermute | solution.py:317
  28.4 2.3 %row_second.1 = (f32[1,2048]{1,0:T(1,128)S(1)}, f32[1,2048]{1,0:T(1,128)S(1)}, f32[16,128]{1,0:T(8,128)S(1)}) custom-call(bf16[2048,2048]{1,0:T(8,128)(2,1)S(1)} %get-tuple-element.27.block, f32[1,2048]{1,0:T(1,128)S(1)} %get-tuple-element.28.peak, f32[1,2048]{1,0:T(1,128)S(1)} %get-tuple-element.29.refs_0_, f32[1,2048]{1,0:T(1,128)S(1)} %collective-permute-done.1.refs_1_, ...), custom_call_target="tpu_custom_call" | custom-call | flops 1073741824 | bytes 8388608 | tf_op jit(solution)/shard_map/row_second/pallas_call | solution.py:22
  30.7 2.8 %collective-permute-start.6 = (f32[16,128]{1,0:T(8,128)S(1)}, f32[16,128]{1,0:T(8,128)S(1)}, u32[]{:S(2)}, u32[]{:S(2)}) collective-permute-start(f32[16,128]{1,0:T(8,128)S(1)} %get-tuple-element.33.refs_0_), channel_id=1, source_target_pairs={{0,6},{1,7},{2,4},{3,5},{4,2},{5,3},{6,0},{7,1},{8,14},{9,15},{10,... | collective-permute-start | bytes 24584 | tf_op jit(solution)/shard_map/ppermute | solution.py:317
  33.5 1.6 %collective-permute-start.4 = (f32[16,128]{1,0:T(8,128)S(1)}, f32[16,128]{1,0:T(8,128)S(1)}, u32[]{:S(2)}, u32[]{:S(2)}) collective-permute-start(f32[16,128]{1,0:T(8,128)S(1)} %get-tuple-element.33.refs_0_), channel_id=1, source_target_pairs={{0,2},{1,3},{2,0},{3,1},{4,6},{5,7},{6,4},{7,5},{8,10},{9,11},{10,... | collective-permute-start | bytes 24584 | tf_op jit(solution)/shard_map/ppermute | solution.py:317
  35.1 1.2 %collective-permute-done.6.refs_3_ = f32[16,128]{1,0:T(8,128)S(1)} collective-permute-done((f32[16,128]{1,0:T(8,128)S(1)}, f32[16,128]{1,0:T(8,128)S(1)}, u32[]{:S(2)}, u32[]{:S(2)}) %collective-permute-start.6) | collective-permute-done | bytes 8224 | tf_op jit(solution)/shard_map/ppermute | solution.py:317
  36.3 1.7 %collective-permute-done.5.refs_2_ = f32[16,128]{1,0:T(8,128)S(1)} collective-permute-done((f32[16,128]{1,0:T(8,128)S(1)}, f32[16,128]{1,0:T(8,128)S(1)}, u32[]{:S(2)}, u32[]{:S(2)}) %collective-permute-start.5) | collective-permute-done | bytes 8224 | tf_op jit(solution)/shard_map/ppermute | solution.py:317
  38.0 1.1 %col_later.2.refs_0_ = f32[1,2048]{1,0:T(1,128)S(1)} custom-call(bf16[2048,2048]{1,0:T(8,128)(2,1)S(1)} %get-tuple-element.27.block, f32[1,2048]{1,0:T(1,128)S(1)} %get-tuple-element.30.scale, f32[16,128]{1,0:T(8,128)S(1)} %get-tuple-element.33.refs_0_, f32[16,128]{1,0:T(8,128)S(1)} %collective-permute-done.4.refs_1_, ...), custom_call_target="tpu_custom_call" | custom-call | flops 1073741824 | bytes 8388608 | tf_op jit(solution)/shard_map/col_later/pallas_call | solution.py:22
  39.2 1.5 %collective-permute-start.8 = (f32[1,2048]{1,0:T(1,128)S(1)}, f32[1,2048]{1,0:T(1,128)S(1)}, u32[]{:S(2)}, u32[]{:S(2)}) collective-permute-start(f32[1,2048]{1,0:T(1,128)S(1)} %col_later.2.refs_0_), channel_id=1, source_target_pairs={{0,16},{8,24},{16,0},{24,8},{1,17},{9,25},{17,1},{25,9},{2,18},{10... | collective-permute-start | bytes 24584 | tf_op jit(solution)/shard_map/ppermute | solution.py:317
  41.1 1.3 %collective-permute-done.9.refs_3_ = f32[1,2048]{1,0:T(1,128)S(1)} collective-permute-done((f32[1,2048]{1,0:T(1,128)S(1)}, f32[1,2048]{1,0:T(1,128)S(1)}, u32[]{:S(2)}, u32[]{:S(2)}) %collective-permute-start.9) | collective-permute-done | bytes 8224 | tf_op jit(solution)/shard_map/ppermute | solution.py:317
  42.9 2.3 %row_later.1.refs_0_ = f32[16,128]{1,0:T(8,128)S(1)} custom-call(bf16[2048,2048]{1,0:T(8,128)(2,1)S(1)} %get-tuple-element.27.block, f32[1,2048]{1,0:T(1,128)S(1)} %get-tuple-element.30.scale, f32[1,2048]{1,0:T(1,128)S(1)} %col_later.2.refs_0_, f32[1,2048]{1,0:T(1,128)S(1)} %collective-permute-done.7.refs_1_, f32[1,2048]{1,0:T(1,128)S(1)} %collective-permute-done.8.refs_2_, ...), custom_call_target="tpu_custom_call" | custom-call | flops 1073741824 | bytes 8388608 | tf_op jit(solution)/shard_map/row_later/pallas_call | solution.py:22
  45.2 1.5 %collective-permute-start.12 = (f32[16,128]{1,0:T(8,128)S(1)}, f32[16,128]{1,0:T(8,128)S(1)}, u32[]{:S(2)}, u32[]{:S(2)}) collective-permute-start(f32[16,128]{1,0:T(8,128)S(1)} %row_later.1.refs_0_), channel_id=1, source_target_pairs={{0,6},{1,7},{2,4},{3,5},{4,2},{5,3},{6,0},{7,1},{8,14},{9,15},{10,... | collective-permute-start | bytes 24584 | tf_op jit(solution)/shard_map/ppermute | solution.py:317
  47.4 2.2 %collective-permute-start.10 = (f32[16,128]{1,0:T(8,128)S(1)}, f32[16,128]{1,0:T(8,128)S(1)}, u32[]{:S(2)}, u32[]{:S(2)}) collective-permute-start(f32[16,128]{1,0:T(8,128)S(1)} %row_later.1.refs_0_), channel_id=1, source_target_pairs={{0,2},{1,3},{2,0},{3,1},{4,6},{5,7},{6,4},{7,5},{8,10},{9,11},{10,... | collective-permute-start | bytes 24584 | tf_op jit(solution)/shard_map/ppermute | solution.py:317
  51.3 1.1 %col_later.3.refs_0_ = f32[1,2048]{1,0:T(1,128)S(1)} custom-call(bf16[2048,2048]{1,0:T(8,128)(2,1)S(1)} %get-tuple-element.27.block, f32[1,2048]{1,0:T(1,128)S(1)} %get-tuple-element.30.scale, f32[16,128]{1,0:T(8,128)S(1)} %row_later.1.refs_0_, f32[16,128]{1,0:T(8,128)S(1)} %collective-permute-done.10.refs_1_, ...), custom_call_target="tpu_custom_call" | custom-call | flops 1073741824 | bytes 8388608 | tf_op jit(solution)/shard_map/col_later/pallas_call | solution.py:22
  52.5 1.5 %collective-permute-start.14 = (f32[1,2048]{1,0:T(1,128)S(1)}, f32[1,2048]{1,0:T(1,128)S(1)}, u32[]{:S(2)}, u32[]{:S(2)}) collective-permute-start(f32[1,2048]{1,0:T(1,128)S(1)} %col_later.3.refs_0_), channel_id=1, source_target_pairs={{0,16},{8,24},{16,0},{24,8},{1,17},{9,25},{17,1},{25,9},{2,18},{10... | collective-permute-start | bytes 24584 | tf_op jit(solution)/shard_map/ppermute | solution.py:317
  54.4 1.3 %collective-permute-done.15.refs_3_ = f32[1,2048]{1,0:T(1,128)S(1)} collective-permute-done((f32[1,2048]{1,0:T(1,128)S(1)}, f32[1,2048]{1,0:T(1,128)S(1)}, u32[]{:S(2)}, u32[]{:S(2)}) %collective-permute-start.15) | collective-permute-done | bytes 8224 | tf_op jit(solution)/shard_map/ppermute | solution.py:317
  56.3 3.3 %row_last.1 = (f32[1,1024]{1,0:T(1,128)}, f32[16,128]{1,0:T(8,128)S(1)}, f32[2048,128]{1,0:T(8,128)S(1)}) custom-call(bf16[2048,2048]{1,0:T(8,128)(2,1)S(1)} %get-tuple-element.27.block, f32[1,2048]{1,0:T(1,128)S(1)} %get-tuple-element.30.scale, f32[1,2048]{1,0:T(1,128)S(1)} %get-tuple-element.31.pot, bf16[2048,128]{1,0:T(8,128)(2,1)S(1)} %get-tuple-element.32.target, ...), custom_call_target="tpu_custom_call" | custom-call | flops 1073741824 | bytes 8388608 | tf_op jit(solution)/shard_map/row_last/pallas_call | solution.py:22
  59.6 2.5 %collective-permute-start.18 = (f32[16,128]{1,0:T(8,128)S(1)}, f32[16,128]{1,0:T(8,128)S(1)}, u32[]{:S(2)}, u32[]{:S(2)}) collective-permute-start(f32[16,128]{1,0:T(8,128)S(1)} %get-tuple-element.36.refs_0_), channel_id=1, source_target_pairs={{0,6},{1,7},{2,4},{3,5},{4,2},{5,3},{6,0},{7,1},{8,14},{9,15},{10,... | collective-permute-start | bytes 24584 | tf_op jit(solution)/shard_map/ppermute | solution.py:317
  65.0 1.7 %collective-permute-done.17.refs_2_ = f32[16,128]{1,0:T(8,128)S(1)} collective-permute-done((f32[16,128]{1,0:T(8,128)S(1)}, f32[16,128]{1,0:T(8,128)S(1)}, u32[]{:S(2)}, u32[]{:S(2)}) %collective-permute-start.17) | collective-permute-done | bytes 8224 | tf_op jit(solution)/shard_map/ppermute | solution.py:317
  67.7 1.5 %collective-permute-start.20 = (f32[32,128]{1,0:T(8,128)S(1)}, f32[32,128]{1,0:T(8,128)S(1)}, u32[]{:S(2)}, u32[]{:S(2)}) collective-permute-start(f32[32,128]{1,0:T(8,128)S(1)} %get-tuple-element.40), channel_id=1, source_target_pairs={{0,16},{8,24},{16,0},{24,8},{1,17},{9,25},{17,1},{25,9},{2,18},{10... | collective-permute-start | bytes 49160 | tf_op jit(solution)/shard_map/ppermute | solution.py:317
  69.6 1.5 %collective-permute-done.19.refs_0_ = f32[32,128]{1,0:T(8,128)S(1)} collective-permute-done((f32[32,128]{1,0:T(8,128)S(1)}, f32[32,128]{1,0:T(8,128)S(1)}, u32[]{:S(2)}, u32[]{:S(2)}) %collective-permute-start.19) | collective-permute-done | bytes 16416 | tf_op jit(solution)/shard_map/ppermute | solution.py:317
  71.5 1.5 %collective-permute-start.24 = (f32[32,128]{1,0:T(8,128)S(1)}, f32[32,128]{1,0:T(8,128)S(1)}, u32[]{:S(2)}, u32[]{:S(2)}) collective-permute-start(f32[32,128]{1,0:T(8,128)S(1)} %share_sum.2.refs_0_), channel_id=1, source_target_pairs={{0,6},{1,7},{2,4},{3,5},{4,2},{5,3},{6,0},{7,1},{8,14},{9,15},{10,... | collective-permute-start | bytes 49160 | tf_op jit(solution)/shard_map/ppermute | solution.py:317
  74.0 2.0 %collective-permute-start.22 = (f32[32,128]{1,0:T(8,128)S(1)}, f32[32,128]{1,0:T(8,128)S(1)}, u32[]{:S(2)}, u32[]{:S(2)}) collective-permute-start(f32[32,128]{1,0:T(8,128)S(1)} %share_sum.2.refs_0_), channel_id=1, source_target_pairs={{0,2},{1,3},{2,0},{3,1},{4,6},{5,7},{6,4},{7,5},{8,10},{9,11},{10,... | collective-permute-start | bytes 49160 | tf_op jit(solution)/shard_map/ppermute | solution.py:317
  76.0 1.2 %collective-permute-done.24.refs_3_ = f32[32,128]{1,0:T(8,128)S(1)} collective-permute-done((f32[32,128]{1,0:T(8,128)S(1)}, f32[32,128]{1,0:T(8,128)S(1)}, u32[]{:S(2)}, u32[]{:S(2)}) %collective-permute-start.24) | collective-permute-done | bytes 16416 | tf_op jit(solution)/shard_map/ppermute | solution.py:317
  77.9 1.5 %collective-permute-start.26 = (f32[32,128]{1,0:T(8,128)S(1)}, f32[32,128]{1,0:T(8,128)S(1)}, u32[]{:S(2)}, u32[]{:S(2)}) collective-permute-start(f32[32,128]{1,0:T(8,128)S(1)} %share_sum.3.refs_0_), channel_id=1, source_target_pairs={{0,16},{8,24},{16,0},{24,8},{1,17},{9,25},{17,1},{25,9},{2,18},{10... | collective-permute-start | bytes 49160 | tf_op jit(solution)/shard_map/ppermute | solution.py:317
  79.7 1.5 %collective-permute-done.27.refs_3_ = f32[32,128]{1,0:T(8,128)S(1)} collective-permute-done((f32[32,128]{1,0:T(8,128)S(1)}, f32[32,128]{1,0:T(8,128)S(1)}, u32[]{:S(2)}, u32[]{:S(2)}) %collective-permute-start.27) | collective-permute-done | bytes 16416 | tf_op jit(solution)/shard_map/ppermute | solution.py:317
  81.7 3.8 %polar.1 = f32[128,128]{1,0:T(8,128)} custom-call(f32[32,128]{1,0:T(8,128)S(1)} %share_sum.3.refs_0_, f32[32,128]{1,0:T(8,128)S(1)} %collective-permute-done.25.refs_1_, f32[32,128]{1,0:T(8,128)S(1)} %collective-permute-done.26.refs_2_, f32[32,128]{1,0:T(8,128)S(1)} %collective-permute-done.27.refs_3_), custom_call_target="tpu_custom_call" | custom-call | flops 134217728 | bytes 8388608 | tf_op jit(solution)/shard_map/polar/pallas_call | solution.py:22
  (38 shorter events, 12.7 us)
Async XLA Ops:
  2.3 16.8 %collective-permute-start = (f32[1024,128]{1,0:T(8,128)S(1)}, f32[1024,128]{1,0:T(8,128)S(1)}, u32[]{:S(2)}, u32[]{:S(2)}) collective-permute-start(f32[1024,128]{1,0:T(8,128)S(1)} %get-tuple-element.26), channel_id=1, source_target_pairs={{0,1},{1,0},{2,3},{3,2},{4,5},{5,4},{6,7},{7,6},{8,9},{9,8},{10,11... | collective-permute-start | bytes 1572872 | tf_op jit(solution)/shard_map/ppermute | solution.py:366
  24.6 3.2 %collective-permute-start.3 = (f32[1,2048]{1,0:T(1,128)S(1)}, f32[1,2048]{1,0:T(1,128)S(1)}, u32[]{:S(2)}, u32[]{:S(2)}) collective-permute-start(f32[1,2048]{1,0:T(1,128)S(1)} %get-tuple-element.29.refs_0_), channel_id=1, source_target_pairs={{0,24},{8,16},{16,8},{24,0},{1,25},{9,17},{17,9},{25,1},{2,26},{10... | collective-permute-start | bytes 24584 | tf_op jit(solution)/shard_map/ppermute | solution.py:317
  24.7 3.7 %collective-permute-start.2 = (f32[1,2048]{1,0:T(1,128)S(1)}, f32[1,2048]{1,0:T(1,128)S(1)}, u32[]{:S(2)}, u32[]{:S(2)}) collective-permute-start(f32[1,2048]{1,0:T(1,128)S(1)} %get-tuple-element.29.refs_0_), channel_id=1, source_target_pairs={{0,16},{8,24},{16,0},{24,8},{1,17},{9,25},{17,1},{25,9},{2,18},{10... | collective-permute-start | bytes 24584 | tf_op jit(solution)/shard_map/ppermute | solution.py:317
  26.3 2.1 %collective-permute-start.1 = (f32[1,2048]{1,0:T(1,128)S(1)}, f32[1,2048]{1,0:T(1,128)S(1)}, u32[]{:S(2)}, u32[]{:S(2)}) collective-permute-start(f32[1,2048]{1,0:T(1,128)S(1)} %get-tuple-element.29.refs_0_), channel_id=1, source_target_pairs={{0,8},{8,0},{16,24},{24,16},{1,9},{9,1},{17,25},{25,17},{2,10},{10... | collective-permute-start | bytes 24584 | tf_op jit(solution)/shard_map/ppermute | solution.py:317
  30.7 5.6 %collective-permute-start.6 = (f32[16,128]{1,0:T(8,128)S(1)}, f32[16,128]{1,0:T(8,128)S(1)}, u32[]{:S(2)}, u32[]{:S(2)}) collective-permute-start(f32[16,128]{1,0:T(8,128)S(1)} %get-tuple-element.33.refs_0_), channel_id=1, source_target_pairs={{0,6},{1,7},{2,4},{3,5},{4,2},{5,3},{6,0},{7,1},{8,14},{9,15},{10,... | collective-permute-start | bytes 24584 | tf_op jit(solution)/shard_map/ppermute | solution.py:317
  33.5 4.5 %collective-permute-start.5 = (f32[16,128]{1,0:T(8,128)S(1)}, f32[16,128]{1,0:T(8,128)S(1)}, u32[]{:S(2)}, u32[]{:S(2)}) collective-permute-start(f32[16,128]{1,0:T(8,128)S(1)} %get-tuple-element.33.refs_0_), channel_id=1, source_target_pairs={{0,4},{1,5},{2,6},{3,7},{4,0},{5,1},{6,2},{7,3},{8,12},{9,13},{10,... | collective-permute-start | bytes 24584 | tf_op jit(solution)/shard_map/ppermute | solution.py:317
  33.5 4.5 %collective-permute-start.4 = (f32[16,128]{1,0:T(8,128)S(1)}, f32[16,128]{1,0:T(8,128)S(1)}, u32[]{:S(2)}, u32[]{:S(2)}) collective-permute-start(f32[16,128]{1,0:T(8,128)S(1)} %get-tuple-element.33.refs_0_), channel_id=1, source_target_pairs={{0,2},{1,3},{2,0},{3,1},{4,6},{5,7},{6,4},{7,5},{8,10},{9,11},{10,... | collective-permute-start | bytes 24584 | tf_op jit(solution)/shard_map/ppermute | solution.py:317
  39.2 3.2 %collective-permute-start.9 = (f32[1,2048]{1,0:T(1,128)S(1)}, f32[1,2048]{1,0:T(1,128)S(1)}, u32[]{:S(2)}, u32[]{:S(2)}) collective-permute-start(f32[1,2048]{1,0:T(1,128)S(1)} %col_later.2.refs_0_), channel_id=1, source_target_pairs={{0,24},{8,16},{16,8},{24,0},{1,25},{9,17},{17,9},{25,1},{2,26},{10... | collective-permute-start | bytes 24584 | tf_op jit(solution)/shard_map/ppermute | solution.py:317
  39.2 3.7 %collective-permute-start.8 = (f32[1,2048]{1,0:T(1,128)S(1)}, f32[1,2048]{1,0:T(1,128)S(1)}, u32[]{:S(2)}, u32[]{:S(2)}) collective-permute-start(f32[1,2048]{1,0:T(1,128)S(1)} %col_later.2.refs_0_), channel_id=1, source_target_pairs={{0,16},{8,24},{16,0},{24,8},{1,17},{9,25},{17,1},{25,9},{2,18},{10... | collective-permute-start | bytes 24584 | tf_op jit(solution)/shard_map/ppermute | solution.py:317
  40.8 2.2 %collective-permute-start.7 = (f32[1,2048]{1,0:T(1,128)S(1)}, f32[1,2048]{1,0:T(1,128)S(1)}, u32[]{:S(2)}, u32[]{:S(2)}) collective-permute-start(f32[1,2048]{1,0:T(1,128)S(1)} %col_later.2.refs_0_), channel_id=1, source_target_pairs={{0,8},{8,0},{16,24},{24,16},{1,9},{9,1},{17,25},{25,17},{2,10},{10... | collective-permute-start | bytes 24584 | tf_op jit(solution)/shard_map/ppermute | solution.py:317
  45.2 5.5 %collective-permute-start.12 = (f32[16,128]{1,0:T(8,128)S(1)}, f32[16,128]{1,0:T(8,128)S(1)}, u32[]{:S(2)}, u32[]{:S(2)}) collective-permute-start(f32[16,128]{1,0:T(8,128)S(1)} %row_later.1.refs_0_), channel_id=1, source_target_pairs={{0,6},{1,7},{2,4},{3,5},{4,2},{5,3},{6,0},{7,1},{8,14},{9,15},{10,... | collective-permute-start | bytes 24584 | tf_op jit(solution)/shard_map/ppermute | solution.py:317
  46.7 4.6 %collective-permute-start.11 = (f32[16,128]{1,0:T(8,128)S(1)}, f32[16,128]{1,0:T(8,128)S(1)}, u32[]{:S(2)}, u32[]{:S(2)}) collective-permute-start(f32[16,128]{1,0:T(8,128)S(1)} %row_later.1.refs_0_), channel_id=1, source_target_pairs={{0,4},{1,5},{2,6},{3,7},{4,0},{5,1},{6,2},{7,3},{8,12},{9,13},{10,... | collective-permute-start | bytes 24584 | tf_op jit(solution)/shard_map/ppermute | solution.py:317
  47.4 3.9 %collective-permute-start.10 = (f32[16,128]{1,0:T(8,128)S(1)}, f32[16,128]{1,0:T(8,128)S(1)}, u32[]{:S(2)}, u32[]{:S(2)}) collective-permute-start(f32[16,128]{1,0:T(8,128)S(1)} %row_later.1.refs_0_), channel_id=1, source_target_pairs={{0,2},{1,3},{2,0},{3,1},{4,6},{5,7},{6,4},{7,5},{8,10},{9,11},{10,... | collective-permute-start | bytes 24584 | tf_op jit(solution)/shard_map/ppermute | solution.py:317
  52.5 3.2 %collective-permute-start.15 = (f32[1,2048]{1,0:T(1,128)S(1)}, f32[1,2048]{1,0:T(1,128)S(1)}, u32[]{:S(2)}, u32[]{:S(2)}) collective-permute-start(f32[1,2048]{1,0:T(1,128)S(1)} %col_later.3.refs_0_), channel_id=1, source_target_pairs={{0,24},{8,16},{16,8},{24,0},{1,25},{9,17},{17,9},{25,1},{2,26},{10... | collective-permute-start | bytes 24584 | tf_op jit(solution)/shard_map/ppermute | solution.py:317
  52.5 3.7 %collective-permute-start.14 = (f32[1,2048]{1,0:T(1,128)S(1)}, f32[1,2048]{1,0:T(1,128)S(1)}, u32[]{:S(2)}, u32[]{:S(2)}) collective-permute-start(f32[1,2048]{1,0:T(1,128)S(1)} %col_later.3.refs_0_), channel_id=1, source_target_pairs={{0,16},{8,24},{16,0},{24,8},{1,17},{9,25},{17,1},{25,9},{2,18},{10... | collective-permute-start | bytes 24584 | tf_op jit(solution)/shard_map/ppermute | solution.py:317
  54.1 2.2 %collective-permute-start.13 = (f32[1,2048]{1,0:T(1,128)S(1)}, f32[1,2048]{1,0:T(1,128)S(1)}, u32[]{:S(2)}, u32[]{:S(2)}) collective-permute-start(f32[1,2048]{1,0:T(1,128)S(1)} %col_later.3.refs_0_), channel_id=1, source_target_pairs={{0,8},{8,0},{16,24},{24,16},{1,9},{9,1},{17,25},{25,17},{2,10},{10... | collective-permute-start | bytes 24584 | tf_op jit(solution)/shard_map/ppermute | solution.py:317
  59.6 5.4 %collective-permute-start.18 = (f32[16,128]{1,0:T(8,128)S(1)}, f32[16,128]{1,0:T(8,128)S(1)}, u32[]{:S(2)}, u32[]{:S(2)}) collective-permute-start(f32[16,128]{1,0:T(8,128)S(1)} %get-tuple-element.36.refs_0_), channel_id=1, source_target_pairs={{0,6},{1,7},{2,4},{3,5},{4,2},{5,3},{6,0},{7,1},{8,14},{9,15},{10,... | collective-permute-start | bytes 24584 | tf_op jit(solution)/shard_map/ppermute | solution.py:317
  62.1 4.6 %collective-permute-start.17 = (f32[16,128]{1,0:T(8,128)S(1)}, f32[16,128]{1,0:T(8,128)S(1)}, u32[]{:S(2)}, u32[]{:S(2)}) collective-permute-start(f32[16,128]{1,0:T(8,128)S(1)} %get-tuple-element.36.refs_0_), channel_id=1, source_target_pairs={{0,4},{1,5},{2,6},{3,7},{4,0},{5,1},{6,2},{7,3},{8,12},{9,13},{10,... | collective-permute-start | bytes 24584 | tf_op jit(solution)/shard_map/ppermute | solution.py:317
  63.0 3.7 %collective-permute-start.16 = (f32[16,128]{1,0:T(8,128)S(1)}, f32[16,128]{1,0:T(8,128)S(1)}, u32[]{:S(2)}, u32[]{:S(2)}) collective-permute-start(f32[16,128]{1,0:T(8,128)S(1)} %get-tuple-element.36.refs_0_), channel_id=1, source_target_pairs={{0,2},{1,3},{2,0},{3,1},{4,6},{5,7},{6,4},{7,5},{8,10},{9,11},{10,... | collective-permute-start | bytes 24584 | tf_op jit(solution)/shard_map/ppermute | solution.py:317
  67.7 3.3 %collective-permute-start.19 = (f32[32,128]{1,0:T(8,128)S(1)}, f32[32,128]{1,0:T(8,128)S(1)}, u32[]{:S(2)}, u32[]{:S(2)}) collective-permute-start(f32[32,128]{1,0:T(8,128)S(1)} %get-tuple-element.39), channel_id=1, source_target_pairs={{0,24},{8,16},{16,8},{24,0},{1,25},{9,17},{17,9},{25,1},{2,26},{10... | collective-permute-start | bytes 49160 | tf_op jit(solution)/shard_map/ppermute | solution.py:317
  67.7 3.8 %collective-permute-start.20 = (f32[32,128]{1,0:T(8,128)S(1)}, f32[32,128]{1,0:T(8,128)S(1)}, u32[]{:S(2)}, u32[]{:S(2)}) collective-permute-start(f32[32,128]{1,0:T(8,128)S(1)} %get-tuple-element.40), channel_id=1, source_target_pairs={{0,16},{8,24},{16,0},{24,8},{1,17},{9,25},{17,1},{25,9},{2,18},{10... | collective-permute-start | bytes 49160 | tf_op jit(solution)/shard_map/ppermute | solution.py:317
  69.2 2.3 %collective-permute-start.21 = (f32[32,128]{1,0:T(8,128)S(1)}, f32[32,128]{1,0:T(8,128)S(1)}, u32[]{:S(2)}, u32[]{:S(2)}) collective-permute-start(f32[32,128]{1,0:T(8,128)S(1)} %get-tuple-element.41), channel_id=1, source_target_pairs={{0,8},{8,0},{16,24},{24,16},{1,9},{9,1},{17,25},{25,17},{2,10},{10... | collective-permute-start | bytes 49160 | tf_op jit(solution)/shard_map/ppermute | solution.py:317
  71.5 5.6 %collective-permute-start.24 = (f32[32,128]{1,0:T(8,128)S(1)}, f32[32,128]{1,0:T(8,128)S(1)}, u32[]{:S(2)}, u32[]{:S(2)}) collective-permute-start(f32[32,128]{1,0:T(8,128)S(1)} %share_sum.2.refs_0_), channel_id=1, source_target_pairs={{0,6},{1,7},{2,4},{3,5},{4,2},{5,3},{6,0},{7,1},{8,14},{9,15},{10,... | collective-permute-start | bytes 49160 | tf_op jit(solution)/shard_map/ppermute | solution.py:317
  73.0 4.6 %collective-permute-start.23 = (f32[32,128]{1,0:T(8,128)S(1)}, f32[32,128]{1,0:T(8,128)S(1)}, u32[]{:S(2)}, u32[]{:S(2)}) collective-permute-start(f32[32,128]{1,0:T(8,128)S(1)} %share_sum.2.refs_0_), channel_id=1, source_target_pairs={{0,4},{1,5},{2,6},{3,7},{4,0},{5,1},{6,2},{7,3},{8,12},{9,13},{10,... | collective-permute-start | bytes 49160 | tf_op jit(solution)/shard_map/ppermute | solution.py:317
  74.0 3.8 %collective-permute-start.22 = (f32[32,128]{1,0:T(8,128)S(1)}, f32[32,128]{1,0:T(8,128)S(1)}, u32[]{:S(2)}, u32[]{:S(2)}) collective-permute-start(f32[32,128]{1,0:T(8,128)S(1)} %share_sum.2.refs_0_), channel_id=1, source_target_pairs={{0,2},{1,3},{2,0},{3,1},{4,6},{5,7},{6,4},{7,5},{8,10},{9,11},{10,... | collective-permute-start | bytes 49160 | tf_op jit(solution)/shard_map/ppermute | solution.py:317
  77.8 3.4 %collective-permute-start.27 = (f32[32,128]{1,0:T(8,128)S(1)}, f32[32,128]{1,0:T(8,128)S(1)}, u32[]{:S(2)}, u32[]{:S(2)}) collective-permute-start(f32[32,128]{1,0:T(8,128)S(1)} %share_sum.3.refs_0_), channel_id=1, source_target_pairs={{0,24},{8,16},{16,8},{24,0},{1,25},{9,17},{17,9},{25,1},{2,26},{10... | collective-permute-start | bytes 49160 | tf_op jit(solution)/shard_map/ppermute | solution.py:317
  77.9 3.8 %collective-permute-start.26 = (f32[32,128]{1,0:T(8,128)S(1)}, f32[32,128]{1,0:T(8,128)S(1)}, u32[]{:S(2)}, u32[]{:S(2)}) collective-permute-start(f32[32,128]{1,0:T(8,128)S(1)} %share_sum.3.refs_0_), channel_id=1, source_target_pairs={{0,16},{8,24},{16,0},{24,8},{1,17},{9,25},{17,1},{25,9},{2,18},{10... | collective-permute-start | bytes 49160 | tf_op jit(solution)/shard_map/ppermute | solution.py:317
  79.4 2.3 %collective-permute-start.25 = (f32[32,128]{1,0:T(8,128)S(1)}, f32[32,128]{1,0:T(8,128)S(1)}, u32[]{:S(2)}, u32[]{:S(2)}) collective-permute-start(f32[32,128]{1,0:T(8,128)S(1)} %share_sum.3.refs_0_), channel_id=1, source_target_pairs={{0,8},{8,0},{16,24},{24,16},{1,9},{9,1},{17,25},{25,17},{2,10},{10... | collective-permute-start | bytes 49160 | tf_op jit(solution)/shard_map/ppermute | solution.py:317

commit v4 on v3

--- a/solution.py
+++ b/solution.py
@@ -31,15 +31,14 @@
     )(*args)
 
 
-def eye_mask(shift=0):
-    shape = (LANES, LANES)
-    row, lane = (lax.broadcasted_iota(jnp.int32, shape, k) for k in range(2))
-    return (row + shift) % LANES == lane if shift else row == lane
-
-
-def to_lanes(column, shift=0):
+def eye_mask():
+    row, lane = (lax.broadcasted_iota(jnp.int32, (LANES, LANES), k) for k in range(2))
+    return row == lane
+
+
+def to_lanes(column):
     wide = jnp.broadcast_to(column, (LANES, LANES))
-    return jnp.sum(jnp.where(eye_mask(shift), wide, 0.0), axis=0, keepdims=True)
+    return jnp.sum(jnp.where(eye_mask(), wide, 0.0), axis=0, keepdims=True)
 
 
 def to_column(row):
@@ -91,8 +90,8 @@
 
 
 def prepare(
-    scale, source_hbm, map_hbm, target_hbm, pot_hbm, left_out, right_out, turned_out, plain_out,
-    source, start_map, target, pot, sems,
+    scale, source_hbm, map_hbm, target_hbm, pot_hbm, source, left_out, right_out, plain_out,
+    start_map, target, pot, sems,
 ):
     copies = [
         pltpu.make_async_copy(src, dst, sems.at[k])
@@ -111,9 +110,6 @@
         right_out[at, :width] = target[at, :]
         right_out[at, width:] = lane_parts(to_column(pot[:, at] * (1.0 / scale)))
     left_out[...] = jnp.dot(source[...], start_map[...].astype(BF16), preferred_element_type=F32).astype(BF16)
-    for part in range(source.shape[0] // LANES):
-        here = slice(part * LANES, (part + 1) * LANES)
-        turned_out[:, here] = source[here, :].T
 
 
 def row_first(unit, left_in, right, lse_out, work, peaks, totals, sums):
@@ -147,9 +143,10 @@
     half = own.shape[0]
     cols = 2 * half
     odd = lax.axis_index("tgt") & 1
-    target_out[pl.ds(pl.multiple_of(odd * half, half), half), :] = own[:, :width]
-    target_out[pl.ds(pl.multiple_of((1 - odd) * half, half), half), :] = other[...].astype(BF16)
-    right[:, :width] = target_out[...]
+    right[pl.ds(pl.multiple_of(odd * half, half), half), :width] = own[:, :width]
+    right[pl.ds(pl.multiple_of((1 - odd) * half, half), half), :width] = other[...].astype(BF16)
+    for at in range(0, cols, LANES):
+        target_out[:, at : at + LANES] = right[at : at + LANES, :width].T
     lane = lax.broadcasted_iota(jnp.int32, (cols, LANES), 1)
     right[:, width:] = jnp.where(lane < 3, 1.0, 0.0).astype(BF16)
     left[:, :width] = left_in[...]
@@ -182,25 +179,32 @@
         lse_out[:, spans[k]] = peak + jnp.log(jnp.sum(total, axis=0, keepdims=True)) * (1.0 / (unit * math.log(2.0)))
 
 
-def column_factors(row):
-    pieces = [to_column(row[:, at : at + LANES]) for at in range(0, row.shape[1], LANES)]
-    return jnp.concatenate(pieces, axis=0)
-
-
 def two_rows(row):
     high, low = split(row)
     zeros = jnp.zeros((14, row.shape[1]), F32)
     return jnp.concatenate([high.astype(F32), low.astype(F32), zeros], axis=0).astype(BF16)
 
 
+def put_rows(out, start, row):
+    for part in range(row.shape[1] // LANES):
+        at = start // LANES + part
+        out[at : at + 1, :] = row[:, part * LANES : (part + 1) * LANES]
+
+
 def row_sums(block, row, sums_out):
-    pair = two_rows(row)
-    for start in range(0, block.shape[0], CHUNK):
-        both = dot_t(pair, block[start : start + CHUNK, :])
-        sums = both[0:1] + both[1:2]
-        for part in range(CHUNK // LANES):
-            at = start // LANES + part
-            sums_out[at : at + 1, :] = sums[:, part * LANES : (part + 1) * LANES]
+    rows, cols = block.shape
+    cut = cols // 2
+    first = lax.broadcasted_iota(jnp.int32, (16, 2 * LANES), 0) == 0
+    pair = jnp.concatenate([two_rows(row[:, :cut]), jnp.where(first, 1.0, 0.0).astype(BF16)], axis=1)
+    tiles = [(at, jnp.broadcast_to(row[:, at : at + LANES], (16, LANES))) for at in range(cut, cols, LANES)]
+    for start in range(0, rows, CHUNK):
+        folded = []
+        for here in range(start, start + CHUNK, 16):
+            terms = [block[here : here + 16, at : at + LANES].astype(F32) * factor for at, factor in tiles]
+            folded.append(functools.reduce(jnp.add, terms))
+        folded = split(jnp.concatenate(folded, axis=0))
+        both = dot_t(pair, jnp.concatenate([block[start : start + CHUNK, :cut], *folded], axis=1))
+        put_rows(sums_out, start, both[0:1] + both[1:2])
 
 
 def row_second(group, unit, log_cols, block, peak, *refs):
@@ -239,40 +243,31 @@
 
 
 def row_last(group, unit, block, scale, pot, target, *refs):
-    parts, (col_out, sums_out, bary_out, other) = received(refs, group)
+    parts, (col_out, sums_out, bary_out) = received(refs, group)
     totals = tree_sum(parts)
     pots = (EPS * math.log(2.0)) * (unit * pot[...] - jnp.log(totals) * (1.0 / math.log(2.0)))
     half = col_out.shape[1]
     col_out[...] = jnp.where((lax.axis_index("tgt") & 1) == 0, pots[:, :half], pots[:, half:])
-    factors = column_factors(scale[...] / totals)
-    high, low = split(factors)
-    lane = lax.broadcasted_iota(jnp.int32, factors.shape, 1)
-    sides = jnp.where(lane < LANES // 2, high.astype(F32), low.astype(F32)).astype(BF16)
-    scaled = (target[...].astype(F32) * factors).astype(BF16)
-    weights = jnp.concatenate([scaled, sides], axis=1)
+    row = scale[...] / totals
+    scaled = (target[...].astype(F32) * row).astype(BF16)
+    left = jnp.concatenate([scaled, two_rows(row)], axis=0)
+    width = target.shape[0]
     for start in range(0, block.shape[0], CHUNK):
-        wide = jnp.dot(block[start : start + CHUNK, :], weights, preferred_element_type=F32)
-        bary_out[start : start + CHUNK, :] = wide[:, :LANES]
-        for part in range(CHUNK // LANES):
-            at = start // LANES + part
-            sides = wide[part * LANES : (part + 1) * LANES, LANES:]
-            sums_out[at : at + 1, :] = to_lanes(sides)
-            other[at : at + 1, :] = to_lanes(sides, LANES // 2)
-    sums_out[...] += pltpu.roll(other[...], LANES // 2, 1)
-
-
-def cross_local(group, unit, ratio, turned, bary, pot, *refs):
+        both = dot_t(left, block[start : start + CHUNK, :])
+        bary_out[:, start : start + CHUNK] = both[:width]
+        put_rows(sums_out, start, both[width : width + 1] + both[width + 1 : width + 2])
+
+
+def cross_local(group, unit, ratio, source, bary, pot, *refs):
     parts, (row_out, *share_outs, square) = received(refs, group)
     totals = tree_sum(parts)
     row_out[...] = (EPS * math.log(2.0)) * (unit * pot[...] + jnp.log(ratio / totals) * (1.0 / math.log(2.0)))
     inverse = 1.0 / totals
-    pieces = []
-    for part in range(totals.shape[0]):
-        piece = bary[part * LANES : (part + 1) * LANES, :] * to_column(inverse[part : part + 1, :])
-        pieces.append(jnp.concatenate(split(piece), axis=1))
-    cross = jnp.dot(turned[...], jnp.concatenate(pieces, axis=0), preferred_element_type=F32)
+    inverse = jnp.concatenate([inverse[k : k + 1, :] for k in range(inverse.shape[0])], axis=1)
+    both = jnp.concatenate(split(bary[...] * inverse), axis=0)
+    cross = jnp.dot(both, source[...], preferred_element_type=F32)
     width = square.shape[0]
-    square[...] = cross[:, :width] + cross[:, width:]
+    square[...] = (cross[:width, :] + cross[width:, :]).T
     index = lax.axis_index("src")
     count = len(share_outs)
     height = width // count
@@ -344,17 +339,16 @@
     pair_vec = jax.ShapeDtypeStruct((1, 2 * cols), F32)
     mac = rows * cols * width
 
-    left, right, turned, plain = call(
+    source, left, right, plain = call(
         functools.partial(prepare, scale),
         "prepare",
         (
             jax.ShapeDtypeStruct((rows, width), BF16),
+            jax.ShapeDtypeStruct((rows, width), BF16),
             jax.ShapeDtypeStruct((cols, width + LANES), BF16),
-            jax.ShapeDtypeStruct((width, rows), BF16),
             jax.ShapeDtypeStruct((cols, width), F32),
         ),
         scratch=[
-            pltpu.VMEM((rows, width), BF16),
             pltpu.VMEM((width, width), F32),
             pltpu.VMEM((cols, width), BF16),
             pltpu.VMEM((1, cols), F32),
@@ -381,7 +375,7 @@
         "col_first",
         (
             jax.ShapeDtypeStruct((rows, 2 * cols), BF16),
-            jax.ShapeDtypeStruct((2 * cols, width), BF16),
+            jax.ShapeDtypeStruct((width, 2 * cols), BF16),
             row_vec,
             pair_vec,
             pair_vec,
@@ -411,8 +405,7 @@
     col_out, sums, bary = call(
         functools.partial(row_last, n_src, unit),
         "row_last",
-        (jax.ShapeDtypeStruct((1, cols), F32), row_vec, jax.ShapeDtypeStruct((rows, width), F32)),
-        scratch=[pltpu.VMEM(row_vec.shape, F32)],
+        (jax.ShapeDtypeStruct((1, cols), F32), row_vec, jax.ShapeDtypeStruct((width, rows), F32)),
         flops=4 * mac,
     )(block, col_scale, col_pot, targets, *over_src(sums))
     square = jax.ShapeDtypeStruct((width, width), F32)
@@ -423,7 +416,7 @@
         (row_vec,) + (share_shape,) * n_src,
         scratch=[pltpu.VMEM((width, width), F32)],
         flops=2 * rows * width * width,
-    )(turned, bary, row_pot, *over_pairs(sums))
+    )(source, bary, row_pot, *over_pairs(sums))
     share = call(share_sum, "share_sum", share_shape)(*partners(shares[::-1], "src", range(n_src - 1, -1, -1)))
     share = call(share_sum, "share_sum", share_shape)(*over_pairs(share))
     new_map = call(polar, "polar", square, scratch=[pltpu.VMEM((width, width), F32)], flops=1 << 27)(*over_src(share))

time: 85.7 us -> 85.1 us (level)
  transfers between devices with their start and end apart: 28 -> 28, of which waited for: 20 -> 21; matrix products, arithmetic and copies ran while one was open for 0% -> 0% of each run, Pallas kernels for 3% -> 3%
where the time goes in v4:
time: 85.1 us; the launch traced here: 85 us
  starting transfers between devices  30.2 us (35%)
  Pallas kernels  23.5 us (28%)
  waiting for transfers between devices  19 us (22%)
  blocking collectives  11.6 us (14%)
    ppermute x27, starting transfers between devices, partners(): lax.ppermute(values[k], axis, [(me, me ^ k) for me in range(size)])  27.2 us
    pallas_call x12, Pallas kernels, call(): pl.pallas_call(body, name=name, out_shape=out_shape, in_specs=[pl.BlockSp...  23.5 us
    ppermute x27, waiting for transfers between devices, partners(): lax.ppermute(values[k], axis, [(me, me ^ k) for me in range(size)])  19 us
    all_to_all x1, blocking collectives, over_tgt(): lax.all_to_all(jnp.broadcast_to(x, (lax.axis_size('tgt'),) + x.shape), 't...  11.6 us
    ppermute x1, starting transfers between devices, shards(): other = lax.ppermute(plain, 'tgt', [(me, me ^ 1) for me in range(n_tgt)])  3 us
  transfers between devices with their start and end apart: 28, of which 21 were waited for; matrix products, arithmetic and copies ran while one was open for 0% of the time, Pallas kernels for 3%

profile of v4, /device:TPU:0, one launch (start us, length us, event | category | flops | bytes accessed | tf_op | source)
XLA Modules:
  0.0 85.0 jit_solution(5380358991601520835)
XLA Ops:
  0.6 1.6 %prepare.1 = (bf16[2048,128]{1,0:T(8,128)(2,1)S(1)}, bf16[2048,128]{1,0:T(8,128)(2,1)S(1)}, bf16[1024,256]{1,0:T(8,128)(2,1)S(1)}, f32[1024,128]{1,0:T(8,128)S(1)}) custom-call(bf16[2048,128]{1,0:T(8,128)(2,1)} %source_hbm.1, f32[128,128]{1,0:T(8,128)} %map_hbm.1, bf16[1024,128]{1,0:T(8,128)(2,1)} %target_hbm.1, f32[1,1024]{1,0:T(1,128)} %bitcast.3), custom_call_target="tpu_custom_call" | custom-call | flops 67108864 | bytes 8388608 | tf_op jit(solution)/shard_map/prepare/pallas_call | solution.py:22
  2.2 3.0 %collective-permute-start = (f32[1024,128]{1,0:T(8,128)S(1)}, f32[1024,128]{1,0:T(8,128)S(1)}, u32[]{:S(2)}, u32[]{:S(2)}) collective-permute-start(f32[1024,128]{1,0:T(8,128)S(1)} %get-tuple-element.26), channel_id=1, source_target_pairs={{0,1},{1,0},{2,3},{3,2},{4,5},{5,4},{6,7},{7,6},{8,9},{9,8},{10,11... | collective-permute-start | bytes 1572872 | tf_op jit(solution)/shard_map/ppermute | solution.py:360
  5.2 2.2 %row_first.1 = f32[16,128]{1,0:T(8,128)S(1)} custom-call(bf16[2048,128]{1,0:T(8,128)(2,1)S(1)} %get-tuple-element.24.left_in, bf16[1024,256]{1,0:T(8,128)(2,1)S(1)} %get-tuple-element.25.right.own), custom_call_target="tpu_custom_call" | custom-call | flops 1073741824 | bytes 8388608 | tf_op jit(solution)/shard_map/row_first/pallas_call | solution.py:22
  7.4 11.6 %all_to_all.5.refs_0_ = f32[8,16,128]{2,1,0:T(8,128)S(1)} all-to-all(f32[8,16,128]{2,1,0:T(8,128)S(1)} %broadcast_in_dim.3), channel_id=1, replica_groups=mesh['src'=4,'tgt'=8] {'tgt'}, dimensions={0} | all-to-all | bytes 131072 | tf_op jit(solution)/shard_map/all_to_all | solution.py:326
  19.0 5.6 %col_first.1 = (bf16[2048,2048]{1,0:T(8,128)(2,1)S(1)}, bf16[128,2048]{1,0:T(8,128)(2,1)S(1)}, f32[16,128]{1,0:T(8,128)S(1)}, f32[1,2048]{1,0:T(1,128)S(1)}, f32[1,2048]{1,0:T(1,128)S(1)}) custom-call(bf16[2048,128]{1,0:T(8,128)(2,1)S(1)} %get-tuple-element.24.left_in, bf16[1024,256]{1,0:T(8,128)(2,1)S(1)} %get-tuple-element.25.right.own, ...), custom_call_target="tpu_custom_call" | custom-call | flops 2147483648 | bytes 8388608 | tf_op jit(solution)/shard_map/col_first/pallas_call | solution.py:22
  24.7 1.6 %collective-permute-start.2 = (f32[1,2048]{1,0:T(1,128)S(1)}, f32[1,2048]{1,0:T(1,128)S(1)}, u32[]{:S(2)}, u32[]{:S(2)}) collective-permute-start(f32[1,2048]{1,0:T(1,128)S(1)} %get-tuple-element.29.refs_0_), channel_id=1, source_target_pairs={{0,16},{8,24},{16,0},{24,8},{1,17},{9,25},{17,1},{25,9},{2,18},{10... | collective-permute-start | bytes 24584 | tf_op jit(solution)/shard_map/ppermute | solution.py:312
  26.5 1.2 %collective-permute-done.3.refs_3_ = f32[1,2048]{1,0:T(1,128)S(1)} collective-permute-done((f32[1,2048]{1,0:T(1,128)S(1)}, f32[1,2048]{1,0:T(1,128)S(1)}, u32[]{:S(2)}, u32[]{:S(2)}) %collective-permute-start.3) | collective-permute-done | bytes 8224 | tf_op jit(solution)/shard_map/ppermute | solution.py:312
  28.4 1.8 %row_second.1 = (f32[1,2048]{1,0:T(1,128)S(1)}, f32[1,2048]{1,0:T(1,128)S(1)}, f32[16,128]{1,0:T(8,128)S(1)}) custom-call(bf16[2048,2048]{1,0:T(8,128)(2,1)S(1)} %get-tuple-element.27.block, f32[1,2048]{1,0:T(1,128)S(1)} %get-tuple-element.28.peak, f32[1,2048]{1,0:T(1,128)S(1)} %get-tuple-element.29.refs_0_, f32[1,2048]{1,0:T(1,128)S(1)} %collective-permute-done.1.refs_1_, ...), custom_call_target="tpu_custom_call" | custom-call | flops 1073741824 | bytes 8388608 | tf_op jit(solution)/shard_map/row_second/pallas_call | solution.py:22
  30.2 2.8 %collective-permute-start.6 = (f32[16,128]{1,0:T(8,128)S(1)}, f32[16,128]{1,0:T(8,128)S(1)}, u32[]{:S(2)}, u32[]{:S(2)}) collective-permute-start(f32[16,128]{1,0:T(8,128)S(1)} %get-tuple-element.33.refs_0_), channel_id=1, source_target_pairs={{0,6},{1,7},{2,4},{3,5},{4,2},{5,3},{6,0},{7,1},{8,14},{9,15},{10,... | collective-permute-start | bytes 24584 | tf_op jit(solution)/shard_map/ppermute | solution.py:312
  33.0 1.6 %collective-permute-start.4 = (f32[16,128]{1,0:T(8,128)S(1)}, f32[16,128]{1,0:T(8,128)S(1)}, u32[]{:S(2)}, u32[]{:S(2)}) collective-permute-start(f32[16,128]{1,0:T(8,128)S(1)} %get-tuple-element.33.refs_0_), channel_id=1, source_target_pairs={{0,2},{1,3},{2,0},{3,1},{4,6},{5,7},{6,4},{7,5},{8,10},{9,11},{10,... | collective-permute-start | bytes 24584 | tf_op jit(solution)/shard_map/ppermute | solution.py:312
  34.6 1.1 %collective-permute-done.6.refs_3_ = f32[16,128]{1,0:T(8,128)S(1)} collective-permute-done((f32[16,128]{1,0:T(8,128)S(1)}, f32[16,128]{1,0:T(8,128)S(1)}, u32[]{:S(2)}, u32[]{:S(2)}) %collective-permute-start.6) | collective-permute-done | bytes 8224 | tf_op jit(solution)/shard_map/ppermute | solution.py:312
  35.8 1.8 %collective-permute-done.5.refs_2_ = f32[16,128]{1,0:T(8,128)S(1)} collective-permute-done((f32[16,128]{1,0:T(8,128)S(1)}, f32[16,128]{1,0:T(8,128)S(1)}, u32[]{:S(2)}, u32[]{:S(2)}) %collective-permute-start.5) | collective-permute-done | bytes 8224 | tf_op jit(solution)/shard_map/ppermute | solution.py:312
  37.6 1.1 %col_later.2.refs_0_ = f32[1,2048]{1,0:T(1,128)S(1)} custom-call(bf16[2048,2048]{1,0:T(8,128)(2,1)S(1)} %get-tuple-element.27.block, f32[1,2048]{1,0:T(1,128)S(1)} %get-tuple-element.30.scale, f32[16,128]{1,0:T(8,128)S(1)} %get-tuple-element.33.refs_0_, f32[16,128]{1,0:T(8,128)S(1)} %collective-permute-done.4.refs_1_, ...), custom_call_target="tpu_custom_call" | custom-call | flops 1073741824 | bytes 8388608 | tf_op jit(solution)/shard_map/col_later/pallas_call | solution.py:22
  38.8 1.5 %collective-permute-start.8 = (f32[1,2048]{1,0:T(1,128)S(1)}, f32[1,2048]{1,0:T(1,128)S(1)}, u32[]{:S(2)}, u32[]{:S(2)}) collective-permute-start(f32[1,2048]{1,0:T(1,128)S(1)} %col_later.2.refs_0_), channel_id=1, source_target_pairs={{0,16},{8,24},{16,0},{24,8},{1,17},{9,25},{17,1},{25,9},{2,18},{10... | collective-permute-start | bytes 24584 | tf_op jit(solution)/shard_map/ppermute | solution.py:312
  40.6 1.3 %collective-permute-done.9.refs_3_ = f32[1,2048]{1,0:T(1,128)S(1)} collective-permute-done((f32[1,2048]{1,0:T(1,128)S(1)}, f32[1,2048]{1,0:T(1,128)S(1)}, u32[]{:S(2)}, u32[]{:S(2)}) %collective-permute-start.9) | collective-permute-done | bytes 8224 | tf_op jit(solution)/shard_map/ppermute | solution.py:312
  42.5 1.8 %row_later.1.refs_0_ = f32[16,128]{1,0:T(8,128)S(1)} custom-call(bf16[2048,2048]{1,0:T(8,128)(2,1)S(1)} %get-tuple-element.27.block, f32[1,2048]{1,0:T(1,128)S(1)} %get-tuple-element.30.scale, f32[1,2048]{1,0:T(1,128)S(1)} %col_later.2.refs_0_, f32[1,2048]{1,0:T(1,128)S(1)} %collective-permute-done.7.refs_1_, f32[1,2048]{1,0:T(1,128)S(1)} %collective-permute-done.8.refs_2_, ...), custom_call_target="tpu_custom_call" | custom-call | flops 1073741824 | bytes 8388608 | tf_op jit(solution)/shard_map/row_later/pallas_call | solution.py:22
  44.4 1.5 %collective-permute-start.12 = (f32[16,128]{1,0:T(8,128)S(1)}, f32[16,128]{1,0:T(8,128)S(1)}, u32[]{:S(2)}, u32[]{:S(2)}) collective-permute-start(f32[16,128]{1,0:T(8,128)S(1)} %row_later.1.refs_0_), channel_id=1, source_target_pairs={{0,6},{1,7},{2,4},{3,5},{4,2},{5,3},{6,0},{7,1},{8,14},{9,15},{10,... | collective-permute-start | bytes 24584 | tf_op jit(solution)/shard_map/ppermute | solution.py:312
  46.5 2.2 %collective-permute-start.10 = (f32[16,128]{1,0:T(8,128)S(1)}, f32[16,128]{1,0:T(8,128)S(1)}, u32[]{:S(2)}, u32[]{:S(2)}) collective-permute-start(f32[16,128]{1,0:T(8,128)S(1)} %row_later.1.refs_0_), channel_id=1, source_target_pairs={{0,2},{1,3},{2,0},{3,1},{4,6},{5,7},{6,4},{7,5},{8,10},{9,11},{10,... | collective-permute-start | bytes 24584 | tf_op jit(solution)/shard_map/ppermute | solution.py:312
  50.5 1.1 %col_later.3.refs_0_ = f32[1,2048]{1,0:T(1,128)S(1)} custom-call(bf16[2048,2048]{1,0:T(8,128)(2,1)S(1)} %get-tuple-element.27.block, f32[1,2048]{1,0:T(1,128)S(1)} %get-tuple-element.30.scale, f32[16,128]{1,0:T(8,128)S(1)} %row_later.1.refs_0_, f32[16,128]{1,0:T(8,128)S(1)} %collective-permute-done.10.refs_1_, ...), custom_call_target="tpu_custom_call" | custom-call | flops 1073741824 | bytes 8388608 | tf_op jit(solution)/shard_map/col_later/pallas_call | solution.py:22
  51.7 1.8 %collective-permute-start.14 = (f32[1,2048]{1,0:T(1,128)S(1)}, f32[1,2048]{1,0:T(1,128)S(1)}, u32[]{:S(2)}, u32[]{:S(2)}) collective-permute-start(f32[1,2048]{1,0:T(1,128)S(1)} %col_later.3.refs_0_), channel_id=1, source_target_pairs={{0,16},{8,24},{16,0},{24,8},{1,17},{9,25},{17,1},{25,9},{2,18},{10... | collective-permute-start | bytes 24584 | tf_op jit(solution)/shard_map/ppermute | solution.py:312
  53.5 1.3 %collective-permute-done.15.refs_3_ = f32[1,2048]{1,0:T(1,128)S(1)} collective-permute-done((f32[1,2048]{1,0:T(1,128)S(1)}, f32[1,2048]{1,0:T(1,128)S(1)}, u32[]{:S(2)}, u32[]{:S(2)}) %collective-permute-start.15) | collective-permute-done | bytes 8224 | tf_op jit(solution)/shard_map/ppermute | solution.py:312
  55.6 3.3 %row_last.1 = (f32[1,1024]{1,0:T(1,128)}, f32[16,128]{1,0:T(8,128)S(1)}, f32[128,2048]{1,0:T(8,128)S(1)}) custom-call(bf16[2048,2048]{1,0:T(8,128)(2,1)S(1)} %get-tuple-element.27.block, f32[1,2048]{1,0:T(1,128)S(1)} %get-tuple-element.30.scale, f32[1,2048]{1,0:T(1,128)S(1)} %get-tuple-element.31.pot, bf16[128,2048]{1,0:T(8,128)(2,1)S(1)} %get-tuple-element.32.target, ...), custom_call_target="tpu_custom_call" | custom-call | flops 1073741824 | bytes 8388608 | tf_op jit(solution)/shard_map/row_last/pallas_call | solution.py:22
  58.9 2.5 %collective-permute-start.18 = (f32[16,128]{1,0:T(8,128)S(1)}, f32[16,128]{1,0:T(8,128)S(1)}, u32[]{:S(2)}, u32[]{:S(2)}) collective-permute-start(f32[16,128]{1,0:T(8,128)S(1)} %get-tuple-element.36.refs_0_), channel_id=1, source_target_pairs={{0,6},{1,7},{2,4},{3,5},{4,2},{5,3},{6,0},{7,1},{8,14},{9,15},{10,... | collective-permute-start | bytes 24584 | tf_op jit(solution)/shard_map/ppermute | solution.py:312
  64.4 1.6 %collective-permute-done.17.refs_2_ = f32[16,128]{1,0:T(8,128)S(1)} collective-permute-done((f32[16,128]{1,0:T(8,128)S(1)}, f32[16,128]{1,0:T(8,128)S(1)}, u32[]{:S(2)}, u32[]{:S(2)}) %collective-permute-start.17) | collective-permute-done | bytes 8224 | tf_op jit(solution)/shard_map/ppermute | solution.py:312
  67.1 1.5 %collective-permute-start.20 = (f32[32,128]{1,0:T(8,128)S(1)}, f32[32,128]{1,0:T(8,128)S(1)}, u32[]{:S(2)}, u32[]{:S(2)}) collective-permute-start(f32[32,128]{1,0:T(8,128)S(1)} %get-tuple-element.40), channel_id=1, source_target_pairs={{0,16},{8,24},{16,0},{24,8},{1,17},{9,25},{17,1},{25,9},{2,18},{10... | collective-permute-start | bytes 49160 | tf_op jit(solution)/shard_map/ppermute | solution.py:312
  69.0 1.4 %collective-permute-done.19.refs_0_ = f32[32,128]{1,0:T(8,128)S(1)} collective-permute-done((f32[32,128]{1,0:T(8,128)S(1)}, f32[32,128]{1,0:T(8,128)S(1)}, u32[]{:S(2)}, u32[]{:S(2)}) %collective-permute-start.19) | collective-permute-done | bytes 16416 | tf_op jit(solution)/shard_map/ppermute | solution.py:312
  70.9 1.5 %collective-permute-start.24 = (f32[32,128]{1,0:T(8,128)S(1)}, f32[32,128]{1,0:T(8,128)S(1)}, u32[]{:S(2)}, u32[]{:S(2)}) collective-permute-start(f32[32,128]{1,0:T(8,128)S(1)} %share_sum.2.refs_0_), channel_id=1, source_target_pairs={{0,6},{1,7},{2,4},{3,5},{4,2},{5,3},{6,0},{7,1},{8,14},{9,15},{10,... | collective-permute-start | bytes 49160 | tf_op jit(solution)/shard_map/ppermute | solution.py:312
  73.4 2.0 %collective-permute-start.22 = (f32[32,128]{1,0:T(8,128)S(1)}, f32[32,128]{1,0:T(8,128)S(1)}, u32[]{:S(2)}, u32[]{:S(2)}) collective-permute-start(f32[32,128]{1,0:T(8,128)S(1)} %share_sum.2.refs_0_), channel_id=1, source_target_pairs={{0,2},{1,3},{2,0},{3,1},{4,6},{5,7},{6,4},{7,5},{8,10},{9,11},{10,... | collective-permute-start | bytes 49160 | tf_op jit(solution)/shard_map/ppermute | solution.py:312
  75.4 1.1 %collective-permute-done.24.refs_3_ = f32[32,128]{1,0:T(8,128)S(1)} collective-permute-done((f32[32,128]{1,0:T(8,128)S(1)}, f32[32,128]{1,0:T(8,128)S(1)}, u32[]{:S(2)}, u32[]{:S(2)}) %collective-permute-start.24) | collective-permute-done | bytes 16416 | tf_op jit(solution)/shard_map/ppermute | solution.py:312
  77.3 1.5 %collective-permute-start.26 = (f32[32,128]{1,0:T(8,128)S(1)}, f32[32,128]{1,0:T(8,128)S(1)}, u32[]{:S(2)}, u32[]{:S(2)}) collective-permute-start(f32[32,128]{1,0:T(8,128)S(1)} %share_sum.3.refs_0_), channel_id=1, source_target_pairs={{0,16},{8,24},{16,0},{24,8},{1,17},{9,25},{17,1},{25,9},{2,18},{10... | collective-permute-start | bytes 49160 | tf_op jit(solution)/shard_map/ppermute | solution.py:312
  79.1 1.5 %collective-permute-done.27.refs_3_ = f32[32,128]{1,0:T(8,128)S(1)} collective-permute-done((f32[32,128]{1,0:T(8,128)S(1)}, f32[32,128]{1,0:T(8,128)S(1)}, u32[]{:S(2)}, u32[]{:S(2)}) %collective-permute-start.27) | collective-permute-done | bytes 16416 | tf_op jit(solution)/shard_map/ppermute | solution.py:312
  81.1 3.8 %polar.1 = f32[128,128]{1,0:T(8,128)} custom-call(f32[32,128]{1,0:T(8,128)S(1)} %share_sum.3.refs_0_, f32[32,128]{1,0:T(8,128)S(1)} %collective-permute-done.25.refs_1_, f32[32,128]{1,0:T(8,128)S(1)} %collective-permute-done.26.refs_2_, f32[32,128]{1,0:T(8,128)S(1)} %collective-permute-done.27.refs_3_), custom_call_target="tpu_custom_call" | custom-call | flops 134217728 | bytes 8388608 | tf_op jit(solution)/shard_map/polar/pallas_call | solution.py:22
  (38 shorter events, 12.8 us)
Async XLA Ops:
  2.2 16.7 %collective-permute-start = (f32[1024,128]{1,0:T(8,128)S(1)}, f32[1024,128]{1,0:T(8,128)S(1)}, u32[]{:S(2)}, u32[]{:S(2)}) collective-permute-start(f32[1024,128]{1,0:T(8,128)S(1)} %get-tuple-element.26), channel_id=1, source_target_pairs={{0,1},{1,0},{2,3},{3,2},{4,5},{5,4},{6,7},{7,6},{8,9},{9,8},{10,11... | collective-permute-start | bytes 1572872 | tf_op jit(solution)/shard_map/ppermute | solution.py:360
  24.6 3.1 %collective-permute-start.3 = (f32[1,2048]{1,0:T(1,128)S(1)}, f32[1,2048]{1,0:T(1,128)S(1)}, u32[]{:S(2)}, u32[]{:S(2)}) collective-permute-start(f32[1,2048]{1,0:T(1,128)S(1)} %get-tuple-element.29.refs_0_), channel_id=1, source_target_pairs={{0,24},{8,16},{16,8},{24,0},{1,25},{9,17},{17,9},{25,1},{2,26},{10... | collective-permute-start | bytes 24584 | tf_op jit(solution)/shard_map/ppermute | solution.py:312
  24.7 3.7 %collective-permute-start.2 = (f32[1,2048]{1,0:T(1,128)S(1)}, f32[1,2048]{1,0:T(1,128)S(1)}, u32[]{:S(2)}, u32[]{:S(2)}) collective-permute-start(f32[1,2048]{1,0:T(1,128)S(1)} %get-tuple-element.29.refs_0_), channel_id=1, source_target_pairs={{0,16},{8,24},{16,0},{24,8},{1,17},{9,25},{17,1},{25,9},{2,18},{10... | collective-permute-start | bytes 24584 | tf_op jit(solution)/shard_map/ppermute | solution.py:312
  26.3 2.1 %collective-permute-start.1 = (f32[1,2048]{1,0:T(1,128)S(1)}, f32[1,2048]{1,0:T(1,128)S(1)}, u32[]{:S(2)}, u32[]{:S(2)}) collective-permute-start(f32[1,2048]{1,0:T(1,128)S(1)} %get-tuple-element.29.refs_0_), channel_id=1, source_target_pairs={{0,8},{8,0},{16,24},{24,16},{1,9},{9,1},{17,25},{25,17},{2,10},{10... | collective-permute-start | bytes 24584 | tf_op jit(solution)/shard_map/ppermute | solution.py:312
  30.2 5.5 %collective-permute-start.6 = (f32[16,128]{1,0:T(8,128)S(1)}, f32[16,128]{1,0:T(8,128)S(1)}, u32[]{:S(2)}, u32[]{:S(2)}) collective-permute-start(f32[16,128]{1,0:T(8,128)S(1)} %get-tuple-element.33.refs_0_), channel_id=1, source_target_pairs={{0,6},{1,7},{2,4},{3,5},{4,2},{5,3},{6,0},{7,1},{8,14},{9,15},{10,... | collective-permute-start | bytes 24584 | tf_op jit(solution)/shard_map/ppermute | solution.py:312
  33.0 4.5 %collective-permute-start.5 = (f32[16,128]{1,0:T(8,128)S(1)}, f32[16,128]{1,0:T(8,128)S(1)}, u32[]{:S(2)}, u32[]{:S(2)}) collective-permute-start(f32[16,128]{1,0:T(8,128)S(1)} %get-tuple-element.33.refs_0_), channel_id=1, source_target_pairs={{0,4},{1,5},{2,6},{3,7},{4,0},{5,1},{6,2},{7,3},{8,12},{9,13},{10,... | collective-permute-start | bytes 24584 | tf_op jit(solution)/shard_map/ppermute | solution.py:312
  33.0 4.5 %collective-permute-start.4 = (f32[16,128]{1,0:T(8,128)S(1)}, f32[16,128]{1,0:T(8,128)S(1)}, u32[]{:S(2)}, u32[]{:S(2)}) collective-permute-start(f32[16,128]{1,0:T(8,128)S(1)} %get-tuple-element.33.refs_0_), channel_id=1, source_target_pairs={{0,2},{1,3},{2,0},{3,1},{4,6},{5,7},{6,4},{7,5},{8,10},{9,11},{10,... | collective-permute-start | bytes 24584 | tf_op jit(solution)/shard_map/ppermute | solution.py:312
  38.7 3.2 %collective-permute-start.9 = (f32[1,2048]{1,0:T(1,128)S(1)}, f32[1,2048]{1,0:T(1,128)S(1)}, u32[]{:S(2)}, u32[]{:S(2)}) collective-permute-start(f32[1,2048]{1,0:T(1,128)S(1)} %col_later.2.refs_0_), channel_id=1, source_target_pairs={{0,24},{8,16},{16,8},{24,0},{1,25},{9,17},{17,9},{25,1},{2,26},{10... | collective-permute-start | bytes 24584 | tf_op jit(solution)/shard_map/ppermute | solution.py:312
  38.8 3.7 %collective-permute-start.8 = (f32[1,2048]{1,0:T(1,128)S(1)}, f32[1,2048]{1,0:T(1,128)S(1)}, u32[]{:S(2)}, u32[]{:S(2)}) collective-permute-start(f32[1,2048]{1,0:T(1,128)S(1)} %col_later.2.refs_0_), channel_id=1, source_target_pairs={{0,16},{8,24},{16,0},{24,8},{1,17},{9,25},{17,1},{25,9},{2,18},{10... | collective-permute-start | bytes 24584 | tf_op jit(solution)/shard_map/ppermute | solution.py:312
  40.3 2.2 %collective-permute-start.7 = (f32[1,2048]{1,0:T(1,128)S(1)}, f32[1,2048]{1,0:T(1,128)S(1)}, u32[]{:S(2)}, u32[]{:S(2)}) collective-permute-start(f32[1,2048]{1,0:T(1,128)S(1)} %col_later.2.refs_0_), channel_id=1, source_target_pairs={{0,8},{8,0},{16,24},{24,16},{1,9},{9,1},{17,25},{25,17},{2,10},{10... | collective-permute-start | bytes 24584 | tf_op jit(solution)/shard_map/ppermute | solution.py:312
  44.4 5.5 %collective-permute-start.12 = (f32[16,128]{1,0:T(8,128)S(1)}, f32[16,128]{1,0:T(8,128)S(1)}, u32[]{:S(2)}, u32[]{:S(2)}) collective-permute-start(f32[16,128]{1,0:T(8,128)S(1)} %row_later.1.refs_0_), channel_id=1, source_target_pairs={{0,6},{1,7},{2,4},{3,5},{4,2},{5,3},{6,0},{7,1},{8,14},{9,15},{10,... | collective-permute-start | bytes 24584 | tf_op jit(solution)/shard_map/ppermute | solution.py:312
  45.8 4.6 %collective-permute-start.11 = (f32[16,128]{1,0:T(8,128)S(1)}, f32[16,128]{1,0:T(8,128)S(1)}, u32[]{:S(2)}, u32[]{:S(2)}) collective-permute-start(f32[16,128]{1,0:T(8,128)S(1)} %row_later.1.refs_0_), channel_id=1, source_target_pairs={{0,4},{1,5},{2,6},{3,7},{4,0},{5,1},{6,2},{7,3},{8,12},{9,13},{10,... | collective-permute-start | bytes 24584 | tf_op jit(solution)/shard_map/ppermute | solution.py:312
  46.5 3.9 %collective-permute-start.10 = (f32[16,128]{1,0:T(8,128)S(1)}, f32[16,128]{1,0:T(8,128)S(1)}, u32[]{:S(2)}, u32[]{:S(2)}) collective-permute-start(f32[16,128]{1,0:T(8,128)S(1)} %row_later.1.refs_0_), channel_id=1, source_target_pairs={{0,2},{1,3},{2,0},{3,1},{4,6},{5,7},{6,4},{7,5},{8,10},{9,11},{10,... | collective-permute-start | bytes 24584 | tf_op jit(solution)/shard_map/ppermute | solution.py:312
  51.6 3.2 %collective-permute-start.15 = (f32[1,2048]{1,0:T(1,128)S(1)}, f32[1,2048]{1,0:T(1,128)S(1)}, u32[]{:S(2)}, u32[]{:S(2)}) collective-permute-start(f32[1,2048]{1,0:T(1,128)S(1)} %col_later.3.refs_0_), channel_id=1, source_target_pairs={{0,24},{8,16},{16,8},{24,0},{1,25},{9,17},{17,9},{25,1},{2,26},{10... | collective-permute-start | bytes 24584 | tf_op jit(solution)/shard_map/ppermute | solution.py:312
  51.7 3.9 %collective-permute-start.14 = (f32[1,2048]{1,0:T(1,128)S(1)}, f32[1,2048]{1,0:T(1,128)S(1)}, u32[]{:S(2)}, u32[]{:S(2)}) collective-permute-start(f32[1,2048]{1,0:T(1,128)S(1)} %col_later.3.refs_0_), channel_id=1, source_target_pairs={{0,16},{8,24},{16,0},{24,8},{1,17},{9,25},{17,1},{25,9},{2,18},{10... | collective-permute-start | bytes 24584 | tf_op jit(solution)/shard_map/ppermute | solution.py:312
  53.4 2.2 %collective-permute-start.13 = (f32[1,2048]{1,0:T(1,128)S(1)}, f32[1,2048]{1,0:T(1,128)S(1)}, u32[]{:S(2)}, u32[]{:S(2)}) collective-permute-start(f32[1,2048]{1,0:T(1,128)S(1)} %col_later.3.refs_0_), channel_id=1, source_target_pairs={{0,8},{8,0},{16,24},{24,16},{1,9},{9,1},{17,25},{25,17},{2,10},{10... | collective-permute-start | bytes 24584 | tf_op jit(solution)/shard_map/ppermute | solution.py:312
  58.9 5.5 %collective-permute-start.18 = (f32[16,128]{1,0:T(8,128)S(1)}, f32[16,128]{1,0:T(8,128)S(1)}, u32[]{:S(2)}, u32[]{:S(2)}) collective-permute-start(f32[16,128]{1,0:T(8,128)S(1)} %get-tuple-element.36.refs_0_), channel_id=1, source_target_pairs={{0,6},{1,7},{2,4},{3,5},{4,2},{5,3},{6,0},{7,1},{8,14},{9,15},{10,... | collective-permute-start | bytes 24584 | tf_op jit(solution)/shard_map/ppermute | solution.py:312
  61.4 4.6 %collective-permute-start.17 = (f32[16,128]{1,0:T(8,128)S(1)}, f32[16,128]{1,0:T(8,128)S(1)}, u32[]{:S(2)}, u32[]{:S(2)}) collective-permute-start(f32[16,128]{1,0:T(8,128)S(1)} %get-tuple-element.36.refs_0_), channel_id=1, source_target_pairs={{0,4},{1,5},{2,6},{3,7},{4,0},{5,1},{6,2},{7,3},{8,12},{9,13},{10,... | collective-permute-start | bytes 24584 | tf_op jit(solution)/shard_map/ppermute | solution.py:312
  62.3 3.7 %collective-permute-start.16 = (f32[16,128]{1,0:T(8,128)S(1)}, f32[16,128]{1,0:T(8,128)S(1)}, u32[]{:S(2)}, u32[]{:S(2)}) collective-permute-start(f32[16,128]{1,0:T(8,128)S(1)} %get-tuple-element.36.refs_0_), channel_id=1, source_target_pairs={{0,2},{1,3},{2,0},{3,1},{4,6},{5,7},{6,4},{7,5},{8,10},{9,11},{10,... | collective-permute-start | bytes 24584 | tf_op jit(solution)/shard_map/ppermute | solution.py:312
  67.1 3.3 %collective-permute-start.19 = (f32[32,128]{1,0:T(8,128)S(1)}, f32[32,128]{1,0:T(8,128)S(1)}, u32[]{:S(2)}, u32[]{:S(2)}) collective-permute-start(f32[32,128]{1,0:T(8,128)S(1)} %get-tuple-element.39), channel_id=1, source_target_pairs={{0,24},{8,16},{16,8},{24,0},{1,25},{9,17},{17,9},{25,1},{2,26},{10... | collective-permute-start | bytes 49160 | tf_op jit(solution)/shard_map/ppermute | solution.py:312
  67.1 3.8 %collective-permute-start.20 = (f32[32,128]{1,0:T(8,128)S(1)}, f32[32,128]{1,0:T(8,128)S(1)}, u32[]{:S(2)}, u32[]{:S(2)}) collective-permute-start(f32[32,128]{1,0:T(8,128)S(1)} %get-tuple-element.40), channel_id=1, source_target_pairs={{0,16},{8,24},{16,0},{24,8},{1,17},{9,25},{17,1},{25,9},{2,18},{10... | collective-permute-start | bytes 49160 | tf_op jit(solution)/shard_map/ppermute | solution.py:312
  68.6 2.3 %collective-permute-start.21 = (f32[32,128]{1,0:T(8,128)S(1)}, f32[32,128]{1,0:T(8,128)S(1)}, u32[]{:S(2)}, u32[]{:S(2)}) collective-permute-start(f32[32,128]{1,0:T(8,128)S(1)} %get-tuple-element.41), channel_id=1, source_target_pairs={{0,8},{8,0},{16,24},{24,16},{1,9},{9,1},{17,25},{25,17},{2,10},{10... | collective-permute-start | bytes 49160 | tf_op jit(solution)/shard_map/ppermute | solution.py:312
  70.9 5.6 %collective-permute-start.24 = (f32[32,128]{1,0:T(8,128)S(1)}, f32[32,128]{1,0:T(8,128)S(1)}, u32[]{:S(2)}, u32[]{:S(2)}) collective-permute-start(f32[32,128]{1,0:T(8,128)S(1)} %share_sum.2.refs_0_), channel_id=1, source_target_pairs={{0,6},{1,7},{2,4},{3,5},{4,2},{5,3},{6,0},{7,1},{8,14},{9,15},{10,... | collective-permute-start | bytes 49160 | tf_op jit(solution)/shard_map/ppermute | solution.py:312
  72.4 4.6 %collective-permute-start.23 = (f32[32,128]{1,0:T(8,128)S(1)}, f32[32,128]{1,0:T(8,128)S(1)}, u32[]{:S(2)}, u32[]{:S(2)}) collective-permute-start(f32[32,128]{1,0:T(8,128)S(1)} %share_sum.2.refs_0_), channel_id=1, source_target_pairs={{0,4},{1,5},{2,6},{3,7},{4,0},{5,1},{6,2},{7,3},{8,12},{9,13},{10,... | collective-permute-start | bytes 49160 | tf_op jit(solution)/shard_map/ppermute | solution.py:312
  73.4 3.9 %collective-permute-start.22 = (f32[32,128]{1,0:T(8,128)S(1)}, f32[32,128]{1,0:T(8,128)S(1)}, u32[]{:S(2)}, u32[]{:S(2)}) collective-permute-start(f32[32,128]{1,0:T(8,128)S(1)} %share_sum.2.refs_0_), channel_id=1, source_target_pairs={{0,2},{1,3},{2,0},{3,1},{4,6},{5,7},{6,4},{7,5},{8,10},{9,11},{10,... | collective-permute-start | bytes 49160 | tf_op jit(solution)/shard_map/ppermute | solution.py:312
  77.2 3.4 %collective-permute-start.27 = (f32[32,128]{1,0:T(8,128)S(1)}, f32[32,128]{1,0:T(8,128)S(1)}, u32[]{:S(2)}, u32[]{:S(2)}) collective-permute-start(f32[32,128]{1,0:T(8,128)S(1)} %share_sum.3.refs_0_), channel_id=1, source_target_pairs={{0,24},{8,16},{16,8},{24,0},{1,25},{9,17},{17,9},{25,1},{2,26},{10... | collective-permute-start | bytes 49160 | tf_op jit(solution)/shard_map/ppermute | solution.py:312
  77.3 3.8 %collective-permute-start.26 = (f32[32,128]{1,0:T(8,128)S(1)}, f32[32,128]{1,0:T(8,128)S(1)}, u32[]{:S(2)}, u32[]{:S(2)}) collective-permute-start(f32[32,128]{1,0:T(8,128)S(1)} %share_sum.3.refs_0_), channel_id=1, source_target_pairs={{0,16},{8,24},{16,0},{24,8},{1,17},{9,25},{17,1},{25,9},{2,18},{10... | collective-permute-start | bytes 49160 | tf_op jit(solution)/shard_map/ppermute | solution.py:312
  78.8 2.3 %collective-permute-start.25 = (f32[32,128]{1,0:T(8,128)S(1)}, f32[32,128]{1,0:T(8,128)S(1)}, u32[]{:S(2)}, u32[]{:S(2)}) collective-permute-start(f32[32,128]{1,0:T(8,128)S(1)} %share_sum.3.refs_0_), channel_id=1, source_target_pairs={{0,8},{8,0},{16,24},{24,16},{1,9},{9,1},{17,25},{25,17},{2,10},{10... | collective-permute-start | bytes 49160 | tf_op jit(solution)/shard_map/ppermute | solution.py:312

commit v5 on v4

--- a/solution.py
+++ b/solution.py
@@ -90,7 +90,7 @@
 
 
 def prepare(
-    scale, source_hbm, map_hbm, target_hbm, pot_hbm, source, left_out, right_out, plain_out,
+    scale, source_hbm, map_hbm, target_hbm, pot_hbm, source, left_out, turned_out, right_out, plain_out,
     start_map, target, pot, sems,
 ):
     copies = [
@@ -110,6 +110,8 @@
         right_out[at, :width] = target[at, :]
         right_out[at, width:] = lane_parts(to_column(pot[:, at] * (1.0 / scale)))
     left_out[...] = jnp.dot(source[...], start_map[...].astype(BF16), preferred_element_type=F32).astype(BF16)
+    for at in range(0, source.shape[0], LANES):
+        turned_out[:, at : at + LANES] = left_out[at : at + LANES, :].T
 
 
 def row_first(unit, left_in, right, lse_out, work, peaks, totals, sums):
@@ -135,11 +137,15 @@
     lse_out[...] = lse_out[...] + jnp.log(sums[...]) * (1.0 / (unit * math.log(2.0)))
 
 
-def col_first(group, unit, log_rows, left_in, own, other, *refs):
+def in_row(parts):
+    return jnp.concatenate([parts[k : k + 1, :] for k in range(parts.shape[0])], axis=1)
+
+
+def col_first(group, unit, log_rows, turned, own, other, *refs):
     parts, (block_out, target_out, pot_out, peak_out, lse_out, left, right, *work) = received(refs, group)
     row_pot = -log_rows - tree_lse(unit, parts)
     pot_out[...] = row_pot
-    rows, width = left_in.shape
+    width, rows = turned.shape
     half = own.shape[0]
     cols = 2 * half
     odd = lax.axis_index("tgt") & 1
@@ -149,34 +155,36 @@
         target_out[:, at : at + LANES] = right[at : at + LANES, :width].T
     lane = lax.broadcasted_iota(jnp.int32, (cols, LANES), 1)
     right[:, width:] = jnp.where(lane < 3, 1.0, 0.0).astype(BF16)
-    left[:, :width] = left_in[...]
-    for part in range(rows // LANES):
-        left[part * LANES : (part + 1) * LANES, width:] = lane_parts(to_column(row_pot[part : part + 1, :]))
-    span = work[0].shape[1]
-    spans = [slice(at, at + span) for at in range(0, cols, span)]
-    low = jnp.full((8, span), -jnp.inf, F32)
-
-    def product(start, top, k):
-        value = dot_t(left[start : start + CHUNK, :], right[spans[k], :])
-        work[k % 2][start : start + CHUNK, :] = value
-        return jnp.maximum(top, jnp.max(value.reshape(CHUNK // 8, 8, span), axis=0))
-
-    top = low
-    for start in range(0, rows, CHUNK):
-        top = product(start, top, 0)
-    for k in range(len(spans)):
-        peak = jnp.max(top, axis=0, keepdims=True)
-        total = jnp.zeros((8, span), F32)
-        top = low
-        for start in range(0, rows, CHUNK):
-            if k + 1 < len(spans):
-                top = product(start, top, k + 1)
-            for at in range(start, start + CHUNK, 16):
-                value = jnp.exp2((work[k % 2][at : at + 16, :] - peak) * unit)
-                block_out[at : at + 16, spans[k]] = value.astype(BF16)
-                total = total + value[:8] + value[8:]
-        peak_out[:, spans[k]] = peak
-        lse_out[:, spans[k]] = peak + jnp.log(jnp.sum(total, axis=0, keepdims=True)) * (1.0 / (unit * math.log(2.0)))
+    left[:width, :] = turned[...]
+    rest = in_row(row_pot)
+    pieces = []
+    for _ in range(3):
+        pieces.append(rest.astype(BF16).astype(F32))
+        rest = rest - pieces[-1]
+    left[width:, :] = jnp.concatenate([*pieces, jnp.zeros((LANES - 3, rows), F32)], axis=0).astype(BF16)
+    for start in range(0, cols, CHUNK):
+        scores = work[start // CHUNK % 2]
+        scores[...] = jnp.dot(right[start : start + CHUNK, :], left[...], preferred_element_type=F32)
+        peaks, sums = [], []
+        for at in range(0, CHUNK, 16):
+            tiles = [scores[at : at + 16, k : k + LANES] for k in range(0, rows, LANES)]
+            peaks.append(functools.reduce(jnp.maximum, tiles))
+        peak = jnp.max(jnp.concatenate(peaks, axis=0), axis=1, keepdims=True)
+        peak = jnp.broadcast_to(peak, (CHUNK, LANES))
+        for at in range(0, CHUNK, 16):
+            top = peak[at : at + 16]
+            total = None
+            for k in range(0, rows, LANES):
+                value = jnp.exp2((scores[at : at + 16, k : k + LANES] - top) * unit)
+                block_out[start + at : start + at + 16, k : k + LANES] = value.astype(BF16)
+                total = value if total is None else total + value
+            sums.append(total)
+        total = jnp.sum(jnp.concatenate(sums, axis=0), axis=1, keepdims=True)
+        for part in range(0, CHUNK, LANES):
+            here = slice(start + part, start + part + LANES)
+            peak_out[:, here] = to_lanes(peak[part : part + LANES])
+            lse_out[:, here] = to_lanes(total[part : part + LANES])
+    lse_out[...] = peak_out[...] + jnp.log(lse_out[...]) * (1.0 / (unit * math.log(2.0)))
 
 
 def two_rows(row):
@@ -191,7 +199,24 @@
         out[at : at + 1, :] = row[:, part * LANES : (part + 1) * LANES]
 
 
-def row_sums(block, row, sums_out):
+def sums_down(block, row, out):
+    rows, cols = block.shape
+    cut = cols * 3 // 4 // LANES * LANES
+    pair = two_rows(row)
+    product = jnp.zeros((16, cut), F32)
+    total = jnp.zeros((8, cols - cut), F32)
+    for start in range(0, rows, CHUNK):
+        product += jnp.dot(pair[:, start : start + CHUNK], block[start : start + CHUNK, :cut], preferred_element_type=F32)
+        for part in range(start, start + CHUNK, LANES):
+            column = to_column(row[:, part : part + LANES])
+            for at in range(0, LANES, 16):
+                factor = jnp.concatenate([column[at : at + 16]] * ((cols - cut) // LANES), axis=1)
+                value = block[part + at : part + at + 16, cut:].astype(F32) * factor
+                total = total + value[:8] + value[8:]
+    put_rows(out, 0, jnp.concatenate([product[0:1] + product[1:2], jnp.sum(total, axis=0, keepdims=True)], axis=1))
+
+
+def sums_across(block, row, out):
     rows, cols = block.shape
     cut = cols // 2
     first = lax.broadcasted_iota(jnp.int32, (16, 2 * LANES), 0) == 0
@@ -204,7 +229,7 @@
             folded.append(functools.reduce(jnp.add, terms))
         folded = split(jnp.concatenate(folded, axis=0))
         both = dot_t(pair, jnp.concatenate([block[start : start + CHUNK, :cut], *folded], axis=1))
-        put_rows(sums_out, start, both[0:1] + both[1:2])
+        out[:, start : start + CHUNK] = both[0:1] + both[1:2]
 
 
 def row_second(group, unit, log_cols, block, peak, *refs):
@@ -213,33 +238,18 @@
     pot_out[...] = -log_cols - lse
     scale = jnp.exp2(unit * (peak[...] - lse))
     scale_out[...] = scale
-    row_sums(block, scale, sums_out)
+    sums_down(block, scale, sums_out)
 
 
 def col_later(group, ratio, block, scale, *refs):
     parts, (sums_out,) = received(refs, group)
-    factors = ratio / tree_sum(parts)
-    rows, cols = block.shape
-    cut = cols * 3 // 4 // LANES * LANES
-    pair = two_rows(jnp.concatenate([factors[k : k + 1, :] for k in range(rows // LANES)], axis=1))
-    product = jnp.zeros((16, cut), F32)
-    total = jnp.zeros((8, cols - cut), F32)
-    for start in range(0, rows, CHUNK):
-        product += jnp.dot(pair[:, start : start + CHUNK], block[start : start + CHUNK, :cut], preferred_element_type=F32)
-        for part in range(start // LANES, (start + CHUNK) // LANES):
-            column = to_column(factors[part : part + 1, :])
-            for at in range(0, LANES, 16):
-                here = slice(part * LANES + at, part * LANES + at + 16)
-                factor = jnp.concatenate([column[at : at + 16]] * ((cols - cut) // LANES), axis=1)
-                value = block[here, cut:].astype(F32) * factor
-                total = total + value[:8] + value[8:]
-    sums_out[:, :cut] = scale[:, :cut] * (product[0:1] + product[1:2])
-    sums_out[:, cut:] = scale[:, cut:] * jnp.sum(total, axis=0, keepdims=True)
+    sums_across(block, in_row(ratio / tree_sum(parts)), sums_out)
+    sums_out[...] *= scale[...]
 
 
 def row_later(group, block, scale, *refs):
     parts, (sums_out,) = received(refs, group)
-    row_sums(block, scale[...] / tree_sum(parts), sums_out)
+    sums_down(block, scale[...] / tree_sum(parts), sums_out)
 
 
 def row_last(group, unit, block, scale, pot, target, *refs):
@@ -252,8 +262,8 @@
     scaled = (target[...].astype(F32) * row).astype(BF16)
     left = jnp.concatenate([scaled, two_rows(row)], axis=0)
     width = target.shape[0]
-    for start in range(0, block.shape[0], CHUNK):
-        both = dot_t(left, block[start : start + CHUNK, :])
+    for start in range(0, block.shape[1], CHUNK):
+        both = jnp.dot(left, block[:, start : start + CHUNK], preferred_element_type=F32)
         bary_out[:, start : start + CHUNK] = both[:width]
         put_rows(sums_out, start, both[width : width + 1] + both[width + 1 : width + 2])
 
@@ -262,8 +272,7 @@
     parts, (row_out, *share_outs, square) = received(refs, group)
     totals = tree_sum(parts)
     row_out[...] = (EPS * math.log(2.0)) * (unit * pot[...] + jnp.log(ratio / totals) * (1.0 / math.log(2.0)))
-    inverse = 1.0 / totals
-    inverse = jnp.concatenate([inverse[k : k + 1, :] for k in range(inverse.shape[0])], axis=1)
+    inverse = in_row(1.0 / totals)
     both = jnp.concatenate(split(bary[...] * inverse), axis=0)
     cross = jnp.dot(both, source[...], preferred_element_type=F32)
     width = square.shape[0]
@@ -339,12 +348,13 @@
     pair_vec = jax.ShapeDtypeStruct((1, 2 * cols), F32)
     mac = rows * cols * width
 
-    source, left, right, plain = call(
+    source, left, turned, right, plain = call(
         functools.partial(prepare, scale),
         "prepare",
         (
             jax.ShapeDtypeStruct((rows, width), BF16),
             jax.ShapeDtypeStruct((rows, width), BF16),
+            jax.ShapeDtypeStruct((width, rows), BF16),
             jax.ShapeDtypeStruct((cols, width + LANES), BF16),
             jax.ShapeDtypeStruct((cols, width), F32),
         ),
@@ -374,20 +384,20 @@
         functools.partial(col_first, n_tgt, unit, log_rows),
         "col_first",
         (
-            jax.ShapeDtypeStruct((rows, 2 * cols), BF16),
+            jax.ShapeDtypeStruct((2 * cols, rows), BF16),
             jax.ShapeDtypeStruct((width, 2 * cols), BF16),
             row_vec,
             pair_vec,
             pair_vec,
         ),
         scratch=[
-            pltpu.VMEM((rows, width + LANES), BF16),
+            pltpu.VMEM((width + LANES, rows), BF16),
             pltpu.VMEM((2 * cols, width + LANES), BF16),
-            pltpu.VMEM((rows, math.gcd(2 * cols, 512)), F32),
-            pltpu.VMEM((rows, math.gcd(2 * cols, 512)), F32),
+            pltpu.VMEM((CHUNK, rows), F32),
+            pltpu.VMEM((CHUNK, rows), F32),
         ],
         flops=8 * mac,
-    )(left, right, other, over_tgt(lse))
+    )(turned, right, other, over_tgt(lse))
     col_pot, col_scale, sums = call(
         functools.partial(row_second, n_src, unit, log_cols), "row_second", (pair_vec, pair_vec, row_vec), flops=4 * mac
     )(block, peak, *over_src(lse))

time: 85.1 us -> 83.1 us (0.976)
  Pallas kernels: 23.5 us -> 21.7 us
    pallas_call x12, Pallas kernels: 23.5 us -> 21.7 us  [call(): pl.pallas_call(body, name=name, out_shape=out_shape, in_specs=[pl.BlockSp...]
where the time goes in v5:
time: 83.1 us; the launch traced here: 82.9 us
  starting transfers between devices  30.3 us (36%)
  Pallas kernels  21.7 us (26%)
  waiting for transfers between devices  18.6 us (22%)
  blocking collectives  11.6 us (14%)
    ppermute x27, starting transfers between devices, partners(): lax.ppermute(values[k], axis, [(me, me ^ k) for me in range(size)])  27.3 us
    pallas_call x12, Pallas kernels, call(): pl.pallas_call(body, name=name, out_shape=out_shape, in_specs=[pl.BlockSp...  21.7 us
    ppermute x27, waiting for transfers between devices, partners(): lax.ppermute(values[k], axis, [(me, me ^ k) for me in range(size)])  18.6 us
    all_to_all x1, blocking collectives, over_tgt(): lax.all_to_all(jnp.broadcast_to(x, (lax.axis_size('tgt'),) + x.shape), 't...  11.6 us
    ppermute x1, starting transfers between devices, shards(): other = lax.ppermute(plain, 'tgt', [(me, me ^ 1) for me in range(n_tgt)])  3 us
  transfers between devices with their start and end apart: 28, of which 21 were waited for; matrix products, arithmetic and copies ran while one was open for 0% of the time, Pallas kernels for 3%

profile of v5, /device:TPU:0, one launch (start us, length us, event | category | flops | bytes accessed | tf_op | source)
XLA Modules:
  0.0 82.9 jit_solution(5404035363533768608)
XLA Ops:
  0.6 1.7 %prepare.1 = (bf16[2048,128]{1,0:T(8,128)(2,1)S(1)}, bf16[2048,128]{1,0:T(8,128)(2,1)S(1)}, bf16[128,2048]{1,0:T(8,128)(2,1)S(1)}, bf16[1024,256]{1,0:T(8,128)(2,1)S(1)}, f32[1024,128]{1,0:T(8,128)S(1)}) custom-call(bf16[2048,128]{1,0:T(8,128)(2,1)} %source_hbm.1, f32[128,128]{1,0:T(8,128)} %map_hbm.1, bf16[1024,128]{1,0:T(8,128)(2,1)} %target_hbm.1, ...), custom_call_target="tpu_custom_call" | custom-call | flops 67108864 | bytes 8388608 | tf_op jit(solution)/shard_map/prepare/pallas_call | solution.py:22
  2.3 3.0 %collective-permute-start = (f32[1024,128]{1,0:T(8,128)S(1)}, f32[1024,128]{1,0:T(8,128)S(1)}, u32[]{:S(2)}, u32[]{:S(2)}) collective-permute-start(f32[1024,128]{1,0:T(8,128)S(1)} %get-tuple-element.27), channel_id=1, source_target_pairs={{0,1},{1,0},{2,3},{3,2},{4,5},{5,4},{6,7},{7,6},{8,9},{9,8},{10,11... | collective-permute-start | bytes 1572872 | tf_op jit(solution)/shard_map/ppermute | solution.py:370
  5.3 2.2 %row_first.1 = f32[16,128]{1,0:T(8,128)S(1)} custom-call(bf16[2048,128]{1,0:T(8,128)(2,1)S(1)} %get-tuple-element.28.left_in, bf16[1024,256]{1,0:T(8,128)(2,1)S(1)} %get-tuple-element.26.right.own), custom_call_target="tpu_custom_call" | custom-call | flops 1073741824 | bytes 8388608 | tf_op jit(solution)/shard_map/row_first/pallas_call | solution.py:22
  7.5 11.6 %all_to_all.5.refs_0_ = f32[8,16,128]{2,1,0:T(8,128)S(1)} all-to-all(f32[8,16,128]{2,1,0:T(8,128)S(1)} %broadcast_in_dim.3), channel_id=1, replica_groups=mesh['src'=4,'tgt'=8] {'tgt'}, dimensions={0} | all-to-all | bytes 131072 | tf_op jit(solution)/shard_map/all_to_all | solution.py:335
  19.1 4.9 %col_first.1 = (bf16[2048,2048]{1,0:T(8,128)(2,1)S(1)}, bf16[128,2048]{1,0:T(8,128)(2,1)S(1)}, f32[16,128]{1,0:T(8,128)S(1)}, f32[1,2048]{1,0:T(1,128)S(1)}, f32[1,2048]{1,0:T(1,128)S(1)}) custom-call(bf16[128,2048]{1,0:T(8,128)(2,1)S(1)} %get-tuple-element.25.turned, bf16[1024,256]{1,0:T(8,128)(2,1)S(1)} %get-tuple-element.26.right.own, ...), custom_call_target="tpu_custom_call" | custom-call | flops 2147483648 | bytes 8388608 | tf_op jit(solution)/shard_map/col_first/pallas_call | solution.py:22
  24.0 1.6 %collective-permute-start.2 = (f32[1,2048]{1,0:T(1,128)S(1)}, f32[1,2048]{1,0:T(1,128)S(1)}, u32[]{:S(2)}, u32[]{:S(2)}) collective-permute-start(f32[1,2048]{1,0:T(1,128)S(1)} %get-tuple-element.31.refs_0_), channel_id=1, source_target_pairs={{0,16},{8,24},{16,0},{24,8},{1,17},{9,25},{17,1},{25,9},{2,18},{10... | collective-permute-start | bytes 24584 | tf_op jit(solution)/shard_map/ppermute | solution.py:321
  25.9 1.2 %collective-permute-done.3.refs_3_ = f32[1,2048]{1,0:T(1,128)S(1)} collective-permute-done((f32[1,2048]{1,0:T(1,128)S(1)}, f32[1,2048]{1,0:T(1,128)S(1)}, u32[]{:S(2)}, u32[]{:S(2)}) %collective-permute-start.3) | collective-permute-done | bytes 8224 | tf_op jit(solution)/shard_map/ppermute | solution.py:321
  27.8 1.1 %row_second.1 = (f32[1,2048]{1,0:T(1,128)S(1)}, f32[1,2048]{1,0:T(1,128)S(1)}, f32[16,128]{1,0:T(8,128)S(1)}) custom-call(bf16[2048,2048]{1,0:T(8,128)(2,1)S(1)} %get-tuple-element.29.block, f32[1,2048]{1,0:T(1,128)S(1)} %get-tuple-element.30.peak, f32[1,2048]{1,0:T(1,128)S(1)} %get-tuple-element.31.refs_0_, f32[1,2048]{1,0:T(1,128)S(1)} %collective-permute-done.1.refs_1_, ...), custom_call_target="tpu_custom_call" | custom-call | flops 1073741824 | bytes 8388608 | tf_op jit(solution)/shard_map/row_second/pallas_call | solution.py:22
  28.9 2.8 %collective-permute-start.6 = (f32[16,128]{1,0:T(8,128)S(1)}, f32[16,128]{1,0:T(8,128)S(1)}, u32[]{:S(2)}, u32[]{:S(2)}) collective-permute-start(f32[16,128]{1,0:T(8,128)S(1)} %get-tuple-element.35.refs_0_), channel_id=1, source_target_pairs={{0,6},{1,7},{2,4},{3,5},{4,2},{5,3},{6,0},{7,1},{8,14},{9,15},{10,... | collective-permute-start | bytes 24584 | tf_op jit(solution)/shard_map/ppermute | solution.py:321
  31.7 1.7 %collective-permute-start.4 = (f32[16,128]{1,0:T(8,128)S(1)}, f32[16,128]{1,0:T(8,128)S(1)}, u32[]{:S(2)}, u32[]{:S(2)}) collective-permute-start(f32[16,128]{1,0:T(8,128)S(1)} %get-tuple-element.35.refs_0_), channel_id=1, source_target_pairs={{0,2},{1,3},{2,0},{3,1},{4,6},{5,7},{6,4},{7,5},{8,10},{9,11},{10,... | collective-permute-start | bytes 24584 | tf_op jit(solution)/shard_map/ppermute | solution.py:321
  33.3 1.1 %collective-permute-done.6.refs_3_ = f32[16,128]{1,0:T(8,128)S(1)} collective-permute-done((f32[16,128]{1,0:T(8,128)S(1)}, f32[16,128]{1,0:T(8,128)S(1)}, u32[]{:S(2)}, u32[]{:S(2)}) %collective-permute-start.6) | collective-permute-done | bytes 8224 | tf_op jit(solution)/shard_map/ppermute | solution.py:321
  34.5 1.7 %collective-permute-done.5.refs_2_ = f32[16,128]{1,0:T(8,128)S(1)} collective-permute-done((f32[16,128]{1,0:T(8,128)S(1)}, f32[16,128]{1,0:T(8,128)S(1)}, u32[]{:S(2)}, u32[]{:S(2)}) %collective-permute-start.5) | collective-permute-done | bytes 8224 | tf_op jit(solution)/shard_map/ppermute | solution.py:321
  36.2 1.8 %col_later.2.refs_0_ = f32[1,2048]{1,0:T(1,128)S(1)} custom-call(bf16[2048,2048]{1,0:T(8,128)(2,1)S(1)} %get-tuple-element.29.block, f32[1,2048]{1,0:T(1,128)S(1)} %get-tuple-element.32.scale, f32[16,128]{1,0:T(8,128)S(1)} %get-tuple-element.35.refs_0_, f32[16,128]{1,0:T(8,128)S(1)} %collective-permute-done.4.refs_1_, ...), custom_call_target="tpu_custom_call" | custom-call | flops 1073741824 | bytes 8388608 | tf_op jit(solution)/shard_map/col_later/pallas_call | solution.py:22
  38.2 1.6 %collective-permute-start.8 = (f32[1,2048]{1,0:T(1,128)S(1)}, f32[1,2048]{1,0:T(1,128)S(1)}, u32[]{:S(2)}, u32[]{:S(2)}) collective-permute-start(f32[1,2048]{1,0:T(1,128)S(1)} %col_later.2.refs_0_), channel_id=1, source_target_pairs={{0,16},{8,24},{16,0},{24,8},{1,17},{9,25},{17,1},{25,9},{2,18},{10... | collective-permute-start | bytes 24584 | tf_op jit(solution)/shard_map/ppermute | solution.py:321
  40.0 1.2 %collective-permute-done.9.refs_3_ = f32[1,2048]{1,0:T(1,128)S(1)} collective-permute-done((f32[1,2048]{1,0:T(1,128)S(1)}, f32[1,2048]{1,0:T(1,128)S(1)}, u32[]{:S(2)}, u32[]{:S(2)}) %collective-permute-start.9) | collective-permute-done | bytes 8224 | tf_op jit(solution)/shard_map/ppermute | solution.py:321
  41.9 1.1 %row_later.1.refs_0_ = f32[16,128]{1,0:T(8,128)S(1)} custom-call(bf16[2048,2048]{1,0:T(8,128)(2,1)S(1)} %get-tuple-element.29.block, f32[1,2048]{1,0:T(1,128)S(1)} %get-tuple-element.32.scale, f32[1,2048]{1,0:T(1,128)S(1)} %col_later.2.refs_0_, f32[1,2048]{1,0:T(1,128)S(1)} %collective-permute-done.7.refs_1_, f32[1,2048]{1,0:T(1,128)S(1)} %collective-permute-done.8.refs_2_, ...), custom_call_target="tpu_custom_call" | custom-call | flops 1073741824 | bytes 8388608 | tf_op jit(solution)/shard_map/row_later/pallas_call | solution.py:22
  43.0 1.5 %collective-permute-start.12 = (f32[16,128]{1,0:T(8,128)S(1)}, f32[16,128]{1,0:T(8,128)S(1)}, u32[]{:S(2)}, u32[]{:S(2)}) collective-permute-start(f32[16,128]{1,0:T(8,128)S(1)} %row_later.1.refs_0_), channel_id=1, source_target_pairs={{0,6},{1,7},{2,4},{3,5},{4,2},{5,3},{6,0},{7,1},{8,14},{9,15},{10,... | collective-permute-start | bytes 24584 | tf_op jit(solution)/shard_map/ppermute | solution.py:321
  45.3 2.2 %collective-permute-start.10 = (f32[16,128]{1,0:T(8,128)S(1)}, f32[16,128]{1,0:T(8,128)S(1)}, u32[]{:S(2)}, u32[]{:S(2)}) collective-permute-start(f32[16,128]{1,0:T(8,128)S(1)} %row_later.1.refs_0_), channel_id=1, source_target_pairs={{0,2},{1,3},{2,0},{3,1},{4,6},{5,7},{6,4},{7,5},{8,10},{9,11},{10,... | collective-permute-start | bytes 24584 | tf_op jit(solution)/shard_map/ppermute | solution.py:321
  49.2 1.8 %col_later.3.refs_0_ = f32[1,2048]{1,0:T(1,128)S(1)} custom-call(bf16[2048,2048]{1,0:T(8,128)(2,1)S(1)} %get-tuple-element.29.block, f32[1,2048]{1,0:T(1,128)S(1)} %get-tuple-element.32.scale, f32[16,128]{1,0:T(8,128)S(1)} %row_later.1.refs_0_, f32[16,128]{1,0:T(8,128)S(1)} %collective-permute-done.10.refs_1_, ...), custom_call_target="tpu_custom_call" | custom-call | flops 1073741824 | bytes 8388608 | tf_op jit(solution)/shard_map/col_later/pallas_call | solution.py:22
  51.1 1.6 %collective-permute-start.14 = (f32[1,2048]{1,0:T(1,128)S(1)}, f32[1,2048]{1,0:T(1,128)S(1)}, u32[]{:S(2)}, u32[]{:S(2)}) collective-permute-start(f32[1,2048]{1,0:T(1,128)S(1)} %col_later.3.refs_0_), channel_id=1, source_target_pairs={{0,16},{8,24},{16,0},{24,8},{1,17},{9,25},{17,1},{25,9},{2,18},{10... | collective-permute-start | bytes 24584 | tf_op jit(solution)/shard_map/ppermute | solution.py:321
  53.0 1.2 %collective-permute-done.15.refs_3_ = f32[1,2048]{1,0:T(1,128)S(1)} collective-permute-done((f32[1,2048]{1,0:T(1,128)S(1)}, f32[1,2048]{1,0:T(1,128)S(1)}, u32[]{:S(2)}, u32[]{:S(2)}) %collective-permute-start.15) | collective-permute-done | bytes 8224 | tf_op jit(solution)/shard_map/ppermute | solution.py:321
  54.8 2.1 %row_last.1 = (f32[1,1024]{1,0:T(1,128)}, f32[16,128]{1,0:T(8,128)S(1)}, f32[128,2048]{1,0:T(8,128)S(1)}) custom-call(bf16[2048,2048]{1,0:T(8,128)(2,1)S(1)} %get-tuple-element.29.block, f32[1,2048]{1,0:T(1,128)S(1)} %get-tuple-element.32.scale, f32[1,2048]{1,0:T(1,128)S(1)} %get-tuple-element.33.pot, bf16[128,2048]{1,0:T(8,128)(2,1)S(1)} %get-tuple-element.34.target, ...), custom_call_target="tpu_custom_call" | custom-call | flops 1073741824 | bytes 8388608 | tf_op jit(solution)/shard_map/row_last/pallas_call | solution.py:22
  56.9 2.5 %collective-permute-start.18 = (f32[16,128]{1,0:T(8,128)S(1)}, f32[16,128]{1,0:T(8,128)S(1)}, u32[]{:S(2)}, u32[]{:S(2)}) collective-permute-start(f32[16,128]{1,0:T(8,128)S(1)} %get-tuple-element.38.refs_0_), channel_id=1, source_target_pairs={{0,6},{1,7},{2,4},{3,5},{4,2},{5,3},{6,0},{7,1},{8,14},{9,15},{10,... | collective-permute-start | bytes 24584 | tf_op jit(solution)/shard_map/ppermute | solution.py:321
  62.4 1.6 %collective-permute-done.17.refs_2_ = f32[16,128]{1,0:T(8,128)S(1)} collective-permute-done((f32[16,128]{1,0:T(8,128)S(1)}, f32[16,128]{1,0:T(8,128)S(1)}, u32[]{:S(2)}, u32[]{:S(2)}) %collective-permute-start.17) | collective-permute-done | bytes 8224 | tf_op jit(solution)/shard_map/ppermute | solution.py:321
  65.1 1.5 %collective-permute-start.20 = (f32[32,128]{1,0:T(8,128)S(1)}, f32[32,128]{1,0:T(8,128)S(1)}, u32[]{:S(2)}, u32[]{:S(2)}) collective-permute-start(f32[32,128]{1,0:T(8,128)S(1)} %get-tuple-element.42), channel_id=1, source_target_pairs={{0,16},{8,24},{16,0},{24,8},{1,17},{9,25},{17,1},{25,9},{2,18},{10... | collective-permute-start | bytes 49160 | tf_op jit(solution)/shard_map/ppermute | solution.py:321
  67.0 1.4 %collective-permute-done.19.refs_0_ = f32[32,128]{1,0:T(8,128)S(1)} collective-permute-done((f32[32,128]{1,0:T(8,128)S(1)}, f32[32,128]{1,0:T(8,128)S(1)}, u32[]{:S(2)}, u32[]{:S(2)}) %collective-permute-start.19) | collective-permute-done | bytes 16416 | tf_op jit(solution)/shard_map/ppermute | solution.py:321
  68.9 1.4 %collective-permute-start.24 = (f32[32,128]{1,0:T(8,128)S(1)}, f32[32,128]{1,0:T(8,128)S(1)}, u32[]{:S(2)}, u32[]{:S(2)}) collective-permute-start(f32[32,128]{1,0:T(8,128)S(1)} %share_sum.2.refs_0_), channel_id=1, source_target_pairs={{0,6},{1,7},{2,4},{3,5},{4,2},{5,3},{6,0},{7,1},{8,14},{9,15},{10,... | collective-permute-start | bytes 49160 | tf_op jit(solution)/shard_map/ppermute | solution.py:321
  71.4 2.0 %collective-permute-start.22 = (f32[32,128]{1,0:T(8,128)S(1)}, f32[32,128]{1,0:T(8,128)S(1)}, u32[]{:S(2)}, u32[]{:S(2)}) collective-permute-start(f32[32,128]{1,0:T(8,128)S(1)} %share_sum.2.refs_0_), channel_id=1, source_target_pairs={{0,2},{1,3},{2,0},{3,1},{4,6},{5,7},{6,4},{7,5},{8,10},{9,11},{10,... | collective-permute-start | bytes 49160 | tf_op jit(solution)/shard_map/ppermute | solution.py:321
  73.4 1.2 %collective-permute-done.24.refs_3_ = f32[32,128]{1,0:T(8,128)S(1)} collective-permute-done((f32[32,128]{1,0:T(8,128)S(1)}, f32[32,128]{1,0:T(8,128)S(1)}, u32[]{:S(2)}, u32[]{:S(2)}) %collective-permute-start.24) | collective-permute-done | bytes 16416 | tf_op jit(solution)/shard_map/ppermute | solution.py:321
  75.2 1.6 %collective-permute-start.26 = (f32[32,128]{1,0:T(8,128)S(1)}, f32[32,128]{1,0:T(8,128)S(1)}, u32[]{:S(2)}, u32[]{:S(2)}) collective-permute-start(f32[32,128]{1,0:T(8,128)S(1)} %share_sum.3.refs_0_), channel_id=1, source_target_pairs={{0,16},{8,24},{16,0},{24,8},{1,17},{9,25},{17,1},{25,9},{2,18},{10... | collective-permute-start | bytes 49160 | tf_op jit(solution)/shard_map/ppermute | solution.py:321
  77.1 1.4 %collective-permute-done.27.refs_3_ = f32[32,128]{1,0:T(8,128)S(1)} collective-permute-done((f32[32,128]{1,0:T(8,128)S(1)}, f32[32,128]{1,0:T(8,128)S(1)}, u32[]{:S(2)}, u32[]{:S(2)}) %collective-permute-start.27) | collective-permute-done | bytes 16416 | tf_op jit(solution)/shard_map/ppermute | solution.py:321
  79.1 3.8 %polar.1 = f32[128,128]{1,0:T(8,128)} custom-call(f32[32,128]{1,0:T(8,128)S(1)} %share_sum.3.refs_0_, f32[32,128]{1,0:T(8,128)S(1)} %collective-permute-done.25.refs_1_, f32[32,128]{1,0:T(8,128)S(1)} %collective-permute-done.26.refs_2_, f32[32,128]{1,0:T(8,128)S(1)} %collective-permute-done.27.refs_3_), custom_call_target="tpu_custom_call" | custom-call | flops 134217728 | bytes 8388608 | tf_op jit(solution)/shard_map/polar/pallas_call | solution.py:22
  (38 shorter events, 12.9 us)
Async XLA Ops:
  2.3 16.8 %collective-permute-start = (f32[1024,128]{1,0:T(8,128)S(1)}, f32[1024,128]{1,0:T(8,128)S(1)}, u32[]{:S(2)}, u32[]{:S(2)}) collective-permute-start(f32[1024,128]{1,0:T(8,128)S(1)} %get-tuple-element.27), channel_id=1, source_target_pairs={{0,1},{1,0},{2,3},{3,2},{4,5},{5,4},{6,7},{7,6},{8,9},{9,8},{10,11... | collective-permute-start | bytes 1572872 | tf_op jit(solution)/shard_map/ppermute | solution.py:370
  24.0 3.1 %collective-permute-start.3 = (f32[1,2048]{1,0:T(1,128)S(1)}, f32[1,2048]{1,0:T(1,128)S(1)}, u32[]{:S(2)}, u32[]{:S(2)}) collective-permute-start(f32[1,2048]{1,0:T(1,128)S(1)} %get-tuple-element.31.refs_0_), channel_id=1, source_target_pairs={{0,24},{8,16},{16,8},{24,0},{1,25},{9,17},{17,9},{25,1},{2,26},{10... | collective-permute-start | bytes 24584 | tf_op jit(solution)/shard_map/ppermute | solution.py:321
  24.0 3.7 %collective-permute-start.2 = (f32[1,2048]{1,0:T(1,128)S(1)}, f32[1,2048]{1,0:T(1,128)S(1)}, u32[]{:S(2)}, u32[]{:S(2)}) collective-permute-start(f32[1,2048]{1,0:T(1,128)S(1)} %get-tuple-element.31.refs_0_), channel_id=1, source_target_pairs={{0,16},{8,24},{16,0},{24,8},{1,17},{9,25},{17,1},{25,9},{2,18},{10... | collective-permute-start | bytes 24584 | tf_op jit(solution)/shard_map/ppermute | solution.py:321
  25.6 2.1 %collective-permute-start.1 = (f32[1,2048]{1,0:T(1,128)S(1)}, f32[1,2048]{1,0:T(1,128)S(1)}, u32[]{:S(2)}, u32[]{:S(2)}) collective-permute-start(f32[1,2048]{1,0:T(1,128)S(1)} %get-tuple-element.31.refs_0_), channel_id=1, source_target_pairs={{0,8},{8,0},{16,24},{24,16},{1,9},{9,1},{17,25},{25,17},{2,10},{10... | collective-permute-start | bytes 24584 | tf_op jit(solution)/shard_map/ppermute | solution.py:321
  28.9 5.6 %collective-permute-start.6 = (f32[16,128]{1,0:T(8,128)S(1)}, f32[16,128]{1,0:T(8,128)S(1)}, u32[]{:S(2)}, u32[]{:S(2)}) collective-permute-start(f32[16,128]{1,0:T(8,128)S(1)} %get-tuple-element.35.refs_0_), channel_id=1, source_target_pairs={{0,6},{1,7},{2,4},{3,5},{4,2},{5,3},{6,0},{7,1},{8,14},{9,15},{10,... | collective-permute-start | bytes 24584 | tf_op jit(solution)/shard_map/ppermute | solution.py:321
  31.7 4.5 %collective-permute-start.5 = (f32[16,128]{1,0:T(8,128)S(1)}, f32[16,128]{1,0:T(8,128)S(1)}, u32[]{:S(2)}, u32[]{:S(2)}) collective-permute-start(f32[16,128]{1,0:T(8,128)S(1)} %get-tuple-element.35.refs_0_), channel_id=1, source_target_pairs={{0,4},{1,5},{2,6},{3,7},{4,0},{5,1},{6,2},{7,3},{8,12},{9,13},{10,... | collective-permute-start | bytes 24584 | tf_op jit(solution)/shard_map/ppermute | solution.py:321
  31.7 4.5 %collective-permute-start.4 = (f32[16,128]{1,0:T(8,128)S(1)}, f32[16,128]{1,0:T(8,128)S(1)}, u32[]{:S(2)}, u32[]{:S(2)}) collective-permute-start(f32[16,128]{1,0:T(8,128)S(1)} %get-tuple-element.35.refs_0_), channel_id=1, source_target_pairs={{0,2},{1,3},{2,0},{3,1},{4,6},{5,7},{6,4},{7,5},{8,10},{9,11},{10,... | collective-permute-start | bytes 24584 | tf_op jit(solution)/shard_map/ppermute | solution.py:321
  38.1 3.2 %collective-permute-start.9 = (f32[1,2048]{1,0:T(1,128)S(1)}, f32[1,2048]{1,0:T(1,128)S(1)}, u32[]{:S(2)}, u32[]{:S(2)}) collective-permute-start(f32[1,2048]{1,0:T(1,128)S(1)} %col_later.2.refs_0_), channel_id=1, source_target_pairs={{0,24},{8,16},{16,8},{24,0},{1,25},{9,17},{17,9},{25,1},{2,26},{10... | collective-permute-start | bytes 24584 | tf_op jit(solution)/shard_map/ppermute | solution.py:321
  38.2 3.7 %collective-permute-start.8 = (f32[1,2048]{1,0:T(1,128)S(1)}, f32[1,2048]{1,0:T(1,128)S(1)}, u32[]{:S(2)}, u32[]{:S(2)}) collective-permute-start(f32[1,2048]{1,0:T(1,128)S(1)} %col_later.2.refs_0_), channel_id=1, source_target_pairs={{0,16},{8,24},{16,0},{24,8},{1,17},{9,25},{17,1},{25,9},{2,18},{10... | collective-permute-start | bytes 24584 | tf_op jit(solution)/shard_map/ppermute | solution.py:321
  39.8 2.1 %collective-permute-start.7 = (f32[1,2048]{1,0:T(1,128)S(1)}, f32[1,2048]{1,0:T(1,128)S(1)}, u32[]{:S(2)}, u32[]{:S(2)}) collective-permute-start(f32[1,2048]{1,0:T(1,128)S(1)} %col_later.2.refs_0_), channel_id=1, source_target_pairs={{0,8},{8,0},{16,24},{24,16},{1,9},{9,1},{17,25},{25,17},{2,10},{10... | collective-permute-start | bytes 24584 | tf_op jit(solution)/shard_map/ppermute | solution.py:321
  43.0 5.5 %collective-permute-start.12 = (f32[16,128]{1,0:T(8,128)S(1)}, f32[16,128]{1,0:T(8,128)S(1)}, u32[]{:S(2)}, u32[]{:S(2)}) collective-permute-start(f32[16,128]{1,0:T(8,128)S(1)} %row_later.1.refs_0_), channel_id=1, source_target_pairs={{0,6},{1,7},{2,4},{3,5},{4,2},{5,3},{6,0},{7,1},{8,14},{9,15},{10,... | collective-permute-start | bytes 24584 | tf_op jit(solution)/shard_map/ppermute | solution.py:321
  44.5 4.6 %collective-permute-start.11 = (f32[16,128]{1,0:T(8,128)S(1)}, f32[16,128]{1,0:T(8,128)S(1)}, u32[]{:S(2)}, u32[]{:S(2)}) collective-permute-start(f32[16,128]{1,0:T(8,128)S(1)} %row_later.1.refs_0_), channel_id=1, source_target_pairs={{0,4},{1,5},{2,6},{3,7},{4,0},{5,1},{6,2},{7,3},{8,12},{9,13},{10,... | collective-permute-start | bytes 24584 | tf_op jit(solution)/shard_map/ppermute | solution.py:321
  45.3 3.9 %collective-permute-start.10 = (f32[16,128]{1,0:T(8,128)S(1)}, f32[16,128]{1,0:T(8,128)S(1)}, u32[]{:S(2)}, u32[]{:S(2)}) collective-permute-start(f32[16,128]{1,0:T(8,128)S(1)} %row_later.1.refs_0_), channel_id=1, source_target_pairs={{0,2},{1,3},{2,0},{3,1},{4,6},{5,7},{6,4},{7,5},{8,10},{9,11},{10,... | collective-permute-start | bytes 24584 | tf_op jit(solution)/shard_map/ppermute | solution.py:321
  51.0 3.2 %collective-permute-start.15 = (f32[1,2048]{1,0:T(1,128)S(1)}, f32[1,2048]{1,0:T(1,128)S(1)}, u32[]{:S(2)}, u32[]{:S(2)}) collective-permute-start(f32[1,2048]{1,0:T(1,128)S(1)} %col_later.3.refs_0_), channel_id=1, source_target_pairs={{0,24},{8,16},{16,8},{24,0},{1,25},{9,17},{17,9},{25,1},{2,26},{10... | collective-permute-start | bytes 24584 | tf_op jit(solution)/shard_map/ppermute | solution.py:321
  51.1 3.7 %collective-permute-start.14 = (f32[1,2048]{1,0:T(1,128)S(1)}, f32[1,2048]{1,0:T(1,128)S(1)}, u32[]{:S(2)}, u32[]{:S(2)}) collective-permute-start(f32[1,2048]{1,0:T(1,128)S(1)} %col_later.3.refs_0_), channel_id=1, source_target_pairs={{0,16},{8,24},{16,0},{24,8},{1,17},{9,25},{17,1},{25,9},{2,18},{10... | collective-permute-start | bytes 24584 | tf_op jit(solution)/shard_map/ppermute | solution.py:321
  52.7 2.1 %collective-permute-start.13 = (f32[1,2048]{1,0:T(1,128)S(1)}, f32[1,2048]{1,0:T(1,128)S(1)}, u32[]{:S(2)}, u32[]{:S(2)}) collective-permute-start(f32[1,2048]{1,0:T(1,128)S(1)} %col_later.3.refs_0_), channel_id=1, source_target_pairs={{0,8},{8,0},{16,24},{24,16},{1,9},{9,1},{17,25},{25,17},{2,10},{10... | collective-permute-start | bytes 24584 | tf_op jit(solution)/shard_map/ppermute | solution.py:321
  56.9 5.4 %collective-permute-start.18 = (f32[16,128]{1,0:T(8,128)S(1)}, f32[16,128]{1,0:T(8,128)S(1)}, u32[]{:S(2)}, u32[]{:S(2)}) collective-permute-start(f32[16,128]{1,0:T(8,128)S(1)} %get-tuple-element.38.refs_0_), channel_id=1, source_target_pairs={{0,6},{1,7},{2,4},{3,5},{4,2},{5,3},{6,0},{7,1},{8,14},{9,15},{10,... | collective-permute-start | bytes 24584 | tf_op jit(solution)/shard_map/ppermute | solution.py:321
  59.4 4.6 %collective-permute-start.17 = (f32[16,128]{1,0:T(8,128)S(1)}, f32[16,128]{1,0:T(8,128)S(1)}, u32[]{:S(2)}, u32[]{:S(2)}) collective-permute-start(f32[16,128]{1,0:T(8,128)S(1)} %get-tuple-element.38.refs_0_), channel_id=1, source_target_pairs={{0,4},{1,5},{2,6},{3,7},{4,0},{5,1},{6,2},{7,3},{8,12},{9,13},{10,... | collective-permute-start | bytes 24584 | tf_op jit(solution)/shard_map/ppermute | solution.py:321
  60.3 3.7 %collective-permute-start.16 = (f32[16,128]{1,0:T(8,128)S(1)}, f32[16,128]{1,0:T(8,128)S(1)}, u32[]{:S(2)}, u32[]{:S(2)}) collective-permute-start(f32[16,128]{1,0:T(8,128)S(1)} %get-tuple-element.38.refs_0_), channel_id=1, source_target_pairs={{0,2},{1,3},{2,0},{3,1},{4,6},{5,7},{6,4},{7,5},{8,10},{9,11},{10,... | collective-permute-start | bytes 24584 | tf_op jit(solution)/shard_map/ppermute | solution.py:321
  65.1 3.3 %collective-permute-start.19 = (f32[32,128]{1,0:T(8,128)S(1)}, f32[32,128]{1,0:T(8,128)S(1)}, u32[]{:S(2)}, u32[]{:S(2)}) collective-permute-start(f32[32,128]{1,0:T(8,128)S(1)} %get-tuple-element.41), channel_id=1, source_target_pairs={{0,24},{8,16},{16,8},{24,0},{1,25},{9,17},{17,9},{25,1},{2,26},{10... | collective-permute-start | bytes 49160 | tf_op jit(solution)/shard_map/ppermute | solution.py:321
  65.1 3.8 %collective-permute-start.20 = (f32[32,128]{1,0:T(8,128)S(1)}, f32[32,128]{1,0:T(8,128)S(1)}, u32[]{:S(2)}, u32[]{:S(2)}) collective-permute-start(f32[32,128]{1,0:T(8,128)S(1)} %get-tuple-element.42), channel_id=1, source_target_pairs={{0,16},{8,24},{16,0},{24,8},{1,17},{9,25},{17,1},{25,9},{2,18},{10... | collective-permute-start | bytes 49160 | tf_op jit(solution)/shard_map/ppermute | solution.py:321
  66.7 2.2 %collective-permute-start.21 = (f32[32,128]{1,0:T(8,128)S(1)}, f32[32,128]{1,0:T(8,128)S(1)}, u32[]{:S(2)}, u32[]{:S(2)}) collective-permute-start(f32[32,128]{1,0:T(8,128)S(1)} %get-tuple-element.43), channel_id=1, source_target_pairs={{0,8},{8,0},{16,24},{24,16},{1,9},{9,1},{17,25},{25,17},{2,10},{10... | collective-permute-start | bytes 49160 | tf_op jit(solution)/shard_map/ppermute | solution.py:321
  68.9 5.6 %collective-permute-start.24 = (f32[32,128]{1,0:T(8,128)S(1)}, f32[32,128]{1,0:T(8,128)S(1)}, u32[]{:S(2)}, u32[]{:S(2)}) collective-permute-start(f32[32,128]{1,0:T(8,128)S(1)} %share_sum.2.refs_0_), channel_id=1, source_target_pairs={{0,6},{1,7},{2,4},{3,5},{4,2},{5,3},{6,0},{7,1},{8,14},{9,15},{10,... | collective-permute-start | bytes 49160 | tf_op jit(solution)/shard_map/ppermute | solution.py:321
  70.3 4.6 %collective-permute-start.23 = (f32[32,128]{1,0:T(8,128)S(1)}, f32[32,128]{1,0:T(8,128)S(1)}, u32[]{:S(2)}, u32[]{:S(2)}) collective-permute-start(f32[32,128]{1,0:T(8,128)S(1)} %share_sum.2.refs_0_), channel_id=1, source_target_pairs={{0,4},{1,5},{2,6},{3,7},{4,0},{5,1},{6,2},{7,3},{8,12},{9,13},{10,... | collective-permute-start | bytes 49160 | tf_op jit(solution)/shard_map/ppermute | solution.py:321
  71.4 3.8 %collective-permute-start.22 = (f32[32,128]{1,0:T(8,128)S(1)}, f32[32,128]{1,0:T(8,128)S(1)}, u32[]{:S(2)}, u32[]{:S(2)}) collective-permute-start(f32[32,128]{1,0:T(8,128)S(1)} %share_sum.2.refs_0_), channel_id=1, source_target_pairs={{0,2},{1,3},{2,0},{3,1},{4,6},{5,7},{6,4},{7,5},{8,10},{9,11},{10,... | collective-permute-start | bytes 49160 | tf_op jit(solution)/shard_map/ppermute | solution.py:321
  75.2 3.3 %collective-permute-start.27 = (f32[32,128]{1,0:T(8,128)S(1)}, f32[32,128]{1,0:T(8,128)S(1)}, u32[]{:S(2)}, u32[]{:S(2)}) collective-permute-start(f32[32,128]{1,0:T(8,128)S(1)} %share_sum.3.refs_0_), channel_id=1, source_target_pairs={{0,24},{8,16},{16,8},{24,0},{1,25},{9,17},{17,9},{25,1},{2,26},{10... | collective-permute-start | bytes 49160 | tf_op jit(solution)/shard_map/ppermute | solution.py:321
  75.2 3.8 %collective-permute-start.26 = (f32[32,128]{1,0:T(8,128)S(1)}, f32[32,128]{1,0:T(8,128)S(1)}, u32[]{:S(2)}, u32[]{:S(2)}) collective-permute-start(f32[32,128]{1,0:T(8,128)S(1)} %share_sum.3.refs_0_), channel_id=1, source_target_pairs={{0,16},{8,24},{16,0},{24,8},{1,17},{9,25},{17,1},{25,9},{2,18},{10... | collective-permute-start | bytes 49160 | tf_op jit(solution)/shard_map/ppermute | solution.py:321
  76.8 2.2 %collective-permute-start.25 = (f32[32,128]{1,0:T(8,128)S(1)}, f32[32,128]{1,0:T(8,128)S(1)}, u32[]{:S(2)}, u32[]{:S(2)}) collective-permute-start(f32[32,128]{1,0:T(8,128)S(1)} %share_sum.3.refs_0_), channel_id=1, source_target_pairs={{0,8},{8,0},{16,24},{24,16},{1,9},{9,1},{17,25},{25,17},{2,10},{10... | collective-permute-start | bytes 49160 | tf_op jit(solution)/shard_map/ppermute | solution.py:321

commit v6 on v5

--- a/solution.py
+++ b/solution.py
@@ -126,7 +126,8 @@
             tiles = [work[at : at + group, k : k + LANES] for k in range(0, work.shape[1], LANES)]
             peak = functools.reduce(jnp.maximum, tiles)
             peaks[at : at + group, :] = peak
-            totals[at : at + group, :] = functools.reduce(jnp.add, [jnp.exp2((tile - peak) * unit) for tile in tiles])
+            values = [jnp.exp2(((tile - peak) * unit).astype(BF16)).astype(F32) for tile in tiles]
+            totals[at : at + group, :] = functools.reduce(jnp.add, values)
     for part in range(rows // LANES):
         here = slice(part * LANES, (part + 1) * LANES)
         lane_peak = peaks[here, :]
@@ -218,7 +219,7 @@
 
 def sums_across(block, row, out):
     rows, cols = block.shape
-    cut = cols // 2
+    cut = cols // 4 // LANES * LANES
     first = lax.broadcasted_iota(jnp.int32, (16, 2 * LANES), 0) == 0
     pair = jnp.concatenate([two_rows(row[:, :cut]), jnp.where(first, 1.0, 0.0).astype(BF16)], axis=1)
     tiles = [(at, jnp.broadcast_to(row[:, at : at + LANES], (16, LANES))) for at in range(cut, cols, LANES)]
@@ -307,13 +308,14 @@
         square[pl.ds(pl.multiple_of((index ^ k) * height, height), height), :] = share[...]
     cross = square[...]
     iterate = cross / jnp.sqrt(jnp.sum(cross * cross) + 1e-06)
-    gram = precise(iterate, iterate, 0)
-    for step in range(NEWTON):
-        factor = jnp.where(eye_mask(), 1.5, 0.0) - 0.5 * gram
-        if step < NEWTON - 1:
-            gram = precise(precise(factor, gram), factor)
-        iterate = precise(iterate, factor)
-    out[...] = iterate
+    unity = jnp.where(eye_mask(), 1.0, 0.0)
+    error = unity - precise(iterate, iterate, 0)
+    size = error.shape[0]
+    for step in range(NEWTON - 1):
+        both = precise(jnp.concatenate([error, iterate], axis=0), error)
+        iterate = iterate + 0.5 * both[size:]
+        error = precise(both[:size], 0.75 * unity + 0.25 * error)
+    out[...] = iterate + 0.5 * precise(iterate, error)
 
 
 def partners(values, axis, order):

time: 83.1 us -> 82.9 us (level)
  no operation moved by 1% of the time
where the time goes in v6:
time: 82.9 us; the launch traced here: 82.7 us
  starting transfers between devices  30.3 us (37%)
  Pallas kernels  21.7 us (26%)
  waiting for transfers between devices  18.3 us (22%)
  blocking collectives  11.6 us (14%)
    ppermute x27, starting transfers between devices, partners(): lax.ppermute(values[k], axis, [(me, me ^ k) for me in range(size)])  27.3 us
    pallas_call x12, Pallas kernels, call(): pl.pallas_call(body, name=name, out_shape=out_shape, in_specs=[pl.BlockSp...  21.7 us
    ppermute x27, waiting for transfers between devices, partners(): lax.ppermute(values[k], axis, [(me, me ^ k) for me in range(size)])  18.3 us
    all_to_all x1, blocking collectives, over_tgt(): lax.all_to_all(jnp.broadcast_to(x, (lax.axis_size('tgt'),) + x.shape), 't...  11.6 us
    ppermute x1, starting transfers between devices, shards(): other = lax.ppermute(plain, 'tgt', [(me, me ^ 1) for me in range(n_tgt)])  3 us
  transfers between devices with their start and end apart: 28, of which 21 were waited for; matrix products, arithmetic and copies ran while one was open for 0% of the time, Pallas kernels for 3%

profile of v6, /device:TPU:0, one launch (start us, length us, event | category | flops | bytes accessed | tf_op | source)
XLA Modules:
  0.0 82.7 jit_solution(17382822970084238309)
XLA Ops:
  0.6 1.7 %prepare.1 = (bf16[2048,128]{1,0:T(8,128)(2,1)S(1)}, bf16[2048,128]{1,0:T(8,128)(2,1)S(1)}, bf16[128,2048]{1,0:T(8,128)(2,1)S(1)}, bf16[1024,256]{1,0:T(8,128)(2,1)S(1)}, f32[1024,128]{1,0:T(8,128)S(1)}) custom-call(bf16[2048,128]{1,0:T(8,128)(2,1)} %source_hbm.1, f32[128,128]{1,0:T(8,128)} %map_hbm.1, bf16[1024,128]{1,0:T(8,128)(2,1)} %target_hbm.1, ...), custom_call_target="tpu_custom_call" | custom-call | flops 67108864 | bytes 8388608 | tf_op jit(solution)/shard_map/prepare/pallas_call | solution.py:22
  2.3 3.0 %collective-permute-start = (f32[1024,128]{1,0:T(8,128)S(1)}, f32[1024,128]{1,0:T(8,128)S(1)}, u32[]{:S(2)}, u32[]{:S(2)}) collective-permute-start(f32[1024,128]{1,0:T(8,128)S(1)} %get-tuple-element.27), channel_id=1, source_target_pairs={{0,1},{1,0},{2,3},{3,2},{4,5},{5,4},{6,7},{7,6},{8,9},{9,8},{10,11... | collective-permute-start | bytes 1572872 | tf_op jit(solution)/shard_map/ppermute | solution.py:372
  5.3 2.5 %row_first.1 = f32[16,128]{1,0:T(8,128)S(1)} custom-call(bf16[2048,128]{1,0:T(8,128)(2,1)S(1)} %get-tuple-element.28.left_in, bf16[1024,256]{1,0:T(8,128)(2,1)S(1)} %get-tuple-element.26.right.own), custom_call_target="tpu_custom_call" | custom-call | flops 1073741824 | bytes 8388608 | tf_op jit(solution)/shard_map/row_first/pallas_call | solution.py:22
  7.8 11.6 %all_to_all.5.refs_0_ = f32[8,16,128]{2,1,0:T(8,128)S(1)} all-to-all(f32[8,16,128]{2,1,0:T(8,128)S(1)} %broadcast_in_dim.3), channel_id=1, replica_groups=mesh['src'=4,'tgt'=8] {'tgt'}, dimensions={0} | all-to-all | bytes 131072 | tf_op jit(solution)/shard_map/all_to_all | solution.py:337
  19.4 4.9 %col_first.1 = (bf16[2048,2048]{1,0:T(8,128)(2,1)S(1)}, bf16[128,2048]{1,0:T(8,128)(2,1)S(1)}, f32[16,128]{1,0:T(8,128)S(1)}, f32[1,2048]{1,0:T(1,128)S(1)}, f32[1,2048]{1,0:T(1,128)S(1)}) custom-call(bf16[128,2048]{1,0:T(8,128)(2,1)S(1)} %get-tuple-element.25.turned, bf16[1024,256]{1,0:T(8,128)(2,1)S(1)} %get-tuple-element.26.right.own, ...), custom_call_target="tpu_custom_call" | custom-call | flops 2147483648 | bytes 8388608 | tf_op jit(solution)/shard_map/col_first/pallas_call | solution.py:22
  24.4 1.6 %collective-permute-start.2 = (f32[1,2048]{1,0:T(1,128)S(1)}, f32[1,2048]{1,0:T(1,128)S(1)}, u32[]{:S(2)}, u32[]{:S(2)}) collective-permute-start(f32[1,2048]{1,0:T(1,128)S(1)} %get-tuple-element.31.refs_0_), channel_id=1, source_target_pairs={{0,16},{8,24},{16,0},{24,8},{1,17},{9,25},{17,1},{25,9},{2,18},{10... | collective-permute-start | bytes 24584 | tf_op jit(solution)/shard_map/ppermute | solution.py:323
  26.2 1.2 %collective-permute-done.3.refs_3_ = f32[1,2048]{1,0:T(1,128)S(1)} collective-permute-done((f32[1,2048]{1,0:T(1,128)S(1)}, f32[1,2048]{1,0:T(1,128)S(1)}, u32[]{:S(2)}, u32[]{:S(2)}) %collective-permute-start.3) | collective-permute-done | bytes 8224 | tf_op jit(solution)/shard_map/ppermute | solution.py:323
  28.1 1.1 %row_second.1 = (f32[1,2048]{1,0:T(1,128)S(1)}, f32[1,2048]{1,0:T(1,128)S(1)}, f32[16,128]{1,0:T(8,128)S(1)}) custom-call(bf16[2048,2048]{1,0:T(8,128)(2,1)S(1)} %get-tuple-element.29.block, f32[1,2048]{1,0:T(1,128)S(1)} %get-tuple-element.30.peak, f32[1,2048]{1,0:T(1,128)S(1)} %get-tuple-element.31.refs_0_, f32[1,2048]{1,0:T(1,128)S(1)} %collective-permute-done.1.refs_1_, ...), custom_call_target="tpu_custom_call" | custom-call | flops 1073741824 | bytes 8388608 | tf_op jit(solution)/shard_map/row_second/pallas_call | solution.py:22
  29.2 2.5 %collective-permute-start.6 = (f32[16,128]{1,0:T(8,128)S(1)}, f32[16,128]{1,0:T(8,128)S(1)}, u32[]{:S(2)}, u32[]{:S(2)}) collective-permute-start(f32[16,128]{1,0:T(8,128)S(1)} %get-tuple-element.35.refs_0_), channel_id=1, source_target_pairs={{0,6},{1,7},{2,4},{3,5},{4,2},{5,3},{6,0},{7,1},{8,14},{9,15},{10,... | collective-permute-start | bytes 24584 | tf_op jit(solution)/shard_map/ppermute | solution.py:323
  31.7 2.0 %collective-permute-start.4 = (f32[16,128]{1,0:T(8,128)S(1)}, f32[16,128]{1,0:T(8,128)S(1)}, u32[]{:S(2)}, u32[]{:S(2)}) collective-permute-start(f32[16,128]{1,0:T(8,128)S(1)} %get-tuple-element.35.refs_0_), channel_id=1, source_target_pairs={{0,2},{1,3},{2,0},{3,1},{4,6},{5,7},{6,4},{7,5},{8,10},{9,11},{10,... | collective-permute-start | bytes 24584 | tf_op jit(solution)/shard_map/ppermute | solution.py:323
  34.7 1.5 %collective-permute-done.5.refs_2_ = f32[16,128]{1,0:T(8,128)S(1)} collective-permute-done((f32[16,128]{1,0:T(8,128)S(1)}, f32[16,128]{1,0:T(8,128)S(1)}, u32[]{:S(2)}, u32[]{:S(2)}) %collective-permute-start.5) | collective-permute-done | bytes 8224 | tf_op jit(solution)/shard_map/ppermute | solution.py:323
  36.2 1.7 %col_later.2.refs_0_ = f32[1,2048]{1,0:T(1,128)S(1)} custom-call(bf16[2048,2048]{1,0:T(8,128)(2,1)S(1)} %get-tuple-element.29.block, f32[1,2048]{1,0:T(1,128)S(1)} %get-tuple-element.32.scale, f32[16,128]{1,0:T(8,128)S(1)} %get-tuple-element.35.refs_0_, f32[16,128]{1,0:T(8,128)S(1)} %collective-permute-done.4.refs_1_, ...), custom_call_target="tpu_custom_call" | custom-call | flops 1073741824 | bytes 8388608 | tf_op jit(solution)/shard_map/col_later/pallas_call | solution.py:22
  38.0 1.6 %collective-permute-start.8 = (f32[1,2048]{1,0:T(1,128)S(1)}, f32[1,2048]{1,0:T(1,128)S(1)}, u32[]{:S(2)}, u32[]{:S(2)}) collective-permute-start(f32[1,2048]{1,0:T(1,128)S(1)} %col_later.2.refs_0_), channel_id=1, source_target_pairs={{0,16},{8,24},{16,0},{24,8},{1,17},{9,25},{17,1},{25,9},{2,18},{10... | collective-permute-start | bytes 24584 | tf_op jit(solution)/shard_map/ppermute | solution.py:323
  39.9 1.2 %collective-permute-done.9.refs_3_ = f32[1,2048]{1,0:T(1,128)S(1)} collective-permute-done((f32[1,2048]{1,0:T(1,128)S(1)}, f32[1,2048]{1,0:T(1,128)S(1)}, u32[]{:S(2)}, u32[]{:S(2)}) %collective-permute-start.9) | collective-permute-done | bytes 8224 | tf_op jit(solution)/shard_map/ppermute | solution.py:323
  41.8 1.1 %row_later.1.refs_0_ = f32[16,128]{1,0:T(8,128)S(1)} custom-call(bf16[2048,2048]{1,0:T(8,128)(2,1)S(1)} %get-tuple-element.29.block, f32[1,2048]{1,0:T(1,128)S(1)} %get-tuple-element.32.scale, f32[1,2048]{1,0:T(1,128)S(1)} %col_later.2.refs_0_, f32[1,2048]{1,0:T(1,128)S(1)} %collective-permute-done.7.refs_1_, f32[1,2048]{1,0:T(1,128)S(1)} %collective-permute-done.8.refs_2_, ...), custom_call_target="tpu_custom_call" | custom-call | flops 1073741824 | bytes 8388608 | tf_op jit(solution)/shard_map/row_later/pallas_call | solution.py:22
  42.9 1.6 %collective-permute-start.12 = (f32[16,128]{1,0:T(8,128)S(1)}, f32[16,128]{1,0:T(8,128)S(1)}, u32[]{:S(2)}, u32[]{:S(2)}) collective-permute-start(f32[16,128]{1,0:T(8,128)S(1)} %row_later.1.refs_0_), channel_id=1, source_target_pairs={{0,6},{1,7},{2,4},{3,5},{4,2},{5,3},{6,0},{7,1},{8,14},{9,15},{10,... | collective-permute-start | bytes 24584 | tf_op jit(solution)/shard_map/ppermute | solution.py:323
  45.5 1.8 %collective-permute-start.10 = (f32[16,128]{1,0:T(8,128)S(1)}, f32[16,128]{1,0:T(8,128)S(1)}, u32[]{:S(2)}, u32[]{:S(2)}) collective-permute-start(f32[16,128]{1,0:T(8,128)S(1)} %row_later.1.refs_0_), channel_id=1, source_target_pairs={{0,2},{1,3},{2,0},{3,1},{4,6},{5,7},{6,4},{7,5},{8,10},{9,11},{10,... | collective-permute-start | bytes 24584 | tf_op jit(solution)/shard_map/ppermute | solution.py:323
  49.1 1.7 %col_later.3.refs_0_ = f32[1,2048]{1,0:T(1,128)S(1)} custom-call(bf16[2048,2048]{1,0:T(8,128)(2,1)S(1)} %get-tuple-element.29.block, f32[1,2048]{1,0:T(1,128)S(1)} %get-tuple-element.32.scale, f32[16,128]{1,0:T(8,128)S(1)} %row_later.1.refs_0_, f32[16,128]{1,0:T(8,128)S(1)} %collective-permute-done.10.refs_1_, ...), custom_call_target="tpu_custom_call" | custom-call | flops 1073741824 | bytes 8388608 | tf_op jit(solution)/shard_map/col_later/pallas_call | solution.py:22
  50.9 1.6 %collective-permute-start.14 = (f32[1,2048]{1,0:T(1,128)S(1)}, f32[1,2048]{1,0:T(1,128)S(1)}, u32[]{:S(2)}, u32[]{:S(2)}) collective-permute-start(f32[1,2048]{1,0:T(1,128)S(1)} %col_later.3.refs_0_), channel_id=1, source_target_pairs={{0,16},{8,24},{16,0},{24,8},{1,17},{9,25},{17,1},{25,9},{2,18},{10... | collective-permute-start | bytes 24584 | tf_op jit(solution)/shard_map/ppermute | solution.py:323
  52.8 1.2 %collective-permute-done.15.refs_3_ = f32[1,2048]{1,0:T(1,128)S(1)} collective-permute-done((f32[1,2048]{1,0:T(1,128)S(1)}, f32[1,2048]{1,0:T(1,128)S(1)}, u32[]{:S(2)}, u32[]{:S(2)}) %collective-permute-start.15) | collective-permute-done | bytes 8224 | tf_op jit(solution)/shard_map/ppermute | solution.py:323
  54.6 2.1 %row_last.1 = (f32[1,1024]{1,0:T(1,128)}, f32[16,128]{1,0:T(8,128)S(1)}, f32[128,2048]{1,0:T(8,128)S(1)}) custom-call(bf16[2048,2048]{1,0:T(8,128)(2,1)S(1)} %get-tuple-element.29.block, f32[1,2048]{1,0:T(1,128)S(1)} %get-tuple-element.32.scale, f32[1,2048]{1,0:T(1,128)S(1)} %get-tuple-element.33.pot, bf16[128,2048]{1,0:T(8,128)(2,1)S(1)} %get-tuple-element.34.target, ...), custom_call_target="tpu_custom_call" | custom-call | flops 1073741824 | bytes 8388608 | tf_op jit(solution)/shard_map/row_last/pallas_call | solution.py:22
  56.7 2.4 %collective-permute-start.18 = (f32[16,128]{1,0:T(8,128)S(1)}, f32[16,128]{1,0:T(8,128)S(1)}, u32[]{:S(2)}, u32[]{:S(2)}) collective-permute-start(f32[16,128]{1,0:T(8,128)S(1)} %get-tuple-element.38.refs_0_), channel_id=1, source_target_pairs={{0,6},{1,7},{2,4},{3,5},{4,2},{5,3},{6,0},{7,1},{8,14},{9,15},{10,... | collective-permute-start | bytes 24584 | tf_op jit(solution)/shard_map/ppermute | solution.py:323
  60.1 1.1 %collective-permute-start.16 = (f32[16,128]{1,0:T(8,128)S(1)}, f32[16,128]{1,0:T(8,128)S(1)}, u32[]{:S(2)}, u32[]{:S(2)}) collective-permute-start(f32[16,128]{1,0:T(8,128)S(1)} %get-tuple-element.38.refs_0_), channel_id=1, source_target_pairs={{0,2},{1,3},{2,0},{3,1},{4,6},{5,7},{6,4},{7,5},{8,10},{9,11},{10,... | collective-permute-start | bytes 24584 | tf_op jit(solution)/shard_map/ppermute | solution.py:323
  62.2 1.5 %collective-permute-done.17.refs_2_ = f32[16,128]{1,0:T(8,128)S(1)} collective-permute-done((f32[16,128]{1,0:T(8,128)S(1)}, f32[16,128]{1,0:T(8,128)S(1)}, u32[]{:S(2)}, u32[]{:S(2)}) %collective-permute-start.17) | collective-permute-done | bytes 8224 | tf_op jit(solution)/shard_map/ppermute | solution.py:323
  64.8 1.5 %collective-permute-start.20 = (f32[32,128]{1,0:T(8,128)S(1)}, f32[32,128]{1,0:T(8,128)S(1)}, u32[]{:S(2)}, u32[]{:S(2)}) collective-permute-start(f32[32,128]{1,0:T(8,128)S(1)} %get-tuple-element.42), channel_id=1, source_target_pairs={{0,16},{8,24},{16,0},{24,8},{1,17},{9,25},{17,1},{25,9},{2,18},{10... | collective-permute-start | bytes 49160 | tf_op jit(solution)/shard_map/ppermute | solution.py:323
  66.7 1.4 %collective-permute-done.19.refs_0_ = f32[32,128]{1,0:T(8,128)S(1)} collective-permute-done((f32[32,128]{1,0:T(8,128)S(1)}, f32[32,128]{1,0:T(8,128)S(1)}, u32[]{:S(2)}, u32[]{:S(2)}) %collective-permute-start.19) | collective-permute-done | bytes 16416 | tf_op jit(solution)/shard_map/ppermute | solution.py:323
  68.6 1.5 %collective-permute-start.24 = (f32[32,128]{1,0:T(8,128)S(1)}, f32[32,128]{1,0:T(8,128)S(1)}, u32[]{:S(2)}, u32[]{:S(2)}) collective-permute-start(f32[32,128]{1,0:T(8,128)S(1)} %share_sum.2.refs_0_), channel_id=1, source_target_pairs={{0,6},{1,7},{2,4},{3,5},{4,2},{5,3},{6,0},{7,1},{8,14},{9,15},{10,... | collective-permute-start | bytes 49160 | tf_op jit(solution)/shard_map/ppermute | solution.py:323
  71.2 1.9 %collective-permute-start.22 = (f32[32,128]{1,0:T(8,128)S(1)}, f32[32,128]{1,0:T(8,128)S(1)}, u32[]{:S(2)}, u32[]{:S(2)}) collective-permute-start(f32[32,128]{1,0:T(8,128)S(1)} %share_sum.2.refs_0_), channel_id=1, source_target_pairs={{0,2},{1,3},{2,0},{3,1},{4,6},{5,7},{6,4},{7,5},{8,10},{9,11},{10,... | collective-permute-start | bytes 49160 | tf_op jit(solution)/shard_map/ppermute | solution.py:323
  73.1 1.2 %collective-permute-done.24.refs_3_ = f32[32,128]{1,0:T(8,128)S(1)} collective-permute-done((f32[32,128]{1,0:T(8,128)S(1)}, f32[32,128]{1,0:T(8,128)S(1)}, u32[]{:S(2)}, u32[]{:S(2)}) %collective-permute-start.24) | collective-permute-done | bytes 16416 | tf_op jit(solution)/shard_map/ppermute | solution.py:323
  75.0 1.6 %collective-permute-start.26 = (f32[32,128]{1,0:T(8,128)S(1)}, f32[32,128]{1,0:T(8,128)S(1)}, u32[]{:S(2)}, u32[]{:S(2)}) collective-permute-start(f32[32,128]{1,0:T(8,128)S(1)} %share_sum.3.refs_0_), channel_id=1, source_target_pairs={{0,16},{8,24},{16,0},{24,8},{1,17},{9,25},{17,1},{25,9},{2,18},{10... | collective-permute-start | bytes 49160 | tf_op jit(solution)/shard_map/ppermute | solution.py:323
  76.9 1.4 %collective-permute-done.27.refs_3_ = f32[32,128]{1,0:T(8,128)S(1)} collective-permute-done((f32[32,128]{1,0:T(8,128)S(1)}, f32[32,128]{1,0:T(8,128)S(1)}, u32[]{:S(2)}, u32[]{:S(2)}) %collective-permute-start.27) | collective-permute-done | bytes 16416 | tf_op jit(solution)/shard_map/ppermute | solution.py:323
  78.8 3.9 %polar.1 = f32[128,128]{1,0:T(8,128)} custom-call(f32[32,128]{1,0:T(8,128)S(1)} %share_sum.3.refs_0_, f32[32,128]{1,0:T(8,128)S(1)} %collective-permute-done.25.refs_1_, f32[32,128]{1,0:T(8,128)S(1)} %collective-permute-done.26.refs_2_, f32[32,128]{1,0:T(8,128)S(1)} %collective-permute-done.27.refs_3_), custom_call_target="tpu_custom_call" | custom-call | flops 134217728 | bytes 8388608 | tf_op jit(solution)/shard_map/polar/pallas_call | solution.py:22
  (38 shorter events, 13.4 us)
Async XLA Ops:
  2.3 17.1 %collective-permute-start = (f32[1024,128]{1,0:T(8,128)S(1)}, f32[1024,128]{1,0:T(8,128)S(1)}, u32[]{:S(2)}, u32[]{:S(2)}) collective-permute-start(f32[1024,128]{1,0:T(8,128)S(1)} %get-tuple-element.27), channel_id=1, source_target_pairs={{0,1},{1,0},{2,3},{3,2},{4,5},{5,4},{6,7},{7,6},{8,9},{9,8},{10,11... | collective-permute-start | bytes 1572872 | tf_op jit(solution)/shard_map/ppermute | solution.py:372
  24.3 3.1 %collective-permute-start.3 = (f32[1,2048]{1,0:T(1,128)S(1)}, f32[1,2048]{1,0:T(1,128)S(1)}, u32[]{:S(2)}, u32[]{:S(2)}) collective-permute-start(f32[1,2048]{1,0:T(1,128)S(1)} %get-tuple-element.31.refs_0_), channel_id=1, source_target_pairs={{0,24},{8,16},{16,8},{24,0},{1,25},{9,17},{17,9},{25,1},{2,26},{10... | collective-permute-start | bytes 24584 | tf_op jit(solution)/shard_map/ppermute | solution.py:323
  24.4 3.7 %collective-permute-start.2 = (f32[1,2048]{1,0:T(1,128)S(1)}, f32[1,2048]{1,0:T(1,128)S(1)}, u32[]{:S(2)}, u32[]{:S(2)}) collective-permute-start(f32[1,2048]{1,0:T(1,128)S(1)} %get-tuple-element.31.refs_0_), channel_id=1, source_target_pairs={{0,16},{8,24},{16,0},{24,8},{1,17},{9,25},{17,1},{25,9},{2,18},{10... | collective-permute-start | bytes 24584 | tf_op jit(solution)/shard_map/ppermute | solution.py:323
  26.0 2.1 %collective-permute-start.1 = (f32[1,2048]{1,0:T(1,128)S(1)}, f32[1,2048]{1,0:T(1,128)S(1)}, u32[]{:S(2)}, u32[]{:S(2)}) collective-permute-start(f32[1,2048]{1,0:T(1,128)S(1)} %get-tuple-element.31.refs_0_), channel_id=1, source_target_pairs={{0,8},{8,0},{16,24},{24,16},{1,9},{9,1},{17,25},{25,17},{2,10},{10... | collective-permute-start | bytes 24584 | tf_op jit(solution)/shard_map/ppermute | solution.py:323
  29.2 5.5 %collective-permute-start.6 = (f32[16,128]{1,0:T(8,128)S(1)}, f32[16,128]{1,0:T(8,128)S(1)}, u32[]{:S(2)}, u32[]{:S(2)}) collective-permute-start(f32[16,128]{1,0:T(8,128)S(1)} %get-tuple-element.35.refs_0_), channel_id=1, source_target_pairs={{0,6},{1,7},{2,4},{3,5},{4,2},{5,3},{6,0},{7,1},{8,14},{9,15},{10,... | collective-permute-start | bytes 24584 | tf_op jit(solution)/shard_map/ppermute | solution.py:323
  31.7 4.5 %collective-permute-start.5 = (f32[16,128]{1,0:T(8,128)S(1)}, f32[16,128]{1,0:T(8,128)S(1)}, u32[]{:S(2)}, u32[]{:S(2)}) collective-permute-start(f32[16,128]{1,0:T(8,128)S(1)} %get-tuple-element.35.refs_0_), channel_id=1, source_target_pairs={{0,4},{1,5},{2,6},{3,7},{4,0},{5,1},{6,2},{7,3},{8,12},{9,13},{10,... | collective-permute-start | bytes 24584 | tf_op jit(solution)/shard_map/ppermute | solution.py:323
  31.7 4.5 %collective-permute-start.4 = (f32[16,128]{1,0:T(8,128)S(1)}, f32[16,128]{1,0:T(8,128)S(1)}, u32[]{:S(2)}, u32[]{:S(2)}) collective-permute-start(f32[16,128]{1,0:T(8,128)S(1)} %get-tuple-element.35.refs_0_), channel_id=1, source_target_pairs={{0,2},{1,3},{2,0},{3,1},{4,6},{5,7},{6,4},{7,5},{8,10},{9,11},{10,... | collective-permute-start | bytes 24584 | tf_op jit(solution)/shard_map/ppermute | solution.py:323
  38.0 3.2 %collective-permute-start.9 = (f32[1,2048]{1,0:T(1,128)S(1)}, f32[1,2048]{1,0:T(1,128)S(1)}, u32[]{:S(2)}, u32[]{:S(2)}) collective-permute-start(f32[1,2048]{1,0:T(1,128)S(1)} %col_later.2.refs_0_), channel_id=1, source_target_pairs={{0,24},{8,16},{16,8},{24,0},{1,25},{9,17},{17,9},{25,1},{2,26},{10... | collective-permute-start | bytes 24584 | tf_op jit(solution)/shard_map/ppermute | solution.py:323
  38.0 3.7 %collective-permute-start.8 = (f32[1,2048]{1,0:T(1,128)S(1)}, f32[1,2048]{1,0:T(1,128)S(1)}, u32[]{:S(2)}, u32[]{:S(2)}) collective-permute-start(f32[1,2048]{1,0:T(1,128)S(1)} %col_later.2.refs_0_), channel_id=1, source_target_pairs={{0,16},{8,24},{16,0},{24,8},{1,17},{9,25},{17,1},{25,9},{2,18},{10... | collective-permute-start | bytes 24584 | tf_op jit(solution)/shard_map/ppermute | solution.py:323
  39.6 2.1 %collective-permute-start.7 = (f32[1,2048]{1,0:T(1,128)S(1)}, f32[1,2048]{1,0:T(1,128)S(1)}, u32[]{:S(2)}, u32[]{:S(2)}) collective-permute-start(f32[1,2048]{1,0:T(1,128)S(1)} %col_later.2.refs_0_), channel_id=1, source_target_pairs={{0,8},{8,0},{16,24},{24,16},{1,9},{9,1},{17,25},{25,17},{2,10},{10... | collective-permute-start | bytes 24584 | tf_op jit(solution)/shard_map/ppermute | solution.py:323
  42.9 5.5 %collective-permute-start.12 = (f32[16,128]{1,0:T(8,128)S(1)}, f32[16,128]{1,0:T(8,128)S(1)}, u32[]{:S(2)}, u32[]{:S(2)}) collective-permute-start(f32[16,128]{1,0:T(8,128)S(1)} %row_later.1.refs_0_), channel_id=1, source_target_pairs={{0,6},{1,7},{2,4},{3,5},{4,2},{5,3},{6,0},{7,1},{8,14},{9,15},{10,... | collective-permute-start | bytes 24584 | tf_op jit(solution)/shard_map/ppermute | solution.py:323
  44.4 4.5 %collective-permute-start.11 = (f32[16,128]{1,0:T(8,128)S(1)}, f32[16,128]{1,0:T(8,128)S(1)}, u32[]{:S(2)}, u32[]{:S(2)}) collective-permute-start(f32[16,128]{1,0:T(8,128)S(1)} %row_later.1.refs_0_), channel_id=1, source_target_pairs={{0,4},{1,5},{2,6},{3,7},{4,0},{5,1},{6,2},{7,3},{8,12},{9,13},{10,... | collective-permute-start | bytes 24584 | tf_op jit(solution)/shard_map/ppermute | solution.py:323
  45.5 3.7 %collective-permute-start.10 = (f32[16,128]{1,0:T(8,128)S(1)}, f32[16,128]{1,0:T(8,128)S(1)}, u32[]{:S(2)}, u32[]{:S(2)}) collective-permute-start(f32[16,128]{1,0:T(8,128)S(1)} %row_later.1.refs_0_), channel_id=1, source_target_pairs={{0,2},{1,3},{2,0},{3,1},{4,6},{5,7},{6,4},{7,5},{8,10},{9,11},{10,... | collective-permute-start | bytes 24584 | tf_op jit(solution)/shard_map/ppermute | solution.py:323
  50.9 3.1 %collective-permute-start.15 = (f32[1,2048]{1,0:T(1,128)S(1)}, f32[1,2048]{1,0:T(1,128)S(1)}, u32[]{:S(2)}, u32[]{:S(2)}) collective-permute-start(f32[1,2048]{1,0:T(1,128)S(1)} %col_later.3.refs_0_), channel_id=1, source_target_pairs={{0,24},{8,16},{16,8},{24,0},{1,25},{9,17},{17,9},{25,1},{2,26},{10... | collective-permute-start | bytes 24584 | tf_op jit(solution)/shard_map/ppermute | solution.py:323
  50.9 3.7 %collective-permute-start.14 = (f32[1,2048]{1,0:T(1,128)S(1)}, f32[1,2048]{1,0:T(1,128)S(1)}, u32[]{:S(2)}, u32[]{:S(2)}) collective-permute-start(f32[1,2048]{1,0:T(1,128)S(1)} %col_later.3.refs_0_), channel_id=1, source_target_pairs={{0,16},{8,24},{16,0},{24,8},{1,17},{9,25},{17,1},{25,9},{2,18},{10... | collective-permute-start | bytes 24584 | tf_op jit(solution)/shard_map/ppermute | solution.py:323
  52.5 2.1 %collective-permute-start.13 = (f32[1,2048]{1,0:T(1,128)S(1)}, f32[1,2048]{1,0:T(1,128)S(1)}, u32[]{:S(2)}, u32[]{:S(2)}) collective-permute-start(f32[1,2048]{1,0:T(1,128)S(1)} %col_later.3.refs_0_), channel_id=1, source_target_pairs={{0,8},{8,0},{16,24},{24,16},{1,9},{9,1},{17,25},{25,17},{2,10},{10... | collective-permute-start | bytes 24584 | tf_op jit(solution)/shard_map/ppermute | solution.py:323
  56.7 5.4 %collective-permute-start.18 = (f32[16,128]{1,0:T(8,128)S(1)}, f32[16,128]{1,0:T(8,128)S(1)}, u32[]{:S(2)}, u32[]{:S(2)}) collective-permute-start(f32[16,128]{1,0:T(8,128)S(1)} %get-tuple-element.38.refs_0_), channel_id=1, source_target_pairs={{0,6},{1,7},{2,4},{3,5},{4,2},{5,3},{6,0},{7,1},{8,14},{9,15},{10,... | collective-permute-start | bytes 24584 | tf_op jit(solution)/shard_map/ppermute | solution.py:323
  59.1 4.6 %collective-permute-start.17 = (f32[16,128]{1,0:T(8,128)S(1)}, f32[16,128]{1,0:T(8,128)S(1)}, u32[]{:S(2)}, u32[]{:S(2)}) collective-permute-start(f32[16,128]{1,0:T(8,128)S(1)} %get-tuple-element.38.refs_0_), channel_id=1, source_target_pairs={{0,4},{1,5},{2,6},{3,7},{4,0},{5,1},{6,2},{7,3},{8,12},{9,13},{10,... | collective-permute-start | bytes 24584 | tf_op jit(solution)/shard_map/ppermute | solution.py:323
  60.1 3.7 %collective-permute-start.16 = (f32[16,128]{1,0:T(8,128)S(1)}, f32[16,128]{1,0:T(8,128)S(1)}, u32[]{:S(2)}, u32[]{:S(2)}) collective-permute-start(f32[16,128]{1,0:T(8,128)S(1)} %get-tuple-element.38.refs_0_), channel_id=1, source_target_pairs={{0,2},{1,3},{2,0},{3,1},{4,6},{5,7},{6,4},{7,5},{8,10},{9,11},{10,... | collective-permute-start | bytes 24584 | tf_op jit(solution)/shard_map/ppermute | solution.py:323
  64.8 3.3 %collective-permute-start.19 = (f32[32,128]{1,0:T(8,128)S(1)}, f32[32,128]{1,0:T(8,128)S(1)}, u32[]{:S(2)}, u32[]{:S(2)}) collective-permute-start(f32[32,128]{1,0:T(8,128)S(1)} %get-tuple-element.41), channel_id=1, source_target_pairs={{0,24},{8,16},{16,8},{24,0},{1,25},{9,17},{17,9},{25,1},{2,26},{10... | collective-permute-start | bytes 49160 | tf_op jit(solution)/shard_map/ppermute | solution.py:323
  64.8 3.8 %collective-permute-start.20 = (f32[32,128]{1,0:T(8,128)S(1)}, f32[32,128]{1,0:T(8,128)S(1)}, u32[]{:S(2)}, u32[]{:S(2)}) collective-permute-start(f32[32,128]{1,0:T(8,128)S(1)} %get-tuple-element.42), channel_id=1, source_target_pairs={{0,16},{8,24},{16,0},{24,8},{1,17},{9,25},{17,1},{25,9},{2,18},{10... | collective-permute-start | bytes 49160 | tf_op jit(solution)/shard_map/ppermute | solution.py:323
  66.4 2.2 %collective-permute-start.21 = (f32[32,128]{1,0:T(8,128)S(1)}, f32[32,128]{1,0:T(8,128)S(1)}, u32[]{:S(2)}, u32[]{:S(2)}) collective-permute-start(f32[32,128]{1,0:T(8,128)S(1)} %get-tuple-element.43), channel_id=1, source_target_pairs={{0,8},{8,0},{16,24},{24,16},{1,9},{9,1},{17,25},{25,17},{2,10},{10... | collective-permute-start | bytes 49160 | tf_op jit(solution)/shard_map/ppermute | solution.py:323
  68.6 5.6 %collective-permute-start.24 = (f32[32,128]{1,0:T(8,128)S(1)}, f32[32,128]{1,0:T(8,128)S(1)}, u32[]{:S(2)}, u32[]{:S(2)}) collective-permute-start(f32[32,128]{1,0:T(8,128)S(1)} %share_sum.2.refs_0_), channel_id=1, source_target_pairs={{0,6},{1,7},{2,4},{3,5},{4,2},{5,3},{6,0},{7,1},{8,14},{9,15},{10,... | collective-permute-start | bytes 49160 | tf_op jit(solution)/shard_map/ppermute | solution.py:323
  70.1 4.6 %collective-permute-start.23 = (f32[32,128]{1,0:T(8,128)S(1)}, f32[32,128]{1,0:T(8,128)S(1)}, u32[]{:S(2)}, u32[]{:S(2)}) collective-permute-start(f32[32,128]{1,0:T(8,128)S(1)} %share_sum.2.refs_0_), channel_id=1, source_target_pairs={{0,4},{1,5},{2,6},{3,7},{4,0},{5,1},{6,2},{7,3},{8,12},{9,13},{10,... | collective-permute-start | bytes 49160 | tf_op jit(solution)/shard_map/ppermute | solution.py:323
  71.2 3.8 %collective-permute-start.22 = (f32[32,128]{1,0:T(8,128)S(1)}, f32[32,128]{1,0:T(8,128)S(1)}, u32[]{:S(2)}, u32[]{:S(2)}) collective-permute-start(f32[32,128]{1,0:T(8,128)S(1)} %share_sum.2.refs_0_), channel_id=1, source_target_pairs={{0,2},{1,3},{2,0},{3,1},{4,6},{5,7},{6,4},{7,5},{8,10},{9,11},{10,... | collective-permute-start | bytes 49160 | tf_op jit(solution)/shard_map/ppermute | solution.py:323
  74.9 3.3 %collective-permute-start.27 = (f32[32,128]{1,0:T(8,128)S(1)}, f32[32,128]{1,0:T(8,128)S(1)}, u32[]{:S(2)}, u32[]{:S(2)}) collective-permute-start(f32[32,128]{1,0:T(8,128)S(1)} %share_sum.3.refs_0_), channel_id=1, source_target_pairs={{0,24},{8,16},{16,8},{24,0},{1,25},{9,17},{17,9},{25,1},{2,26},{10... | collective-permute-start | bytes 49160 | tf_op jit(solution)/shard_map/ppermute | solution.py:323
  75.0 3.8 %collective-permute-start.26 = (f32[32,128]{1,0:T(8,128)S(1)}, f32[32,128]{1,0:T(8,128)S(1)}, u32[]{:S(2)}, u32[]{:S(2)}) collective-permute-start(f32[32,128]{1,0:T(8,128)S(1)} %share_sum.3.refs_0_), channel_id=1, source_target_pairs={{0,16},{8,24},{16,0},{24,8},{1,17},{9,25},{17,1},{25,9},{2,18},{10... | collective-permute-start | bytes 49160 | tf_op jit(solution)/shard_map/ppermute | solution.py:323
  76.6 2.2 %collective-permute-start.25 = (f32[32,128]{1,0:T(8,128)S(1)}, f32[32,128]{1,0:T(8,128)S(1)}, u32[]{:S(2)}, u32[]{:S(2)}) collective-permute-start(f32[32,128]{1,0:T(8,128)S(1)} %share_sum.3.refs_0_), channel_id=1, source_target_pairs={{0,8},{8,0},{16,24},{24,16},{1,9},{9,1},{17,25},{25,17},{2,10},{10... | collective-permute-start | bytes 49160 | tf_op jit(solution)/shard_map/ppermute | solution.py:323

commit v7 on v6

--- a/solution.py
+++ b/solution.py
@@ -116,6 +116,7 @@
 
 def row_first(unit, left_in, right, lse_out, work, peaks, totals, sums):
     rows = left_in.shape[0]
+    natural = unit * math.log(2.0)
     lane = lax.broadcasted_iota(jnp.int32, (CHUNK, LANES), 1)
     ones = jnp.where(lane < 3, 1.0, 0.0).astype(BF16)
     group = 16
@@ -126,8 +127,7 @@
             tiles = [work[at : at + group, k : k + LANES] for k in range(0, work.shape[1], LANES)]
             peak = functools.reduce(jnp.maximum, tiles)
             peaks[at : at + group, :] = peak
-            values = [jnp.exp2(((tile - peak) * unit).astype(BF16)).astype(F32) for tile in tiles]
-            totals[at : at + group, :] = functools.reduce(jnp.add, values)
+            totals[at : at + group, :] = functools.reduce(jnp.add, [jnp.exp((tile - peak) * natural) for tile in tiles])
     for part in range(rows // LANES):
         here = slice(part * LANES, (part + 1) * LANES)
         lane_peak = peaks[here, :]
@@ -147,6 +147,7 @@
     row_pot = -log_rows - tree_lse(unit, parts)
     pot_out[...] = row_pot
     width, rows = turned.shape
+    natural = unit * math.log(2.0)
     half = own.shape[0]
     cols = 2 * half
     odd = lax.axis_index("tgt") & 1
@@ -176,7 +177,7 @@
             top = peak[at : at + 16]
             total = None
             for k in range(0, rows, LANES):
-                value = jnp.exp2((scores[at : at + 16, k : k + LANES] - top) * unit)
+                value = jnp.exp((scores[at : at + 16, k : k + LANES] - top) * natural)
                 block_out[start + at : start + at + 16, k : k + LANES] = value.astype(BF16)
                 total = value if total is None else total + value
             sums.append(total)

time: 82.9 us -> 83.4 us (level)
  no operation moved by 1% of the time
where the time goes in v7:
time: 83.4 us; the launch traced here: 83.2 us
  starting transfers between devices  30.3 us (36%)
  Pallas kernels  22.3 us (27%)
  waiting for transfers between devices  18.3 us (22%)
  blocking collectives  11.6 us (14%)
    ppermute x27, starting transfers between devices, partners(): lax.ppermute(values[k], axis, [(me, me ^ k) for me in range(size)])  27.3 us
    pallas_call x12, Pallas kernels, call(): pl.pallas_call(body, name=name, out_shape=out_shape, in_specs=[pl.BlockSp...  22.3 us
    ppermute x27, waiting for transfers between devices, partners(): lax.ppermute(values[k], axis, [(me, me ^ k) for me in range(size)])  18.3 us
    all_to_all x1, blocking collectives, over_tgt(): lax.all_to_all(jnp.broadcast_to(x, (lax.axis_size('tgt'),) + x.shape), 't...  11.6 us
    ppermute x1, starting transfers between devices, shards(): other = lax.ppermute(plain, 'tgt', [(me, me ^ 1) for me in range(n_tgt)])  3 us
  transfers between devices with their start and end apart: 28, of which 21 were waited for; matrix products, arithmetic and copies ran while one was open for 0% of the time, Pallas kernels for 3%

profile of v7, /device:TPU:0, one launch (start us, length us, event | category | flops | bytes accessed | tf_op | source)
XLA Modules:
  0.0 83.2 jit_solution(6436861988691230851)
XLA Ops:
  0.6 1.7 %prepare.1 = (bf16[2048,128]{1,0:T(8,128)(2,1)S(1)}, bf16[2048,128]{1,0:T(8,128)(2,1)S(1)}, bf16[128,2048]{1,0:T(8,128)(2,1)S(1)}, bf16[1024,256]{1,0:T(8,128)(2,1)S(1)}, f32[1024,128]{1,0:T(8,128)S(1)}) custom-call(bf16[2048,128]{1,0:T(8,128)(2,1)} %source_hbm.1, f32[128,128]{1,0:T(8,128)} %map_hbm.1, bf16[1024,128]{1,0:T(8,128)(2,1)} %target_hbm.1, ...), custom_call_target="tpu_custom_call" | custom-call | flops 67108864 | bytes 8388608 | tf_op jit(solution)/shard_map/prepare/pallas_call | solution.py:22
  2.3 3.0 %collective-permute-start = (f32[1024,128]{1,0:T(8,128)S(1)}, f32[1024,128]{1,0:T(8,128)S(1)}, u32[]{:S(2)}, u32[]{:S(2)}) collective-permute-start(f32[1024,128]{1,0:T(8,128)S(1)} %get-tuple-element.27), channel_id=1, source_target_pairs={{0,1},{1,0},{2,3},{3,2},{4,5},{5,4},{6,7},{7,6},{8,9},{9,8},{10,11... | collective-permute-start | bytes 1572872 | tf_op jit(solution)/shard_map/ppermute | solution.py:373
  5.3 2.5 %row_first.1 = f32[16,128]{1,0:T(8,128)S(1)} custom-call(bf16[2048,128]{1,0:T(8,128)(2,1)S(1)} %get-tuple-element.28.left_in, bf16[1024,256]{1,0:T(8,128)(2,1)S(1)} %get-tuple-element.26.right.own), custom_call_target="tpu_custom_call" | custom-call | flops 1073741824 | bytes 8388608 | tf_op jit(solution)/shard_map/row_first/pallas_call | solution.py:22
  7.8 11.6 %all_to_all.5.refs_0_ = f32[8,16,128]{2,1,0:T(8,128)S(1)} all-to-all(f32[8,16,128]{2,1,0:T(8,128)S(1)} %broadcast_in_dim.3), channel_id=1, replica_groups=mesh['src'=4,'tgt'=8] {'tgt'}, dimensions={0} | all-to-all | bytes 131072 | tf_op jit(solution)/shard_map/all_to_all | solution.py:338
  19.4 5.5 %col_first.1 = (bf16[2048,2048]{1,0:T(8,128)(2,1)S(1)}, bf16[128,2048]{1,0:T(8,128)(2,1)S(1)}, f32[16,128]{1,0:T(8,128)S(1)}, f32[1,2048]{1,0:T(1,128)S(1)}, f32[1,2048]{1,0:T(1,128)S(1)}) custom-call(bf16[128,2048]{1,0:T(8,128)(2,1)S(1)} %get-tuple-element.25.turned, bf16[1024,256]{1,0:T(8,128)(2,1)S(1)} %get-tuple-element.26.right.own, ...), custom_call_target="tpu_custom_call" | custom-call | flops 2147483648 | bytes 8388608 | tf_op jit(solution)/shard_map/col_first/pallas_call | solution.py:22
  24.9 1.6 %collective-permute-start.2 = (f32[1,2048]{1,0:T(1,128)S(1)}, f32[1,2048]{1,0:T(1,128)S(1)}, u32[]{:S(2)}, u32[]{:S(2)}) collective-permute-start(f32[1,2048]{1,0:T(1,128)S(1)} %get-tuple-element.31.refs_0_), channel_id=1, source_target_pairs={{0,16},{8,24},{16,0},{24,8},{1,17},{9,25},{17,1},{25,9},{2,18},{10... | collective-permute-start | bytes 24584 | tf_op jit(solution)/shard_map/ppermute | solution.py:324
  26.8 1.2 %collective-permute-done.3.refs_3_ = f32[1,2048]{1,0:T(1,128)S(1)} collective-permute-done((f32[1,2048]{1,0:T(1,128)S(1)}, f32[1,2048]{1,0:T(1,128)S(1)}, u32[]{:S(2)}, u32[]{:S(2)}) %collective-permute-start.3) | collective-permute-done | bytes 8224 | tf_op jit(solution)/shard_map/ppermute | solution.py:324
  28.6 1.1 %row_second.1 = (f32[1,2048]{1,0:T(1,128)S(1)}, f32[1,2048]{1,0:T(1,128)S(1)}, f32[16,128]{1,0:T(8,128)S(1)}) custom-call(bf16[2048,2048]{1,0:T(8,128)(2,1)S(1)} %get-tuple-element.29.block, f32[1,2048]{1,0:T(1,128)S(1)} %get-tuple-element.30.peak, f32[1,2048]{1,0:T(1,128)S(1)} %get-tuple-element.31.refs_0_, f32[1,2048]{1,0:T(1,128)S(1)} %collective-permute-done.1.refs_1_, ...), custom_call_target="tpu_custom_call" | custom-call | flops 1073741824 | bytes 8388608 | tf_op jit(solution)/shard_map/row_second/pallas_call | solution.py:22
  29.8 2.5 %collective-permute-start.6 = (f32[16,128]{1,0:T(8,128)S(1)}, f32[16,128]{1,0:T(8,128)S(1)}, u32[]{:S(2)}, u32[]{:S(2)}) collective-permute-start(f32[16,128]{1,0:T(8,128)S(1)} %get-tuple-element.35.refs_0_), channel_id=1, source_target_pairs={{0,6},{1,7},{2,4},{3,5},{4,2},{5,3},{6,0},{7,1},{8,14},{9,15},{10,... | collective-permute-start | bytes 24584 | tf_op jit(solution)/shard_map/ppermute | solution.py:324
  32.3 1.9 %collective-permute-start.4 = (f32[16,128]{1,0:T(8,128)S(1)}, f32[16,128]{1,0:T(8,128)S(1)}, u32[]{:S(2)}, u32[]{:S(2)}) collective-permute-start(f32[16,128]{1,0:T(8,128)S(1)} %get-tuple-element.35.refs_0_), channel_id=1, source_target_pairs={{0,2},{1,3},{2,0},{3,1},{4,6},{5,7},{6,4},{7,5},{8,10},{9,11},{10,... | collective-permute-start | bytes 24584 | tf_op jit(solution)/shard_map/ppermute | solution.py:324
  34.2 1.1 %collective-permute-done.6.refs_3_ = f32[16,128]{1,0:T(8,128)S(1)} collective-permute-done((f32[16,128]{1,0:T(8,128)S(1)}, f32[16,128]{1,0:T(8,128)S(1)}, u32[]{:S(2)}, u32[]{:S(2)}) %collective-permute-start.6) | collective-permute-done | bytes 8224 | tf_op jit(solution)/shard_map/ppermute | solution.py:324
  35.3 1.5 %collective-permute-done.5.refs_2_ = f32[16,128]{1,0:T(8,128)S(1)} collective-permute-done((f32[16,128]{1,0:T(8,128)S(1)}, f32[16,128]{1,0:T(8,128)S(1)}, u32[]{:S(2)}, u32[]{:S(2)}) %collective-permute-start.5) | collective-permute-done | bytes 8224 | tf_op jit(solution)/shard_map/ppermute | solution.py:324
  36.8 1.7 %col_later.2.refs_0_ = f32[1,2048]{1,0:T(1,128)S(1)} custom-call(bf16[2048,2048]{1,0:T(8,128)(2,1)S(1)} %get-tuple-element.29.block, f32[1,2048]{1,0:T(1,128)S(1)} %get-tuple-element.32.scale, f32[16,128]{1,0:T(8,128)S(1)} %get-tuple-element.35.refs_0_, f32[16,128]{1,0:T(8,128)S(1)} %collective-permute-done.4.refs_1_, ...), custom_call_target="tpu_custom_call" | custom-call | flops 1073741824 | bytes 8388608 | tf_op jit(solution)/shard_map/col_later/pallas_call | solution.py:22
  38.6 1.6 %collective-permute-start.8 = (f32[1,2048]{1,0:T(1,128)S(1)}, f32[1,2048]{1,0:T(1,128)S(1)}, u32[]{:S(2)}, u32[]{:S(2)}) collective-permute-start(f32[1,2048]{1,0:T(1,128)S(1)} %col_later.2.refs_0_), channel_id=1, source_target_pairs={{0,16},{8,24},{16,0},{24,8},{1,17},{9,25},{17,1},{25,9},{2,18},{10... | collective-permute-start | bytes 24584 | tf_op jit(solution)/shard_map/ppermute | solution.py:324
  40.5 1.2 %collective-permute-done.9.refs_3_ = f32[1,2048]{1,0:T(1,128)S(1)} collective-permute-done((f32[1,2048]{1,0:T(1,128)S(1)}, f32[1,2048]{1,0:T(1,128)S(1)}, u32[]{:S(2)}, u32[]{:S(2)}) %collective-permute-start.9) | collective-permute-done | bytes 8224 | tf_op jit(solution)/shard_map/ppermute | solution.py:324
  42.3 1.1 %row_later.1.refs_0_ = f32[16,128]{1,0:T(8,128)S(1)} custom-call(bf16[2048,2048]{1,0:T(8,128)(2,1)S(1)} %get-tuple-element.29.block, f32[1,2048]{1,0:T(1,128)S(1)} %get-tuple-element.32.scale, f32[1,2048]{1,0:T(1,128)S(1)} %col_later.2.refs_0_, f32[1,2048]{1,0:T(1,128)S(1)} %collective-permute-done.7.refs_1_, f32[1,2048]{1,0:T(1,128)S(1)} %collective-permute-done.8.refs_2_, ...), custom_call_target="tpu_custom_call" | custom-call | flops 1073741824 | bytes 8388608 | tf_op jit(solution)/shard_map/row_later/pallas_call | solution.py:22
  43.5 1.5 %collective-permute-start.12 = (f32[16,128]{1,0:T(8,128)S(1)}, f32[16,128]{1,0:T(8,128)S(1)}, u32[]{:S(2)}, u32[]{:S(2)}) collective-permute-start(f32[16,128]{1,0:T(8,128)S(1)} %row_later.1.refs_0_), channel_id=1, source_target_pairs={{0,6},{1,7},{2,4},{3,5},{4,2},{5,3},{6,0},{7,1},{8,14},{9,15},{10,... | collective-permute-start | bytes 24584 | tf_op jit(solution)/shard_map/ppermute | solution.py:324
  46.0 1.9 %collective-permute-start.10 = (f32[16,128]{1,0:T(8,128)S(1)}, f32[16,128]{1,0:T(8,128)S(1)}, u32[]{:S(2)}, u32[]{:S(2)}) collective-permute-start(f32[16,128]{1,0:T(8,128)S(1)} %row_later.1.refs_0_), channel_id=1, source_target_pairs={{0,2},{1,3},{2,0},{3,1},{4,6},{5,7},{6,4},{7,5},{8,10},{9,11},{10,... | collective-permute-start | bytes 24584 | tf_op jit(solution)/shard_map/ppermute | solution.py:324
  49.7 1.7 %col_later.3.refs_0_ = f32[1,2048]{1,0:T(1,128)S(1)} custom-call(bf16[2048,2048]{1,0:T(8,128)(2,1)S(1)} %get-tuple-element.29.block, f32[1,2048]{1,0:T(1,128)S(1)} %get-tuple-element.32.scale, f32[16,128]{1,0:T(8,128)S(1)} %row_later.1.refs_0_, f32[16,128]{1,0:T(8,128)S(1)} %collective-permute-done.10.refs_1_, ...), custom_call_target="tpu_custom_call" | custom-call | flops 1073741824 | bytes 8388608 | tf_op jit(solution)/shard_map/col_later/pallas_call | solution.py:22
  51.5 1.6 %collective-permute-start.14 = (f32[1,2048]{1,0:T(1,128)S(1)}, f32[1,2048]{1,0:T(1,128)S(1)}, u32[]{:S(2)}, u32[]{:S(2)}) collective-permute-start(f32[1,2048]{1,0:T(1,128)S(1)} %col_later.3.refs_0_), channel_id=1, source_target_pairs={{0,16},{8,24},{16,0},{24,8},{1,17},{9,25},{17,1},{25,9},{2,18},{10... | collective-permute-start | bytes 24584 | tf_op jit(solution)/shard_map/ppermute | solution.py:324
  53.3 1.2 %collective-permute-done.15.refs_3_ = f32[1,2048]{1,0:T(1,128)S(1)} collective-permute-done((f32[1,2048]{1,0:T(1,128)S(1)}, f32[1,2048]{1,0:T(1,128)S(1)}, u32[]{:S(2)}, u32[]{:S(2)}) %collective-permute-start.15) | collective-permute-done | bytes 8224 | tf_op jit(solution)/shard_map/ppermute | solution.py:324
  55.2 2.1 %row_last.1 = (f32[1,1024]{1,0:T(1,128)}, f32[16,128]{1,0:T(8,128)S(1)}, f32[128,2048]{1,0:T(8,128)S(1)}) custom-call(bf16[2048,2048]{1,0:T(8,128)(2,1)S(1)} %get-tuple-element.29.block, f32[1,2048]{1,0:T(1,128)S(1)} %get-tuple-element.32.scale, f32[1,2048]{1,0:T(1,128)S(1)} %get-tuple-element.33.pot, bf16[128,2048]{1,0:T(8,128)(2,1)S(1)} %get-tuple-element.34.target, ...), custom_call_target="tpu_custom_call" | custom-call | flops 1073741824 | bytes 8388608 | tf_op jit(solution)/shard_map/row_last/pallas_call | solution.py:22
  57.3 2.4 %collective-permute-start.18 = (f32[16,128]{1,0:T(8,128)S(1)}, f32[16,128]{1,0:T(8,128)S(1)}, u32[]{:S(2)}, u32[]{:S(2)}) collective-permute-start(f32[16,128]{1,0:T(8,128)S(1)} %get-tuple-element.38.refs_0_), channel_id=1, source_target_pairs={{0,6},{1,7},{2,4},{3,5},{4,2},{5,3},{6,0},{7,1},{8,14},{9,15},{10,... | collective-permute-start | bytes 24584 | tf_op jit(solution)/shard_map/ppermute | solution.py:324
  62.7 1.5 %collective-permute-done.17.refs_2_ = f32[16,128]{1,0:T(8,128)S(1)} collective-permute-done((f32[16,128]{1,0:T(8,128)S(1)}, f32[16,128]{1,0:T(8,128)S(1)}, u32[]{:S(2)}, u32[]{:S(2)}) %collective-permute-start.17) | collective-permute-done | bytes 8224 | tf_op jit(solution)/shard_map/ppermute | solution.py:324
  65.4 1.6 %collective-permute-start.20 = (f32[32,128]{1,0:T(8,128)S(1)}, f32[32,128]{1,0:T(8,128)S(1)}, u32[]{:S(2)}, u32[]{:S(2)}) collective-permute-start(f32[32,128]{1,0:T(8,128)S(1)} %get-tuple-element.42), channel_id=1, source_target_pairs={{0,16},{8,24},{16,0},{24,8},{1,17},{9,25},{17,1},{25,9},{2,18},{10... | collective-permute-start | bytes 49160 | tf_op jit(solution)/shard_map/ppermute | solution.py:324
  67.3 1.4 %collective-permute-done.19.refs_0_ = f32[32,128]{1,0:T(8,128)S(1)} collective-permute-done((f32[32,128]{1,0:T(8,128)S(1)}, f32[32,128]{1,0:T(8,128)S(1)}, u32[]{:S(2)}, u32[]{:S(2)}) %collective-permute-start.19) | collective-permute-done | bytes 16416 | tf_op jit(solution)/shard_map/ppermute | solution.py:324
  69.2 1.5 %collective-permute-start.24 = (f32[32,128]{1,0:T(8,128)S(1)}, f32[32,128]{1,0:T(8,128)S(1)}, u32[]{:S(2)}, u32[]{:S(2)}) collective-permute-start(f32[32,128]{1,0:T(8,128)S(1)} %share_sum.2.refs_0_), channel_id=1, source_target_pairs={{0,6},{1,7},{2,4},{3,5},{4,2},{5,3},{6,0},{7,1},{8,14},{9,15},{10,... | collective-permute-start | bytes 49160 | tf_op jit(solution)/shard_map/ppermute | solution.py:324
  71.7 2.0 %collective-permute-start.22 = (f32[32,128]{1,0:T(8,128)S(1)}, f32[32,128]{1,0:T(8,128)S(1)}, u32[]{:S(2)}, u32[]{:S(2)}) collective-permute-start(f32[32,128]{1,0:T(8,128)S(1)} %share_sum.2.refs_0_), channel_id=1, source_target_pairs={{0,2},{1,3},{2,0},{3,1},{4,6},{5,7},{6,4},{7,5},{8,10},{9,11},{10,... | collective-permute-start | bytes 49160 | tf_op jit(solution)/shard_map/ppermute | solution.py:324
  73.6 1.2 %collective-permute-done.24.refs_3_ = f32[32,128]{1,0:T(8,128)S(1)} collective-permute-done((f32[32,128]{1,0:T(8,128)S(1)}, f32[32,128]{1,0:T(8,128)S(1)}, u32[]{:S(2)}, u32[]{:S(2)}) %collective-permute-start.24) | collective-permute-done | bytes 16416 | tf_op jit(solution)/shard_map/ppermute | solution.py:324
  75.5 1.6 %collective-permute-start.26 = (f32[32,128]{1,0:T(8,128)S(1)}, f32[32,128]{1,0:T(8,128)S(1)}, u32[]{:S(2)}, u32[]{:S(2)}) collective-permute-start(f32[32,128]{1,0:T(8,128)S(1)} %share_sum.3.refs_0_), channel_id=1, source_target_pairs={{0,16},{8,24},{16,0},{24,8},{1,17},{9,25},{17,1},{25,9},{2,18},{10... | collective-permute-start | bytes 49160 | tf_op jit(solution)/shard_map/ppermute | solution.py:324
  77.4 1.4 %collective-permute-done.27.refs_3_ = f32[32,128]{1,0:T(8,128)S(1)} collective-permute-done((f32[32,128]{1,0:T(8,128)S(1)}, f32[32,128]{1,0:T(8,128)S(1)}, u32[]{:S(2)}, u32[]{:S(2)}) %collective-permute-start.27) | collective-permute-done | bytes 16416 | tf_op jit(solution)/shard_map/ppermute | solution.py:324
  79.3 3.8 %polar.1 = f32[128,128]{1,0:T(8,128)} custom-call(f32[32,128]{1,0:T(8,128)S(1)} %share_sum.3.refs_0_, f32[32,128]{1,0:T(8,128)S(1)} %collective-permute-done.25.refs_1_, f32[32,128]{1,0:T(8,128)S(1)} %collective-permute-done.26.refs_2_, f32[32,128]{1,0:T(8,128)S(1)} %collective-permute-done.27.refs_3_), custom_call_target="tpu_custom_call" | custom-call | flops 134217728 | bytes 8388608 | tf_op jit(solution)/shard_map/polar/pallas_call | solution.py:22
  (38 shorter events, 13.3 us)
Async XLA Ops:
  2.3 17.0 %collective-permute-start = (f32[1024,128]{1,0:T(8,128)S(1)}, f32[1024,128]{1,0:T(8,128)S(1)}, u32[]{:S(2)}, u32[]{:S(2)}) collective-permute-start(f32[1024,128]{1,0:T(8,128)S(1)} %get-tuple-element.27), channel_id=1, source_target_pairs={{0,1},{1,0},{2,3},{3,2},{4,5},{5,4},{6,7},{7,6},{8,9},{9,8},{10,11... | collective-permute-start | bytes 1572872 | tf_op jit(solution)/shard_map/ppermute | solution.py:373
  24.8 3.1 %collective-permute-start.3 = (f32[1,2048]{1,0:T(1,128)S(1)}, f32[1,2048]{1,0:T(1,128)S(1)}, u32[]{:S(2)}, u32[]{:S(2)}) collective-permute-start(f32[1,2048]{1,0:T(1,128)S(1)} %get-tuple-element.31.refs_0_), channel_id=1, source_target_pairs={{0,24},{8,16},{16,8},{24,0},{1,25},{9,17},{17,9},{25,1},{2,26},{10... | collective-permute-start | bytes 24584 | tf_op jit(solution)/shard_map/ppermute | solution.py:324
  24.9 3.7 %collective-permute-start.2 = (f32[1,2048]{1,0:T(1,128)S(1)}, f32[1,2048]{1,0:T(1,128)S(1)}, u32[]{:S(2)}, u32[]{:S(2)}) collective-permute-start(f32[1,2048]{1,0:T(1,128)S(1)} %get-tuple-element.31.refs_0_), channel_id=1, source_target_pairs={{0,16},{8,24},{16,0},{24,8},{1,17},{9,25},{17,1},{25,9},{2,18},{10... | collective-permute-start | bytes 24584 | tf_op jit(solution)/shard_map/ppermute | solution.py:324
  26.5 2.1 %collective-permute-start.1 = (f32[1,2048]{1,0:T(1,128)S(1)}, f32[1,2048]{1,0:T(1,128)S(1)}, u32[]{:S(2)}, u32[]{:S(2)}) collective-permute-start(f32[1,2048]{1,0:T(1,128)S(1)} %get-tuple-element.31.refs_0_), channel_id=1, source_target_pairs={{0,8},{8,0},{16,24},{24,16},{1,9},{9,1},{17,25},{25,17},{2,10},{10... | collective-permute-start | bytes 24584 | tf_op jit(solution)/shard_map/ppermute | solution.py:324
  29.8 5.5 %collective-permute-start.6 = (f32[16,128]{1,0:T(8,128)S(1)}, f32[16,128]{1,0:T(8,128)S(1)}, u32[]{:S(2)}, u32[]{:S(2)}) collective-permute-start(f32[16,128]{1,0:T(8,128)S(1)} %get-tuple-element.35.refs_0_), channel_id=1, source_target_pairs={{0,6},{1,7},{2,4},{3,5},{4,2},{5,3},{6,0},{7,1},{8,14},{9,15},{10,... | collective-permute-start | bytes 24584 | tf_op jit(solution)/shard_map/ppermute | solution.py:324
  32.3 4.5 %collective-permute-start.5 = (f32[16,128]{1,0:T(8,128)S(1)}, f32[16,128]{1,0:T(8,128)S(1)}, u32[]{:S(2)}, u32[]{:S(2)}) collective-permute-start(f32[16,128]{1,0:T(8,128)S(1)} %get-tuple-element.35.refs_0_), channel_id=1, source_target_pairs={{0,4},{1,5},{2,6},{3,7},{4,0},{5,1},{6,2},{7,3},{8,12},{9,13},{10,... | collective-permute-start | bytes 24584 | tf_op jit(solution)/shard_map/ppermute | solution.py:324
  32.3 4.5 %collective-permute-start.4 = (f32[16,128]{1,0:T(8,128)S(1)}, f32[16,128]{1,0:T(8,128)S(1)}, u32[]{:S(2)}, u32[]{:S(2)}) collective-permute-start(f32[16,128]{1,0:T(8,128)S(1)} %get-tuple-element.35.refs_0_), channel_id=1, source_target_pairs={{0,2},{1,3},{2,0},{3,1},{4,6},{5,7},{6,4},{7,5},{8,10},{9,11},{10,... | collective-permute-start | bytes 24584 | tf_op jit(solution)/shard_map/ppermute | solution.py:324
  38.5 3.2 %collective-permute-start.9 = (f32[1,2048]{1,0:T(1,128)S(1)}, f32[1,2048]{1,0:T(1,128)S(1)}, u32[]{:S(2)}, u32[]{:S(2)}) collective-permute-start(f32[1,2048]{1,0:T(1,128)S(1)} %col_later.2.refs_0_), channel_id=1, source_target_pairs={{0,24},{8,16},{16,8},{24,0},{1,25},{9,17},{17,9},{25,1},{2,26},{10... | collective-permute-start | bytes 24584 | tf_op jit(solution)/shard_map/ppermute | solution.py:324
  38.6 3.7 %collective-permute-start.8 = (f32[1,2048]{1,0:T(1,128)S(1)}, f32[1,2048]{1,0:T(1,128)S(1)}, u32[]{:S(2)}, u32[]{:S(2)}) collective-permute-start(f32[1,2048]{1,0:T(1,128)S(1)} %col_later.2.refs_0_), channel_id=1, source_target_pairs={{0,16},{8,24},{16,0},{24,8},{1,17},{9,25},{17,1},{25,9},{2,18},{10... | collective-permute-start | bytes 24584 | tf_op jit(solution)/shard_map/ppermute | solution.py:324
  40.2 2.1 %collective-permute-start.7 = (f32[1,2048]{1,0:T(1,128)S(1)}, f32[1,2048]{1,0:T(1,128)S(1)}, u32[]{:S(2)}, u32[]{:S(2)}) collective-permute-start(f32[1,2048]{1,0:T(1,128)S(1)} %col_later.2.refs_0_), channel_id=1, source_target_pairs={{0,8},{8,0},{16,24},{24,16},{1,9},{9,1},{17,25},{25,17},{2,10},{10... | collective-permute-start | bytes 24584 | tf_op jit(solution)/shard_map/ppermute | solution.py:324
  43.5 5.5 %collective-permute-start.12 = (f32[16,128]{1,0:T(8,128)S(1)}, f32[16,128]{1,0:T(8,128)S(1)}, u32[]{:S(2)}, u32[]{:S(2)}) collective-permute-start(f32[16,128]{1,0:T(8,128)S(1)} %row_later.1.refs_0_), channel_id=1, source_target_pairs={{0,6},{1,7},{2,4},{3,5},{4,2},{5,3},{6,0},{7,1},{8,14},{9,15},{10,... | collective-permute-start | bytes 24584 | tf_op jit(solution)/shard_map/ppermute | solution.py:324
  45.0 4.5 %collective-permute-start.11 = (f32[16,128]{1,0:T(8,128)S(1)}, f32[16,128]{1,0:T(8,128)S(1)}, u32[]{:S(2)}, u32[]{:S(2)}) collective-permute-start(f32[16,128]{1,0:T(8,128)S(1)} %row_later.1.refs_0_), channel_id=1, source_target_pairs={{0,4},{1,5},{2,6},{3,7},{4,0},{5,1},{6,2},{7,3},{8,12},{9,13},{10,... | collective-permute-start | bytes 24584 | tf_op jit(solution)/shard_map/ppermute | solution.py:324
  46.0 3.7 %collective-permute-start.10 = (f32[16,128]{1,0:T(8,128)S(1)}, f32[16,128]{1,0:T(8,128)S(1)}, u32[]{:S(2)}, u32[]{:S(2)}) collective-permute-start(f32[16,128]{1,0:T(8,128)S(1)} %row_later.1.refs_0_), channel_id=1, source_target_pairs={{0,2},{1,3},{2,0},{3,1},{4,6},{5,7},{6,4},{7,5},{8,10},{9,11},{10,... | collective-permute-start | bytes 24584 | tf_op jit(solution)/shard_map/ppermute | solution.py:324
  51.4 3.1 %collective-permute-start.15 = (f32[1,2048]{1,0:T(1,128)S(1)}, f32[1,2048]{1,0:T(1,128)S(1)}, u32[]{:S(2)}, u32[]{:S(2)}) collective-permute-start(f32[1,2048]{1,0:T(1,128)S(1)} %col_later.3.refs_0_), channel_id=1, source_target_pairs={{0,24},{8,16},{16,8},{24,0},{1,25},{9,17},{17,9},{25,1},{2,26},{10... | collective-permute-start | bytes 24584 | tf_op jit(solution)/shard_map/ppermute | solution.py:324
  51.5 3.7 %collective-permute-start.14 = (f32[1,2048]{1,0:T(1,128)S(1)}, f32[1,2048]{1,0:T(1,128)S(1)}, u32[]{:S(2)}, u32[]{:S(2)}) collective-permute-start(f32[1,2048]{1,0:T(1,128)S(1)} %col_later.3.refs_0_), channel_id=1, source_target_pairs={{0,16},{8,24},{16,0},{24,8},{1,17},{9,25},{17,1},{25,9},{2,18},{10... | collective-permute-start | bytes 24584 | tf_op jit(solution)/shard_map/ppermute | solution.py:324
  53.1 2.1 %collective-permute-start.13 = (f32[1,2048]{1,0:T(1,128)S(1)}, f32[1,2048]{1,0:T(1,128)S(1)}, u32[]{:S(2)}, u32[]{:S(2)}) collective-permute-start(f32[1,2048]{1,0:T(1,128)S(1)} %col_later.3.refs_0_), channel_id=1, source_target_pairs={{0,8},{8,0},{16,24},{24,16},{1,9},{9,1},{17,25},{25,17},{2,10},{10... | collective-permute-start | bytes 24584 | tf_op jit(solution)/shard_map/ppermute | solution.py:324
  57.3 5.4 %collective-permute-start.18 = (f32[16,128]{1,0:T(8,128)S(1)}, f32[16,128]{1,0:T(8,128)S(1)}, u32[]{:S(2)}, u32[]{:S(2)}) collective-permute-start(f32[16,128]{1,0:T(8,128)S(1)} %get-tuple-element.38.refs_0_), channel_id=1, source_target_pairs={{0,6},{1,7},{2,4},{3,5},{4,2},{5,3},{6,0},{7,1},{8,14},{9,15},{10,... | collective-permute-start | bytes 24584 | tf_op jit(solution)/shard_map/ppermute | solution.py:324
  59.7 4.6 %collective-permute-start.17 = (f32[16,128]{1,0:T(8,128)S(1)}, f32[16,128]{1,0:T(8,128)S(1)}, u32[]{:S(2)}, u32[]{:S(2)}) collective-permute-start(f32[16,128]{1,0:T(8,128)S(1)} %get-tuple-element.38.refs_0_), channel_id=1, source_target_pairs={{0,4},{1,5},{2,6},{3,7},{4,0},{5,1},{6,2},{7,3},{8,12},{9,13},{10,... | collective-permute-start | bytes 24584 | tf_op jit(solution)/shard_map/ppermute | solution.py:324
  60.6 3.7 %collective-permute-start.16 = (f32[16,128]{1,0:T(8,128)S(1)}, f32[16,128]{1,0:T(8,128)S(1)}, u32[]{:S(2)}, u32[]{:S(2)}) collective-permute-start(f32[16,128]{1,0:T(8,128)S(1)} %get-tuple-element.38.refs_0_), channel_id=1, source_target_pairs={{0,2},{1,3},{2,0},{3,1},{4,6},{5,7},{6,4},{7,5},{8,10},{9,11},{10,... | collective-permute-start | bytes 24584 | tf_op jit(solution)/shard_map/ppermute | solution.py:324
  65.4 3.3 %collective-permute-start.19 = (f32[32,128]{1,0:T(8,128)S(1)}, f32[32,128]{1,0:T(8,128)S(1)}, u32[]{:S(2)}, u32[]{:S(2)}) collective-permute-start(f32[32,128]{1,0:T(8,128)S(1)} %get-tuple-element.41), channel_id=1, source_target_pairs={{0,24},{8,16},{16,8},{24,0},{1,25},{9,17},{17,9},{25,1},{2,26},{10... | collective-permute-start | bytes 49160 | tf_op jit(solution)/shard_map/ppermute | solution.py:324
  65.4 3.8 %collective-permute-start.20 = (f32[32,128]{1,0:T(8,128)S(1)}, f32[32,128]{1,0:T(8,128)S(1)}, u32[]{:S(2)}, u32[]{:S(2)}) collective-permute-start(f32[32,128]{1,0:T(8,128)S(1)} %get-tuple-element.42), channel_id=1, source_target_pairs={{0,16},{8,24},{16,0},{24,8},{1,17},{9,25},{17,1},{25,9},{2,18},{10... | collective-permute-start | bytes 49160 | tf_op jit(solution)/shard_map/ppermute | solution.py:324
  67.0 2.2 %collective-permute-start.21 = (f32[32,128]{1,0:T(8,128)S(1)}, f32[32,128]{1,0:T(8,128)S(1)}, u32[]{:S(2)}, u32[]{:S(2)}) collective-permute-start(f32[32,128]{1,0:T(8,128)S(1)} %get-tuple-element.43), channel_id=1, source_target_pairs={{0,8},{8,0},{16,24},{24,16},{1,9},{9,1},{17,25},{25,17},{2,10},{10... | collective-permute-start | bytes 49160 | tf_op jit(solution)/shard_map/ppermute | solution.py:324
  69.2 5.6 %collective-permute-start.24 = (f32[32,128]{1,0:T(8,128)S(1)}, f32[32,128]{1,0:T(8,128)S(1)}, u32[]{:S(2)}, u32[]{:S(2)}) collective-permute-start(f32[32,128]{1,0:T(8,128)S(1)} %share_sum.2.refs_0_), channel_id=1, source_target_pairs={{0,6},{1,7},{2,4},{3,5},{4,2},{5,3},{6,0},{7,1},{8,14},{9,15},{10,... | collective-permute-start | bytes 49160 | tf_op jit(solution)/shard_map/ppermute | solution.py:324
  70.6 4.6 %collective-permute-start.23 = (f32[32,128]{1,0:T(8,128)S(1)}, f32[32,128]{1,0:T(8,128)S(1)}, u32[]{:S(2)}, u32[]{:S(2)}) collective-permute-start(f32[32,128]{1,0:T(8,128)S(1)} %share_sum.2.refs_0_), channel_id=1, source_target_pairs={{0,4},{1,5},{2,6},{3,7},{4,0},{5,1},{6,2},{7,3},{8,12},{9,13},{10,... | collective-permute-start | bytes 49160 | tf_op jit(solution)/shard_map/ppermute | solution.py:324
  71.7 3.8 %collective-permute-start.22 = (f32[32,128]{1,0:T(8,128)S(1)}, f32[32,128]{1,0:T(8,128)S(1)}, u32[]{:S(2)}, u32[]{:S(2)}) collective-permute-start(f32[32,128]{1,0:T(8,128)S(1)} %share_sum.2.refs_0_), channel_id=1, source_target_pairs={{0,2},{1,3},{2,0},{3,1},{4,6},{5,7},{6,4},{7,5},{8,10},{9,11},{10,... | collective-permute-start | bytes 49160 | tf_op jit(solution)/shard_map/ppermute | solution.py:324
  75.5 3.3 %collective-permute-start.27 = (f32[32,128]{1,0:T(8,128)S(1)}, f32[32,128]{1,0:T(8,128)S(1)}, u32[]{:S(2)}, u32[]{:S(2)}) collective-permute-start(f32[32,128]{1,0:T(8,128)S(1)} %share_sum.3.refs_0_), channel_id=1, source_target_pairs={{0,24},{8,16},{16,8},{24,0},{1,25},{9,17},{17,9},{25,1},{2,26},{10... | collective-permute-start | bytes 49160 | tf_op jit(solution)/shard_map/ppermute | solution.py:324
  75.5 3.8 %collective-permute-start.26 = (f32[32,128]{1,0:T(8,128)S(1)}, f32[32,128]{1,0:T(8,128)S(1)}, u32[]{:S(2)}, u32[]{:S(2)}) collective-permute-start(f32[32,128]{1,0:T(8,128)S(1)} %share_sum.3.refs_0_), channel_id=1, source_target_pairs={{0,16},{8,24},{16,0},{24,8},{1,17},{9,25},{17,1},{25,9},{2,18},{10... | collective-permute-start | bytes 49160 | tf_op jit(solution)/shard_map/ppermute | solution.py:324
  77.1 2.2 %collective-permute-start.25 = (f32[32,128]{1,0:T(8,128)S(1)}, f32[32,128]{1,0:T(8,128)S(1)}, u32[]{:S(2)}, u32[]{:S(2)}) collective-permute-start(f32[32,128]{1,0:T(8,128)S(1)} %share_sum.3.refs_0_), channel_id=1, source_target_pairs={{0,8},{8,0},{16,24},{24,16},{1,9},{9,1},{17,25},{25,17},{2,10},{10... | collective-permute-start | bytes 49160 | tf_op jit(solution)/shard_map/ppermute | solution.py:324

commit v8 on v6

--- a/solution.py
+++ b/solution.py
@@ -126,8 +126,7 @@
             tiles = [work[at : at + group, k : k + LANES] for k in range(0, work.shape[1], LANES)]
             peak = functools.reduce(jnp.maximum, tiles)
             peaks[at : at + group, :] = peak
-            values = [jnp.exp2(((tile - peak) * unit).astype(BF16)).astype(F32) for tile in tiles]
-            totals[at : at + group, :] = functools.reduce(jnp.add, values)
+            totals[at : at + group, :] = functools.reduce(jnp.add, [jnp.exp2((tile - peak) * unit) for tile in tiles])
     for part in range(rows // LANES):
         here = slice(part * LANES, (part + 1) * LANES)
         lane_peak = peaks[here, :]
@@ -152,8 +151,7 @@
     odd = lax.axis_index("tgt") & 1
     right[pl.ds(pl.multiple_of(odd * half, half), half), :width] = own[:, :width]
     right[pl.ds(pl.multiple_of((1 - odd) * half, half), half), :width] = other[...].astype(BF16)
-    for at in range(0, cols, LANES):
-        target_out[:, at : at + LANES] = right[at : at + LANES, :width].T
+    target_out[...] = right[:, :width]
     lane = lax.broadcasted_iota(jnp.int32, (cols, LANES), 1)
     right[:, width:] = jnp.where(lane < 3, 1.0, 0.0).astype(BF16)
     left[:width, :] = turned[...]
@@ -253,20 +251,26 @@
     sums_down(block, scale[...] / tree_sum(parts), sums_out)
 
 
-def row_last(group, unit, block, scale, pot, target, *refs):
-    parts, (col_out, sums_out, bary_out) = received(refs, group)
+def row_last(group, unit, block, scale, pot, *refs):
+    parts, (col_out, factor_out, sums_out) = received(refs, group)
     totals = tree_sum(parts)
     pots = (EPS * math.log(2.0)) * (unit * pot[...] - jnp.log(totals) * (1.0 / math.log(2.0)))
     half = col_out.shape[1]
     col_out[...] = jnp.where((lax.axis_index("tgt") & 1) == 0, pots[:, :half], pots[:, half:])
     row = scale[...] / totals
-    scaled = (target[...].astype(F32) * row).astype(BF16)
-    left = jnp.concatenate([scaled, two_rows(row)], axis=0)
-    width = target.shape[0]
+    factor_out[...] = row
+    sums_down(block, row, sums_out)
+
+
+def barycentre(block, factor, target, bary_out):
+    pieces = []
+    for at in range(0, target.shape[0], LANES):
+        pieces.append((target[at : at + LANES, :].T.astype(F32) * factor[:, at : at + LANES]).astype(BF16))
+    left = jnp.concatenate(pieces, axis=1)
     for start in range(0, block.shape[1], CHUNK):
-        both = jnp.dot(left, block[:, start : start + CHUNK], preferred_element_type=F32)
-        bary_out[:, start : start + CHUNK] = both[:width]
-        put_rows(sums_out, start, both[width : width + 1] + both[width + 1 : width + 2])
+        bary_out[:, start : start + CHUNK] = jnp.dot(
+            left, block[:, start : start + CHUNK], preferred_element_type=F32
+        )
 
 
 def cross_local(group, unit, ratio, source, bary, pot, *refs):
@@ -387,7 +391,7 @@
         "col_first",
         (
             jax.ShapeDtypeStruct((2 * cols, rows), BF16),
-            jax.ShapeDtypeStruct((width, 2 * cols), BF16),
+            jax.ShapeDtypeStruct((2 * cols, width), BF16),
             row_vec,
             pair_vec,
             pair_vec,
@@ -414,12 +418,15 @@
         block, col_scale, *over_src(sums)
     )
     sums = col_later_call(block, col_scale, *over_pairs(sums))
-    col_out, sums, bary = call(
+    col_out, factor, sums = call(
         functools.partial(row_last, n_src, unit),
         "row_last",
-        (jax.ShapeDtypeStruct((1, cols), F32), row_vec, jax.ShapeDtypeStruct((width, rows), F32)),
+        (jax.ShapeDtypeStruct((1, cols), F32), pair_vec, row_vec),
         flops=4 * mac,
-    )(block, col_scale, col_pot, targets, *over_src(sums))
+    )(block, col_scale, col_pot, *over_src(sums))
+    bary = call(barycentre, "barycentre", jax.ShapeDtypeStruct((width, rows), F32), flops=4 * mac)(
+        block, factor, targets
+    )
     square = jax.ShapeDtypeStruct((width, width), F32)
     share_shape = jax.ShapeDtypeStruct((width // n_src, width), F32)
     row_out, *shares = call(

time: 82.9 us -> 82.8 us (level)
  Pallas kernels: 21.7 us -> 22.6 us
  waiting for transfers between devices: 18.3 us -> 17.4 us
    ppermute x27, waiting for transfers between devices: 18.3 us -> 17.4 us  [partners(): lax.ppermute(values[k], axis, [(me, me ^ k) for me in range(size)])]
    pallas_call x12 -> x13, Pallas kernels: 21.7 us -> 22.6 us  [call(): pl.pallas_call(body, name=name, out_shape=out_shape, in_specs=[pl.BlockSp...]
  transfers between devices with their start and end apart: 28 -> 28, of which waited for: 21 -> 20; matrix products, arithmetic and copies ran while one was open for 0% -> 0% of each run, Pallas kernels for 3% -> 4%
where the time goes in v8:
time: 82.8 us; the launch traced here: 82.7 us
  starting transfers between devices  30.3 us (37%)
  Pallas kernels  22.6 us (27%)
  waiting for transfers between devices  17.4 us (21%)
  blocking collectives  11.6 us (14%)
    ppermute x27, starting transfers between devices, partners(): lax.ppermute(values[k], axis, [(me, me ^ k) for me in range(size)])  27.3 us
    pallas_call x13, Pallas kernels, call(): pl.pallas_call(body, name=name, out_shape=out_shape, in_specs=[pl.BlockSp...  22.6 us
    ppermute x27, waiting for transfers between devices, partners(): lax.ppermute(values[k], axis, [(me, me ^ k) for me in range(size)])  17.4 us
    all_to_all x1, blocking collectives, over_tgt(): lax.all_to_all(jnp.broadcast_to(x, (lax.axis_size('tgt'),) + x.shape), 't...  11.6 us
    ppermute x1, starting transfers between devices, shards(): other = lax.ppermute(plain, 'tgt', [(me, me ^ 1) for me in range(n_tgt)])  3 us
  transfers between devices with their start and end apart: 28, of which 20 were waited for; matrix products, arithmetic and copies ran while one was open for 0% of the time, Pallas kernels for 4%

profile of v8, /device:TPU:0, one launch (start us, length us, event | category | flops | bytes accessed | tf_op | source)
XLA Modules:
  0.0 82.7 jit_solution(5503751806804236177)
XLA Ops:
  0.6 1.7 %prepare.1 = (bf16[2048,128]{1,0:T(8,128)(2,1)S(1)}, bf16[2048,128]{1,0:T(8,128)(2,1)S(1)}, bf16[128,2048]{1,0:T(8,128)(2,1)S(1)}, bf16[1024,256]{1,0:T(8,128)(2,1)S(1)}, f32[1024,128]{1,0:T(8,128)S(1)}) custom-call(bf16[2048,128]{1,0:T(8,128)(2,1)} %source_hbm.1, f32[128,128]{1,0:T(8,128)} %map_hbm.1, bf16[1024,128]{1,0:T(8,128)(2,1)} %target_hbm.1, ...), custom_call_target="tpu_custom_call" | custom-call | flops 67108864 | bytes 8388608 | tf_op jit(solution)/shard_map/prepare/pallas_call | solution.py:22
  2.3 3.0 %collective-permute-start = (f32[1024,128]{1,0:T(8,128)S(1)}, f32[1024,128]{1,0:T(8,128)S(1)}, u32[]{:S(2)}, u32[]{:S(2)}) collective-permute-start(f32[1024,128]{1,0:T(8,128)S(1)} %get-tuple-element.27), channel_id=1, source_target_pairs={{0,1},{1,0},{2,3},{3,2},{4,5},{5,4},{6,7},{7,6},{8,9},{9,8},{10,11... | collective-permute-start | bytes 1572872 | tf_op jit(solution)/shard_map/ppermute | solution.py:376
  5.3 2.2 %row_first.1 = f32[16,128]{1,0:T(8,128)S(1)} custom-call(bf16[2048,128]{1,0:T(8,128)(2,1)S(1)} %get-tuple-element.28.left_in, bf16[1024,256]{1,0:T(8,128)(2,1)S(1)} %get-tuple-element.26.right.own), custom_call_target="tpu_custom_call" | custom-call | flops 1073741824 | bytes 8388608 | tf_op jit(solution)/shard_map/row_first/pallas_call | solution.py:22
  7.5 11.6 %all_to_all.5.refs_0_ = f32[8,16,128]{2,1,0:T(8,128)S(1)} all-to-all(f32[8,16,128]{2,1,0:T(8,128)S(1)} %broadcast_in_dim.3), channel_id=1, replica_groups=mesh['src'=4,'tgt'=8] {'tgt'}, dimensions={0} | all-to-all | bytes 131072 | tf_op jit(solution)/shard_map/all_to_all | solution.py:341
  19.1 5.0 %col_first.1 = (bf16[2048,2048]{1,0:T(8,128)(2,1)S(1)}, bf16[2048,128]{1,0:T(8,128)(2,1)S(1)}, f32[16,128]{1,0:T(8,128)S(1)}, f32[1,2048]{1,0:T(1,128)S(1)}, f32[1,2048]{1,0:T(1,128)S(1)}) custom-call(bf16[128,2048]{1,0:T(8,128)(2,1)S(1)} %get-tuple-element.25.turned, bf16[1024,256]{1,0:T(8,128)(2,1)S(1)} %get-tuple-element.26.right.own, ...), custom_call_target="tpu_custom_call" | custom-call | flops 2147483648 | bytes 8388608 | tf_op jit(solution)/shard_map/col_first/pallas_call | solution.py:22
  24.1 1.6 %collective-permute-start.2 = (f32[1,2048]{1,0:T(1,128)S(1)}, f32[1,2048]{1,0:T(1,128)S(1)}, u32[]{:S(2)}, u32[]{:S(2)}) collective-permute-start(f32[1,2048]{1,0:T(1,128)S(1)} %get-tuple-element.31.refs_0_), channel_id=1, source_target_pairs={{0,16},{8,24},{16,0},{24,8},{1,17},{9,25},{17,1},{25,9},{2,18},{10... | collective-permute-start | bytes 24584 | tf_op jit(solution)/shard_map/ppermute | solution.py:327
  26.0 1.2 %collective-permute-done.3.refs_3_ = f32[1,2048]{1,0:T(1,128)S(1)} collective-permute-done((f32[1,2048]{1,0:T(1,128)S(1)}, f32[1,2048]{1,0:T(1,128)S(1)}, u32[]{:S(2)}, u32[]{:S(2)}) %collective-permute-start.3) | collective-permute-done | bytes 8224 | tf_op jit(solution)/shard_map/ppermute | solution.py:327
  27.9 1.1 %row_second.1 = (f32[1,2048]{1,0:T(1,128)S(1)}, f32[1,2048]{1,0:T(1,128)S(1)}, f32[16,128]{1,0:T(8,128)S(1)}) custom-call(bf16[2048,2048]{1,0:T(8,128)(2,1)S(1)} %get-tuple-element.29.block, f32[1,2048]{1,0:T(1,128)S(1)} %get-tuple-element.30.peak, f32[1,2048]{1,0:T(1,128)S(1)} %get-tuple-element.31.refs_0_, f32[1,2048]{1,0:T(1,128)S(1)} %collective-permute-done.1.refs_1_, ...), custom_call_target="tpu_custom_call" | custom-call | flops 1073741824 | bytes 8388608 | tf_op jit(solution)/shard_map/row_second/pallas_call | solution.py:22
  29.0 2.8 %collective-permute-start.6 = (f32[16,128]{1,0:T(8,128)S(1)}, f32[16,128]{1,0:T(8,128)S(1)}, u32[]{:S(2)}, u32[]{:S(2)}) collective-permute-start(f32[16,128]{1,0:T(8,128)S(1)} %get-tuple-element.34.refs_0_), channel_id=1, source_target_pairs={{0,6},{1,7},{2,4},{3,5},{4,2},{5,3},{6,0},{7,1},{8,14},{9,15},{10,... | collective-permute-start | bytes 24584 | tf_op jit(solution)/shard_map/ppermute | solution.py:327
  31.8 1.6 %collective-permute-start.4 = (f32[16,128]{1,0:T(8,128)S(1)}, f32[16,128]{1,0:T(8,128)S(1)}, u32[]{:S(2)}, u32[]{:S(2)}) collective-permute-start(f32[16,128]{1,0:T(8,128)S(1)} %get-tuple-element.34.refs_0_), channel_id=1, source_target_pairs={{0,2},{1,3},{2,0},{3,1},{4,6},{5,7},{6,4},{7,5},{8,10},{9,11},{10,... | collective-permute-start | bytes 24584 | tf_op jit(solution)/shard_map/ppermute | solution.py:327
  33.4 1.1 %collective-permute-done.6.refs_3_ = f32[16,128]{1,0:T(8,128)S(1)} collective-permute-done((f32[16,128]{1,0:T(8,128)S(1)}, f32[16,128]{1,0:T(8,128)S(1)}, u32[]{:S(2)}, u32[]{:S(2)}) %collective-permute-start.6) | collective-permute-done | bytes 8224 | tf_op jit(solution)/shard_map/ppermute | solution.py:327
  34.6 1.8 %collective-permute-done.5.refs_2_ = f32[16,128]{1,0:T(8,128)S(1)} collective-permute-done((f32[16,128]{1,0:T(8,128)S(1)}, f32[16,128]{1,0:T(8,128)S(1)}, u32[]{:S(2)}, u32[]{:S(2)}) %collective-permute-start.5) | collective-permute-done | bytes 8224 | tf_op jit(solution)/shard_map/ppermute | solution.py:327
  36.4 1.7 %col_later.2.refs_0_ = f32[1,2048]{1,0:T(1,128)S(1)} custom-call(bf16[2048,2048]{1,0:T(8,128)(2,1)S(1)} %get-tuple-element.29.block, f32[1,2048]{1,0:T(1,128)S(1)} %get-tuple-element.32.scale, f32[16,128]{1,0:T(8,128)S(1)} %get-tuple-element.34.refs_0_, f32[16,128]{1,0:T(8,128)S(1)} %collective-permute-done.4.refs_1_, ...), custom_call_target="tpu_custom_call" | custom-call | flops 1073741824 | bytes 8388608 | tf_op jit(solution)/shard_map/col_later/pallas_call | solution.py:22
  38.2 1.5 %collective-permute-start.8 = (f32[1,2048]{1,0:T(1,128)S(1)}, f32[1,2048]{1,0:T(1,128)S(1)}, u32[]{:S(2)}, u32[]{:S(2)}) collective-permute-start(f32[1,2048]{1,0:T(1,128)S(1)} %col_later.2.refs_0_), channel_id=1, source_target_pairs={{0,16},{8,24},{16,0},{24,8},{1,17},{9,25},{17,1},{25,9},{2,18},{10... | collective-permute-start | bytes 24584 | tf_op jit(solution)/shard_map/ppermute | solution.py:327
  40.0 1.3 %collective-permute-done.9.refs_3_ = f32[1,2048]{1,0:T(1,128)S(1)} collective-permute-done((f32[1,2048]{1,0:T(1,128)S(1)}, f32[1,2048]{1,0:T(1,128)S(1)}, u32[]{:S(2)}, u32[]{:S(2)}) %collective-permute-start.9) | collective-permute-done | bytes 8224 | tf_op jit(solution)/shard_map/ppermute | solution.py:327
  43.0 1.5 %collective-permute-start.12 = (f32[16,128]{1,0:T(8,128)S(1)}, f32[16,128]{1,0:T(8,128)S(1)}, u32[]{:S(2)}, u32[]{:S(2)}) collective-permute-start(f32[16,128]{1,0:T(8,128)S(1)} %row_later.1.refs_0_), channel_id=1, source_target_pairs={{0,6},{1,7},{2,4},{3,5},{4,2},{5,3},{6,0},{7,1},{8,14},{9,15},{10,... | collective-permute-start | bytes 24584 | tf_op jit(solution)/shard_map/ppermute | solution.py:327
  45.3 2.2 %collective-permute-start.10 = (f32[16,128]{1,0:T(8,128)S(1)}, f32[16,128]{1,0:T(8,128)S(1)}, u32[]{:S(2)}, u32[]{:S(2)}) collective-permute-start(f32[16,128]{1,0:T(8,128)S(1)} %row_later.1.refs_0_), channel_id=1, source_target_pairs={{0,2},{1,3},{2,0},{3,1},{4,6},{5,7},{6,4},{7,5},{8,10},{9,11},{10,... | collective-permute-start | bytes 24584 | tf_op jit(solution)/shard_map/ppermute | solution.py:327
  49.2 1.7 %col_later.3.refs_0_ = f32[1,2048]{1,0:T(1,128)S(1)} custom-call(bf16[2048,2048]{1,0:T(8,128)(2,1)S(1)} %get-tuple-element.29.block, f32[1,2048]{1,0:T(1,128)S(1)} %get-tuple-element.32.scale, f32[16,128]{1,0:T(8,128)S(1)} %row_later.1.refs_0_, f32[16,128]{1,0:T(8,128)S(1)} %collective-permute-done.10.refs_1_, ...), custom_call_target="tpu_custom_call" | custom-call | flops 1073741824 | bytes 8388608 | tf_op jit(solution)/shard_map/col_later/pallas_call | solution.py:22
  51.0 1.5 %collective-permute-start.14 = (f32[1,2048]{1,0:T(1,128)S(1)}, f32[1,2048]{1,0:T(1,128)S(1)}, u32[]{:S(2)}, u32[]{:S(2)}) collective-permute-start(f32[1,2048]{1,0:T(1,128)S(1)} %col_later.3.refs_0_), channel_id=1, source_target_pairs={{0,16},{8,24},{16,0},{24,8},{1,17},{9,25},{17,1},{25,9},{2,18},{10... | collective-permute-start | bytes 24584 | tf_op jit(solution)/shard_map/ppermute | solution.py:327
  52.8 1.3 %collective-permute-done.15.refs_3_ = f32[1,2048]{1,0:T(1,128)S(1)} collective-permute-done((f32[1,2048]{1,0:T(1,128)S(1)}, f32[1,2048]{1,0:T(1,128)S(1)}, u32[]{:S(2)}, u32[]{:S(2)}) %collective-permute-start.15) | collective-permute-done | bytes 8224 | tf_op jit(solution)/shard_map/ppermute | solution.py:327
  54.7 1.9 %row_last.1 = (f32[1,1024]{1,0:T(1,128)}, f32[1,2048]{1,0:T(1,128)S(1)}, f32[16,128]{1,0:T(8,128)S(1)}) custom-call(bf16[2048,2048]{1,0:T(8,128)(2,1)S(1)} %get-tuple-element.29.block, f32[1,2048]{1,0:T(1,128)S(1)} %get-tuple-element.32.scale, f32[1,2048]{1,0:T(1,128)S(1)} %get-tuple-element.33.pot, f32[1,2048]{1,0:T(1,128)S(1)} %col_later.3.refs_0_, ...), custom_call_target="tpu_custom_call" | custom-call | flops 1073741824 | bytes 8388608 | tf_op jit(solution)/shard_map/row_last/pallas_call | solution.py:22
  56.6 2.5 %collective-permute-start.18 = (f32[16,128]{1,0:T(8,128)S(1)}, f32[16,128]{1,0:T(8,128)S(1)}, u32[]{:S(2)}, u32[]{:S(2)}) collective-permute-start(f32[16,128]{1,0:T(8,128)S(1)} %get-tuple-element.38.refs_0_), channel_id=1, source_target_pairs={{0,6},{1,7},{2,4},{3,5},{4,2},{5,3},{6,0},{7,1},{8,14},{9,15},{10,... | collective-permute-start | bytes 24584 | tf_op jit(solution)/shard_map/ppermute | solution.py:327
  61.0 1.3 %barycentre.1.bary = f32[128,2048]{1,0:T(8,128)S(1)} custom-call(bf16[2048,2048]{1,0:T(8,128)(2,1)S(1)} %get-tuple-element.29.block, f32[1,2048]{1,0:T(1,128)S(1)} %get-tuple-element.35.factor, bf16[2048,128]{1,0:T(8,128)(2,1)S(1)} %get-tuple-element.36.target), custom_call_target="tpu_custom_call" | custom-call | flops 1073741824 | bytes 8388608 | tf_op jit(solution)/shard_map/barycentre/pallas_call | solution.py:22
  62.3 1.4 %collective-permute-done.17.refs_2_ = f32[16,128]{1,0:T(8,128)S(1)} collective-permute-done((f32[16,128]{1,0:T(8,128)S(1)}, f32[16,128]{1,0:T(8,128)S(1)}, u32[]{:S(2)}, u32[]{:S(2)}) %collective-permute-start.17) | collective-permute-done | bytes 8224 | tf_op jit(solution)/shard_map/ppermute | solution.py:327
  64.8 1.5 %collective-permute-start.20 = (f32[32,128]{1,0:T(8,128)S(1)}, f32[32,128]{1,0:T(8,128)S(1)}, u32[]{:S(2)}, u32[]{:S(2)}) collective-permute-start(f32[32,128]{1,0:T(8,128)S(1)} %get-tuple-element.42), channel_id=1, source_target_pairs={{0,16},{8,24},{16,0},{24,8},{1,17},{9,25},{17,1},{25,9},{2,18},{10... | collective-permute-start | bytes 49160 | tf_op jit(solution)/shard_map/ppermute | solution.py:327
  66.7 1.5 %collective-permute-done.19.refs_0_ = f32[32,128]{1,0:T(8,128)S(1)} collective-permute-done((f32[32,128]{1,0:T(8,128)S(1)}, f32[32,128]{1,0:T(8,128)S(1)}, u32[]{:S(2)}, u32[]{:S(2)}) %collective-permute-start.19) | collective-permute-done | bytes 16416 | tf_op jit(solution)/shard_map/ppermute | solution.py:327
  68.6 1.5 %collective-permute-start.24 = (f32[32,128]{1,0:T(8,128)S(1)}, f32[32,128]{1,0:T(8,128)S(1)}, u32[]{:S(2)}, u32[]{:S(2)}) collective-permute-start(f32[32,128]{1,0:T(8,128)S(1)} %share_sum.2.refs_0_), channel_id=1, source_target_pairs={{0,6},{1,7},{2,4},{3,5},{4,2},{5,3},{6,0},{7,1},{8,14},{9,15},{10,... | collective-permute-start | bytes 49160 | tf_op jit(solution)/shard_map/ppermute | solution.py:327
  71.1 2.0 %collective-permute-start.22 = (f32[32,128]{1,0:T(8,128)S(1)}, f32[32,128]{1,0:T(8,128)S(1)}, u32[]{:S(2)}, u32[]{:S(2)}) collective-permute-start(f32[32,128]{1,0:T(8,128)S(1)} %share_sum.2.refs_0_), channel_id=1, source_target_pairs={{0,2},{1,3},{2,0},{3,1},{4,6},{5,7},{6,4},{7,5},{8,10},{9,11},{10,... | collective-permute-start | bytes 49160 | tf_op jit(solution)/shard_map/ppermute | solution.py:327
  73.1 1.2 %collective-permute-done.24.refs_3_ = f32[32,128]{1,0:T(8,128)S(1)} collective-permute-done((f32[32,128]{1,0:T(8,128)S(1)}, f32[32,128]{1,0:T(8,128)S(1)}, u32[]{:S(2)}, u32[]{:S(2)}) %collective-permute-start.24) | collective-permute-done | bytes 16416 | tf_op jit(solution)/shard_map/ppermute | solution.py:327
  75.0 1.5 %collective-permute-start.26 = (f32[32,128]{1,0:T(8,128)S(1)}, f32[32,128]{1,0:T(8,128)S(1)}, u32[]{:S(2)}, u32[]{:S(2)}) collective-permute-start(f32[32,128]{1,0:T(8,128)S(1)} %share_sum.3.refs_0_), channel_id=1, source_target_pairs={{0,16},{8,24},{16,0},{24,8},{1,17},{9,25},{17,1},{25,9},{2,18},{10... | collective-permute-start | bytes 49160 | tf_op jit(solution)/shard_map/ppermute | solution.py:327
  76.8 1.5 %collective-permute-done.27.refs_3_ = f32[32,128]{1,0:T(8,128)S(1)} collective-permute-done((f32[32,128]{1,0:T(8,128)S(1)}, f32[32,128]{1,0:T(8,128)S(1)}, u32[]{:S(2)}, u32[]{:S(2)}) %collective-permute-start.27) | collective-permute-done | bytes 16416 | tf_op jit(solution)/shard_map/ppermute | solution.py:327
  78.8 3.9 %polar.1 = f32[128,128]{1,0:T(8,128)} custom-call(f32[32,128]{1,0:T(8,128)S(1)} %share_sum.3.refs_0_, f32[32,128]{1,0:T(8,128)S(1)} %collective-permute-done.25.refs_1_, f32[32,128]{1,0:T(8,128)S(1)} %collective-permute-done.26.refs_2_, f32[32,128]{1,0:T(8,128)S(1)} %collective-permute-done.27.refs_3_), custom_call_target="tpu_custom_call" | custom-call | flops 134217728 | bytes 8388608 | tf_op jit(solution)/shard_map/polar/pallas_call | solution.py:22
  (39 shorter events, 12.9 us)
Async XLA Ops:
  2.3 16.8 %collective-permute-start = (f32[1024,128]{1,0:T(8,128)S(1)}, f32[1024,128]{1,0:T(8,128)S(1)}, u32[]{:S(2)}, u32[]{:S(2)}) collective-permute-start(f32[1024,128]{1,0:T(8,128)S(1)} %get-tuple-element.27), channel_id=1, source_target_pairs={{0,1},{1,0},{2,3},{3,2},{4,5},{5,4},{6,7},{7,6},{8,9},{9,8},{10,11... | collective-permute-start | bytes 1572872 | tf_op jit(solution)/shard_map/ppermute | solution.py:376
  24.1 3.1 %collective-permute-start.3 = (f32[1,2048]{1,0:T(1,128)S(1)}, f32[1,2048]{1,0:T(1,128)S(1)}, u32[]{:S(2)}, u32[]{:S(2)}) collective-permute-start(f32[1,2048]{1,0:T(1,128)S(1)} %get-tuple-element.31.refs_0_), channel_id=1, source_target_pairs={{0,24},{8,16},{16,8},{24,0},{1,25},{9,17},{17,9},{25,1},{2,26},{10... | collective-permute-start | bytes 24584 | tf_op jit(solution)/shard_map/ppermute | solution.py:327
  24.1 3.7 %collective-permute-start.2 = (f32[1,2048]{1,0:T(1,128)S(1)}, f32[1,2048]{1,0:T(1,128)S(1)}, u32[]{:S(2)}, u32[]{:S(2)}) collective-permute-start(f32[1,2048]{1,0:T(1,128)S(1)} %get-tuple-element.31.refs_0_), channel_id=1, source_target_pairs={{0,16},{8,24},{16,0},{24,8},{1,17},{9,25},{17,1},{25,9},{2,18},{10... | collective-permute-start | bytes 24584 | tf_op jit(solution)/shard_map/ppermute | solution.py:327
  25.7 2.1 %collective-permute-start.1 = (f32[1,2048]{1,0:T(1,128)S(1)}, f32[1,2048]{1,0:T(1,128)S(1)}, u32[]{:S(2)}, u32[]{:S(2)}) collective-permute-start(f32[1,2048]{1,0:T(1,128)S(1)} %get-tuple-element.31.refs_0_), channel_id=1, source_target_pairs={{0,8},{8,0},{16,24},{24,16},{1,9},{9,1},{17,25},{25,17},{2,10},{10... | collective-permute-start | bytes 24584 | tf_op jit(solution)/shard_map/ppermute | solution.py:327
  29.0 5.6 %collective-permute-start.6 = (f32[16,128]{1,0:T(8,128)S(1)}, f32[16,128]{1,0:T(8,128)S(1)}, u32[]{:S(2)}, u32[]{:S(2)}) collective-permute-start(f32[16,128]{1,0:T(8,128)S(1)} %get-tuple-element.34.refs_0_), channel_id=1, source_target_pairs={{0,6},{1,7},{2,4},{3,5},{4,2},{5,3},{6,0},{7,1},{8,14},{9,15},{10,... | collective-permute-start | bytes 24584 | tf_op jit(solution)/shard_map/ppermute | solution.py:327
  31.8 4.5 %collective-permute-start.5 = (f32[16,128]{1,0:T(8,128)S(1)}, f32[16,128]{1,0:T(8,128)S(1)}, u32[]{:S(2)}, u32[]{:S(2)}) collective-permute-start(f32[16,128]{1,0:T(8,128)S(1)} %get-tuple-element.34.refs_0_), channel_id=1, source_target_pairs={{0,4},{1,5},{2,6},{3,7},{4,0},{5,1},{6,2},{7,3},{8,12},{9,13},{10,... | collective-permute-start | bytes 24584 | tf_op jit(solution)/shard_map/ppermute | solution.py:327
  31.8 4.5 %collective-permute-start.4 = (f32[16,128]{1,0:T(8,128)S(1)}, f32[16,128]{1,0:T(8,128)S(1)}, u32[]{:S(2)}, u32[]{:S(2)}) collective-permute-start(f32[16,128]{1,0:T(8,128)S(1)} %get-tuple-element.34.refs_0_), channel_id=1, source_target_pairs={{0,2},{1,3},{2,0},{3,1},{4,6},{5,7},{6,4},{7,5},{8,10},{9,11},{10,... | collective-permute-start | bytes 24584 | tf_op jit(solution)/shard_map/ppermute | solution.py:327
  38.1 3.2 %collective-permute-start.9 = (f32[1,2048]{1,0:T(1,128)S(1)}, f32[1,2048]{1,0:T(1,128)S(1)}, u32[]{:S(2)}, u32[]{:S(2)}) collective-permute-start(f32[1,2048]{1,0:T(1,128)S(1)} %col_later.2.refs_0_), channel_id=1, source_target_pairs={{0,24},{8,16},{16,8},{24,0},{1,25},{9,17},{17,9},{25,1},{2,26},{10... | collective-permute-start | bytes 24584 | tf_op jit(solution)/shard_map/ppermute | solution.py:327
  38.2 3.7 %collective-permute-start.8 = (f32[1,2048]{1,0:T(1,128)S(1)}, f32[1,2048]{1,0:T(1,128)S(1)}, u32[]{:S(2)}, u32[]{:S(2)}) collective-permute-start(f32[1,2048]{1,0:T(1,128)S(1)} %col_later.2.refs_0_), channel_id=1, source_target_pairs={{0,16},{8,24},{16,0},{24,8},{1,17},{9,25},{17,1},{25,9},{2,18},{10... | collective-permute-start | bytes 24584 | tf_op jit(solution)/shard_map/ppermute | solution.py:327
  39.7 2.2 %collective-permute-start.7 = (f32[1,2048]{1,0:T(1,128)S(1)}, f32[1,2048]{1,0:T(1,128)S(1)}, u32[]{:S(2)}, u32[]{:S(2)}) collective-permute-start(f32[1,2048]{1,0:T(1,128)S(1)} %col_later.2.refs_0_), channel_id=1, source_target_pairs={{0,8},{8,0},{16,24},{24,16},{1,9},{9,1},{17,25},{25,17},{2,10},{10... | collective-permute-start | bytes 24584 | tf_op jit(solution)/shard_map/ppermute | solution.py:327
  43.0 5.5 %collective-permute-start.12 = (f32[16,128]{1,0:T(8,128)S(1)}, f32[16,128]{1,0:T(8,128)S(1)}, u32[]{:S(2)}, u32[]{:S(2)}) collective-permute-start(f32[16,128]{1,0:T(8,128)S(1)} %row_later.1.refs_0_), channel_id=1, source_target_pairs={{0,6},{1,7},{2,4},{3,5},{4,2},{5,3},{6,0},{7,1},{8,14},{9,15},{10,... | collective-permute-start | bytes 24584 | tf_op jit(solution)/shard_map/ppermute | solution.py:327
  44.6 4.6 %collective-permute-start.11 = (f32[16,128]{1,0:T(8,128)S(1)}, f32[16,128]{1,0:T(8,128)S(1)}, u32[]{:S(2)}, u32[]{:S(2)}) collective-permute-start(f32[16,128]{1,0:T(8,128)S(1)} %row_later.1.refs_0_), channel_id=1, source_target_pairs={{0,4},{1,5},{2,6},{3,7},{4,0},{5,1},{6,2},{7,3},{8,12},{9,13},{10,... | collective-permute-start | bytes 24584 | tf_op jit(solution)/shard_map/ppermute | solution.py:327
  45.3 3.9 %collective-permute-start.10 = (f32[16,128]{1,0:T(8,128)S(1)}, f32[16,128]{1,0:T(8,128)S(1)}, u32[]{:S(2)}, u32[]{:S(2)}) collective-permute-start(f32[16,128]{1,0:T(8,128)S(1)} %row_later.1.refs_0_), channel_id=1, source_target_pairs={{0,2},{1,3},{2,0},{3,1},{4,6},{5,7},{6,4},{7,5},{8,10},{9,11},{10,... | collective-permute-start | bytes 24584 | tf_op jit(solution)/shard_map/ppermute | solution.py:327
  50.9 3.2 %collective-permute-start.15 = (f32[1,2048]{1,0:T(1,128)S(1)}, f32[1,2048]{1,0:T(1,128)S(1)}, u32[]{:S(2)}, u32[]{:S(2)}) collective-permute-start(f32[1,2048]{1,0:T(1,128)S(1)} %col_later.3.refs_0_), channel_id=1, source_target_pairs={{0,24},{8,16},{16,8},{24,0},{1,25},{9,17},{17,9},{25,1},{2,26},{10... | collective-permute-start | bytes 24584 | tf_op jit(solution)/shard_map/ppermute | solution.py:327
  51.0 3.7 %collective-permute-start.14 = (f32[1,2048]{1,0:T(1,128)S(1)}, f32[1,2048]{1,0:T(1,128)S(1)}, u32[]{:S(2)}, u32[]{:S(2)}) collective-permute-start(f32[1,2048]{1,0:T(1,128)S(1)} %col_later.3.refs_0_), channel_id=1, source_target_pairs={{0,16},{8,24},{16,0},{24,8},{1,17},{9,25},{17,1},{25,9},{2,18},{10... | collective-permute-start | bytes 24584 | tf_op jit(solution)/shard_map/ppermute | solution.py:327
  52.5 2.2 %collective-permute-start.13 = (f32[1,2048]{1,0:T(1,128)S(1)}, f32[1,2048]{1,0:T(1,128)S(1)}, u32[]{:S(2)}, u32[]{:S(2)}) collective-permute-start(f32[1,2048]{1,0:T(1,128)S(1)} %col_later.3.refs_0_), channel_id=1, source_target_pairs={{0,8},{8,0},{16,24},{24,16},{1,9},{9,1},{17,25},{25,17},{2,10},{10... | collective-permute-start | bytes 24584 | tf_op jit(solution)/shard_map/ppermute | solution.py:327
  56.6 5.7 %collective-permute-start.18 = (f32[16,128]{1,0:T(8,128)S(1)}, f32[16,128]{1,0:T(8,128)S(1)}, u32[]{:S(2)}, u32[]{:S(2)}) collective-permute-start(f32[16,128]{1,0:T(8,128)S(1)} %get-tuple-element.38.refs_0_), channel_id=1, source_target_pairs={{0,6},{1,7},{2,4},{3,5},{4,2},{5,3},{6,0},{7,1},{8,14},{9,15},{10,... | collective-permute-start | bytes 24584 | tf_op jit(solution)/shard_map/ppermute | solution.py:327
  59.1 4.6 %collective-permute-start.17 = (f32[16,128]{1,0:T(8,128)S(1)}, f32[16,128]{1,0:T(8,128)S(1)}, u32[]{:S(2)}, u32[]{:S(2)}) collective-permute-start(f32[16,128]{1,0:T(8,128)S(1)} %get-tuple-element.38.refs_0_), channel_id=1, source_target_pairs={{0,4},{1,5},{2,6},{3,7},{4,0},{5,1},{6,2},{7,3},{8,12},{9,13},{10,... | collective-permute-start | bytes 24584 | tf_op jit(solution)/shard_map/ppermute | solution.py:327
  60.0 3.7 %collective-permute-start.16 = (f32[16,128]{1,0:T(8,128)S(1)}, f32[16,128]{1,0:T(8,128)S(1)}, u32[]{:S(2)}, u32[]{:S(2)}) collective-permute-start(f32[16,128]{1,0:T(8,128)S(1)} %get-tuple-element.38.refs_0_), channel_id=1, source_target_pairs={{0,2},{1,3},{2,0},{3,1},{4,6},{5,7},{6,4},{7,5},{8,10},{9,11},{10,... | collective-permute-start | bytes 24584 | tf_op jit(solution)/shard_map/ppermute | solution.py:327
  64.8 3.3 %collective-permute-start.19 = (f32[32,128]{1,0:T(8,128)S(1)}, f32[32,128]{1,0:T(8,128)S(1)}, u32[]{:S(2)}, u32[]{:S(2)}) collective-permute-start(f32[32,128]{1,0:T(8,128)S(1)} %get-tuple-element.41), channel_id=1, source_target_pairs={{0,24},{8,16},{16,8},{24,0},{1,25},{9,17},{17,9},{25,1},{2,26},{10... | collective-permute-start | bytes 49160 | tf_op jit(solution)/shard_map/ppermute | solution.py:327
  64.8 3.8 %collective-permute-start.20 = (f32[32,128]{1,0:T(8,128)S(1)}, f32[32,128]{1,0:T(8,128)S(1)}, u32[]{:S(2)}, u32[]{:S(2)}) collective-permute-start(f32[32,128]{1,0:T(8,128)S(1)} %get-tuple-element.42), channel_id=1, source_target_pairs={{0,16},{8,24},{16,0},{24,8},{1,17},{9,25},{17,1},{25,9},{2,18},{10... | collective-permute-start | bytes 49160 | tf_op jit(solution)/shard_map/ppermute | solution.py:327
  66.3 2.3 %collective-permute-start.21 = (f32[32,128]{1,0:T(8,128)S(1)}, f32[32,128]{1,0:T(8,128)S(1)}, u32[]{:S(2)}, u32[]{:S(2)}) collective-permute-start(f32[32,128]{1,0:T(8,128)S(1)} %get-tuple-element.43), channel_id=1, source_target_pairs={{0,8},{8,0},{16,24},{24,16},{1,9},{9,1},{17,25},{25,17},{2,10},{10... | collective-permute-start | bytes 49160 | tf_op jit(solution)/shard_map/ppermute | solution.py:327
  68.6 5.6 %collective-permute-start.24 = (f32[32,128]{1,0:T(8,128)S(1)}, f32[32,128]{1,0:T(8,128)S(1)}, u32[]{:S(2)}, u32[]{:S(2)}) collective-permute-start(f32[32,128]{1,0:T(8,128)S(1)} %share_sum.2.refs_0_), channel_id=1, source_target_pairs={{0,6},{1,7},{2,4},{3,5},{4,2},{5,3},{6,0},{7,1},{8,14},{9,15},{10,... | collective-permute-start | bytes 49160 | tf_op jit(solution)/shard_map/ppermute | solution.py:327
  70.1 4.6 %collective-permute-start.23 = (f32[32,128]{1,0:T(8,128)S(1)}, f32[32,128]{1,0:T(8,128)S(1)}, u32[]{:S(2)}, u32[]{:S(2)}) collective-permute-start(f32[32,128]{1,0:T(8,128)S(1)} %share_sum.2.refs_0_), channel_id=1, source_target_pairs={{0,4},{1,5},{2,6},{3,7},{4,0},{5,1},{6,2},{7,3},{8,12},{9,13},{10,... | collective-permute-start | bytes 49160 | tf_op jit(solution)/shard_map/ppermute | solution.py:327
  71.1 3.8 %collective-permute-start.22 = (f32[32,128]{1,0:T(8,128)S(1)}, f32[32,128]{1,0:T(8,128)S(1)}, u32[]{:S(2)}, u32[]{:S(2)}) collective-permute-start(f32[32,128]{1,0:T(8,128)S(1)} %share_sum.2.refs_0_), channel_id=1, source_target_pairs={{0,2},{1,3},{2,0},{3,1},{4,6},{5,7},{6,4},{7,5},{8,10},{9,11},{10,... | collective-permute-start | bytes 49160 | tf_op jit(solution)/shard_map/ppermute | solution.py:327
  74.9 3.4 %collective-permute-start.27 = (f32[32,128]{1,0:T(8,128)S(1)}, f32[32,128]{1,0:T(8,128)S(1)}, u32[]{:S(2)}, u32[]{:S(2)}) collective-permute-start(f32[32,128]{1,0:T(8,128)S(1)} %share_sum.3.refs_0_), channel_id=1, source_target_pairs={{0,24},{8,16},{16,8},{24,0},{1,25},{9,17},{17,9},{25,1},{2,26},{10... | collective-permute-start | bytes 49160 | tf_op jit(solution)/shard_map/ppermute | solution.py:327
  75.0 3.8 %collective-permute-start.26 = (f32[32,128]{1,0:T(8,128)S(1)}, f32[32,128]{1,0:T(8,128)S(1)}, u32[]{:S(2)}, u32[]{:S(2)}) collective-permute-start(f32[32,128]{1,0:T(8,128)S(1)} %share_sum.3.refs_0_), channel_id=1, source_target_pairs={{0,16},{8,24},{16,0},{24,8},{1,17},{9,25},{17,1},{25,9},{2,18},{10... | collective-permute-start | bytes 49160 | tf_op jit(solution)/shard_map/ppermute | solution.py:327
  76.5 2.3 %collective-permute-start.25 = (f32[32,128]{1,0:T(8,128)S(1)}, f32[32,128]{1,0:T(8,128)S(1)}, u32[]{:S(2)}, u32[]{:S(2)}) collective-permute-start(f32[32,128]{1,0:T(8,128)S(1)} %share_sum.3.refs_0_), channel_id=1, source_target_pairs={{0,8},{8,0},{16,24},{24,16},{1,9},{9,1},{17,25},{25,17},{2,10},{10... | collective-permute-start | bytes 49160 | tf_op jit(solution)/shard_map/ppermute | solution.py:327

commit v9 on v8

--- a/solution.py
+++ b/solution.py
@@ -251,18 +251,19 @@
     sums_down(block, scale[...] / tree_sum(parts), sums_out)
 
 
-def row_last(group, unit, block, scale, pot, *refs):
-    parts, (col_out, factor_out, sums_out) = received(refs, group)
+def row_last(group, block, scale, *refs):
+    parts, (totals_out, factor_out, sums_out) = received(refs, group)
     totals = tree_sum(parts)
-    pots = (EPS * math.log(2.0)) * (unit * pot[...] - jnp.log(totals) * (1.0 / math.log(2.0)))
-    half = col_out.shape[1]
-    col_out[...] = jnp.where((lax.axis_index("tgt") & 1) == 0, pots[:, :half], pots[:, half:])
+    totals_out[...] = totals
     row = scale[...] / totals
     factor_out[...] = row
     sums_down(block, row, sums_out)
 
 
-def barycentre(block, factor, target, bary_out):
+def barycentre(unit, block, factor, target, pot, totals, bary_out, col_out):
+    pots = (EPS * math.log(2.0)) * (unit * pot[...] - jnp.log(totals[...]) * (1.0 / math.log(2.0)))
+    half = col_out.shape[1]
+    col_out[...] = jnp.where((lax.axis_index("tgt") & 1) == 0, pots[:, :half], pots[:, half:])
     pieces = []
     for at in range(0, target.shape[0], LANES):
         pieces.append((target[at : at + LANES, :].T.astype(F32) * factor[:, at : at + LANES]).astype(BF16))
@@ -273,10 +274,14 @@
         )
 
 
-def cross_local(group, unit, ratio, source, bary, pot, *refs):
-    parts, (row_out, *share_outs, square) = received(refs, group)
+def row_potential(unit, ratio, pot, totals, out):
+    out[...] = (EPS * math.log(2.0)) * (unit * pot[...] + jnp.log(ratio / totals[...]) * (1.0 / math.log(2.0)))
+
+
+def cross_local(group, source, bary, *refs):
+    parts, (totals_out, *share_outs, square) = received(refs, group)
     totals = tree_sum(parts)
-    row_out[...] = (EPS * math.log(2.0)) * (unit * pot[...] + jnp.log(ratio / totals) * (1.0 / math.log(2.0)))
+    totals_out[...] = totals
     inverse = in_row(1.0 / totals)
     both = jnp.concatenate(split(bary[...] * inverse), axis=0)
     cross = jnp.dot(both, source[...], preferred_element_type=F32)
@@ -418,24 +423,25 @@
         block, col_scale, *over_src(sums)
     )
     sums = col_later_call(block, col_scale, *over_pairs(sums))
-    col_out, factor, sums = call(
-        functools.partial(row_last, n_src, unit),
-        "row_last",
-        (jax.ShapeDtypeStruct((1, cols), F32), pair_vec, row_vec),
+    col_totals, factor, sums = call(
+        functools.partial(row_last, n_src), "row_last", (pair_vec, pair_vec, row_vec), flops=4 * mac
+    )(block, col_scale, *over_src(sums))
+    bary, col_out = call(
+        functools.partial(barycentre, unit),
+        "barycentre",
+        (jax.ShapeDtypeStruct((width, rows), F32), jax.ShapeDtypeStruct((1, cols), F32)),
         flops=4 * mac,
-    )(block, col_scale, col_pot, *over_src(sums))
-    bary = call(barycentre, "barycentre", jax.ShapeDtypeStruct((width, rows), F32), flops=4 * mac)(
-        block, factor, targets
-    )
+    )(block, factor, targets, col_pot, col_totals)
     square = jax.ShapeDtypeStruct((width, width), F32)
     share_shape = jax.ShapeDtypeStruct((width // n_src, width), F32)
-    row_out, *shares = call(
-        functools.partial(cross_local, n_pairs, unit, ratio),
+    row_totals, *shares = call(
+        functools.partial(cross_local, n_pairs),
         "cross_local",
         (row_vec,) + (share_shape,) * n_src,
         scratch=[pltpu.VMEM((width, width), F32)],
         flops=2 * rows * width * width,
-    )(source, bary, row_pot, *over_pairs(sums))
+    )(source, bary, *over_pairs(sums))
+    row_out = call(functools.partial(row_potential, unit, ratio), "row_potential", row_vec, flops=mac)(row_pot, row_totals)
     share = call(share_sum, "share_sum", share_shape)(*partners(shares[::-1], "src", range(n_src - 1, -1, -1)))
     share = call(share_sum, "share_sum", share_shape)(*over_pairs(share))
     new_map = call(polar, "polar", square, scratch=[pltpu.VMEM((width, width), F32)], flops=1 << 27)(*over_src(share))

time: 82.8 us -> 81.9 us (0.989)
  waiting for transfers between devices: 17.4 us -> 16.4 us
    ppermute x27, waiting for transfers between devices: 17.4 us -> 16.4 us  [partners(): lax.ppermute(values[k], axis, [(me, me ^ k) for me in range(size)])]
    pallas_call x13 -> x14, Pallas kernels: 22.6 us -> 22.6 us  [call(): pl.pallas_call(body, name=name, out_shape=out_shape, in_specs=[pl.BlockSp...]
  transfers between devices with their start and end apart: 28 -> 28, of which waited for: 20 -> 20; matrix products, arithmetic and copies ran while one was open for 0% -> 0% of each run, Pallas kernels for 4% -> 6%
where the time goes in v9:
time: 81.9 us; the launch traced here: 81.7 us
  starting transfers between devices  30.4 us (37%)
  Pallas kernels  22.6 us (28%)
  waiting for transfers between devices  16.4 us (20%)
  blocking collectives  11.6 us (14%)
    ppermute x27, starting transfers between devices, partners(): lax.ppermute(values[k], axis, [(me, me ^ k) for me in range(size)])  27.4 us
    pallas_call x14, Pallas kernels, call(): pl.pallas_call(body, name=name, out_shape=out_shape, in_specs=[pl.BlockSp...  22.6 us
    ppermute x27, waiting for transfers between devices, partners(): lax.ppermute(values[k], axis, [(me, me ^ k) for me in range(size)])  16.4 us
    all_to_all x1, blocking collectives, over_tgt(): lax.all_to_all(jnp.broadcast_to(x, (lax.axis_size('tgt'),) + x.shape), 't...  11.6 us
    ppermute x1, starting transfers between devices, shards(): other = lax.ppermute(plain, 'tgt', [(me, me ^ 1) for me in range(n_tgt)])  3 us
  transfers between devices with their start and end apart: 28, of which 20 were waited for; matrix products, arithmetic and copies ran while one was open for 0% of the time, Pallas kernels for 6%

profile of v9, /device:TPU:0, one launch (start us, length us, event | category | flops | bytes accessed | tf_op | source)
XLA Modules:
  0.0 81.7 jit_solution(512188631381945794)
XLA Ops:
  0.6 1.7 %prepare.1 = (bf16[2048,128]{1,0:T(8,128)(2,1)S(1)}, bf16[2048,128]{1,0:T(8,128)(2,1)S(1)}, bf16[128,2048]{1,0:T(8,128)(2,1)S(1)}, bf16[1024,256]{1,0:T(8,128)(2,1)S(1)}, f32[1024,128]{1,0:T(8,128)S(1)}) custom-call(bf16[2048,128]{1,0:T(8,128)(2,1)} %source_hbm.1, f32[128,128]{1,0:T(8,128)} %map_hbm.1, bf16[1024,128]{1,0:T(8,128)(2,1)} %target_hbm.1, ...), custom_call_target="tpu_custom_call" | custom-call | flops 67108864 | bytes 8388608 | tf_op jit(solution)/shard_map/prepare/pallas_call | solution.py:22
  2.3 3.0 %collective-permute-start = (f32[1024,128]{1,0:T(8,128)S(1)}, f32[1024,128]{1,0:T(8,128)S(1)}, u32[]{:S(2)}, u32[]{:S(2)}) collective-permute-start(f32[1024,128]{1,0:T(8,128)S(1)} %get-tuple-element.28), channel_id=1, source_target_pairs={{0,1},{1,0},{2,3},{3,2},{4,5},{5,4},{6,7},{7,6},{8,9},{9,8},{10,11... | collective-permute-start | bytes 1572872 | tf_op jit(solution)/shard_map/ppermute | solution.py:381
  5.3 2.2 %row_first.1 = f32[16,128]{1,0:T(8,128)S(1)} custom-call(bf16[2048,128]{1,0:T(8,128)(2,1)S(1)} %get-tuple-element.29.left_in, bf16[1024,256]{1,0:T(8,128)(2,1)S(1)} %get-tuple-element.27.right.own), custom_call_target="tpu_custom_call" | custom-call | flops 1073741824 | bytes 8388608 | tf_op jit(solution)/shard_map/row_first/pallas_call | solution.py:22
  7.5 11.6 %all_to_all.5.refs_0_ = f32[8,16,128]{2,1,0:T(8,128)S(1)} all-to-all(f32[8,16,128]{2,1,0:T(8,128)S(1)} %broadcast_in_dim.3), channel_id=1, replica_groups=mesh['src'=4,'tgt'=8] {'tgt'}, dimensions={0} | all-to-all | bytes 131072 | tf_op jit(solution)/shard_map/all_to_all | solution.py:346
  19.1 5.0 %col_first.1 = (bf16[2048,2048]{1,0:T(8,128)(2,1)S(1)}, bf16[2048,128]{1,0:T(8,128)(2,1)S(1)}, f32[16,128]{1,0:T(8,128)S(1)}, f32[1,2048]{1,0:T(1,128)S(1)}, f32[1,2048]{1,0:T(1,128)S(1)}) custom-call(bf16[128,2048]{1,0:T(8,128)(2,1)S(1)} %get-tuple-element.26.turned, bf16[1024,256]{1,0:T(8,128)(2,1)S(1)} %get-tuple-element.27.right.own, ...), custom_call_target="tpu_custom_call" | custom-call | flops 2147483648 | bytes 8388608 | tf_op jit(solution)/shard_map/col_first/pallas_call | solution.py:22
  24.1 1.6 %collective-permute-start.2 = (f32[1,2048]{1,0:T(1,128)S(1)}, f32[1,2048]{1,0:T(1,128)S(1)}, u32[]{:S(2)}, u32[]{:S(2)}) collective-permute-start(f32[1,2048]{1,0:T(1,128)S(1)} %get-tuple-element.34.refs_0_), channel_id=1, source_target_pairs={{0,16},{8,24},{16,0},{24,8},{1,17},{9,25},{17,1},{25,9},{2,18},{10... | collective-permute-start | bytes 24584 | tf_op jit(solution)/shard_map/ppermute | solution.py:332
  26.0 1.2 %collective-permute-done.3.refs_3_ = f32[1,2048]{1,0:T(1,128)S(1)} collective-permute-done((f32[1,2048]{1,0:T(1,128)S(1)}, f32[1,2048]{1,0:T(1,128)S(1)}, u32[]{:S(2)}, u32[]{:S(2)}) %collective-permute-start.3) | collective-permute-done | bytes 8224 | tf_op jit(solution)/shard_map/ppermute | solution.py:332
  27.9 1.1 %row_second.1 = (f32[1,2048]{1,0:T(1,128)S(1)}, f32[1,2048]{1,0:T(1,128)S(1)}, f32[16,128]{1,0:T(8,128)S(1)}) custom-call(bf16[2048,2048]{1,0:T(8,128)(2,1)S(1)} %get-tuple-element.32.block, f32[1,2048]{1,0:T(1,128)S(1)} %get-tuple-element.33.peak, f32[1,2048]{1,0:T(1,128)S(1)} %get-tuple-element.34.refs_0_, f32[1,2048]{1,0:T(1,128)S(1)} %collective-permute-done.1.refs_1_, ...), custom_call_target="tpu_custom_call" | custom-call | flops 1073741824 | bytes 8388608 | tf_op jit(solution)/shard_map/row_second/pallas_call | solution.py:22
  29.0 2.8 %collective-permute-start.6 = (f32[16,128]{1,0:T(8,128)S(1)}, f32[16,128]{1,0:T(8,128)S(1)}, u32[]{:S(2)}, u32[]{:S(2)}) collective-permute-start(f32[16,128]{1,0:T(8,128)S(1)} %get-tuple-element.36.refs_0_), channel_id=1, source_target_pairs={{0,6},{1,7},{2,4},{3,5},{4,2},{5,3},{6,0},{7,1},{8,14},{9,15},{10,... | collective-permute-start | bytes 24584 | tf_op jit(solution)/shard_map/ppermute | solution.py:332
  31.8 1.7 %collective-permute-start.4 = (f32[16,128]{1,0:T(8,128)S(1)}, f32[16,128]{1,0:T(8,128)S(1)}, u32[]{:S(2)}, u32[]{:S(2)}) collective-permute-start(f32[16,128]{1,0:T(8,128)S(1)} %get-tuple-element.36.refs_0_), channel_id=1, source_target_pairs={{0,2},{1,3},{2,0},{3,1},{4,6},{5,7},{6,4},{7,5},{8,10},{9,11},{10,... | collective-permute-start | bytes 24584 | tf_op jit(solution)/shard_map/ppermute | solution.py:332
  33.4 1.1 %collective-permute-done.6.refs_3_ = f32[16,128]{1,0:T(8,128)S(1)} collective-permute-done((f32[16,128]{1,0:T(8,128)S(1)}, f32[16,128]{1,0:T(8,128)S(1)}, u32[]{:S(2)}, u32[]{:S(2)}) %collective-permute-start.6) | collective-permute-done | bytes 8224 | tf_op jit(solution)/shard_map/ppermute | solution.py:332
  34.6 1.7 %collective-permute-done.5.refs_2_ = f32[16,128]{1,0:T(8,128)S(1)} collective-permute-done((f32[16,128]{1,0:T(8,128)S(1)}, f32[16,128]{1,0:T(8,128)S(1)}, u32[]{:S(2)}, u32[]{:S(2)}) %collective-permute-start.5) | collective-permute-done | bytes 8224 | tf_op jit(solution)/shard_map/ppermute | solution.py:332
  36.3 1.7 %col_later.2.refs_0_ = f32[1,2048]{1,0:T(1,128)S(1)} custom-call(bf16[2048,2048]{1,0:T(8,128)(2,1)S(1)} %get-tuple-element.32.block, f32[1,2048]{1,0:T(1,128)S(1)} %get-tuple-element.35.scale, f32[16,128]{1,0:T(8,128)S(1)} %get-tuple-element.36.refs_0_, f32[16,128]{1,0:T(8,128)S(1)} %collective-permute-done.4.refs_1_, ...), custom_call_target="tpu_custom_call" | custom-call | flops 1073741824 | bytes 8388608 | tf_op jit(solution)/shard_map/col_later/pallas_call | solution.py:22
  38.1 1.6 %collective-permute-start.8 = (f32[1,2048]{1,0:T(1,128)S(1)}, f32[1,2048]{1,0:T(1,128)S(1)}, u32[]{:S(2)}, u32[]{:S(2)}) collective-permute-start(f32[1,2048]{1,0:T(1,128)S(1)} %col_later.2.refs_0_), channel_id=1, source_target_pairs={{0,16},{8,24},{16,0},{24,8},{1,17},{9,25},{17,1},{25,9},{2,18},{10... | collective-permute-start | bytes 24584 | tf_op jit(solution)/shard_map/ppermute | solution.py:332
  40.0 1.2 %collective-permute-done.9.refs_3_ = f32[1,2048]{1,0:T(1,128)S(1)} collective-permute-done((f32[1,2048]{1,0:T(1,128)S(1)}, f32[1,2048]{1,0:T(1,128)S(1)}, u32[]{:S(2)}, u32[]{:S(2)}) %collective-permute-start.9) | collective-permute-done | bytes 8224 | tf_op jit(solution)/shard_map/ppermute | solution.py:332
  41.9 1.1 %row_later.1.refs_0_ = f32[16,128]{1,0:T(8,128)S(1)} custom-call(bf16[2048,2048]{1,0:T(8,128)(2,1)S(1)} %get-tuple-element.32.block, f32[1,2048]{1,0:T(1,128)S(1)} %get-tuple-element.35.scale, f32[1,2048]{1,0:T(1,128)S(1)} %col_later.2.refs_0_, f32[1,2048]{1,0:T(1,128)S(1)} %collective-permute-done.7.refs_1_, f32[1,2048]{1,0:T(1,128)S(1)} %collective-permute-done.8.refs_2_, ...), custom_call_target="tpu_custom_call" | custom-call | flops 1073741824 | bytes 8388608 | tf_op jit(solution)/shard_map/row_later/pallas_call | solution.py:22
  43.0 1.5 %collective-permute-start.12 = (f32[16,128]{1,0:T(8,128)S(1)}, f32[16,128]{1,0:T(8,128)S(1)}, u32[]{:S(2)}, u32[]{:S(2)}) collective-permute-start(f32[16,128]{1,0:T(8,128)S(1)} %row_later.1.refs_0_), channel_id=1, source_target_pairs={{0,6},{1,7},{2,4},{3,5},{4,2},{5,3},{6,0},{7,1},{8,14},{9,15},{10,... | collective-permute-start | bytes 24584 | tf_op jit(solution)/shard_map/ppermute | solution.py:332
  45.3 2.2 %collective-permute-start.10 = (f32[16,128]{1,0:T(8,128)S(1)}, f32[16,128]{1,0:T(8,128)S(1)}, u32[]{:S(2)}, u32[]{:S(2)}) collective-permute-start(f32[16,128]{1,0:T(8,128)S(1)} %row_later.1.refs_0_), channel_id=1, source_target_pairs={{0,2},{1,3},{2,0},{3,1},{4,6},{5,7},{6,4},{7,5},{8,10},{9,11},{10,... | collective-permute-start | bytes 24584 | tf_op jit(solution)/shard_map/ppermute | solution.py:332
  47.4 1.1 %collective-permute-done.12.refs_3_ = f32[16,128]{1,0:T(8,128)S(1)} collective-permute-done((f32[16,128]{1,0:T(8,128)S(1)}, f32[16,128]{1,0:T(8,128)S(1)}, u32[]{:S(2)}, u32[]{:S(2)}) %collective-permute-start.12) | collective-permute-done | bytes 8224 | tf_op jit(solution)/shard_map/ppermute | solution.py:332
  49.1 1.7 %col_later.3.refs_0_ = f32[1,2048]{1,0:T(1,128)S(1)} custom-call(bf16[2048,2048]{1,0:T(8,128)(2,1)S(1)} %get-tuple-element.32.block, f32[1,2048]{1,0:T(1,128)S(1)} %get-tuple-element.35.scale, f32[16,128]{1,0:T(8,128)S(1)} %row_later.1.refs_0_, f32[16,128]{1,0:T(8,128)S(1)} %collective-permute-done.10.refs_1_, ...), custom_call_target="tpu_custom_call" | custom-call | flops 1073741824 | bytes 8388608 | tf_op jit(solution)/shard_map/col_later/pallas_call | solution.py:22
  50.9 1.6 %collective-permute-start.14 = (f32[1,2048]{1,0:T(1,128)S(1)}, f32[1,2048]{1,0:T(1,128)S(1)}, u32[]{:S(2)}, u32[]{:S(2)}) collective-permute-start(f32[1,2048]{1,0:T(1,128)S(1)} %col_later.3.refs_0_), channel_id=1, source_target_pairs={{0,16},{8,24},{16,0},{24,8},{1,17},{9,25},{17,1},{25,9},{2,18},{10... | collective-permute-start | bytes 24584 | tf_op jit(solution)/shard_map/ppermute | solution.py:332
  52.8 1.2 %collective-permute-done.15.refs_3_ = f32[1,2048]{1,0:T(1,128)S(1)} collective-permute-done((f32[1,2048]{1,0:T(1,128)S(1)}, f32[1,2048]{1,0:T(1,128)S(1)}, u32[]{:S(2)}, u32[]{:S(2)}) %collective-permute-start.15) | collective-permute-done | bytes 8224 | tf_op jit(solution)/shard_map/ppermute | solution.py:332
  54.7 1.3 %row_last.1 = (f32[1,2048]{1,0:T(1,128)S(1)}, f32[1,2048]{1,0:T(1,128)S(1)}, f32[16,128]{1,0:T(8,128)S(1)}) custom-call(bf16[2048,2048]{1,0:T(8,128)(2,1)S(1)} %get-tuple-element.32.block, f32[1,2048]{1,0:T(1,128)S(1)} %get-tuple-element.35.scale, f32[1,2048]{1,0:T(1,128)S(1)} %col_later.3.refs_0_, f32[1,2048]{1,0:T(1,128)S(1)} %collective-permute-done.13.refs_1_, ...), custom_call_target="tpu_custom_call" | custom-call | flops 1073741824 | bytes 8388608 | tf_op jit(solution)/shard_map/row_last/pallas_call | solution.py:22
  56.0 2.6 %collective-permute-start.18 = (f32[16,128]{1,0:T(8,128)S(1)}, f32[16,128]{1,0:T(8,128)S(1)}, u32[]{:S(2)}, u32[]{:S(2)}) collective-permute-start(f32[16,128]{1,0:T(8,128)S(1)} %get-tuple-element.42.refs_0_), channel_id=1, source_target_pairs={{0,6},{1,7},{2,4},{3,5},{4,2},{5,3},{6,0},{7,1},{8,14},{9,15},{10,... | collective-permute-start | bytes 24584 | tf_op jit(solution)/shard_map/ppermute | solution.py:332
  60.4 1.8 %barycentre.1 = (f32[128,2048]{1,0:T(8,128)S(1)}, f32[1,1024]{1,0:T(1,128)}) custom-call(bf16[2048,2048]{1,0:T(8,128)(2,1)S(1)} %get-tuple-element.32.block, f32[1,2048]{1,0:T(1,128)S(1)} %get-tuple-element.37.factor, bf16[2048,128]{1,0:T(8,128)(2,1)S(1)} %get-tuple-element.38.target, f32[1,2048]{1,0:T(1,128)S(1)} %get-tuple-element.39.pot, ...), custom_call_target="tpu_custom_call" | custom-call | flops 1073741824 | bytes 8388608 | tf_op jit(solution)/shard_map/barycentre/pallas_call | solution.py:22
  63.8 1.6 %collective-permute-start.20 = (f32[32,128]{1,0:T(8,128)S(1)}, f32[32,128]{1,0:T(8,128)S(1)}, u32[]{:S(2)}, u32[]{:S(2)}) collective-permute-start(f32[32,128]{1,0:T(8,128)S(1)} %get-tuple-element.46), channel_id=1, source_target_pairs={{0,16},{8,24},{16,0},{24,8},{1,17},{9,25},{17,1},{25,9},{2,18},{10... | collective-permute-start | bytes 49160 | tf_op jit(solution)/shard_map/ppermute | solution.py:332
  65.6 1.4 %collective-permute-done.19.refs_0_ = f32[32,128]{1,0:T(8,128)S(1)} collective-permute-done((f32[32,128]{1,0:T(8,128)S(1)}, f32[32,128]{1,0:T(8,128)S(1)}, u32[]{:S(2)}, u32[]{:S(2)}) %collective-permute-start.19) | collective-permute-done | bytes 16416 | tf_op jit(solution)/shard_map/ppermute | solution.py:332
  67.6 1.6 %collective-permute-start.24 = (f32[32,128]{1,0:T(8,128)S(1)}, f32[32,128]{1,0:T(8,128)S(1)}, u32[]{:S(2)}, u32[]{:S(2)}) collective-permute-start(f32[32,128]{1,0:T(8,128)S(1)} %share_sum.2.refs_0_), channel_id=1, source_target_pairs={{0,6},{1,7},{2,4},{3,5},{4,2},{5,3},{6,0},{7,1},{8,14},{9,15},{10,... | collective-permute-start | bytes 49160 | tf_op jit(solution)/shard_map/ppermute | solution.py:332
  70.0 2.0 %collective-permute-start.22 = (f32[32,128]{1,0:T(8,128)S(1)}, f32[32,128]{1,0:T(8,128)S(1)}, u32[]{:S(2)}, u32[]{:S(2)}) collective-permute-start(f32[32,128]{1,0:T(8,128)S(1)} %share_sum.2.refs_0_), channel_id=1, source_target_pairs={{0,2},{1,3},{2,0},{3,1},{4,6},{5,7},{6,4},{7,5},{8,10},{9,11},{10,... | collective-permute-start | bytes 49160 | tf_op jit(solution)/shard_map/ppermute | solution.py:332
  72.1 1.2 %collective-permute-done.24.refs_3_ = f32[32,128]{1,0:T(8,128)S(1)} collective-permute-done((f32[32,128]{1,0:T(8,128)S(1)}, f32[32,128]{1,0:T(8,128)S(1)}, u32[]{:S(2)}, u32[]{:S(2)}) %collective-permute-start.24) | collective-permute-done | bytes 16416 | tf_op jit(solution)/shard_map/ppermute | solution.py:332
  74.0 1.6 %collective-permute-start.26 = (f32[32,128]{1,0:T(8,128)S(1)}, f32[32,128]{1,0:T(8,128)S(1)}, u32[]{:S(2)}, u32[]{:S(2)}) collective-permute-start(f32[32,128]{1,0:T(8,128)S(1)} %share_sum.3.refs_0_), channel_id=1, source_target_pairs={{0,16},{8,24},{16,0},{24,8},{1,17},{9,25},{17,1},{25,9},{2,18},{10... | collective-permute-start | bytes 49160 | tf_op jit(solution)/shard_map/ppermute | solution.py:332
  77.8 3.8 %polar.1 = f32[128,128]{1,0:T(8,128)} custom-call(f32[32,128]{1,0:T(8,128)S(1)} %share_sum.3.refs_0_, f32[32,128]{1,0:T(8,128)S(1)} %collective-permute-done.25.refs_1_, f32[32,128]{1,0:T(8,128)S(1)} %collective-permute-done.26.refs_2_, f32[32,128]{1,0:T(8,128)S(1)} %collective-permute-done.27.refs_3_), custom_call_target="tpu_custom_call" | custom-call | flops 134217728 | bytes 8388608 | tf_op jit(solution)/shard_map/polar/pallas_call | solution.py:22
  (40 shorter events, 12.4 us)
Async XLA Ops:
  2.3 16.8 %collective-permute-start = (f32[1024,128]{1,0:T(8,128)S(1)}, f32[1024,128]{1,0:T(8,128)S(1)}, u32[]{:S(2)}, u32[]{:S(2)}) collective-permute-start(f32[1024,128]{1,0:T(8,128)S(1)} %get-tuple-element.28), channel_id=1, source_target_pairs={{0,1},{1,0},{2,3},{3,2},{4,5},{5,4},{6,7},{7,6},{8,9},{9,8},{10,11... | collective-permute-start | bytes 1572872 | tf_op jit(solution)/shard_map/ppermute | solution.py:381
  24.1 3.1 %collective-permute-start.3 = (f32[1,2048]{1,0:T(1,128)S(1)}, f32[1,2048]{1,0:T(1,128)S(1)}, u32[]{:S(2)}, u32[]{:S(2)}) collective-permute-start(f32[1,2048]{1,0:T(1,128)S(1)} %get-tuple-element.34.refs_0_), channel_id=1, source_target_pairs={{0,24},{8,16},{16,8},{24,0},{1,25},{9,17},{17,9},{25,1},{2,26},{10... | collective-permute-start | bytes 24584 | tf_op jit(solution)/shard_map/ppermute | solution.py:332
  24.1 3.7 %collective-permute-start.2 = (f32[1,2048]{1,0:T(1,128)S(1)}, f32[1,2048]{1,0:T(1,128)S(1)}, u32[]{:S(2)}, u32[]{:S(2)}) collective-permute-start(f32[1,2048]{1,0:T(1,128)S(1)} %get-tuple-element.34.refs_0_), channel_id=1, source_target_pairs={{0,16},{8,24},{16,0},{24,8},{1,17},{9,25},{17,1},{25,9},{2,18},{10... | collective-permute-start | bytes 24584 | tf_op jit(solution)/shard_map/ppermute | solution.py:332
  25.7 2.1 %collective-permute-start.1 = (f32[1,2048]{1,0:T(1,128)S(1)}, f32[1,2048]{1,0:T(1,128)S(1)}, u32[]{:S(2)}, u32[]{:S(2)}) collective-permute-start(f32[1,2048]{1,0:T(1,128)S(1)} %get-tuple-element.34.refs_0_), channel_id=1, source_target_pairs={{0,8},{8,0},{16,24},{24,16},{1,9},{9,1},{17,25},{25,17},{2,10},{10... | collective-permute-start | bytes 24584 | tf_op jit(solution)/shard_map/ppermute | solution.py:332
  29.0 5.6 %collective-permute-start.6 = (f32[16,128]{1,0:T(8,128)S(1)}, f32[16,128]{1,0:T(8,128)S(1)}, u32[]{:S(2)}, u32[]{:S(2)}) collective-permute-start(f32[16,128]{1,0:T(8,128)S(1)} %get-tuple-element.36.refs_0_), channel_id=1, source_target_pairs={{0,6},{1,7},{2,4},{3,5},{4,2},{5,3},{6,0},{7,1},{8,14},{9,15},{10,... | collective-permute-start | bytes 24584 | tf_op jit(solution)/shard_map/ppermute | solution.py:332
  31.8 4.5 %collective-permute-start.5 = (f32[16,128]{1,0:T(8,128)S(1)}, f32[16,128]{1,0:T(8,128)S(1)}, u32[]{:S(2)}, u32[]{:S(2)}) collective-permute-start(f32[16,128]{1,0:T(8,128)S(1)} %get-tuple-element.36.refs_0_), channel_id=1, source_target_pairs={{0,4},{1,5},{2,6},{3,7},{4,0},{5,1},{6,2},{7,3},{8,12},{9,13},{10,... | collective-permute-start | bytes 24584 | tf_op jit(solution)/shard_map/ppermute | solution.py:332
  31.8 4.5 %collective-permute-start.4 = (f32[16,128]{1,0:T(8,128)S(1)}, f32[16,128]{1,0:T(8,128)S(1)}, u32[]{:S(2)}, u32[]{:S(2)}) collective-permute-start(f32[16,128]{1,0:T(8,128)S(1)} %get-tuple-element.36.refs_0_), channel_id=1, source_target_pairs={{0,2},{1,3},{2,0},{3,1},{4,6},{5,7},{6,4},{7,5},{8,10},{9,11},{10,... | collective-permute-start | bytes 24584 | tf_op jit(solution)/shard_map/ppermute | solution.py:332
  38.1 3.2 %collective-permute-start.9 = (f32[1,2048]{1,0:T(1,128)S(1)}, f32[1,2048]{1,0:T(1,128)S(1)}, u32[]{:S(2)}, u32[]{:S(2)}) collective-permute-start(f32[1,2048]{1,0:T(1,128)S(1)} %col_later.2.refs_0_), channel_id=1, source_target_pairs={{0,24},{8,16},{16,8},{24,0},{1,25},{9,17},{17,9},{25,1},{2,26},{10... | collective-permute-start | bytes 24584 | tf_op jit(solution)/shard_map/ppermute | solution.py:332
  38.1 3.7 %collective-permute-start.8 = (f32[1,2048]{1,0:T(1,128)S(1)}, f32[1,2048]{1,0:T(1,128)S(1)}, u32[]{:S(2)}, u32[]{:S(2)}) collective-permute-start(f32[1,2048]{1,0:T(1,128)S(1)} %col_later.2.refs_0_), channel_id=1, source_target_pairs={{0,16},{8,24},{16,0},{24,8},{1,17},{9,25},{17,1},{25,9},{2,18},{10... | collective-permute-start | bytes 24584 | tf_op jit(solution)/shard_map/ppermute | solution.py:332
  39.7 2.1 %collective-permute-start.7 = (f32[1,2048]{1,0:T(1,128)S(1)}, f32[1,2048]{1,0:T(1,128)S(1)}, u32[]{:S(2)}, u32[]{:S(2)}) collective-permute-start(f32[1,2048]{1,0:T(1,128)S(1)} %col_later.2.refs_0_), channel_id=1, source_target_pairs={{0,8},{8,0},{16,24},{24,16},{1,9},{9,1},{17,25},{25,17},{2,10},{10... | collective-permute-start | bytes 24584 | tf_op jit(solution)/shard_map/ppermute | solution.py:332
  43.0 5.5 %collective-permute-start.12 = (f32[16,128]{1,0:T(8,128)S(1)}, f32[16,128]{1,0:T(8,128)S(1)}, u32[]{:S(2)}, u32[]{:S(2)}) collective-permute-start(f32[16,128]{1,0:T(8,128)S(1)} %row_later.1.refs_0_), channel_id=1, source_target_pairs={{0,6},{1,7},{2,4},{3,5},{4,2},{5,3},{6,0},{7,1},{8,14},{9,15},{10,... | collective-permute-start | bytes 24584 | tf_op jit(solution)/shard_map/ppermute | solution.py:332
  44.5 4.6 %collective-permute-start.11 = (f32[16,128]{1,0:T(8,128)S(1)}, f32[16,128]{1,0:T(8,128)S(1)}, u32[]{:S(2)}, u32[]{:S(2)}) collective-permute-start(f32[16,128]{1,0:T(8,128)S(1)} %row_later.1.refs_0_), channel_id=1, source_target_pairs={{0,4},{1,5},{2,6},{3,7},{4,0},{5,1},{6,2},{7,3},{8,12},{9,13},{10,... | collective-permute-start | bytes 24584 | tf_op jit(solution)/shard_map/ppermute | solution.py:332
  45.3 3.9 %collective-permute-start.10 = (f32[16,128]{1,0:T(8,128)S(1)}, f32[16,128]{1,0:T(8,128)S(1)}, u32[]{:S(2)}, u32[]{:S(2)}) collective-permute-start(f32[16,128]{1,0:T(8,128)S(1)} %row_later.1.refs_0_), channel_id=1, source_target_pairs={{0,2},{1,3},{2,0},{3,1},{4,6},{5,7},{6,4},{7,5},{8,10},{9,11},{10,... | collective-permute-start | bytes 24584 | tf_op jit(solution)/shard_map/ppermute | solution.py:332
  50.9 3.2 %collective-permute-start.15 = (f32[1,2048]{1,0:T(1,128)S(1)}, f32[1,2048]{1,0:T(1,128)S(1)}, u32[]{:S(2)}, u32[]{:S(2)}) collective-permute-start(f32[1,2048]{1,0:T(1,128)S(1)} %col_later.3.refs_0_), channel_id=1, source_target_pairs={{0,24},{8,16},{16,8},{24,0},{1,25},{9,17},{17,9},{25,1},{2,26},{10... | collective-permute-start | bytes 24584 | tf_op jit(solution)/shard_map/ppermute | solution.py:332
  50.9 3.7 %collective-permute-start.14 = (f32[1,2048]{1,0:T(1,128)S(1)}, f32[1,2048]{1,0:T(1,128)S(1)}, u32[]{:S(2)}, u32[]{:S(2)}) collective-permute-start(f32[1,2048]{1,0:T(1,128)S(1)} %col_later.3.refs_0_), channel_id=1, source_target_pairs={{0,16},{8,24},{16,0},{24,8},{1,17},{9,25},{17,1},{25,9},{2,18},{10... | collective-permute-start | bytes 24584 | tf_op jit(solution)/shard_map/ppermute | solution.py:332
  52.5 2.1 %collective-permute-start.13 = (f32[1,2048]{1,0:T(1,128)S(1)}, f32[1,2048]{1,0:T(1,128)S(1)}, u32[]{:S(2)}, u32[]{:S(2)}) collective-permute-start(f32[1,2048]{1,0:T(1,128)S(1)} %col_later.3.refs_0_), channel_id=1, source_target_pairs={{0,8},{8,0},{16,24},{24,16},{1,9},{9,1},{17,25},{25,17},{2,10},{10... | collective-permute-start | bytes 24584 | tf_op jit(solution)/shard_map/ppermute | solution.py:332
  56.0 6.2 %collective-permute-start.18 = (f32[16,128]{1,0:T(8,128)S(1)}, f32[16,128]{1,0:T(8,128)S(1)}, u32[]{:S(2)}, u32[]{:S(2)}) collective-permute-start(f32[16,128]{1,0:T(8,128)S(1)} %get-tuple-element.42.refs_0_), channel_id=1, source_target_pairs={{0,6},{1,7},{2,4},{3,5},{4,2},{5,3},{6,0},{7,1},{8,14},{9,15},{10,... | collective-permute-start | bytes 24584 | tf_op jit(solution)/shard_map/ppermute | solution.py:332
  58.6 4.6 %collective-permute-start.17 = (f32[16,128]{1,0:T(8,128)S(1)}, f32[16,128]{1,0:T(8,128)S(1)}, u32[]{:S(2)}, u32[]{:S(2)}) collective-permute-start(f32[16,128]{1,0:T(8,128)S(1)} %get-tuple-element.42.refs_0_), channel_id=1, source_target_pairs={{0,4},{1,5},{2,6},{3,7},{4,0},{5,1},{6,2},{7,3},{8,12},{9,13},{10,... | collective-permute-start | bytes 24584 | tf_op jit(solution)/shard_map/ppermute | solution.py:332
  59.5 3.7 %collective-permute-start.16 = (f32[16,128]{1,0:T(8,128)S(1)}, f32[16,128]{1,0:T(8,128)S(1)}, u32[]{:S(2)}, u32[]{:S(2)}) collective-permute-start(f32[16,128]{1,0:T(8,128)S(1)} %get-tuple-element.42.refs_0_), channel_id=1, source_target_pairs={{0,2},{1,3},{2,0},{3,1},{4,6},{5,7},{6,4},{7,5},{8,10},{9,11},{10,... | collective-permute-start | bytes 24584 | tf_op jit(solution)/shard_map/ppermute | solution.py:332
  63.7 3.3 %collective-permute-start.19 = (f32[32,128]{1,0:T(8,128)S(1)}, f32[32,128]{1,0:T(8,128)S(1)}, u32[]{:S(2)}, u32[]{:S(2)}) collective-permute-start(f32[32,128]{1,0:T(8,128)S(1)} %get-tuple-element.45), channel_id=1, source_target_pairs={{0,24},{8,16},{16,8},{24,0},{1,25},{9,17},{17,9},{25,1},{2,26},{10... | collective-permute-start | bytes 49160 | tf_op jit(solution)/shard_map/ppermute | solution.py:332
  63.8 3.8 %collective-permute-start.20 = (f32[32,128]{1,0:T(8,128)S(1)}, f32[32,128]{1,0:T(8,128)S(1)}, u32[]{:S(2)}, u32[]{:S(2)}) collective-permute-start(f32[32,128]{1,0:T(8,128)S(1)} %get-tuple-element.46), channel_id=1, source_target_pairs={{0,16},{8,24},{16,0},{24,8},{1,17},{9,25},{17,1},{25,9},{2,18},{10... | collective-permute-start | bytes 49160 | tf_op jit(solution)/shard_map/ppermute | solution.py:332
  65.4 2.2 %collective-permute-start.21 = (f32[32,128]{1,0:T(8,128)S(1)}, f32[32,128]{1,0:T(8,128)S(1)}, u32[]{:S(2)}, u32[]{:S(2)}) collective-permute-start(f32[32,128]{1,0:T(8,128)S(1)} %get-tuple-element.47), channel_id=1, source_target_pairs={{0,8},{8,0},{16,24},{24,16},{1,9},{9,1},{17,25},{25,17},{2,10},{10... | collective-permute-start | bytes 49160 | tf_op jit(solution)/shard_map/ppermute | solution.py:332
  67.6 5.7 %collective-permute-start.24 = (f32[32,128]{1,0:T(8,128)S(1)}, f32[32,128]{1,0:T(8,128)S(1)}, u32[]{:S(2)}, u32[]{:S(2)}) collective-permute-start(f32[32,128]{1,0:T(8,128)S(1)} %share_sum.2.refs_0_), channel_id=1, source_target_pairs={{0,6},{1,7},{2,4},{3,5},{4,2},{5,3},{6,0},{7,1},{8,14},{9,15},{10,... | collective-permute-start | bytes 49160 | tf_op jit(solution)/shard_map/ppermute | solution.py:332
  69.2 4.7 %collective-permute-start.23 = (f32[32,128]{1,0:T(8,128)S(1)}, f32[32,128]{1,0:T(8,128)S(1)}, u32[]{:S(2)}, u32[]{:S(2)}) collective-permute-start(f32[32,128]{1,0:T(8,128)S(1)} %share_sum.2.refs_0_), channel_id=1, source_target_pairs={{0,4},{1,5},{2,6},{3,7},{4,0},{5,1},{6,2},{7,3},{8,12},{9,13},{10,... | collective-permute-start | bytes 49160 | tf_op jit(solution)/shard_map/ppermute | solution.py:332
  70.0 3.9 %collective-permute-start.22 = (f32[32,128]{1,0:T(8,128)S(1)}, f32[32,128]{1,0:T(8,128)S(1)}, u32[]{:S(2)}, u32[]{:S(2)}) collective-permute-start(f32[32,128]{1,0:T(8,128)S(1)} %share_sum.2.refs_0_), channel_id=1, source_target_pairs={{0,2},{1,3},{2,0},{3,1},{4,6},{5,7},{6,4},{7,5},{8,10},{9,11},{10,... | collective-permute-start | bytes 49160 | tf_op jit(solution)/shard_map/ppermute | solution.py:332
  74.0 3.3 %collective-permute-start.27 = (f32[32,128]{1,0:T(8,128)S(1)}, f32[32,128]{1,0:T(8,128)S(1)}, u32[]{:S(2)}, u32[]{:S(2)}) collective-permute-start(f32[32,128]{1,0:T(8,128)S(1)} %share_sum.3.refs_0_), channel_id=1, source_target_pairs={{0,24},{8,16},{16,8},{24,0},{1,25},{9,17},{17,9},{25,1},{2,26},{10... | collective-permute-start | bytes 49160 | tf_op jit(solution)/shard_map/ppermute | solution.py:332
  74.0 3.8 %collective-permute-start.26 = (f32[32,128]{1,0:T(8,128)S(1)}, f32[32,128]{1,0:T(8,128)S(1)}, u32[]{:S(2)}, u32[]{:S(2)}) collective-permute-start(f32[32,128]{1,0:T(8,128)S(1)} %share_sum.3.refs_0_), channel_id=1, source_target_pairs={{0,16},{8,24},{16,0},{24,8},{1,17},{9,25},{17,1},{25,9},{2,18},{10... | collective-permute-start | bytes 49160 | tf_op jit(solution)/shard_map/ppermute | solution.py:332
  75.6 2.2 %collective-permute-start.25 = (f32[32,128]{1,0:T(8,128)S(1)}, f32[32,128]{1,0:T(8,128)S(1)}, u32[]{:S(2)}, u32[]{:S(2)}) collective-permute-start(f32[32,128]{1,0:T(8,128)S(1)} %share_sum.3.refs_0_), channel_id=1, source_target_pairs={{0,8},{8,0},{16,24},{24,16},{1,9},{9,1},{17,25},{25,17},{2,10},{10... | collective-permute-start | bytes 49160 | tf_op jit(solution)/shard_map/ppermute | solution.py:332

commit v10 on v9

--- a/solution.py
+++ b/solution.py
@@ -90,7 +90,7 @@
 
 
 def prepare(
-    scale, source_hbm, map_hbm, target_hbm, pot_hbm, source, left_out, turned_out, right_out, plain_out,
+    scale, source_hbm, map_hbm, target_hbm, pot_hbm, source, left_out, right_out, plain_out,
     start_map, target, pot, sems,
 ):
     copies = [
@@ -110,11 +110,9 @@
         right_out[at, :width] = target[at, :]
         right_out[at, width:] = lane_parts(to_column(pot[:, at] * (1.0 / scale)))
     left_out[...] = jnp.dot(source[...], start_map[...].astype(BF16), preferred_element_type=F32).astype(BF16)
-    for at in range(0, source.shape[0], LANES):
-        turned_out[:, at : at + LANES] = left_out[at : at + LANES, :].T
-
-
-def row_first(unit, left_in, right, lse_out, work, peaks, totals, sums):
+
+
+def row_first(unit, left_in, right, lse_out, turned_out, work, peaks, totals, sums):
     rows = left_in.shape[0]
     lane = lax.broadcasted_iota(jnp.int32, (CHUNK, LANES), 1)
     ones = jnp.where(lane < 3, 1.0, 0.0).astype(BF16)
@@ -127,6 +125,8 @@
             peak = functools.reduce(jnp.maximum, tiles)
             peaks[at : at + group, :] = peak
             totals[at : at + group, :] = functools.reduce(jnp.add, [jnp.exp2((tile - peak) * unit) for tile in tiles])
+        for at in range(start, start + CHUNK, LANES):
+            turned_out[:, at : at + LANES] = left_in[at : at + LANES, :].T
     for part in range(rows // LANES):
         here = slice(part * LANES, (part + 1) * LANES)
         lane_peak = peaks[here, :]
@@ -316,9 +316,10 @@
     for k, share in enumerate(shares):
         square[pl.ds(pl.multiple_of((index ^ k) * height, height), height), :] = share[...]
     cross = square[...]
-    iterate = cross / jnp.sqrt(jnp.sum(cross * cross) + 1e-06)
     unity = jnp.where(eye_mask(), 1.0, 0.0)
-    error = unity - precise(iterate, iterate, 0)
+    square_sum = jnp.sum(cross * cross) + 1e-06
+    error = unity - precise(cross, cross, 0) / square_sum
+    iterate = cross / jnp.sqrt(square_sum)
     size = error.shape[0]
     for step in range(NEWTON - 1):
         both = precise(jnp.concatenate([error, iterate], axis=0), error)
@@ -359,13 +360,12 @@
     pair_vec = jax.ShapeDtypeStruct((1, 2 * cols), F32)
     mac = rows * cols * width
 
-    source, left, turned, right, plain = call(
+    source, left, right, plain = call(
         functools.partial(prepare, scale),
         "prepare",
         (
             jax.ShapeDtypeStruct((rows, width), BF16),
             jax.ShapeDtypeStruct((rows, width), BF16),
-            jax.ShapeDtypeStruct((width, rows), BF16),
             jax.ShapeDtypeStruct((cols, width + LANES), BF16),
             jax.ShapeDtypeStruct((cols, width), F32),
         ),
@@ -379,10 +379,10 @@
         space=pltpu.HBM,
     )(*[pltpu.with_memory_space_constraint(x, pltpu.HBM) for x in (source, start_map, target, warm_potential.reshape(1, cols))])
     other = lax.ppermute(plain, "tgt", [(me, me ^ 1) for me in range(n_tgt)])
-    lse = call(
+    lse, turned = call(
         functools.partial(row_first, unit),
         "row_first",
-        row_vec,
+        (row_vec, jax.ShapeDtypeStruct((width, rows), BF16)),
         scratch=[
             pltpu.VMEM((rows, cols), F32),
             pltpu.VMEM((rows, LANES), F32),

time: 81.9 us -> 81.6 us (level)
  no operation moved by 1% of the time
where the time goes in v10:
time: 81.6 us; the launch traced here: 81.4 us
  starting transfers between devices  30.4 us (37%)
  Pallas kernels  22.3 us (27%)
  waiting for transfers between devices  16.4 us (20%)
  blocking collectives  11.6 us (14%)
    ppermute x27, starting transfers between devices, partners(): lax.ppermute(values[k], axis, [(me, me ^ k) for me in range(size)])  27.4 us
    pallas_call x14, Pallas kernels, call(): pl.pallas_call(body, name=name, out_shape=out_shape, in_specs=[pl.BlockSp...  22.3 us
    ppermute x27, waiting for transfers between devices, partners(): lax.ppermute(values[k], axis, [(me, me ^ k) for me in range(size)])  16.4 us
    all_to_all x1, blocking collectives, over_tgt(): lax.all_to_all(jnp.broadcast_to(x, (lax.axis_size('tgt'),) + x.shape), 't...  11.6 us
    ppermute x1, starting transfers between devices, shards(): other = lax.ppermute(plain, 'tgt', [(me, me ^ 1) for me in range(n_tgt)])  3 us
  transfers between devices with their start and end apart: 28, of which 20 were waited for; matrix products, arithmetic and copies ran while one was open for 0% of the time, Pallas kernels for 6%

profile of v10, /device:TPU:0, one launch (start us, length us, event | category | flops | bytes accessed | tf_op | source)
XLA Modules:
  0.0 81.4 jit_solution(3574179634468318930)
XLA Ops:
  0.6 1.6 %prepare.1 = (bf16[2048,128]{1,0:T(8,128)(2,1)S(1)}, bf16[2048,128]{1,0:T(8,128)(2,1)S(1)}, bf16[1024,256]{1,0:T(8,128)(2,1)S(1)}, f32[1024,128]{1,0:T(8,128)S(1)}) custom-call(bf16[2048,128]{1,0:T(8,128)(2,1)} %source_hbm.1, f32[128,128]{1,0:T(8,128)} %map_hbm.1, bf16[1024,128]{1,0:T(8,128)(2,1)} %target_hbm.1, f32[1,1024]{1,0:T(1,128)} %bitcast.3), custom_call_target="tpu_custom_call" | custom-call | flops 67108864 | bytes 8388608 | tf_op jit(solution)/shard_map/prepare/pallas_call | solution.py:22
  2.2 3.0 %collective-permute-start = (f32[1024,128]{1,0:T(8,128)S(1)}, f32[1024,128]{1,0:T(8,128)S(1)}, u32[]{:S(2)}, u32[]{:S(2)}) collective-permute-start(f32[1024,128]{1,0:T(8,128)S(1)} %get-tuple-element.30), channel_id=1, source_target_pairs={{0,1},{1,0},{2,3},{3,2},{4,5},{5,4},{6,7},{7,6},{8,9},{9,8},{10,11... | collective-permute-start | bytes 1572872 | tf_op jit(solution)/shard_map/ppermute | solution.py:381
  5.2 2.2 %row_first.1 = (f32[16,128]{1,0:T(8,128)S(1)}, bf16[128,2048]{1,0:T(8,128)(2,1)S(1)}) custom-call(bf16[2048,128]{1,0:T(8,128)(2,1)S(1)} %get-tuple-element.27.left_in, bf16[1024,256]{1,0:T(8,128)(2,1)S(1)} %get-tuple-element.28.right.own), custom_call_target="tpu_custom_call" | custom-call | flops 1073741824 | bytes 8388608 | tf_op jit(solution)/shard_map/row_first/pallas_call | solution.py:22
  7.4 11.6 %all_to_all.5.refs_0_ = f32[8,16,128]{2,1,0:T(8,128)S(1)} all-to-all(f32[8,16,128]{2,1,0:T(8,128)S(1)} %broadcast_in_dim.3), channel_id=1, replica_groups=mesh['src'=4,'tgt'=8] {'tgt'}, dimensions={0} | all-to-all | bytes 131072 | tf_op jit(solution)/shard_map/all_to_all | solution.py:347
  19.0 5.0 %col_first.1 = (bf16[2048,2048]{1,0:T(8,128)(2,1)S(1)}, bf16[2048,128]{1,0:T(8,128)(2,1)S(1)}, f32[16,128]{1,0:T(8,128)S(1)}, f32[1,2048]{1,0:T(1,128)S(1)}, f32[1,2048]{1,0:T(1,128)S(1)}) custom-call(bf16[128,2048]{1,0:T(8,128)(2,1)S(1)} %get-tuple-element.29.turned, bf16[1024,256]{1,0:T(8,128)(2,1)S(1)} %get-tuple-element.28.right.own, ...), custom_call_target="tpu_custom_call" | custom-call | flops 2147483648 | bytes 8388608 | tf_op jit(solution)/shard_map/col_first/pallas_call | solution.py:22
  24.0 1.6 %collective-permute-start.2 = (f32[1,2048]{1,0:T(1,128)S(1)}, f32[1,2048]{1,0:T(1,128)S(1)}, u32[]{:S(2)}, u32[]{:S(2)}) collective-permute-start(f32[1,2048]{1,0:T(1,128)S(1)} %get-tuple-element.36.refs_0_), channel_id=1, source_target_pairs={{0,16},{8,24},{16,0},{24,8},{1,17},{9,25},{17,1},{25,9},{2,18},{10... | collective-permute-start | bytes 24584 | tf_op jit(solution)/shard_map/ppermute | solution.py:333
  25.8 1.2 %collective-permute-done.3.refs_3_ = f32[1,2048]{1,0:T(1,128)S(1)} collective-permute-done((f32[1,2048]{1,0:T(1,128)S(1)}, f32[1,2048]{1,0:T(1,128)S(1)}, u32[]{:S(2)}, u32[]{:S(2)}) %collective-permute-start.3) | collective-permute-done | bytes 8224 | tf_op jit(solution)/shard_map/ppermute | solution.py:333
  27.7 1.1 %row_second.1 = (f32[1,2048]{1,0:T(1,128)S(1)}, f32[1,2048]{1,0:T(1,128)S(1)}, f32[16,128]{1,0:T(8,128)S(1)}) custom-call(bf16[2048,2048]{1,0:T(8,128)(2,1)S(1)} %get-tuple-element.34.block, f32[1,2048]{1,0:T(1,128)S(1)} %get-tuple-element.35.peak, f32[1,2048]{1,0:T(1,128)S(1)} %get-tuple-element.36.refs_0_, f32[1,2048]{1,0:T(1,128)S(1)} %collective-permute-done.1.refs_1_, ...), custom_call_target="tpu_custom_call" | custom-call | flops 1073741824 | bytes 8388608 | tf_op jit(solution)/shard_map/row_second/pallas_call | solution.py:22
  28.9 2.8 %collective-permute-start.6 = (f32[16,128]{1,0:T(8,128)S(1)}, f32[16,128]{1,0:T(8,128)S(1)}, u32[]{:S(2)}, u32[]{:S(2)}) collective-permute-start(f32[16,128]{1,0:T(8,128)S(1)} %get-tuple-element.38.refs_0_), channel_id=1, source_target_pairs={{0,6},{1,7},{2,4},{3,5},{4,2},{5,3},{6,0},{7,1},{8,14},{9,15},{10,... | collective-permute-start | bytes 24584 | tf_op jit(solution)/shard_map/ppermute | solution.py:333
  31.7 1.6 %collective-permute-start.4 = (f32[16,128]{1,0:T(8,128)S(1)}, f32[16,128]{1,0:T(8,128)S(1)}, u32[]{:S(2)}, u32[]{:S(2)}) collective-permute-start(f32[16,128]{1,0:T(8,128)S(1)} %get-tuple-element.38.refs_0_), channel_id=1, source_target_pairs={{0,2},{1,3},{2,0},{3,1},{4,6},{5,7},{6,4},{7,5},{8,10},{9,11},{10,... | collective-permute-start | bytes 24584 | tf_op jit(solution)/shard_map/ppermute | solution.py:333
  33.3 1.1 %collective-permute-done.6.refs_3_ = f32[16,128]{1,0:T(8,128)S(1)} collective-permute-done((f32[16,128]{1,0:T(8,128)S(1)}, f32[16,128]{1,0:T(8,128)S(1)}, u32[]{:S(2)}, u32[]{:S(2)}) %collective-permute-start.6) | collective-permute-done | bytes 8224 | tf_op jit(solution)/shard_map/ppermute | solution.py:333
  34.5 1.8 %collective-permute-done.5.refs_2_ = f32[16,128]{1,0:T(8,128)S(1)} collective-permute-done((f32[16,128]{1,0:T(8,128)S(1)}, f32[16,128]{1,0:T(8,128)S(1)}, u32[]{:S(2)}, u32[]{:S(2)}) %collective-permute-start.5) | collective-permute-done | bytes 8224 | tf_op jit(solution)/shard_map/ppermute | solution.py:333
  36.2 1.7 %col_later.2.refs_0_ = f32[1,2048]{1,0:T(1,128)S(1)} custom-call(bf16[2048,2048]{1,0:T(8,128)(2,1)S(1)} %get-tuple-element.34.block, f32[1,2048]{1,0:T(1,128)S(1)} %get-tuple-element.37.scale, f32[16,128]{1,0:T(8,128)S(1)} %get-tuple-element.38.refs_0_, f32[16,128]{1,0:T(8,128)S(1)} %collective-permute-done.4.refs_1_, ...), custom_call_target="tpu_custom_call" | custom-call | flops 1073741824 | bytes 8388608 | tf_op jit(solution)/shard_map/col_later/pallas_call | solution.py:22
  38.0 1.5 %collective-permute-start.8 = (f32[1,2048]{1,0:T(1,128)S(1)}, f32[1,2048]{1,0:T(1,128)S(1)}, u32[]{:S(2)}, u32[]{:S(2)}) collective-permute-start(f32[1,2048]{1,0:T(1,128)S(1)} %col_later.2.refs_0_), channel_id=1, source_target_pairs={{0,16},{8,24},{16,0},{24,8},{1,17},{9,25},{17,1},{25,9},{2,18},{10... | collective-permute-start | bytes 24584 | tf_op jit(solution)/shard_map/ppermute | solution.py:333
  39.9 1.3 %collective-permute-done.9.refs_3_ = f32[1,2048]{1,0:T(1,128)S(1)} collective-permute-done((f32[1,2048]{1,0:T(1,128)S(1)}, f32[1,2048]{1,0:T(1,128)S(1)}, u32[]{:S(2)}, u32[]{:S(2)}) %collective-permute-start.9) | collective-permute-done | bytes 8224 | tf_op jit(solution)/shard_map/ppermute | solution.py:333
  41.8 1.1 %row_later.1.refs_0_ = f32[16,128]{1,0:T(8,128)S(1)} custom-call(bf16[2048,2048]{1,0:T(8,128)(2,1)S(1)} %get-tuple-element.34.block, f32[1,2048]{1,0:T(1,128)S(1)} %get-tuple-element.37.scale, f32[1,2048]{1,0:T(1,128)S(1)} %col_later.2.refs_0_, f32[1,2048]{1,0:T(1,128)S(1)} %collective-permute-done.7.refs_1_, f32[1,2048]{1,0:T(1,128)S(1)} %collective-permute-done.8.refs_2_, ...), custom_call_target="tpu_custom_call" | custom-call | flops 1073741824 | bytes 8388608 | tf_op jit(solution)/shard_map/row_later/pallas_call | solution.py:22
  42.9 1.5 %collective-permute-start.12 = (f32[16,128]{1,0:T(8,128)S(1)}, f32[16,128]{1,0:T(8,128)S(1)}, u32[]{:S(2)}, u32[]{:S(2)}) collective-permute-start(f32[16,128]{1,0:T(8,128)S(1)} %row_later.1.refs_0_), channel_id=1, source_target_pairs={{0,6},{1,7},{2,4},{3,5},{4,2},{5,3},{6,0},{7,1},{8,14},{9,15},{10,... | collective-permute-start | bytes 24584 | tf_op jit(solution)/shard_map/ppermute | solution.py:333
  45.1 2.2 %collective-permute-start.10 = (f32[16,128]{1,0:T(8,128)S(1)}, f32[16,128]{1,0:T(8,128)S(1)}, u32[]{:S(2)}, u32[]{:S(2)}) collective-permute-start(f32[16,128]{1,0:T(8,128)S(1)} %row_later.1.refs_0_), channel_id=1, source_target_pairs={{0,2},{1,3},{2,0},{3,1},{4,6},{5,7},{6,4},{7,5},{8,10},{9,11},{10,... | collective-permute-start | bytes 24584 | tf_op jit(solution)/shard_map/ppermute | solution.py:333
  47.3 1.1 %collective-permute-done.12.refs_3_ = f32[16,128]{1,0:T(8,128)S(1)} collective-permute-done((f32[16,128]{1,0:T(8,128)S(1)}, f32[16,128]{1,0:T(8,128)S(1)}, u32[]{:S(2)}, u32[]{:S(2)}) %collective-permute-start.12) | collective-permute-done | bytes 8224 | tf_op jit(solution)/shard_map/ppermute | solution.py:333
  49.1 1.7 %col_later.3.refs_0_ = f32[1,2048]{1,0:T(1,128)S(1)} custom-call(bf16[2048,2048]{1,0:T(8,128)(2,1)S(1)} %get-tuple-element.34.block, f32[1,2048]{1,0:T(1,128)S(1)} %get-tuple-element.37.scale, f32[16,128]{1,0:T(8,128)S(1)} %row_later.1.refs_0_, f32[16,128]{1,0:T(8,128)S(1)} %collective-permute-done.10.refs_1_, ...), custom_call_target="tpu_custom_call" | custom-call | flops 1073741824 | bytes 8388608 | tf_op jit(solution)/shard_map/col_later/pallas_call | solution.py:22
  50.8 1.5 %collective-permute-start.14 = (f32[1,2048]{1,0:T(1,128)S(1)}, f32[1,2048]{1,0:T(1,128)S(1)}, u32[]{:S(2)}, u32[]{:S(2)}) collective-permute-start(f32[1,2048]{1,0:T(1,128)S(1)} %col_later.3.refs_0_), channel_id=1, source_target_pairs={{0,16},{8,24},{16,0},{24,8},{1,17},{9,25},{17,1},{25,9},{2,18},{10... | collective-permute-start | bytes 24584 | tf_op jit(solution)/shard_map/ppermute | solution.py:333
  52.7 1.3 %collective-permute-done.15.refs_3_ = f32[1,2048]{1,0:T(1,128)S(1)} collective-permute-done((f32[1,2048]{1,0:T(1,128)S(1)}, f32[1,2048]{1,0:T(1,128)S(1)}, u32[]{:S(2)}, u32[]{:S(2)}) %collective-permute-start.15) | collective-permute-done | bytes 8224 | tf_op jit(solution)/shard_map/ppermute | solution.py:333
  54.6 1.3 %row_last.1 = (f32[1,2048]{1,0:T(1,128)S(1)}, f32[1,2048]{1,0:T(1,128)S(1)}, f32[16,128]{1,0:T(8,128)S(1)}) custom-call(bf16[2048,2048]{1,0:T(8,128)(2,1)S(1)} %get-tuple-element.34.block, f32[1,2048]{1,0:T(1,128)S(1)} %get-tuple-element.37.scale, f32[1,2048]{1,0:T(1,128)S(1)} %col_later.3.refs_0_, f32[1,2048]{1,0:T(1,128)S(1)} %collective-permute-done.13.refs_1_, ...), custom_call_target="tpu_custom_call" | custom-call | flops 1073741824 | bytes 8388608 | tf_op jit(solution)/shard_map/row_last/pallas_call | solution.py:22
  55.9 2.6 %collective-permute-start.18 = (f32[16,128]{1,0:T(8,128)S(1)}, f32[16,128]{1,0:T(8,128)S(1)}, u32[]{:S(2)}, u32[]{:S(2)}) collective-permute-start(f32[16,128]{1,0:T(8,128)S(1)} %get-tuple-element.44.refs_0_), channel_id=1, source_target_pairs={{0,6},{1,7},{2,4},{3,5},{4,2},{5,3},{6,0},{7,1},{8,14},{9,15},{10,... | collective-permute-start | bytes 24584 | tf_op jit(solution)/shard_map/ppermute | solution.py:333
  60.4 1.8 %barycentre.1 = (f32[128,2048]{1,0:T(8,128)S(1)}, f32[1,1024]{1,0:T(1,128)}) custom-call(bf16[2048,2048]{1,0:T(8,128)(2,1)S(1)} %get-tuple-element.34.block, f32[1,2048]{1,0:T(1,128)S(1)} %get-tuple-element.39.factor, bf16[2048,128]{1,0:T(8,128)(2,1)S(1)} %get-tuple-element.40.target, f32[1,2048]{1,0:T(1,128)S(1)} %get-tuple-element.41.pot, ...), custom_call_target="tpu_custom_call" | custom-call | flops 1073741824 | bytes 8388608 | tf_op jit(solution)/shard_map/barycentre/pallas_call | solution.py:22
  63.7 1.5 %collective-permute-start.20 = (f32[32,128]{1,0:T(8,128)S(1)}, f32[32,128]{1,0:T(8,128)S(1)}, u32[]{:S(2)}, u32[]{:S(2)}) collective-permute-start(f32[32,128]{1,0:T(8,128)S(1)} %get-tuple-element.48), channel_id=1, source_target_pairs={{0,16},{8,24},{16,0},{24,8},{1,17},{9,25},{17,1},{25,9},{2,18},{10... | collective-permute-start | bytes 49160 | tf_op jit(solution)/shard_map/ppermute | solution.py:333
  65.6 1.4 %collective-permute-done.19.refs_0_ = f32[32,128]{1,0:T(8,128)S(1)} collective-permute-done((f32[32,128]{1,0:T(8,128)S(1)}, f32[32,128]{1,0:T(8,128)S(1)}, u32[]{:S(2)}, u32[]{:S(2)}) %collective-permute-start.19) | collective-permute-done | bytes 16416 | tf_op jit(solution)/shard_map/ppermute | solution.py:333
  67.5 1.6 %collective-permute-start.24 = (f32[32,128]{1,0:T(8,128)S(1)}, f32[32,128]{1,0:T(8,128)S(1)}, u32[]{:S(2)}, u32[]{:S(2)}) collective-permute-start(f32[32,128]{1,0:T(8,128)S(1)} %share_sum.2.refs_0_), channel_id=1, source_target_pairs={{0,6},{1,7},{2,4},{3,5},{4,2},{5,3},{6,0},{7,1},{8,14},{9,15},{10,... | collective-permute-start | bytes 49160 | tf_op jit(solution)/shard_map/ppermute | solution.py:333
  69.9 2.0 %collective-permute-start.22 = (f32[32,128]{1,0:T(8,128)S(1)}, f32[32,128]{1,0:T(8,128)S(1)}, u32[]{:S(2)}, u32[]{:S(2)}) collective-permute-start(f32[32,128]{1,0:T(8,128)S(1)} %share_sum.2.refs_0_), channel_id=1, source_target_pairs={{0,2},{1,3},{2,0},{3,1},{4,6},{5,7},{6,4},{7,5},{8,10},{9,11},{10,... | collective-permute-start | bytes 49160 | tf_op jit(solution)/shard_map/ppermute | solution.py:333
  72.0 1.2 %collective-permute-done.24.refs_3_ = f32[32,128]{1,0:T(8,128)S(1)} collective-permute-done((f32[32,128]{1,0:T(8,128)S(1)}, f32[32,128]{1,0:T(8,128)S(1)}, u32[]{:S(2)}, u32[]{:S(2)}) %collective-permute-start.24) | collective-permute-done | bytes 16416 | tf_op jit(solution)/shard_map/ppermute | solution.py:333
  74.0 1.5 %collective-permute-start.26 = (f32[32,128]{1,0:T(8,128)S(1)}, f32[32,128]{1,0:T(8,128)S(1)}, u32[]{:S(2)}, u32[]{:S(2)}) collective-permute-start(f32[32,128]{1,0:T(8,128)S(1)} %share_sum.3.refs_0_), channel_id=1, source_target_pairs={{0,16},{8,24},{16,0},{24,8},{1,17},{9,25},{17,1},{25,9},{2,18},{10... | collective-permute-start | bytes 49160 | tf_op jit(solution)/shard_map/ppermute | solution.py:333
  77.8 3.7 %polar.1 = f32[128,128]{1,0:T(8,128)} custom-call(f32[32,128]{1,0:T(8,128)S(1)} %share_sum.3.refs_0_, f32[32,128]{1,0:T(8,128)S(1)} %collective-permute-done.25.refs_1_, f32[32,128]{1,0:T(8,128)S(1)} %collective-permute-done.26.refs_2_, f32[32,128]{1,0:T(8,128)S(1)} %collective-permute-done.27.refs_3_), custom_call_target="tpu_custom_call" | custom-call | flops 134217728 | bytes 8388608 | tf_op jit(solution)/shard_map/polar/pallas_call | solution.py:22
  (40 shorter events, 12.4 us)
Async XLA Ops:
  2.2 16.8 %collective-permute-start = (f32[1024,128]{1,0:T(8,128)S(1)}, f32[1024,128]{1,0:T(8,128)S(1)}, u32[]{:S(2)}, u32[]{:S(2)}) collective-permute-start(f32[1024,128]{1,0:T(8,128)S(1)} %get-tuple-element.30), channel_id=1, source_target_pairs={{0,1},{1,0},{2,3},{3,2},{4,5},{5,4},{6,7},{7,6},{8,9},{9,8},{10,11... | collective-permute-start | bytes 1572872 | tf_op jit(solution)/shard_map/ppermute | solution.py:381
  23.9 3.1 %collective-permute-start.3 = (f32[1,2048]{1,0:T(1,128)S(1)}, f32[1,2048]{1,0:T(1,128)S(1)}, u32[]{:S(2)}, u32[]{:S(2)}) collective-permute-start(f32[1,2048]{1,0:T(1,128)S(1)} %get-tuple-element.36.refs_0_), channel_id=1, source_target_pairs={{0,24},{8,16},{16,8},{24,0},{1,25},{9,17},{17,9},{25,1},{2,26},{10... | collective-permute-start | bytes 24584 | tf_op jit(solution)/shard_map/ppermute | solution.py:333
  24.0 3.7 %collective-permute-start.2 = (f32[1,2048]{1,0:T(1,128)S(1)}, f32[1,2048]{1,0:T(1,128)S(1)}, u32[]{:S(2)}, u32[]{:S(2)}) collective-permute-start(f32[1,2048]{1,0:T(1,128)S(1)} %get-tuple-element.36.refs_0_), channel_id=1, source_target_pairs={{0,16},{8,24},{16,0},{24,8},{1,17},{9,25},{17,1},{25,9},{2,18},{10... | collective-permute-start | bytes 24584 | tf_op jit(solution)/shard_map/ppermute | solution.py:333
  25.6 2.1 %collective-permute-start.1 = (f32[1,2048]{1,0:T(1,128)S(1)}, f32[1,2048]{1,0:T(1,128)S(1)}, u32[]{:S(2)}, u32[]{:S(2)}) collective-permute-start(f32[1,2048]{1,0:T(1,128)S(1)} %get-tuple-element.36.refs_0_), channel_id=1, source_target_pairs={{0,8},{8,0},{16,24},{24,16},{1,9},{9,1},{17,25},{25,17},{2,10},{10... | collective-permute-start | bytes 24584 | tf_op jit(solution)/shard_map/ppermute | solution.py:333
  28.9 5.6 %collective-permute-start.6 = (f32[16,128]{1,0:T(8,128)S(1)}, f32[16,128]{1,0:T(8,128)S(1)}, u32[]{:S(2)}, u32[]{:S(2)}) collective-permute-start(f32[16,128]{1,0:T(8,128)S(1)} %get-tuple-element.38.refs_0_), channel_id=1, source_target_pairs={{0,6},{1,7},{2,4},{3,5},{4,2},{5,3},{6,0},{7,1},{8,14},{9,15},{10,... | collective-permute-start | bytes 24584 | tf_op jit(solution)/shard_map/ppermute | solution.py:333
  31.7 4.5 %collective-permute-start.5 = (f32[16,128]{1,0:T(8,128)S(1)}, f32[16,128]{1,0:T(8,128)S(1)}, u32[]{:S(2)}, u32[]{:S(2)}) collective-permute-start(f32[16,128]{1,0:T(8,128)S(1)} %get-tuple-element.38.refs_0_), channel_id=1, source_target_pairs={{0,4},{1,5},{2,6},{3,7},{4,0},{5,1},{6,2},{7,3},{8,12},{9,13},{10,... | collective-permute-start | bytes 24584 | tf_op jit(solution)/shard_map/ppermute | solution.py:333
  31.7 4.5 %collective-permute-start.4 = (f32[16,128]{1,0:T(8,128)S(1)}, f32[16,128]{1,0:T(8,128)S(1)}, u32[]{:S(2)}, u32[]{:S(2)}) collective-permute-start(f32[16,128]{1,0:T(8,128)S(1)} %get-tuple-element.38.refs_0_), channel_id=1, source_target_pairs={{0,2},{1,3},{2,0},{3,1},{4,6},{5,7},{6,4},{7,5},{8,10},{9,11},{10,... | collective-permute-start | bytes 24584 | tf_op jit(solution)/shard_map/ppermute | solution.py:333
  38.0 3.2 %collective-permute-start.9 = (f32[1,2048]{1,0:T(1,128)S(1)}, f32[1,2048]{1,0:T(1,128)S(1)}, u32[]{:S(2)}, u32[]{:S(2)}) collective-permute-start(f32[1,2048]{1,0:T(1,128)S(1)} %col_later.2.refs_0_), channel_id=1, source_target_pairs={{0,24},{8,16},{16,8},{24,0},{1,25},{9,17},{17,9},{25,1},{2,26},{10... | collective-permute-start | bytes 24584 | tf_op jit(solution)/shard_map/ppermute | solution.py:333
  38.0 3.7 %collective-permute-start.8 = (f32[1,2048]{1,0:T(1,128)S(1)}, f32[1,2048]{1,0:T(1,128)S(1)}, u32[]{:S(2)}, u32[]{:S(2)}) collective-permute-start(f32[1,2048]{1,0:T(1,128)S(1)} %col_later.2.refs_0_), channel_id=1, source_target_pairs={{0,16},{8,24},{16,0},{24,8},{1,17},{9,25},{17,1},{25,9},{2,18},{10... | collective-permute-start | bytes 24584 | tf_op jit(solution)/shard_map/ppermute | solution.py:333
  39.6 2.2 %collective-permute-start.7 = (f32[1,2048]{1,0:T(1,128)S(1)}, f32[1,2048]{1,0:T(1,128)S(1)}, u32[]{:S(2)}, u32[]{:S(2)}) collective-permute-start(f32[1,2048]{1,0:T(1,128)S(1)} %col_later.2.refs_0_), channel_id=1, source_target_pairs={{0,8},{8,0},{16,24},{24,16},{1,9},{9,1},{17,25},{25,17},{2,10},{10... | collective-permute-start | bytes 24584 | tf_op jit(solution)/shard_map/ppermute | solution.py:333
  42.9 5.5 %collective-permute-start.12 = (f32[16,128]{1,0:T(8,128)S(1)}, f32[16,128]{1,0:T(8,128)S(1)}, u32[]{:S(2)}, u32[]{:S(2)}) collective-permute-start(f32[16,128]{1,0:T(8,128)S(1)} %row_later.1.refs_0_), channel_id=1, source_target_pairs={{0,6},{1,7},{2,4},{3,5},{4,2},{5,3},{6,0},{7,1},{8,14},{9,15},{10,... | collective-permute-start | bytes 24584 | tf_op jit(solution)/shard_map/ppermute | solution.py:333
  44.4 4.6 %collective-permute-start.11 = (f32[16,128]{1,0:T(8,128)S(1)}, f32[16,128]{1,0:T(8,128)S(1)}, u32[]{:S(2)}, u32[]{:S(2)}) collective-permute-start(f32[16,128]{1,0:T(8,128)S(1)} %row_later.1.refs_0_), channel_id=1, source_target_pairs={{0,4},{1,5},{2,6},{3,7},{4,0},{5,1},{6,2},{7,3},{8,12},{9,13},{10,... | collective-permute-start | bytes 24584 | tf_op jit(solution)/shard_map/ppermute | solution.py:333
  45.1 3.9 %collective-permute-start.10 = (f32[16,128]{1,0:T(8,128)S(1)}, f32[16,128]{1,0:T(8,128)S(1)}, u32[]{:S(2)}, u32[]{:S(2)}) collective-permute-start(f32[16,128]{1,0:T(8,128)S(1)} %row_later.1.refs_0_), channel_id=1, source_target_pairs={{0,2},{1,3},{2,0},{3,1},{4,6},{5,7},{6,4},{7,5},{8,10},{9,11},{10,... | collective-permute-start | bytes 24584 | tf_op jit(solution)/shard_map/ppermute | solution.py:333
  50.8 3.2 %collective-permute-start.15 = (f32[1,2048]{1,0:T(1,128)S(1)}, f32[1,2048]{1,0:T(1,128)S(1)}, u32[]{:S(2)}, u32[]{:S(2)}) collective-permute-start(f32[1,2048]{1,0:T(1,128)S(1)} %col_later.3.refs_0_), channel_id=1, source_target_pairs={{0,24},{8,16},{16,8},{24,0},{1,25},{9,17},{17,9},{25,1},{2,26},{10... | collective-permute-start | bytes 24584 | tf_op jit(solution)/shard_map/ppermute | solution.py:333
  50.8 3.7 %collective-permute-start.14 = (f32[1,2048]{1,0:T(1,128)S(1)}, f32[1,2048]{1,0:T(1,128)S(1)}, u32[]{:S(2)}, u32[]{:S(2)}) collective-permute-start(f32[1,2048]{1,0:T(1,128)S(1)} %col_later.3.refs_0_), channel_id=1, source_target_pairs={{0,16},{8,24},{16,0},{24,8},{1,17},{9,25},{17,1},{25,9},{2,18},{10... | collective-permute-start | bytes 24584 | tf_op jit(solution)/shard_map/ppermute | solution.py:333
  52.4 2.2 %collective-permute-start.13 = (f32[1,2048]{1,0:T(1,128)S(1)}, f32[1,2048]{1,0:T(1,128)S(1)}, u32[]{:S(2)}, u32[]{:S(2)}) collective-permute-start(f32[1,2048]{1,0:T(1,128)S(1)} %col_later.3.refs_0_), channel_id=1, source_target_pairs={{0,8},{8,0},{16,24},{24,16},{1,9},{9,1},{17,25},{25,17},{2,10},{10... | collective-permute-start | bytes 24584 | tf_op jit(solution)/shard_map/ppermute | solution.py:333
  55.9 6.2 %collective-permute-start.18 = (f32[16,128]{1,0:T(8,128)S(1)}, f32[16,128]{1,0:T(8,128)S(1)}, u32[]{:S(2)}, u32[]{:S(2)}) collective-permute-start(f32[16,128]{1,0:T(8,128)S(1)} %get-tuple-element.44.refs_0_), channel_id=1, source_target_pairs={{0,6},{1,7},{2,4},{3,5},{4,2},{5,3},{6,0},{7,1},{8,14},{9,15},{10,... | collective-permute-start | bytes 24584 | tf_op jit(solution)/shard_map/ppermute | solution.py:333
  58.5 4.6 %collective-permute-start.17 = (f32[16,128]{1,0:T(8,128)S(1)}, f32[16,128]{1,0:T(8,128)S(1)}, u32[]{:S(2)}, u32[]{:S(2)}) collective-permute-start(f32[16,128]{1,0:T(8,128)S(1)} %get-tuple-element.44.refs_0_), channel_id=1, source_target_pairs={{0,4},{1,5},{2,6},{3,7},{4,0},{5,1},{6,2},{7,3},{8,12},{9,13},{10,... | collective-permute-start | bytes 24584 | tf_op jit(solution)/shard_map/ppermute | solution.py:333
  59.4 3.7 %collective-permute-start.16 = (f32[16,128]{1,0:T(8,128)S(1)}, f32[16,128]{1,0:T(8,128)S(1)}, u32[]{:S(2)}, u32[]{:S(2)}) collective-permute-start(f32[16,128]{1,0:T(8,128)S(1)} %get-tuple-element.44.refs_0_), channel_id=1, source_target_pairs={{0,2},{1,3},{2,0},{3,1},{4,6},{5,7},{6,4},{7,5},{8,10},{9,11},{10,... | collective-permute-start | bytes 24584 | tf_op jit(solution)/shard_map/ppermute | solution.py:333
  63.6 3.4 %collective-permute-start.19 = (f32[32,128]{1,0:T(8,128)S(1)}, f32[32,128]{1,0:T(8,128)S(1)}, u32[]{:S(2)}, u32[]{:S(2)}) collective-permute-start(f32[32,128]{1,0:T(8,128)S(1)} %get-tuple-element.47), channel_id=1, source_target_pairs={{0,24},{8,16},{16,8},{24,0},{1,25},{9,17},{17,9},{25,1},{2,26},{10... | collective-permute-start | bytes 49160 | tf_op jit(solution)/shard_map/ppermute | solution.py:333
  63.7 3.8 %collective-permute-start.20 = (f32[32,128]{1,0:T(8,128)S(1)}, f32[32,128]{1,0:T(8,128)S(1)}, u32[]{:S(2)}, u32[]{:S(2)}) collective-permute-start(f32[32,128]{1,0:T(8,128)S(1)} %get-tuple-element.48), channel_id=1, source_target_pairs={{0,16},{8,24},{16,0},{24,8},{1,17},{9,25},{17,1},{25,9},{2,18},{10... | collective-permute-start | bytes 49160 | tf_op jit(solution)/shard_map/ppermute | solution.py:333
  65.2 2.3 %collective-permute-start.21 = (f32[32,128]{1,0:T(8,128)S(1)}, f32[32,128]{1,0:T(8,128)S(1)}, u32[]{:S(2)}, u32[]{:S(2)}) collective-permute-start(f32[32,128]{1,0:T(8,128)S(1)} %get-tuple-element.49), channel_id=1, source_target_pairs={{0,8},{8,0},{16,24},{24,16},{1,9},{9,1},{17,25},{25,17},{2,10},{10... | collective-permute-start | bytes 49160 | tf_op jit(solution)/shard_map/ppermute | solution.py:333
  67.5 5.7 %collective-permute-start.24 = (f32[32,128]{1,0:T(8,128)S(1)}, f32[32,128]{1,0:T(8,128)S(1)}, u32[]{:S(2)}, u32[]{:S(2)}) collective-permute-start(f32[32,128]{1,0:T(8,128)S(1)} %share_sum.2.refs_0_), channel_id=1, source_target_pairs={{0,6},{1,7},{2,4},{3,5},{4,2},{5,3},{6,0},{7,1},{8,14},{9,15},{10,... | collective-permute-start | bytes 49160 | tf_op jit(solution)/shard_map/ppermute | solution.py:333
  69.1 4.7 %collective-permute-start.23 = (f32[32,128]{1,0:T(8,128)S(1)}, f32[32,128]{1,0:T(8,128)S(1)}, u32[]{:S(2)}, u32[]{:S(2)}) collective-permute-start(f32[32,128]{1,0:T(8,128)S(1)} %share_sum.2.refs_0_), channel_id=1, source_target_pairs={{0,4},{1,5},{2,6},{3,7},{4,0},{5,1},{6,2},{7,3},{8,12},{9,13},{10,... | collective-permute-start | bytes 49160 | tf_op jit(solution)/shard_map/ppermute | solution.py:333
  69.9 3.9 %collective-permute-start.22 = (f32[32,128]{1,0:T(8,128)S(1)}, f32[32,128]{1,0:T(8,128)S(1)}, u32[]{:S(2)}, u32[]{:S(2)}) collective-permute-start(f32[32,128]{1,0:T(8,128)S(1)} %share_sum.2.refs_0_), channel_id=1, source_target_pairs={{0,2},{1,3},{2,0},{3,1},{4,6},{5,7},{6,4},{7,5},{8,10},{9,11},{10,... | collective-permute-start | bytes 49160 | tf_op jit(solution)/shard_map/ppermute | solution.py:333
  73.9 3.4 %collective-permute-start.27 = (f32[32,128]{1,0:T(8,128)S(1)}, f32[32,128]{1,0:T(8,128)S(1)}, u32[]{:S(2)}, u32[]{:S(2)}) collective-permute-start(f32[32,128]{1,0:T(8,128)S(1)} %share_sum.3.refs_0_), channel_id=1, source_target_pairs={{0,24},{8,16},{16,8},{24,0},{1,25},{9,17},{17,9},{25,1},{2,26},{10... | collective-permute-start | bytes 49160 | tf_op jit(solution)/shard_map/ppermute | solution.py:333
  74.0 3.8 %collective-permute-start.26 = (f32[32,128]{1,0:T(8,128)S(1)}, f32[32,128]{1,0:T(8,128)S(1)}, u32[]{:S(2)}, u32[]{:S(2)}) collective-permute-start(f32[32,128]{1,0:T(8,128)S(1)} %share_sum.3.refs_0_), channel_id=1, source_target_pairs={{0,16},{8,24},{16,0},{24,8},{1,17},{9,25},{17,1},{25,9},{2,18},{10... | collective-permute-start | bytes 49160 | tf_op jit(solution)/shard_map/ppermute | solution.py:333
  75.5 2.3 %collective-permute-start.25 = (f32[32,128]{1,0:T(8,128)S(1)}, f32[32,128]{1,0:T(8,128)S(1)}, u32[]{:S(2)}, u32[]{:S(2)}) collective-permute-start(f32[32,128]{1,0:T(8,128)S(1)} %share_sum.3.refs_0_), channel_id=1, source_target_pairs={{0,8},{8,0},{16,24},{24,16},{1,9},{9,1},{17,25},{25,17},{2,10},{10... | collective-permute-start | bytes 49160 | tf_op jit(solution)/shard_map/ppermute | solution.py:333

commit v11 on v10

--- a/solution.py
+++ b/solution.py
@@ -200,7 +200,7 @@
 
 def sums_down(block, row, out):
     rows, cols = block.shape
-    cut = cols * 3 // 4 // LANES * LANES
+    cut = cols * 5 // 8 // LANES * LANES
     pair = two_rows(row)
     product = jnp.zeros((16, cut), F32)
     total = jnp.zeros((8, cols - cut), F32)
@@ -217,7 +217,7 @@
 
 def sums_across(block, row, out):
     rows, cols = block.shape
-    cut = cols // 4 // LANES * LANES
+    cut = cols * 3 // 8 // LANES * LANES
     first = lax.broadcasted_iota(jnp.int32, (16, 2 * LANES), 0) == 0
     pair = jnp.concatenate([two_rows(row[:, :cut]), jnp.where(first, 1.0, 0.0).astype(BF16)], axis=1)
     tiles = [(at, jnp.broadcast_to(row[:, at : at + LANES], (16, LANES))) for at in range(cut, cols, LANES)]

time: 81.6 us -> 82 us (level)
  no operation moved by 1% of the time
where the time goes in v11:
time: 82 us; the launch traced here: 81.8 us
  starting transfers between devices  30.4 us (37%)
  Pallas kernels  22.6 us (28%)
  waiting for transfers between devices  16.4 us (20%)
  blocking collectives  11.6 us (14%)
    ppermute x27, starting transfers between devices, partners(): lax.ppermute(values[k], axis, [(me, me ^ k) for me in range(size)])  27.4 us
    pallas_call x14, Pallas kernels, call(): pl.pallas_call(body, name=name, out_shape=out_shape, in_specs=[pl.BlockSp...  22.6 us
    ppermute x27, waiting for transfers between devices, partners(): lax.ppermute(values[k], axis, [(me, me ^ k) for me in range(size)])  16.4 us
    all_to_all x1, blocking collectives, over_tgt(): lax.all_to_all(jnp.broadcast_to(x, (lax.axis_size('tgt'),) + x.shape), 't...  11.6 us
    ppermute x1, starting transfers between devices, shards(): other = lax.ppermute(plain, 'tgt', [(me, me ^ 1) for me in range(n_tgt)])  3 us
  transfers between devices with their start and end apart: 28, of which 20 were waited for; matrix products, arithmetic and copies ran while one was open for 0% of the time, Pallas kernels for 6%

profile of v11, /device:TPU:0, one launch (start us, length us, event | category | flops | bytes accessed | tf_op | source)
XLA Modules:
  0.0 81.8 jit_solution(8785211475790125521)
XLA Ops:
  0.6 1.6 %prepare.1 = (bf16[2048,128]{1,0:T(8,128)(2,1)S(1)}, bf16[2048,128]{1,0:T(8,128)(2,1)S(1)}, bf16[1024,256]{1,0:T(8,128)(2,1)S(1)}, f32[1024,128]{1,0:T(8,128)S(1)}) custom-call(bf16[2048,128]{1,0:T(8,128)(2,1)} %source_hbm.1, f32[128,128]{1,0:T(8,128)} %map_hbm.1, bf16[1024,128]{1,0:T(8,128)(2,1)} %target_hbm.1, f32[1,1024]{1,0:T(1,128)} %bitcast.3), custom_call_target="tpu_custom_call" | custom-call | flops 67108864 | bytes 8388608 | tf_op jit(solution)/shard_map/prepare/pallas_call | solution.py:22
  2.2 3.0 %collective-permute-start = (f32[1024,128]{1,0:T(8,128)S(1)}, f32[1024,128]{1,0:T(8,128)S(1)}, u32[]{:S(2)}, u32[]{:S(2)}) collective-permute-start(f32[1024,128]{1,0:T(8,128)S(1)} %get-tuple-element.30), channel_id=1, source_target_pairs={{0,1},{1,0},{2,3},{3,2},{4,5},{5,4},{6,7},{7,6},{8,9},{9,8},{10,11... | collective-permute-start | bytes 1572872 | tf_op jit(solution)/shard_map/ppermute | solution.py:381
  5.2 2.2 %row_first.1 = (f32[16,128]{1,0:T(8,128)S(1)}, bf16[128,2048]{1,0:T(8,128)(2,1)S(1)}) custom-call(bf16[2048,128]{1,0:T(8,128)(2,1)S(1)} %get-tuple-element.27.left_in, bf16[1024,256]{1,0:T(8,128)(2,1)S(1)} %get-tuple-element.28.right.own), custom_call_target="tpu_custom_call" | custom-call | flops 1073741824 | bytes 8388608 | tf_op jit(solution)/shard_map/row_first/pallas_call | solution.py:22
  7.4 11.6 %all_to_all.5.refs_0_ = f32[8,16,128]{2,1,0:T(8,128)S(1)} all-to-all(f32[8,16,128]{2,1,0:T(8,128)S(1)} %broadcast_in_dim.3), channel_id=1, replica_groups=mesh['src'=4,'tgt'=8] {'tgt'}, dimensions={0} | all-to-all | bytes 131072 | tf_op jit(solution)/shard_map/all_to_all | solution.py:347
  19.0 5.0 %col_first.1 = (bf16[2048,2048]{1,0:T(8,128)(2,1)S(1)}, bf16[2048,128]{1,0:T(8,128)(2,1)S(1)}, f32[16,128]{1,0:T(8,128)S(1)}, f32[1,2048]{1,0:T(1,128)S(1)}, f32[1,2048]{1,0:T(1,128)S(1)}) custom-call(bf16[128,2048]{1,0:T(8,128)(2,1)S(1)} %get-tuple-element.29.turned, bf16[1024,256]{1,0:T(8,128)(2,1)S(1)} %get-tuple-element.28.right.own, ...), custom_call_target="tpu_custom_call" | custom-call | flops 2147483648 | bytes 8388608 | tf_op jit(solution)/shard_map/col_first/pallas_call | solution.py:22
  24.0 1.6 %collective-permute-start.2 = (f32[1,2048]{1,0:T(1,128)S(1)}, f32[1,2048]{1,0:T(1,128)S(1)}, u32[]{:S(2)}, u32[]{:S(2)}) collective-permute-start(f32[1,2048]{1,0:T(1,128)S(1)} %get-tuple-element.36.refs_0_), channel_id=1, source_target_pairs={{0,16},{8,24},{16,0},{24,8},{1,17},{9,25},{17,1},{25,9},{2,18},{10... | collective-permute-start | bytes 24584 | tf_op jit(solution)/shard_map/ppermute | solution.py:333
  25.8 1.2 %collective-permute-done.3.refs_3_ = f32[1,2048]{1,0:T(1,128)S(1)} collective-permute-done((f32[1,2048]{1,0:T(1,128)S(1)}, f32[1,2048]{1,0:T(1,128)S(1)}, u32[]{:S(2)}, u32[]{:S(2)}) %collective-permute-start.3) | collective-permute-done | bytes 8224 | tf_op jit(solution)/shard_map/ppermute | solution.py:333
  27.7 1.2 %row_second.1 = (f32[1,2048]{1,0:T(1,128)S(1)}, f32[1,2048]{1,0:T(1,128)S(1)}, f32[16,128]{1,0:T(8,128)S(1)}) custom-call(bf16[2048,2048]{1,0:T(8,128)(2,1)S(1)} %get-tuple-element.34.block, f32[1,2048]{1,0:T(1,128)S(1)} %get-tuple-element.35.peak, f32[1,2048]{1,0:T(1,128)S(1)} %get-tuple-element.36.refs_0_, f32[1,2048]{1,0:T(1,128)S(1)} %collective-permute-done.1.refs_1_, ...), custom_call_target="tpu_custom_call" | custom-call | flops 1073741824 | bytes 8388608 | tf_op jit(solution)/shard_map/row_second/pallas_call | solution.py:22
  28.9 2.8 %collective-permute-start.6 = (f32[16,128]{1,0:T(8,128)S(1)}, f32[16,128]{1,0:T(8,128)S(1)}, u32[]{:S(2)}, u32[]{:S(2)}) collective-permute-start(f32[16,128]{1,0:T(8,128)S(1)} %get-tuple-element.38.refs_0_), channel_id=1, source_target_pairs={{0,6},{1,7},{2,4},{3,5},{4,2},{5,3},{6,0},{7,1},{8,14},{9,15},{10,... | collective-permute-start | bytes 24584 | tf_op jit(solution)/shard_map/ppermute | solution.py:333
  31.8 1.6 %collective-permute-start.4 = (f32[16,128]{1,0:T(8,128)S(1)}, f32[16,128]{1,0:T(8,128)S(1)}, u32[]{:S(2)}, u32[]{:S(2)}) collective-permute-start(f32[16,128]{1,0:T(8,128)S(1)} %get-tuple-element.38.refs_0_), channel_id=1, source_target_pairs={{0,2},{1,3},{2,0},{3,1},{4,6},{5,7},{6,4},{7,5},{8,10},{9,11},{10,... | collective-permute-start | bytes 24584 | tf_op jit(solution)/shard_map/ppermute | solution.py:333
  33.4 1.1 %collective-permute-done.6.refs_3_ = f32[16,128]{1,0:T(8,128)S(1)} collective-permute-done((f32[16,128]{1,0:T(8,128)S(1)}, f32[16,128]{1,0:T(8,128)S(1)}, u32[]{:S(2)}, u32[]{:S(2)}) %collective-permute-start.6) | collective-permute-done | bytes 8224 | tf_op jit(solution)/shard_map/ppermute | solution.py:333
  34.5 1.8 %collective-permute-done.5.refs_2_ = f32[16,128]{1,0:T(8,128)S(1)} collective-permute-done((f32[16,128]{1,0:T(8,128)S(1)}, f32[16,128]{1,0:T(8,128)S(1)}, u32[]{:S(2)}, u32[]{:S(2)}) %collective-permute-start.5) | collective-permute-done | bytes 8224 | tf_op jit(solution)/shard_map/ppermute | solution.py:333
  36.3 1.8 %col_later.2.refs_0_ = f32[1,2048]{1,0:T(1,128)S(1)} custom-call(bf16[2048,2048]{1,0:T(8,128)(2,1)S(1)} %get-tuple-element.34.block, f32[1,2048]{1,0:T(1,128)S(1)} %get-tuple-element.37.scale, f32[16,128]{1,0:T(8,128)S(1)} %get-tuple-element.38.refs_0_, f32[16,128]{1,0:T(8,128)S(1)} %collective-permute-done.4.refs_1_, ...), custom_call_target="tpu_custom_call" | custom-call | flops 1073741824 | bytes 8388608 | tf_op jit(solution)/shard_map/col_later/pallas_call | solution.py:22
  38.2 1.5 %collective-permute-start.8 = (f32[1,2048]{1,0:T(1,128)S(1)}, f32[1,2048]{1,0:T(1,128)S(1)}, u32[]{:S(2)}, u32[]{:S(2)}) collective-permute-start(f32[1,2048]{1,0:T(1,128)S(1)} %col_later.2.refs_0_), channel_id=1, source_target_pairs={{0,16},{8,24},{16,0},{24,8},{1,17},{9,25},{17,1},{25,9},{2,18},{10... | collective-permute-start | bytes 24584 | tf_op jit(solution)/shard_map/ppermute | solution.py:333
  40.0 1.3 %collective-permute-done.9.refs_3_ = f32[1,2048]{1,0:T(1,128)S(1)} collective-permute-done((f32[1,2048]{1,0:T(1,128)S(1)}, f32[1,2048]{1,0:T(1,128)S(1)}, u32[]{:S(2)}, u32[]{:S(2)}) %collective-permute-start.9) | collective-permute-done | bytes 8224 | tf_op jit(solution)/shard_map/ppermute | solution.py:333
  41.9 1.2 %row_later.1.refs_0_ = f32[16,128]{1,0:T(8,128)S(1)} custom-call(bf16[2048,2048]{1,0:T(8,128)(2,1)S(1)} %get-tuple-element.34.block, f32[1,2048]{1,0:T(1,128)S(1)} %get-tuple-element.37.scale, f32[1,2048]{1,0:T(1,128)S(1)} %col_later.2.refs_0_, f32[1,2048]{1,0:T(1,128)S(1)} %collective-permute-done.7.refs_1_, f32[1,2048]{1,0:T(1,128)S(1)} %collective-permute-done.8.refs_2_, ...), custom_call_target="tpu_custom_call" | custom-call | flops 1073741824 | bytes 8388608 | tf_op jit(solution)/shard_map/row_later/pallas_call | solution.py:22
  43.1 1.5 %collective-permute-start.12 = (f32[16,128]{1,0:T(8,128)S(1)}, f32[16,128]{1,0:T(8,128)S(1)}, u32[]{:S(2)}, u32[]{:S(2)}) collective-permute-start(f32[16,128]{1,0:T(8,128)S(1)} %row_later.1.refs_0_), channel_id=1, source_target_pairs={{0,6},{1,7},{2,4},{3,5},{4,2},{5,3},{6,0},{7,1},{8,14},{9,15},{10,... | collective-permute-start | bytes 24584 | tf_op jit(solution)/shard_map/ppermute | solution.py:333
  45.3 2.2 %collective-permute-start.10 = (f32[16,128]{1,0:T(8,128)S(1)}, f32[16,128]{1,0:T(8,128)S(1)}, u32[]{:S(2)}, u32[]{:S(2)}) collective-permute-start(f32[16,128]{1,0:T(8,128)S(1)} %row_later.1.refs_0_), channel_id=1, source_target_pairs={{0,2},{1,3},{2,0},{3,1},{4,6},{5,7},{6,4},{7,5},{8,10},{9,11},{10,... | collective-permute-start | bytes 24584 | tf_op jit(solution)/shard_map/ppermute | solution.py:333
  47.5 1.1 %collective-permute-done.12.refs_3_ = f32[16,128]{1,0:T(8,128)S(1)} collective-permute-done((f32[16,128]{1,0:T(8,128)S(1)}, f32[16,128]{1,0:T(8,128)S(1)}, u32[]{:S(2)}, u32[]{:S(2)}) %collective-permute-start.12) | collective-permute-done | bytes 8224 | tf_op jit(solution)/shard_map/ppermute | solution.py:333
  49.3 1.8 %col_later.3.refs_0_ = f32[1,2048]{1,0:T(1,128)S(1)} custom-call(bf16[2048,2048]{1,0:T(8,128)(2,1)S(1)} %get-tuple-element.34.block, f32[1,2048]{1,0:T(1,128)S(1)} %get-tuple-element.37.scale, f32[16,128]{1,0:T(8,128)S(1)} %row_later.1.refs_0_, f32[16,128]{1,0:T(8,128)S(1)} %collective-permute-done.10.refs_1_, ...), custom_call_target="tpu_custom_call" | custom-call | flops 1073741824 | bytes 8388608 | tf_op jit(solution)/shard_map/col_later/pallas_call | solution.py:22
  51.1 1.5 %collective-permute-start.14 = (f32[1,2048]{1,0:T(1,128)S(1)}, f32[1,2048]{1,0:T(1,128)S(1)}, u32[]{:S(2)}, u32[]{:S(2)}) collective-permute-start(f32[1,2048]{1,0:T(1,128)S(1)} %col_later.3.refs_0_), channel_id=1, source_target_pairs={{0,16},{8,24},{16,0},{24,8},{1,17},{9,25},{17,1},{25,9},{2,18},{10... | collective-permute-start | bytes 24584 | tf_op jit(solution)/shard_map/ppermute | solution.py:333
  53.0 1.3 %collective-permute-done.15.refs_3_ = f32[1,2048]{1,0:T(1,128)S(1)} collective-permute-done((f32[1,2048]{1,0:T(1,128)S(1)}, f32[1,2048]{1,0:T(1,128)S(1)}, u32[]{:S(2)}, u32[]{:S(2)}) %collective-permute-start.15) | collective-permute-done | bytes 8224 | tf_op jit(solution)/shard_map/ppermute | solution.py:333
  54.8 1.4 %row_last.1 = (f32[1,2048]{1,0:T(1,128)S(1)}, f32[1,2048]{1,0:T(1,128)S(1)}, f32[16,128]{1,0:T(8,128)S(1)}) custom-call(bf16[2048,2048]{1,0:T(8,128)(2,1)S(1)} %get-tuple-element.34.block, f32[1,2048]{1,0:T(1,128)S(1)} %get-tuple-element.37.scale, f32[1,2048]{1,0:T(1,128)S(1)} %col_later.3.refs_0_, f32[1,2048]{1,0:T(1,128)S(1)} %collective-permute-done.13.refs_1_, ...), custom_call_target="tpu_custom_call" | custom-call | flops 1073741824 | bytes 8388608 | tf_op jit(solution)/shard_map/row_last/pallas_call | solution.py:22
  56.2 2.6 %collective-permute-start.18 = (f32[16,128]{1,0:T(8,128)S(1)}, f32[16,128]{1,0:T(8,128)S(1)}, u32[]{:S(2)}, u32[]{:S(2)}) collective-permute-start(f32[16,128]{1,0:T(8,128)S(1)} %get-tuple-element.44.refs_0_), channel_id=1, source_target_pairs={{0,6},{1,7},{2,4},{3,5},{4,2},{5,3},{6,0},{7,1},{8,14},{9,15},{10,... | collective-permute-start | bytes 24584 | tf_op jit(solution)/shard_map/ppermute | solution.py:333
  60.7 1.8 %barycentre.1 = (f32[128,2048]{1,0:T(8,128)S(1)}, f32[1,1024]{1,0:T(1,128)}) custom-call(bf16[2048,2048]{1,0:T(8,128)(2,1)S(1)} %get-tuple-element.34.block, f32[1,2048]{1,0:T(1,128)S(1)} %get-tuple-element.39.factor, bf16[2048,128]{1,0:T(8,128)(2,1)S(1)} %get-tuple-element.40.target, f32[1,2048]{1,0:T(1,128)S(1)} %get-tuple-element.41.pot, ...), custom_call_target="tpu_custom_call" | custom-call | flops 1073741824 | bytes 8388608 | tf_op jit(solution)/shard_map/barycentre/pallas_call | solution.py:22
  64.0 1.5 %collective-permute-start.20 = (f32[32,128]{1,0:T(8,128)S(1)}, f32[32,128]{1,0:T(8,128)S(1)}, u32[]{:S(2)}, u32[]{:S(2)}) collective-permute-start(f32[32,128]{1,0:T(8,128)S(1)} %get-tuple-element.48), channel_id=1, source_target_pairs={{0,16},{8,24},{16,0},{24,8},{1,17},{9,25},{17,1},{25,9},{2,18},{10... | collective-permute-start | bytes 49160 | tf_op jit(solution)/shard_map/ppermute | solution.py:333
  65.9 1.5 %collective-permute-done.19.refs_0_ = f32[32,128]{1,0:T(8,128)S(1)} collective-permute-done((f32[32,128]{1,0:T(8,128)S(1)}, f32[32,128]{1,0:T(8,128)S(1)}, u32[]{:S(2)}, u32[]{:S(2)}) %collective-permute-start.19) | collective-permute-done | bytes 16416 | tf_op jit(solution)/shard_map/ppermute | solution.py:333
  67.9 1.6 %collective-permute-start.24 = (f32[32,128]{1,0:T(8,128)S(1)}, f32[32,128]{1,0:T(8,128)S(1)}, u32[]{:S(2)}, u32[]{:S(2)}) collective-permute-start(f32[32,128]{1,0:T(8,128)S(1)} %share_sum.2.refs_0_), channel_id=1, source_target_pairs={{0,6},{1,7},{2,4},{3,5},{4,2},{5,3},{6,0},{7,1},{8,14},{9,15},{10,... | collective-permute-start | bytes 49160 | tf_op jit(solution)/shard_map/ppermute | solution.py:333
  70.3 2.0 %collective-permute-start.22 = (f32[32,128]{1,0:T(8,128)S(1)}, f32[32,128]{1,0:T(8,128)S(1)}, u32[]{:S(2)}, u32[]{:S(2)}) collective-permute-start(f32[32,128]{1,0:T(8,128)S(1)} %share_sum.2.refs_0_), channel_id=1, source_target_pairs={{0,2},{1,3},{2,0},{3,1},{4,6},{5,7},{6,4},{7,5},{8,10},{9,11},{10,... | collective-permute-start | bytes 49160 | tf_op jit(solution)/shard_map/ppermute | solution.py:333
  72.3 1.2 %collective-permute-done.24.refs_3_ = f32[32,128]{1,0:T(8,128)S(1)} collective-permute-done((f32[32,128]{1,0:T(8,128)S(1)}, f32[32,128]{1,0:T(8,128)S(1)}, u32[]{:S(2)}, u32[]{:S(2)}) %collective-permute-start.24) | collective-permute-done | bytes 16416 | tf_op jit(solution)/shard_map/ppermute | solution.py:333
  74.3 1.5 %collective-permute-start.26 = (f32[32,128]{1,0:T(8,128)S(1)}, f32[32,128]{1,0:T(8,128)S(1)}, u32[]{:S(2)}, u32[]{:S(2)}) collective-permute-start(f32[32,128]{1,0:T(8,128)S(1)} %share_sum.3.refs_0_), channel_id=1, source_target_pairs={{0,16},{8,24},{16,0},{24,8},{1,17},{9,25},{17,1},{25,9},{2,18},{10... | collective-permute-start | bytes 49160 | tf_op jit(solution)/shard_map/ppermute | solution.py:333
  78.1 3.7 %polar.1 = f32[128,128]{1,0:T(8,128)} custom-call(f32[32,128]{1,0:T(8,128)S(1)} %share_sum.3.refs_0_, f32[32,128]{1,0:T(8,128)S(1)} %collective-permute-done.25.refs_1_, f32[32,128]{1,0:T(8,128)S(1)} %collective-permute-done.26.refs_2_, f32[32,128]{1,0:T(8,128)S(1)} %collective-permute-done.27.refs_3_), custom_call_target="tpu_custom_call" | custom-call | flops 134217728 | bytes 8388608 | tf_op jit(solution)/shard_map/polar/pallas_call | solution.py:22
  (40 shorter events, 12.4 us)
Async XLA Ops:
  2.2 16.8 %collective-permute-start = (f32[1024,128]{1,0:T(8,128)S(1)}, f32[1024,128]{1,0:T(8,128)S(1)}, u32[]{:S(2)}, u32[]{:S(2)}) collective-permute-start(f32[1024,128]{1,0:T(8,128)S(1)} %get-tuple-element.30), channel_id=1, source_target_pairs={{0,1},{1,0},{2,3},{3,2},{4,5},{5,4},{6,7},{7,6},{8,9},{9,8},{10,11... | collective-permute-start | bytes 1572872 | tf_op jit(solution)/shard_map/ppermute | solution.py:381
  23.9 3.1 %collective-permute-start.3 = (f32[1,2048]{1,0:T(1,128)S(1)}, f32[1,2048]{1,0:T(1,128)S(1)}, u32[]{:S(2)}, u32[]{:S(2)}) collective-permute-start(f32[1,2048]{1,0:T(1,128)S(1)} %get-tuple-element.36.refs_0_), channel_id=1, source_target_pairs={{0,24},{8,16},{16,8},{24,0},{1,25},{9,17},{17,9},{25,1},{2,26},{10... | collective-permute-start | bytes 24584 | tf_op jit(solution)/shard_map/ppermute | solution.py:333
  24.0 3.7 %collective-permute-start.2 = (f32[1,2048]{1,0:T(1,128)S(1)}, f32[1,2048]{1,0:T(1,128)S(1)}, u32[]{:S(2)}, u32[]{:S(2)}) collective-permute-start(f32[1,2048]{1,0:T(1,128)S(1)} %get-tuple-element.36.refs_0_), channel_id=1, source_target_pairs={{0,16},{8,24},{16,0},{24,8},{1,17},{9,25},{17,1},{25,9},{2,18},{10... | collective-permute-start | bytes 24584 | tf_op jit(solution)/shard_map/ppermute | solution.py:333
  25.6 2.1 %collective-permute-start.1 = (f32[1,2048]{1,0:T(1,128)S(1)}, f32[1,2048]{1,0:T(1,128)S(1)}, u32[]{:S(2)}, u32[]{:S(2)}) collective-permute-start(f32[1,2048]{1,0:T(1,128)S(1)} %get-tuple-element.36.refs_0_), channel_id=1, source_target_pairs={{0,8},{8,0},{16,24},{24,16},{1,9},{9,1},{17,25},{25,17},{2,10},{10... | collective-permute-start | bytes 24584 | tf_op jit(solution)/shard_map/ppermute | solution.py:333
  28.9 5.6 %collective-permute-start.6 = (f32[16,128]{1,0:T(8,128)S(1)}, f32[16,128]{1,0:T(8,128)S(1)}, u32[]{:S(2)}, u32[]{:S(2)}) collective-permute-start(f32[16,128]{1,0:T(8,128)S(1)} %get-tuple-element.38.refs_0_), channel_id=1, source_target_pairs={{0,6},{1,7},{2,4},{3,5},{4,2},{5,3},{6,0},{7,1},{8,14},{9,15},{10,... | collective-permute-start | bytes 24584 | tf_op jit(solution)/shard_map/ppermute | solution.py:333
  31.8 4.5 %collective-permute-start.5 = (f32[16,128]{1,0:T(8,128)S(1)}, f32[16,128]{1,0:T(8,128)S(1)}, u32[]{:S(2)}, u32[]{:S(2)}) collective-permute-start(f32[16,128]{1,0:T(8,128)S(1)} %get-tuple-element.38.refs_0_), channel_id=1, source_target_pairs={{0,4},{1,5},{2,6},{3,7},{4,0},{5,1},{6,2},{7,3},{8,12},{9,13},{10,... | collective-permute-start | bytes 24584 | tf_op jit(solution)/shard_map/ppermute | solution.py:333
  31.8 4.5 %collective-permute-start.4 = (f32[16,128]{1,0:T(8,128)S(1)}, f32[16,128]{1,0:T(8,128)S(1)}, u32[]{:S(2)}, u32[]{:S(2)}) collective-permute-start(f32[16,128]{1,0:T(8,128)S(1)} %get-tuple-element.38.refs_0_), channel_id=1, source_target_pairs={{0,2},{1,3},{2,0},{3,1},{4,6},{5,7},{6,4},{7,5},{8,10},{9,11},{10,... | collective-permute-start | bytes 24584 | tf_op jit(solution)/shard_map/ppermute | solution.py:333
  38.1 3.2 %collective-permute-start.9 = (f32[1,2048]{1,0:T(1,128)S(1)}, f32[1,2048]{1,0:T(1,128)S(1)}, u32[]{:S(2)}, u32[]{:S(2)}) collective-permute-start(f32[1,2048]{1,0:T(1,128)S(1)} %col_later.2.refs_0_), channel_id=1, source_target_pairs={{0,24},{8,16},{16,8},{24,0},{1,25},{9,17},{17,9},{25,1},{2,26},{10... | collective-permute-start | bytes 24584 | tf_op jit(solution)/shard_map/ppermute | solution.py:333
  38.2 3.7 %collective-permute-start.8 = (f32[1,2048]{1,0:T(1,128)S(1)}, f32[1,2048]{1,0:T(1,128)S(1)}, u32[]{:S(2)}, u32[]{:S(2)}) collective-permute-start(f32[1,2048]{1,0:T(1,128)S(1)} %col_later.2.refs_0_), channel_id=1, source_target_pairs={{0,16},{8,24},{16,0},{24,8},{1,17},{9,25},{17,1},{25,9},{2,18},{10... | collective-permute-start | bytes 24584 | tf_op jit(solution)/shard_map/ppermute | solution.py:333
  39.7 2.2 %collective-permute-start.7 = (f32[1,2048]{1,0:T(1,128)S(1)}, f32[1,2048]{1,0:T(1,128)S(1)}, u32[]{:S(2)}, u32[]{:S(2)}) collective-permute-start(f32[1,2048]{1,0:T(1,128)S(1)} %col_later.2.refs_0_), channel_id=1, source_target_pairs={{0,8},{8,0},{16,24},{24,16},{1,9},{9,1},{17,25},{25,17},{2,10},{10... | collective-permute-start | bytes 24584 | tf_op jit(solution)/shard_map/ppermute | solution.py:333
  43.1 5.5 %collective-permute-start.12 = (f32[16,128]{1,0:T(8,128)S(1)}, f32[16,128]{1,0:T(8,128)S(1)}, u32[]{:S(2)}, u32[]{:S(2)}) collective-permute-start(f32[16,128]{1,0:T(8,128)S(1)} %row_later.1.refs_0_), channel_id=1, source_target_pairs={{0,6},{1,7},{2,4},{3,5},{4,2},{5,3},{6,0},{7,1},{8,14},{9,15},{10,... | collective-permute-start | bytes 24584 | tf_op jit(solution)/shard_map/ppermute | solution.py:333
  44.6 4.6 %collective-permute-start.11 = (f32[16,128]{1,0:T(8,128)S(1)}, f32[16,128]{1,0:T(8,128)S(1)}, u32[]{:S(2)}, u32[]{:S(2)}) collective-permute-start(f32[16,128]{1,0:T(8,128)S(1)} %row_later.1.refs_0_), channel_id=1, source_target_pairs={{0,4},{1,5},{2,6},{3,7},{4,0},{5,1},{6,2},{7,3},{8,12},{9,13},{10,... | collective-permute-start | bytes 24584 | tf_op jit(solution)/shard_map/ppermute | solution.py:333
  45.3 3.9 %collective-permute-start.10 = (f32[16,128]{1,0:T(8,128)S(1)}, f32[16,128]{1,0:T(8,128)S(1)}, u32[]{:S(2)}, u32[]{:S(2)}) collective-permute-start(f32[16,128]{1,0:T(8,128)S(1)} %row_later.1.refs_0_), channel_id=1, source_target_pairs={{0,2},{1,3},{2,0},{3,1},{4,6},{5,7},{6,4},{7,5},{8,10},{9,11},{10,... | collective-permute-start | bytes 24584 | tf_op jit(solution)/shard_map/ppermute | solution.py:333
  51.0 3.2 %collective-permute-start.15 = (f32[1,2048]{1,0:T(1,128)S(1)}, f32[1,2048]{1,0:T(1,128)S(1)}, u32[]{:S(2)}, u32[]{:S(2)}) collective-permute-start(f32[1,2048]{1,0:T(1,128)S(1)} %col_later.3.refs_0_), channel_id=1, source_target_pairs={{0,24},{8,16},{16,8},{24,0},{1,25},{9,17},{17,9},{25,1},{2,26},{10... | collective-permute-start | bytes 24584 | tf_op jit(solution)/shard_map/ppermute | solution.py:333
  51.1 3.7 %collective-permute-start.14 = (f32[1,2048]{1,0:T(1,128)S(1)}, f32[1,2048]{1,0:T(1,128)S(1)}, u32[]{:S(2)}, u32[]{:S(2)}) collective-permute-start(f32[1,2048]{1,0:T(1,128)S(1)} %col_later.3.refs_0_), channel_id=1, source_target_pairs={{0,16},{8,24},{16,0},{24,8},{1,17},{9,25},{17,1},{25,9},{2,18},{10... | collective-permute-start | bytes 24584 | tf_op jit(solution)/shard_map/ppermute | solution.py:333
  52.6 2.2 %collective-permute-start.13 = (f32[1,2048]{1,0:T(1,128)S(1)}, f32[1,2048]{1,0:T(1,128)S(1)}, u32[]{:S(2)}, u32[]{:S(2)}) collective-permute-start(f32[1,2048]{1,0:T(1,128)S(1)} %col_later.3.refs_0_), channel_id=1, source_target_pairs={{0,8},{8,0},{16,24},{24,16},{1,9},{9,1},{17,25},{25,17},{2,10},{10... | collective-permute-start | bytes 24584 | tf_op jit(solution)/shard_map/ppermute | solution.py:333
  56.2 6.2 %collective-permute-start.18 = (f32[16,128]{1,0:T(8,128)S(1)}, f32[16,128]{1,0:T(8,128)S(1)}, u32[]{:S(2)}, u32[]{:S(2)}) collective-permute-start(f32[16,128]{1,0:T(8,128)S(1)} %get-tuple-element.44.refs_0_), channel_id=1, source_target_pairs={{0,6},{1,7},{2,4},{3,5},{4,2},{5,3},{6,0},{7,1},{8,14},{9,15},{10,... | collective-permute-start | bytes 24584 | tf_op jit(solution)/shard_map/ppermute | solution.py:333
  58.8 4.6 %collective-permute-start.17 = (f32[16,128]{1,0:T(8,128)S(1)}, f32[16,128]{1,0:T(8,128)S(1)}, u32[]{:S(2)}, u32[]{:S(2)}) collective-permute-start(f32[16,128]{1,0:T(8,128)S(1)} %get-tuple-element.44.refs_0_), channel_id=1, source_target_pairs={{0,4},{1,5},{2,6},{3,7},{4,0},{5,1},{6,2},{7,3},{8,12},{9,13},{10,... | collective-permute-start | bytes 24584 | tf_op jit(solution)/shard_map/ppermute | solution.py:333
  59.7 3.7 %collective-permute-start.16 = (f32[16,128]{1,0:T(8,128)S(1)}, f32[16,128]{1,0:T(8,128)S(1)}, u32[]{:S(2)}, u32[]{:S(2)}) collective-permute-start(f32[16,128]{1,0:T(8,128)S(1)} %get-tuple-element.44.refs_0_), channel_id=1, source_target_pairs={{0,2},{1,3},{2,0},{3,1},{4,6},{5,7},{6,4},{7,5},{8,10},{9,11},{10,... | collective-permute-start | bytes 24584 | tf_op jit(solution)/shard_map/ppermute | solution.py:333
  64.0 3.4 %collective-permute-start.19 = (f32[32,128]{1,0:T(8,128)S(1)}, f32[32,128]{1,0:T(8,128)S(1)}, u32[]{:S(2)}, u32[]{:S(2)}) collective-permute-start(f32[32,128]{1,0:T(8,128)S(1)} %get-tuple-element.47), channel_id=1, source_target_pairs={{0,24},{8,16},{16,8},{24,0},{1,25},{9,17},{17,9},{25,1},{2,26},{10... | collective-permute-start | bytes 49160 | tf_op jit(solution)/shard_map/ppermute | solution.py:333
  64.0 3.8 %collective-permute-start.20 = (f32[32,128]{1,0:T(8,128)S(1)}, f32[32,128]{1,0:T(8,128)S(1)}, u32[]{:S(2)}, u32[]{:S(2)}) collective-permute-start(f32[32,128]{1,0:T(8,128)S(1)} %get-tuple-element.48), channel_id=1, source_target_pairs={{0,16},{8,24},{16,0},{24,8},{1,17},{9,25},{17,1},{25,9},{2,18},{10... | collective-permute-start | bytes 49160 | tf_op jit(solution)/shard_map/ppermute | solution.py:333
  65.6 2.3 %collective-permute-start.21 = (f32[32,128]{1,0:T(8,128)S(1)}, f32[32,128]{1,0:T(8,128)S(1)}, u32[]{:S(2)}, u32[]{:S(2)}) collective-permute-start(f32[32,128]{1,0:T(8,128)S(1)} %get-tuple-element.49), channel_id=1, source_target_pairs={{0,8},{8,0},{16,24},{24,16},{1,9},{9,1},{17,25},{25,17},{2,10},{10... | collective-permute-start | bytes 49160 | tf_op jit(solution)/shard_map/ppermute | solution.py:333
  67.9 5.6 %collective-permute-start.24 = (f32[32,128]{1,0:T(8,128)S(1)}, f32[32,128]{1,0:T(8,128)S(1)}, u32[]{:S(2)}, u32[]{:S(2)}) collective-permute-start(f32[32,128]{1,0:T(8,128)S(1)} %share_sum.2.refs_0_), channel_id=1, source_target_pairs={{0,6},{1,7},{2,4},{3,5},{4,2},{5,3},{6,0},{7,1},{8,14},{9,15},{10,... | collective-permute-start | bytes 49160 | tf_op jit(solution)/shard_map/ppermute | solution.py:333
  69.5 4.7 %collective-permute-start.23 = (f32[32,128]{1,0:T(8,128)S(1)}, f32[32,128]{1,0:T(8,128)S(1)}, u32[]{:S(2)}, u32[]{:S(2)}) collective-permute-start(f32[32,128]{1,0:T(8,128)S(1)} %share_sum.2.refs_0_), channel_id=1, source_target_pairs={{0,4},{1,5},{2,6},{3,7},{4,0},{5,1},{6,2},{7,3},{8,12},{9,13},{10,... | collective-permute-start | bytes 49160 | tf_op jit(solution)/shard_map/ppermute | solution.py:333
  70.3 3.9 %collective-permute-start.22 = (f32[32,128]{1,0:T(8,128)S(1)}, f32[32,128]{1,0:T(8,128)S(1)}, u32[]{:S(2)}, u32[]{:S(2)}) collective-permute-start(f32[32,128]{1,0:T(8,128)S(1)} %share_sum.2.refs_0_), channel_id=1, source_target_pairs={{0,2},{1,3},{2,0},{3,1},{4,6},{5,7},{6,4},{7,5},{8,10},{9,11},{10,... | collective-permute-start | bytes 49160 | tf_op jit(solution)/shard_map/ppermute | solution.py:333
  74.2 3.4 %collective-permute-start.27 = (f32[32,128]{1,0:T(8,128)S(1)}, f32[32,128]{1,0:T(8,128)S(1)}, u32[]{:S(2)}, u32[]{:S(2)}) collective-permute-start(f32[32,128]{1,0:T(8,128)S(1)} %share_sum.3.refs_0_), channel_id=1, source_target_pairs={{0,24},{8,16},{16,8},{24,0},{1,25},{9,17},{17,9},{25,1},{2,26},{10... | collective-permute-start | bytes 49160 | tf_op jit(solution)/shard_map/ppermute | solution.py:333
  74.3 3.8 %collective-permute-start.26 = (f32[32,128]{1,0:T(8,128)S(1)}, f32[32,128]{1,0:T(8,128)S(1)}, u32[]{:S(2)}, u32[]{:S(2)}) collective-permute-start(f32[32,128]{1,0:T(8,128)S(1)} %share_sum.3.refs_0_), channel_id=1, source_target_pairs={{0,16},{8,24},{16,0},{24,8},{1,17},{9,25},{17,1},{25,9},{2,18},{10... | collective-permute-start | bytes 49160 | tf_op jit(solution)/shard_map/ppermute | solution.py:333
  75.8 2.3 %collective-permute-start.25 = (f32[32,128]{1,0:T(8,128)S(1)}, f32[32,128]{1,0:T(8,128)S(1)}, u32[]{:S(2)}, u32[]{:S(2)}) collective-permute-start(f32[32,128]{1,0:T(8,128)S(1)} %share_sum.3.refs_0_), channel_id=1, source_target_pairs={{0,8},{8,0},{16,24},{24,16},{1,9},{9,1},{17,25},{25,17},{2,10},{10... | collective-permute-start | bytes 49160 | tf_op jit(solution)/shard_map/ppermute | solution.py:333
